TPU v7x, 32 devices: a whole 2x2x4 slice. The times are simulated.
32 devices in a mesh: wide: 16 (over z, y, core), narrow: 2 (over x).
Axes of the slice: x: 2, y: 2, z: 4, core: 2. Of those that a mesh axis runs over, the one named last changes fastest.
Arguments:
- tokens: bfloat16 [128, 8192], P('wide', 'narrow'), may hold values from -6 to 6
- cotangent: bfloat16 [128, 8192], P('wide', 'narrow'), may hold values from -2.390625 to 2.390625
- gate_vals: bfloat16 [2, 16, 192, 128, 128], P('narrow', 'wide'), may hold values from -0.125 to 0.125
- up_vals: bfloat16 [2, 16, 192, 128, 128], P('narrow', 'wide'), may hold values from -0.125 to 0.125
- gu_index: int32 [2, 16, 192], P('narrow', 'wide'), may hold values from 0 to 255, as said below
- gu_count: int32 [2, 16], P('narrow', 'wide'), may hold values from 1 to 192, as said below
- down_vals: bfloat16 [16, 2, 192, 128, 128], P('wide', 'narrow'), may hold values from -0.09375 to 0.09375
- down_index: int32 [16, 2, 192], P('wide', 'narrow'), may hold values from 0 to 255, as said below
- down_count: int32 [16, 2], P('wide', 'narrow'), may hold values from 1 to 192, as said below
Outputs:
- d_tokens: bfloat16 [128, 8192], P('wide', 'narrow')
- gate_grad: bfloat16 [2, 16, 192, 128, 128], P('narrow', 'wide')
- up_grad: bfloat16 [2, 16, 192, 128, 128], P('narrow', 'wide')
- down_grad: bfloat16 [16, 2, 192, 128, 128], P('wide', 'narrow')
Inputs may be any that keep to these rules, and one draw needn't show every extreme that they name: `gu_index`: within each tile all 192 entries are different. `gu_count`: some tile has exactly 192 live slots. `down_index`: within each tile all 192 entries are different. `down_count`: some tile has exactly 192 live slots.
All inputs are finite; a program needn't handle non-finite values.
Results may differ from a plain program's by a relative error of at most 0.005.
Values may be sent and summed in bfloat16 or wider, within the bound.
No kernel may reach another device: no remote copies, remote signals or barrier semaphores. Data moves between devices by JAX's collectives and lax.ppermute only.
A program may use at most 192 MiB of HBM per device.

v0:
```python
import functools

import jax
import jax.numpy as jnp
from jax import lax
from jax.experimental import pallas as pl
from jax.experimental.pallas import tpu as pltpu
from jax.sharding import PartitionSpec as P

FF = 16384
F32 = jnp.float32
BF16 = jnp.bfloat16
VMEM_LIMIT = 24 * 1024 * 1024

WHOLE = pl.BlockSpec(memory_space=pltpu.VMEM)
SCALARS = pl.BlockSpec(memory_space=pltpu.SMEM)
ANYWHERE = pl.BlockSpec(memory_space=pl.ANY)


def params():
    return pltpu.CompilerParams(vmem_limit_bytes=VMEM_LIMIT)


def cost(flops, bytes_accessed):
    return pl.CostEstimate(flops=int(flops), bytes_accessed=int(bytes_accessed), transcendentals=0)


def resident(array):
    return pltpu.with_memory_space_constraint(array, pltpu.VMEM)


def swap(array, axis, size, flip):
    return lax.ppermute(array, axis, [(i, i ^ flip) for i in range(size)])


def fill_body(gu_index, gu_count, down_index, down_count, gate, up, down, gate_w, up_w, down_w, sem):
    f_blocks, d_blocks = gate_w.shape[:2]
    zeros = jnp.zeros(gate_w.shape[1:], gate_w.dtype)

    def clear(ref):
        @pl.loop(0, f_blocks)
        def _(c):
            ref[c] = zeros

    def gu_copies(s):
        place = gu_index[s]
        row, col = place // f_blocks, place % f_blocks
        return (
            pltpu.make_async_copy(gate.at[s], gate_w.at[col, row], sem.at[0]),
            pltpu.make_async_copy(up.at[s], up_w.at[col, row], sem.at[0]),
        )

    def down_copy(s):
        place = down_index[s]
        return pltpu.make_async_copy(
            down.at[s], down_w.at[place // d_blocks, place % d_blocks], sem.at[1]
        )

    clear(gate_w)
    clear(up_w)

    @pl.loop(0, gu_count[0])
    def _(s):
        for copy in gu_copies(s):
            copy.start()

    clear(down_w)

    @pl.loop(0, down_count[0])
    def _(s):
        down_copy(s).start()

    @pl.loop(0, gu_count[0])
    def _(s):
        for copy in gu_copies(s):
            copy.wait()

    @pl.loop(0, down_count[0])
    def _(s):
        down_copy(s).wait()


def fill(gu_index, gu_count, down_index, down_count, gate, up, down, f_blocks, d_blocks):
    block = gate.shape[-1]
    dense = pltpu.VMEM((f_blocks, d_blocks, block, block), BF16)
    return pl.pallas_call(
        fill_body,
        out_shape=(dense,) * 3,
        in_specs=[SCALARS] * 4 + [ANYWHERE] * 3,
        out_specs=(WHOLE,) * 3,
        scratch_shapes=[pltpu.SemaphoreType.DMA((2,))],
        compiler_params=params(),
        cost_estimate=cost(0, 3 * gate.size * 2),
        name="fill",
    )(gu_index, gu_count, down_index, down_count, gate, up, down)


def gate_up_body(mine, other, gate_w, up_w, own, send):
    f_blocks, d_blocks, block, _ = gate_w.shape
    x = jnp.concatenate([mine[...], other[...]], axis=0)

    @pl.loop(0, f_blocks)
    def _(c):
        weights = jnp.concatenate(
            [
                gate_w[c].reshape(d_blocks * block, block),
                up_w[c].reshape(d_blocks * block, block),
            ],
            axis=1,
        )
        result = jnp.dot(x, weights, preferred_element_type=F32)
        own[c] = result
        send[c] = result.astype(BF16)


def gate_up(mine, other, gate_w, up_w):
    f_blocks, d_blocks, block, _ = gate_w.shape
    tokens = 2 * mine.shape[0]
    shape = (f_blocks, tokens, 2 * block)
    return pl.pallas_call(
        gate_up_body,
        out_shape=(jax.ShapeDtypeStruct(shape, F32), jax.ShapeDtypeStruct(shape, BF16)),
        in_specs=[WHOLE] * 4,
        out_specs=(WHOLE,) * 2,
        compiler_params=params(),
        cost_estimate=cost(4 * tokens * gate_w.size, 4 * gate_w.size),
        name="gate_up",
    )(mine, other, resident(gate_w), resident(up_w))


def d_hidden_body(mine, other, down_w, own, send):
    f_blocks, d_blocks, block, _ = down_w.shape
    y = jnp.concatenate([mine[...], other[...]], axis=0)

    @pl.loop(0, f_blocks // 2)
    def _(pair):
        weights = jnp.concatenate(
            [
                down_w[pl.ds(2 * pair, 2), d].reshape(2 * block, block)
                for d in range(d_blocks)
            ],
            axis=1,
        )
        result = lax.dot_general(
            y, weights, (((1,), (1,)), ((), ())), preferred_element_type=F32
        )
        for half in range(2):
            part = result[:, half * block : (half + 1) * block]
            own[2 * pair + half] = part
            send[2 * pair + half] = part.astype(BF16)


def d_hidden(mine, other, down_w):
    f_blocks, d_blocks, block, _ = down_w.shape
    tokens = 2 * mine.shape[0]
    shape = (f_blocks, tokens, block)
    return pl.pallas_call(
        d_hidden_body,
        out_shape=(jax.ShapeDtypeStruct(shape, F32), jax.ShapeDtypeStruct(shape, BF16)),
        in_specs=[WHOLE] * 3,
        out_specs=(WHOLE,) * 2,
        compiler_params=params(),
        cost_estimate=cost(2 * tokens * down_w.size, 2 * down_w.size),
        name="d_hidden",
    )(mine, other, resident(down_w))


def d_tokens_body(others, *refs):
    gu_own, dh_own = refs[:2]
    gu_recv = refs[2 : 2 + others]
    dh_recv = refs[2 + others : 2 + 2 * others]
    gate_w, up_w, own, send, d_pair, hidden, packed = refs[2 + 2 * others :]
    f_blocks, d_blocks, block, _ = gate_w.shape
    half = own.shape[0]
    for c in range(f_blocks):
        gu = gu_own[c]
        dh = dh_own[c]
        for k in range(others):
            gu = gu + gu_recv[k][c].astype(F32)
            dh = dh + dh_recv[k][c].astype(F32)
        gate, up = gu[:, :block], gu[:, block:]
        sig = jax.nn.sigmoid(gate)
        silu = gate * sig
        hidden[c] = (silu * up).astype(BF16)
        d_gate = (dh * up * sig * (1.0 + gate * (1.0 - sig))).astype(BF16)
        d_up = (dh * silu).astype(BF16)
        both = jnp.concatenate([d_gate, d_up], axis=1)
        d_pair[c] = both
        packed[:, 2 * block * c : 2 * block * (c + 1)] = both
    grads = packed[...]

    @pl.loop(0, d_blocks // 2)
    def _(pair):
        rows = pl.ds(2 * pair, 2)
        weights = jnp.concatenate(
            [
                ref[c, rows].reshape(2 * block, block)
                for c in range(f_blocks)
                for ref in (gate_w, up_w)
            ],
            axis=1,
        )
        result = lax.dot_general(
            grads, weights, (((1,), (1,)), ((), ())), preferred_element_type=F32
        )
        columns = pl.ds(pl.multiple_of(pair * 2 * block, 2 * block), 2 * block)
        own[:, columns] = result[:half]
        send[:, columns] = result[half:].astype(BF16)


def d_tokens_part(gu_own, dh_own, gu_recv, dh_recv, gate_w, up_w):
    f_blocks, d_blocks, block, _ = gate_w.shape
    tokens = gu_own.shape[1]
    width = d_blocks * block
    others = len(gu_recv)
    return pl.pallas_call(
        functools.partial(d_tokens_body, others),
        out_shape=(
            jax.ShapeDtypeStruct((tokens // 2, width), F32),
            jax.ShapeDtypeStruct((tokens // 2, width), BF16),
            jax.ShapeDtypeStruct((f_blocks, tokens, 2 * block), BF16),
            jax.ShapeDtypeStruct((f_blocks, tokens, block), BF16),
        ),
        in_specs=[WHOLE] * (4 + 2 * others),
        out_specs=(WHOLE,) * 4,
        scratch_shapes=[pltpu.VMEM((tokens, f_blocks * 2 * block), BF16)],
        compiler_params=params(),
        cost_estimate=cost(4 * tokens * gate_w.size, 4 * gate_w.size),
        name="d_tokens",
    )(gu_own, dh_own, *gu_recv, *dh_recv, resident(gate_w), resident(up_w))


def step_slots(slots):
    return max(n for n in range(1, 17) if slots % n == 0)


def gu_grad_body(index, count, mine, other, d_pair, gate_out, up_out, turned):
    f_blocks = d_pair.shape[0]
    d_blocks, block, _ = turned.shape
    step = pl.program_id(0)

    @pl.when(step == 0)
    def _():
        for d in range(d_blocks):
            columns = slice(d * block, (d + 1) * block)
            x = jnp.concatenate([mine[:, columns], other[:, columns]], axis=0)
            turned[d] = x.T

    for j in range(gate_out.shape[0]):
        slot = step * gate_out.shape[0] + j
        place = index[slot]
        result = jnp.dot(
            turned[place // f_blocks], d_pair[place % f_blocks], preferred_element_type=F32
        )
        result = jnp.where(slot < count[0], result, 0.0).astype(BF16)
        gate_out[j] = result[:, :block]
        up_out[j] = result[:, block:]


def gu_grads(index, count, mine, other, d_pair, slots):
    f_blocks, tokens, pair = d_pair.shape
    block = pair // 2
    d_blocks = mine.shape[1] // block
    chunk = step_slots(slots)
    shape = jax.ShapeDtypeStruct((slots, block, block), BF16)
    out = pl.BlockSpec((chunk, block, block), lambda i, *_: (i, 0, 0))
    return pl.pallas_call(
        gu_grad_body,
        out_shape=(shape,) * 2,
        grid_spec=pltpu.PrefetchScalarGridSpec(
            num_scalar_prefetch=2,
            grid=(slots // chunk,),
            in_specs=[WHOLE] * 3,
            out_specs=(out,) * 2,
            scratch_shapes=[pltpu.VMEM((d_blocks, block, tokens), BF16)],
        ),
        compiler_params=params(),
        cost_estimate=cost(4 * slots * block * block * tokens, 4 * slots * block * block),
        name="gu_grads",
    )(index, count, mine, other, d_pair)


def down_grad_body(index, count, mine, other, hidden, out, turned, columns):
    f_blocks = hidden.shape[0]
    d_blocks = columns.shape[0]
    block = hidden.shape[2]
    step = pl.program_id(0)

    @pl.when(step == 0)
    def _():
        for f in range(f_blocks):
            turned[f] = hidden[f].T
        for d in range(d_blocks):
            at = slice(d * block, (d + 1) * block)
            columns[d] = jnp.concatenate([mine[:, at], other[:, at]], axis=0)

    for j in range(out.shape[0]):
        slot = step * out.shape[0] + j
        place = index[slot]
        result = jnp.dot(
            turned[place // d_blocks], columns[place % d_blocks], preferred_element_type=F32
        )
        out[j] = jnp.where(slot < count[0], result, 0.0).astype(BF16)


def down_grads(index, count, mine, other, hidden, slots):
    f_blocks, tokens, block = hidden.shape
    d_blocks = mine.shape[1] // block
    chunk = step_slots(slots)
    return pl.pallas_call(
        down_grad_body,
        out_shape=jax.ShapeDtypeStruct((slots, block, block), BF16),
        grid_spec=pltpu.PrefetchScalarGridSpec(
            num_scalar_prefetch=2,
            grid=(slots // chunk,),
            in_specs=[WHOLE] * 3,
            out_specs=pl.BlockSpec((chunk, block, block), lambda i, *_: (i, 0, 0)),
            scratch_shapes=[
                pltpu.VMEM((f_blocks, block, tokens), BF16),
                pltpu.VMEM((d_blocks, tokens, block), BF16),
            ],
        ),
        compiler_params=params(),
        cost_estimate=cost(2 * slots * block * block * tokens, 2 * slots * block * block),
        name="down_grads",
    )(index, count, mine, other, hidden)


def on_device(
    tokens, cotangent, gate_vals, up_vals, gu_index, gu_count, down_vals, down_index, down_count
):
    block = gate_vals.shape[-1]
    slots = gate_vals.shape[2]
    wide = lax.axis_size("wide")
    narrow = lax.axis_size("narrow")
    chips = wide // 2
    rows = tokens.shape[0]
    d_blocks = tokens.shape[1] // block
    f_blocks = FF // (block * wide)
    gu_index, down_index = gu_index[0, 0], down_index[0, 0]
    gu_count, down_count = gu_count[0], down_count[0]

    def gather(piece):
        pieces = [piece] + [swap(piece, "wide", wide, 2 * k) for k in range(1, chips)]
        return pieces

    def share(pieces):
        mine = jnp.concatenate(pieces, axis=0)
        return mine, swap(mine, "wide", wide, 1)

    def exchange(array):
        return [swap(array, "narrow", narrow, k) for k in range(1, narrow)]

    x_pieces = gather(tokens)
    gate_w, up_w, down_w = fill(
        gu_index, gu_count, down_index, down_count,
        gate_vals[0, 0], up_vals[0, 0], down_vals[0, 0], f_blocks, d_blocks,
    )
    x_pieces, cotangent = lax.optimization_barrier((x_pieces, cotangent))
    y_pieces = gather(cotangent)
    x_mine, x_other = share(x_pieces)
    gu_own, gu_send = gate_up(x_mine, x_other, gate_w, up_w)
    gu_recv = exchange(gu_send)
    y_mine, y_other = share(y_pieces)
    dh_own, dh_send = d_hidden(y_mine, y_other, down_w)
    dh_recv = exchange(dh_send)
    own, send, d_pair, hidden = d_tokens_part(gu_own, dh_own, gu_recv, dh_recv, gate_w, up_w)
    own = own + swap(send, "wide", wide, 1).astype(F32)
    down_grad = down_grads(down_index, down_count, y_mine, y_other, hidden, slots)
    parts = [own[k * rows : (k + 1) * rows] for k in range(chips)]
    sends = [part.astype(BF16) for part in parts[1:]]
    sends, d_pair = lax.optimization_barrier((sends, d_pair))
    gate_grad, up_grad = gu_grads(gu_index, gu_count, x_mine, x_other, d_pair, slots)
    total = parts[0]
    for k in range(1, chips):
        total = total + swap(sends[k - 1], "wide", wide, 2 * k).astype(F32)
    return (
        total.astype(BF16),
        gate_grad[None, None],
        up_grad[None, None],
        down_grad[None, None],
    )


def solution(mesh):
    in_specs = (
        P("wide", "narrow"),
        P("wide", "narrow"),
        P("narrow", "wide", None, None, None),
        P("narrow", "wide", None, None, None),
        P("narrow", "wide", None),
        P("narrow", "wide"),
        P("wide", "narrow", None, None, None),
        P("wide", "narrow", None),
        P("wide", "narrow"),
    )
    out_specs = (
        P("wide", "narrow"),
        P("narrow", "wide", None, None, None),
        P("narrow", "wide", None, None, None),
        P("wide", "narrow", None, None, None),
    )
    return jax.shard_map(
        on_device, mesh=mesh, in_specs=in_specs, out_specs=out_specs, check_vma=False
    )
```

profile of v0, /device:TPU:0, one launch (start us, length us, event | category | flops | bytes accessed | tf_op | source)
XLA Modules:
  0.0 118.1 jit_solution(16069404269463645641)
XLA Ops:
  0.6 3.0 %collective-permute-start = (bf16[8,4096]{1,0:T(8,128)(2,1)}, bf16[8,4096]{1,0:T(8,128)(2,1)S(1)}, u32[]{:S(2)}, u32[]{:S(2)}) collective-permute-start(bf16[8,4096]{1,0:T(8,128)(2,1)} %param.9), channel_id=1, source_target_pairs={{0,4},{2,6},{4,0},{6,2},{8,12},{10,14},{12,8},{14,10},{16,20},{18,... | collective-permute-start | bytes 196616 | tf_op jit(solution)/shard_map/ppermute | solution.py:33
  3.7 1.6 %collective-permute-start.1 = (bf16[8,4096]{1,0:T(8,128)(2,1)}, bf16[8,4096]{1,0:T(8,128)(2,1)S(1)}, u32[]{:S(2)}, u32[]{:S(2)}) collective-permute-start(bf16[8,4096]{1,0:T(8,128)(2,1)} %param.9), channel_id=1, source_target_pairs={{0,8},{2,10},{4,12},{6,14},{8,0},{10,2},{12,4},{14,6},{16,24},{18,... | collective-permute-start | bytes 196616 | tf_op jit(solution)/shard_map/ppermute | solution.py:33
  5.2 3.0 %collective-permute-start.3 = (bf16[8,4096]{1,0:T(8,128)(2,1)}, bf16[8,4096]{1,0:T(8,128)(2,1)S(1)}, u32[]{:S(2)}, u32[]{:S(2)}) collective-permute-start(bf16[8,4096]{1,0:T(8,128)(2,1)} %param.9), channel_id=1, source_target_pairs={{0,16},{2,18},{4,20},{6,22},{8,24},{10,26},{12,28},{14,30},{16,0},... | collective-permute-start | bytes 196616 | tf_op jit(solution)/shard_map/ppermute | solution.py:33
  8.2 1.3 %collective-permute-start.4 = (bf16[8,4096]{1,0:T(8,128)(2,1)}, bf16[8,4096]{1,0:T(8,128)(2,1)S(1)}, u32[]{:S(2)}, u32[]{:S(2)}) collective-permute-start(bf16[8,4096]{1,0:T(8,128)(2,1)} %param.9), channel_id=1, source_target_pairs={{0,20},{2,22},{4,16},{6,18},{8,28},{10,30},{12,24},{14,26},{16,4},... | collective-permute-start | bytes 196616 | tf_op jit(solution)/shard_map/ppermute | solution.py:33
  9.5 3.6 %collective-permute-start.5 = (bf16[8,4096]{1,0:T(8,128)(2,1)}, bf16[8,4096]{1,0:T(8,128)(2,1)S(1)}, u32[]{:S(2)}, u32[]{:S(2)}) collective-permute-start(bf16[8,4096]{1,0:T(8,128)(2,1)} %param.9), channel_id=1, source_target_pairs={{0,24},{2,26},{4,28},{6,30},{8,16},{10,18},{12,20},{14,22},{16,8},... | collective-permute-start | bytes 196616 | tf_op jit(solution)/shard_map/ppermute | solution.py:33
  13.1 5.5 %collective-permute-done.4 = bf16[8,4096]{1,0:T(8,128)(2,1)S(1)} collective-permute-done((bf16[8,4096]{1,0:T(8,128)(2,1)}, bf16[8,4096]{1,0:T(8,128)(2,1)S(1)}, u32[]{:S(2)}, u32[]{:S(2)}) %collective-permute-start.4) | collective-permute-done | bytes 65568 | tf_op jit(solution)/shard_map/ppermute | solution.py:33
  18.6 1.8 %collective-permute-done.6 = bf16[8,4096]{1,0:T(8,128)(2,1)S(1)} collective-permute-done((bf16[8,4096]{1,0:T(8,128)(2,1)}, bf16[8,4096]{1,0:T(8,128)(2,1)S(1)}, u32[]{:S(2)}, u32[]{:S(2)}) %collective-permute-start.6) | collective-permute-done | bytes 65568 | tf_op jit(solution)/shard_map/ppermute | solution.py:33
  21.7 1.9 %collective-permute-start.9 = (bf16[8,4096]{1,0:T(8,128)(2,1)}, bf16[8,4096]{1,0:T(8,128)(2,1)S(1)}, u32[]{:S(2)}, u32[]{:S(2)}) collective-permute-start(bf16[8,4096]{1,0:T(8,128)(2,1)} %param.10), channel_id=1, source_target_pairs={{0,8},{2,10},{4,12},{6,14},{8,0},{10,2},{12,4},{14,6},{16,24},{18,... | collective-permute-start | bytes 196616 | tf_op jit(solution)/shard_map/ppermute | solution.py:33
  23.7 1.1 collective-permute-start.10
  24.7 2.7 %collective-permute-start.11 = (bf16[8,4096]{1,0:T(8,128)(2,1)}, bf16[8,4096]{1,0:T(8,128)(2,1)S(1)}, u32[]{:S(2)}, u32[]{:S(2)}) collective-permute-start(bf16[8,4096]{1,0:T(8,128)(2,1)} %param.10), channel_id=1, source_target_pairs={{0,16},{2,18},{4,20},{6,22},{8,24},{10,26},{12,28},{14,30},{16,0},... | collective-permute-start | bytes 196616 | tf_op jit(solution)/shard_map/ppermute | solution.py:33
  28.6 2.3 %collective-permute-start.13 = (bf16[8,4096]{1,0:T(8,128)(2,1)}, bf16[8,4096]{1,0:T(8,128)(2,1)S(1)}, u32[]{:S(2)}, u32[]{:S(2)}) collective-permute-start(bf16[8,4096]{1,0:T(8,128)(2,1)} %param.10), channel_id=1, source_target_pairs={{0,24},{2,26},{4,28},{6,30},{8,16},{10,18},{12,20},{14,22},{16,8},... | collective-permute-start | bytes 196616 | tf_op jit(solution)/shard_map/ppermute | solution.py:33
  30.9 2.6 %collective-permute-start.14 = (bf16[8,4096]{1,0:T(8,128)(2,1)}, bf16[8,4096]{1,0:T(8,128)(2,1)S(1)}, u32[]{:S(2)}, u32[]{:S(2)}) collective-permute-start(bf16[8,4096]{1,0:T(8,128)(2,1)} %param.10), channel_id=1, source_target_pairs={{0,28},{2,30},{4,24},{6,26},{8,20},{10,22},{12,16},{14,18},{16,12}... | collective-permute-start | bytes 196616 | tf_op jit(solution)/shard_map/ppermute | solution.py:33
  33.6 3.0 %collective-permute-done.12 = bf16[8,4096]{1,0:T(8,128)(2,1)S(1)} collective-permute-done((bf16[8,4096]{1,0:T(8,128)(2,1)}, bf16[8,4096]{1,0:T(8,128)(2,1)S(1)}, u32[]{:S(2)}, u32[]{:S(2)}) %collective-permute-start.12) | collective-permute-done | bytes 65568 | tf_op jit(solution)/shard_map/ppermute | solution.py:33
  36.7 1.5 %collective-permute-done.14 = bf16[8,4096]{1,0:T(8,128)(2,1)S(1)} collective-permute-done((bf16[8,4096]{1,0:T(8,128)(2,1)}, bf16[8,4096]{1,0:T(8,128)(2,1)S(1)}, u32[]{:S(2)}, u32[]{:S(2)}) %collective-permute-start.14) | collective-permute-done | bytes 65568 | tf_op jit(solution)/shard_map/ppermute | solution.py:33
  40.9 5.8 %fill.1 = (bf16[8,32,128,128]{3,2,1,0:T(8,128)(2,1)S(1)}, bf16[8,32,128,128]{3,2,1,0:T(8,128)(2,1)S(1)}, bf16[8,32,128,128]{3,2,1,0:T(8,128)(2,1)S(1)}) custom-call(s32[192]{0:T(256)S(1)} %bitcast.16, s32[1]{0:T(128)} %bitcast.10.gu_count, s32[192]{0:T(256)S(1)} %bitcast.14, s32[1]{0:T(128)} %bitcast.12.down_count, bf16[192,128,128]{2,1,0:T(8,128)(2,1)} %bitcast.18, ...), custom_call_target="tpu_custom_call" | custom-call | bytes 18874368 | tf_op jit(solution)/shard_map/fill/pallas_call | solution.py:86
  46.7 3.3 %copy-done.2 = bf16[8,32,128,128]{3,2,1,0:T(8,128)(2,1)} copy-done((bf16[8,32,128,128]{3,2,1,0:T(8,128)(2,1)}, bf16[8,32,128,128]{3,2,1,0:T(8,128)(2,1)S(1)}, u32[]{:S(2)}) %copy-start.2) | copy-done | bytes 8388632
  50.0 3.8 %gate_up.1 = (f32[8,128,256]{2,1,0:T(8,128)S(1)}, bf16[8,128,256]{2,1,0:T(8,128)(2,1)S(1)}) custom-call(bf16[64,4096]{1,0:T(8,128)(2,1)S(1)} %constant_dynamic-update-slice_fusion.mine, bf16[64,4096]{1,0:T(8,128)(2,1)S(1)} %collective-permute-done.7.other, bf16[8,32,128,128]{3,2,1,0:T(8,128)(2,1)S(1)} %get-tuple-element.42.gate_w.refs_4_, ...), custom_call_target="tpu_custom_call" | custom-call | flops 2147483648 | bytes 16777216 | tf_op jit(solution)/shard_map/gate_up/pallas_call | solution.py:120
  53.8 5.0 %collective-permute-start.16 = (bf16[8,128,256]{2,1,0:T(8,128)(2,1)S(1)}, bf16[8,128,256]{2,1,0:T(8,128)(2,1)S(1)}, u32[]{:S(2)}, u32[]{:S(2)}) collective-permute-start(bf16[8,128,256]{2,1,0:T(8,128)(2,1)S(1)} %get-tuple-element.48), channel_id=1, source_target_pairs={{0,1},{1,0},{2,3},{3,2},{4,5},{5,4},{6,7},{7,6},{8,9},{9,8},{10,11... | collective-permute-start | bytes 1572872 | tf_op jit(solution)/shard_map/ppermute | solution.py:33
  58.8 3.4 %copy-done.3 = bf16[8,32,128,128]{3,2,1,0:T(8,128)(2,1)S(1)} copy-done((bf16[8,32,128,128]{3,2,1,0:T(8,128)(2,1)S(1)}, bf16[8,32,128,128]{3,2,1,0:T(8,128)(2,1)}, u32[]{:S(2)}) %copy-start.3) | copy-done | bytes 8388632
  62.2 3.3 %d_hidden.1 = (f32[8,128,128]{2,1,0:T(8,128)S(1)}, bf16[8,128,128]{2,1,0:T(8,128)(2,1)S(1)}) custom-call(bf16[64,4096]{1,0:T(8,128)(2,1)S(1)} %constant_dynamic-update-slice_fusion.8.mine, bf16[64,4096]{1,0:T(8,128)(2,1)S(1)} %collective-permute-done.15.other, bf16[8,32,128,128]{3,2,1,0:T(8,128)(2,1)S(1)} %copy-done.3), custom_call_target="tpu_custom_call" | custom-call | flops 1073741824 | bytes 8388608 | tf_op jit(solution)/shard_map/d_hidden/pallas_call | solution.py:157
  65.5 9.3 %collective-permute-done.17.refs_3_ = bf16[8,128,128]{2,1,0:T(8,128)(2,1)S(1)} collective-permute-done((bf16[8,128,128]{2,1,0:T(8,128)(2,1)S(1)}, bf16[8,128,128]{2,1,0:T(8,128)(2,1)S(1)}, u32[]{:S(2)}, u32[]{:S(2)}) %collective-permute-start.17) | collective-permute-done | bytes 262176 | tf_op jit(solution)/shard_map/ppermute | solution.py:33
  74.8 3.4 %copy-done.1 = bf16[8,32,128,128]{3,2,1,0:T(8,128)(2,1)S(1)} copy-done((bf16[8,32,128,128]{3,2,1,0:T(8,128)(2,1)S(1)}, bf16[8,32,128,128]{3,2,1,0:T(8,128)(2,1)}, u32[]{:S(2)}) %copy-start.1) | copy-done | bytes 8388632
  78.2 8.0 %d_tokens.1 = (f32[64,4096]{1,0:T(8,128)S(1)}, bf16[64,4096]{1,0:T(8,128)(2,1)S(1)}, bf16[8,128,256]{2,1,0:T(8,128)(2,1)S(1)}, bf16[8,128,128]{2,1,0:T(8,128)(2,1)S(1)}) custom-call(f32[8,128,256]{2,1,0:T(8,128)S(1)} %get-tuple-element.44.refs_0_, f32[8,128,128]{2,1,0:T(8,128)S(1)} %get-tuple-element.47.refs_1_, ...), custom_call_target="tpu_custom_call" | custom-call | flops 2147483648 | bytes 16777216 | tf_op jit(solution)/shard_map/d_tokens/pallas_call | solution.py:216
  86.4 1.9 %collective-permute-done.18 = bf16[64,4096]{1,0:T(8,128)(2,1)S(1)} collective-permute-done((bf16[64,4096]{1,0:T(8,128)(2,1)S(1)}, bf16[64,4096]{1,0:T(8,128)(2,1)S(1)}, u32[]{:S(2)}, u32[]{:S(2)}) %collective-permute-start.18) | collective-permute-done | bytes 524320 | tf_op jit(solution)/shard_map/ppermute | solution.py:33
  88.4 2.3 %collective-permute-start.19 = (bf16[8,4096]{1,0:T(8,128)(2,1)S(1)}, bf16[8,4096]{1,0:T(8,128)(2,1)S(1)}, u32[]{:S(2)}, u32[]{:S(2)}) collective-permute-start(bf16[8,4096]{1,0:T(8,128)(2,1)S(1)} %get-tuple-element.53), channel_id=1, source_target_pairs={{0,4},{2,6},{4,0},{6,2},{8,12},{10,14},{12,8},{14,10},{16,20},{18,... | collective-permute-start | bytes 196616 | tf_op jit(solution)/shard_map/ppermute | solution.py:33
  90.8 1.0 collective-permute-start.20
  91.8 7.7 %down_grads.1 = bf16[192,128,128]{2,1,0:T(8,128)(2,1)} custom-call(s32[192]{0:T(256)S(1)} %bitcast.15, s32[1]{0:T(128)} %bitcast.13.count, bf16[64,4096]{1,0:T(8,128)(2,1)S(1)} %constant_dynamic-update-slice_fusion.8.mine, bf16[64,4096]{1,0:T(8,128)(2,1)S(1)} %collective-permute-done.15.other, bf16[8,128,128]{2,1,0:T(8,128)(2,1)S(1)} %get-tuple-element.63.hidden), custom_call_target="tpu_custom_call" | custom-call | flops 805306368 | bytes 6291456 | tf_op jit(solution)/shard_map/down_grads/pallas_call | solution.py:310
  100.0 2.6 %collective-permute-start.22 = (bf16[8,4096]{1,0:T(8,128)(2,1)S(1)}, bf16[8,4096]{1,0:T(8,128)(2,1)S(1)}, u32[]{:S(2)}, u32[]{:S(2)}) collective-permute-start(bf16[8,4096]{1,0:T(8,128)(2,1)S(1)} %get-tuple-element.56), channel_id=1, source_target_pairs={{0,16},{2,18},{4,20},{6,22},{8,24},{10,26},{12,28},{14,30},{16,0},... | collective-permute-start | bytes 196616 | tf_op jit(solution)/shard_map/ppermute | solution.py:33
  102.6 1.7 %collective-permute-start.23 = (bf16[8,4096]{1,0:T(8,128)(2,1)S(1)}, bf16[8,4096]{1,0:T(8,128)(2,1)S(1)}, u32[]{:S(2)}, u32[]{:S(2)}) collective-permute-start(bf16[8,4096]{1,0:T(8,128)(2,1)S(1)} %get-tuple-element.57), channel_id=1, source_target_pairs={{0,20},{2,22},{4,16},{6,18},{8,28},{10,30},{12,24},{14,26},{16,4},... | collective-permute-start | bytes 196616 | tf_op jit(solution)/shard_map/ppermute | solution.py:33
  104.3 1.0 collective-permute-start.24
  105.3 2.4 %collective-permute-start.25 = (bf16[8,4096]{1,0:T(8,128)(2,1)S(1)}, bf16[8,4096]{1,0:T(8,128)(2,1)S(1)}, u32[]{:S(2)}, u32[]{:S(2)}) collective-permute-start(bf16[8,4096]{1,0:T(8,128)(2,1)S(1)} %get-tuple-element.59), channel_id=1, source_target_pairs={{0,28},{2,30},{4,24},{6,26},{8,20},{10,22},{12,16},{14,18},{16,12}... | collective-permute-start | bytes 196616 | tf_op jit(solution)/shard_map/ppermute | solution.py:33
  107.7 9.7 %gu_grads.1 = (bf16[192,128,128]{2,1,0:T(8,128)(2,1)}, bf16[192,128,128]{2,1,0:T(8,128)(2,1)}) custom-call(s32[192]{0:T(256)S(1)} %bitcast.17, s32[1]{0:T(128)} %bitcast.11.count, bf16[64,4096]{1,0:T(8,128)(2,1)S(1)} %constant_dynamic-update-slice_fusion.mine, bf16[64,4096]{1,0:T(8,128)(2,1)S(1)} %collective-permute-done.7.other, ...), custom_call_target="tpu_custom_call" | custom-call | flops 1610612736 | bytes 12582912 | tf_op jit(solution)/shard_map/gu_grads/pallas_call | solution.py:267
  (61 shorter events, 5.5 us)
Async XLA Ops:
  0.6 8.9 %collective-permute-start = (bf16[8,4096]{1,0:T(8,128)(2,1)}, bf16[8,4096]{1,0:T(8,128)(2,1)S(1)}, u32[]{:S(2)}, u32[]{:S(2)}) collective-permute-start(bf16[8,4096]{1,0:T(8,128)(2,1)} %param.9), channel_id=1, source_target_pairs={{0,4},{2,6},{4,0},{6,2},{8,12},{10,14},{12,8},{14,10},{16,20},{18,... | collective-permute-start | bytes 196616 | tf_op jit(solution)/shard_map/ppermute | solution.py:33
  3.7 9.5 %collective-permute-start.1 = (bf16[8,4096]{1,0:T(8,128)(2,1)}, bf16[8,4096]{1,0:T(8,128)(2,1)S(1)}, u32[]{:S(2)}, u32[]{:S(2)}) collective-permute-start(bf16[8,4096]{1,0:T(8,128)(2,1)} %param.9), channel_id=1, source_target_pairs={{0,8},{2,10},{4,12},{6,14},{8,0},{10,2},{12,4},{14,6},{16,24},{18,... | collective-permute-start | bytes 196616 | tf_op jit(solution)/shard_map/ppermute | solution.py:33
  5.2 7.9 %collective-permute-start.2 = (bf16[8,4096]{1,0:T(8,128)(2,1)}, bf16[8,4096]{1,0:T(8,128)(2,1)S(1)}, u32[]{:S(2)}, u32[]{:S(2)}) collective-permute-start(bf16[8,4096]{1,0:T(8,128)(2,1)} %param.9), channel_id=1, source_target_pairs={{0,12},{2,14},{4,8},{6,10},{8,4},{10,6},{12,0},{14,2},{16,28},{18,... | collective-permute-start | bytes 196616 | tf_op jit(solution)/shard_map/ppermute | solution.py:33
  5.2 7.9 %collective-permute-start.3 = (bf16[8,4096]{1,0:T(8,128)(2,1)}, bf16[8,4096]{1,0:T(8,128)(2,1)S(1)}, u32[]{:S(2)}, u32[]{:S(2)}) collective-permute-start(bf16[8,4096]{1,0:T(8,128)(2,1)} %param.9), channel_id=1, source_target_pairs={{0,16},{2,18},{4,20},{6,22},{8,24},{10,26},{12,28},{14,30},{16,0},... | collective-permute-start | bytes 196616 | tf_op jit(solution)/shard_map/ppermute | solution.py:33
  8.2 10.4 %collective-permute-start.4 = (bf16[8,4096]{1,0:T(8,128)(2,1)}, bf16[8,4096]{1,0:T(8,128)(2,1)S(1)}, u32[]{:S(2)}, u32[]{:S(2)}) collective-permute-start(bf16[8,4096]{1,0:T(8,128)(2,1)} %param.9), channel_id=1, source_target_pairs={{0,20},{2,22},{4,16},{6,18},{8,28},{10,30},{12,24},{14,26},{16,4},... | collective-permute-start | bytes 196616 | tf_op jit(solution)/shard_map/ppermute | solution.py:33
  9.5 9.1 %collective-permute-start.5 = (bf16[8,4096]{1,0:T(8,128)(2,1)}, bf16[8,4096]{1,0:T(8,128)(2,1)S(1)}, u32[]{:S(2)}, u32[]{:S(2)}) collective-permute-start(bf16[8,4096]{1,0:T(8,128)(2,1)} %param.9), channel_id=1, source_target_pairs={{0,24},{2,26},{4,28},{6,30},{8,16},{10,18},{12,20},{14,22},{16,8},... | collective-permute-start | bytes 196616 | tf_op jit(solution)/shard_map/ppermute | solution.py:33
  13.1 7.3 %collective-permute-start.6 = (bf16[8,4096]{1,0:T(8,128)(2,1)}, bf16[8,4096]{1,0:T(8,128)(2,1)S(1)}, u32[]{:S(2)}, u32[]{:S(2)}) collective-permute-start(bf16[8,4096]{1,0:T(8,128)(2,1)} %param.9), channel_id=1, source_target_pairs={{0,28},{2,30},{4,24},{6,26},{8,20},{10,22},{12,16},{14,18},{16,12}... | collective-permute-start | bytes 196616 | tf_op jit(solution)/shard_map/ppermute | solution.py:33
  21.2 7.3 %collective-permute-start.8 = (bf16[8,4096]{1,0:T(8,128)(2,1)}, bf16[8,4096]{1,0:T(8,128)(2,1)S(1)}, u32[]{:S(2)}, u32[]{:S(2)}) collective-permute-start(bf16[8,4096]{1,0:T(8,128)(2,1)} %param.10), channel_id=1, source_target_pairs={{0,4},{2,6},{4,0},{6,2},{8,12},{10,14},{12,8},{14,10},{16,20},{18,... | collective-permute-start | bytes 196616 | tf_op jit(solution)/shard_map/ppermute | solution.py:33
  21.7 9.1 %collective-permute-start.9 = (bf16[8,4096]{1,0:T(8,128)(2,1)}, bf16[8,4096]{1,0:T(8,128)(2,1)S(1)}, u32[]{:S(2)}, u32[]{:S(2)}) collective-permute-start(bf16[8,4096]{1,0:T(8,128)(2,1)} %param.10), channel_id=1, source_target_pairs={{0,8},{2,10},{4,12},{6,14},{8,0},{10,2},{12,4},{14,6},{16,24},{18,... | collective-permute-start | bytes 196616 | tf_op jit(solution)/shard_map/ppermute | solution.py:33
  23.7 9.8 %collective-permute-start.10 = (bf16[8,4096]{1,0:T(8,128)(2,1)}, bf16[8,4096]{1,0:T(8,128)(2,1)S(1)}, u32[]{:S(2)}, u32[]{:S(2)}) collective-permute-start(bf16[8,4096]{1,0:T(8,128)(2,1)} %param.10), channel_id=1, source_target_pairs={{0,12},{2,14},{4,8},{6,10},{8,4},{10,6},{12,0},{14,2},{16,28},{18,... | collective-permute-start | bytes 196616 | tf_op jit(solution)/shard_map/ppermute | solution.py:33
  24.7 8.9 %collective-permute-start.11 = (bf16[8,4096]{1,0:T(8,128)(2,1)}, bf16[8,4096]{1,0:T(8,128)(2,1)S(1)}, u32[]{:S(2)}, u32[]{:S(2)}) collective-permute-start(bf16[8,4096]{1,0:T(8,128)(2,1)} %param.10), channel_id=1, source_target_pairs={{0,16},{2,18},{4,20},{6,22},{8,24},{10,26},{12,28},{14,30},{16,0},... | collective-permute-start | bytes 196616 | tf_op jit(solution)/shard_map/ppermute | solution.py:33
  27.5 9.2 %collective-permute-start.12 = (bf16[8,4096]{1,0:T(8,128)(2,1)}, bf16[8,4096]{1,0:T(8,128)(2,1)S(1)}, u32[]{:S(2)}, u32[]{:S(2)}) collective-permute-start(bf16[8,4096]{1,0:T(8,128)(2,1)} %param.10), channel_id=1, source_target_pairs={{0,20},{2,22},{4,16},{6,18},{8,28},{10,30},{12,24},{14,26},{16,4},... | collective-permute-start | bytes 196616 | tf_op jit(solution)/shard_map/ppermute | solution.py:33
  28.6 8.1 %collective-permute-start.13 = (bf16[8,4096]{1,0:T(8,128)(2,1)}, bf16[8,4096]{1,0:T(8,128)(2,1)S(1)}, u32[]{:S(2)}, u32[]{:S(2)}) collective-permute-start(bf16[8,4096]{1,0:T(8,128)(2,1)} %param.10), channel_id=1, source_target_pairs={{0,24},{2,26},{4,28},{6,30},{8,16},{10,18},{12,20},{14,22},{16,8},... | collective-permute-start | bytes 196616 | tf_op jit(solution)/shard_map/ppermute | solution.py:33
  30.9 7.3 %collective-permute-start.14 = (bf16[8,4096]{1,0:T(8,128)(2,1)}, bf16[8,4096]{1,0:T(8,128)(2,1)S(1)}, u32[]{:S(2)}, u32[]{:S(2)}) collective-permute-start(bf16[8,4096]{1,0:T(8,128)(2,1)} %param.10), channel_id=1, source_target_pairs={{0,28},{2,30},{4,24},{6,26},{8,20},{10,22},{12,16},{14,18},{16,12}... | collective-permute-start | bytes 196616 | tf_op jit(solution)/shard_map/ppermute | solution.py:33
  33.5 16.5 %collective-permute-start.7 = (bf16[64,4096]{1,0:T(8,128)(2,1)S(1)}, bf16[64,4096]{1,0:T(8,128)(2,1)S(1)}, u32[]{:S(2)}, u32[]{:S(2)}) collective-permute-start(bf16[64,4096]{1,0:T(8,128)(2,1)S(1)} %constant_dynamic-update-slice_fusion.mine), channel_id=1, source_target_pairs={{0,2},{2,0},{4,6},{6,4},{8,10},{10,8},{12,14},{14,12},{16,18},{18,... | collective-permute-start | bytes 1572872 | tf_op jit(solution)/shard_map/ppermute | solution.py:33
  38.2 20.6 %collective-permute-start.15 = (bf16[64,4096]{1,0:T(8,128)(2,1)S(1)}, bf16[64,4096]{1,0:T(8,128)(2,1)S(1)}, u32[]{:S(2)}, u32[]{:S(2)}) collective-permute-start(bf16[64,4096]{1,0:T(8,128)(2,1)S(1)} %constant_dynamic-update-slice_fusion.8.mine), channel_id=1, source_target_pairs={{0,2},{2,0},{4,6},{6,4},{8,10},{10,8},{12,14},{14,12},{16,18},{18,... | collective-permute-start | bytes 1572872 | tf_op jit(solution)/shard_map/ppermute | solution.py:33
  46.7 3.3 %copy-start.2 = (bf16[8,32,128,128]{3,2,1,0:T(8,128)(2,1)}, bf16[8,32,128,128]{3,2,1,0:T(8,128)(2,1)S(1)}, u32[]{:S(2)}) copy-start(bf16[8,32,128,128]{3,2,1,0:T(8,128)(2,1)S(1)} %get-tuple-element.46.down_w) | copy-start | bytes 25165828
  50.0 3.8 %copy-start = (bf16[8,32,128,128]{3,2,1,0:T(8,128)(2,1)}, bf16[8,32,128,128]{3,2,1,0:T(8,128)(2,1)S(1)}, u32[]{:S(2)}) copy-start(bf16[8,32,128,128]{3,2,1,0:T(8,128)(2,1)S(1)} %get-tuple-element.43.up_w.refs_5_) | copy-start | bytes 25165828
  53.8 21.0 %collective-permute-start.16 = (bf16[8,128,256]{2,1,0:T(8,128)(2,1)S(1)}, bf16[8,128,256]{2,1,0:T(8,128)(2,1)S(1)}, u32[]{:S(2)}, u32[]{:S(2)}) collective-permute-start(bf16[8,128,256]{2,1,0:T(8,128)(2,1)S(1)} %get-tuple-element.48), channel_id=1, source_target_pairs={{0,1},{1,0},{2,3},{3,2},{4,5},{5,4},{6,7},{7,6},{8,9},{9,8},{10,11... | collective-permute-start | bytes 1572872 | tf_op jit(solution)/shard_map/ppermute | solution.py:33
  58.8 3.4 %copy-start.3 = (bf16[8,32,128,128]{3,2,1,0:T(8,128)(2,1)S(1)}, bf16[8,32,128,128]{3,2,1,0:T(8,128)(2,1)}, u32[]{:S(2)}) copy-start(bf16[8,32,128,128]{3,2,1,0:T(8,128)(2,1)} %copy-done.2) | copy-start | bytes 25165828
  65.4 9.4 %collective-permute-start.17 = (bf16[8,128,128]{2,1,0:T(8,128)(2,1)S(1)}, bf16[8,128,128]{2,1,0:T(8,128)(2,1)S(1)}, u32[]{:S(2)}, u32[]{:S(2)}) collective-permute-start(bf16[8,128,128]{2,1,0:T(8,128)(2,1)S(1)} %get-tuple-element.49), channel_id=1, source_target_pairs={{0,1},{1,0},{2,3},{3,2},{4,5},{5,4},{6,7},{7,6},{8,9},{9,8},{10,11... | collective-permute-start | bytes 786440 | tf_op jit(solution)/shard_map/ppermute | solution.py:33
  74.8 3.4 %copy-start.1 = (bf16[8,32,128,128]{3,2,1,0:T(8,128)(2,1)S(1)}, bf16[8,32,128,128]{3,2,1,0:T(8,128)(2,1)}, u32[]{:S(2)}) copy-start(bf16[8,32,128,128]{3,2,1,0:T(8,128)(2,1)} %copy-done) | copy-start | bytes 25165828
  78.2 13.5 %copy-start.5 = (s32[1,1,192]{2,1,0:T(1,128)S(1)}, s32[1,1,192]{2,1,0:T(1,128)}, u32[]{:S(2)}) copy-start(s32[1,1,192]{2,1,0:T(1,128)} %param.16) | copy-start | bytes 2308
  86.3 21.4 %copy-start.7 = (s32[1,1,192]{2,1,0:T(1,128)S(1)}, s32[1,1,192]{2,1,0:T(1,128)}, u32[]{:S(2)}) copy-start(s32[1,1,192]{2,1,0:T(1,128)} %param.13) | copy-start | bytes 2308
  86.3 2.0 %collective-permute-start.18 = (bf16[64,4096]{1,0:T(8,128)(2,1)S(1)}, bf16[64,4096]{1,0:T(8,128)(2,1)S(1)}, u32[]{:S(2)}, u32[]{:S(2)}) collective-permute-start(bf16[64,4096]{1,0:T(8,128)(2,1)S(1)} %get-tuple-element.51), channel_id=1, source_target_pairs={{0,2},{2,0},{4,6},{6,4},{8,10},{10,8},{12,14},{14,12},{16,18},{18,... | collective-permute-start | bytes 1572872 | tf_op jit(solution)/shard_map/ppermute | solution.py:33
  88.4 15.9 %collective-permute-start.19 = (bf16[8,4096]{1,0:T(8,128)(2,1)S(1)}, bf16[8,4096]{1,0:T(8,128)(2,1)S(1)}, u32[]{:S(2)}, u32[]{:S(2)}) collective-permute-start(bf16[8,4096]{1,0:T(8,128)(2,1)S(1)} %get-tuple-element.53), channel_id=1, source_target_pairs={{0,4},{2,6},{4,0},{6,2},{8,12},{10,14},{12,8},{14,10},{16,20},{18,... | collective-permute-start | bytes 196616 | tf_op jit(solution)/shard_map/ppermute | solution.py:33
  90.8 14.5 %collective-permute-start.20 = (bf16[8,4096]{1,0:T(8,128)(2,1)S(1)}, bf16[8,4096]{1,0:T(8,128)(2,1)S(1)}, u32[]{:S(2)}, u32[]{:S(2)}) collective-permute-start(bf16[8,4096]{1,0:T(8,128)(2,1)S(1)} %get-tuple-element.54), channel_id=1, source_target_pairs={{0,8},{2,10},{4,12},{6,14},{8,0},{10,2},{12,4},{14,6},{16,24},{18,... | collective-permute-start | bytes 196616 | tf_op jit(solution)/shard_map/ppermute | solution.py:33
  99.4 17.9 %collective-permute-start.21 = (bf16[8,4096]{1,0:T(8,128)(2,1)S(1)}, bf16[8,4096]{1,0:T(8,128)(2,1)S(1)}, u32[]{:S(2)}, u32[]{:S(2)}) collective-permute-start(bf16[8,4096]{1,0:T(8,128)(2,1)S(1)} %get-tuple-element.55), channel_id=1, source_target_pairs={{0,12},{2,14},{4,8},{6,10},{8,4},{10,6},{12,0},{14,2},{16,28},{18,... | collective-permute-start | bytes 196616 | tf_op jit(solution)/shard_map/ppermute | solution.py:33
  100.0 17.3 %collective-permute-start.22 = (bf16[8,4096]{1,0:T(8,128)(2,1)S(1)}, bf16[8,4096]{1,0:T(8,128)(2,1)S(1)}, u32[]{:S(2)}, u32[]{:S(2)}) collective-permute-start(bf16[8,4096]{1,0:T(8,128)(2,1)S(1)} %get-tuple-element.56), channel_id=1, source_target_pairs={{0,16},{2,18},{4,20},{6,22},{8,24},{10,26},{12,28},{14,30},{16,0},... | collective-permute-start | bytes 196616 | tf_op jit(solution)/shard_map/ppermute | solution.py:33
  102.6 14.7 %collective-permute-start.23 = (bf16[8,4096]{1,0:T(8,128)(2,1)S(1)}, bf16[8,4096]{1,0:T(8,128)(2,1)S(1)}, u32[]{:S(2)}, u32[]{:S(2)}) collective-permute-start(bf16[8,4096]{1,0:T(8,128)(2,1)S(1)} %get-tuple-element.57), channel_id=1, source_target_pairs={{0,20},{2,22},{4,16},{6,18},{8,28},{10,30},{12,24},{14,26},{16,4},... | collective-permute-start | bytes 196616 | tf_op jit(solution)/shard_map/ppermute | solution.py:33
  104.3 13.0 %collective-permute-start.24 = (bf16[8,4096]{1,0:T(8,128)(2,1)S(1)}, bf16[8,4096]{1,0:T(8,128)(2,1)S(1)}, u32[]{:S(2)}, u32[]{:S(2)}) collective-permute-start(bf16[8,4096]{1,0:T(8,128)(2,1)S(1)} %get-tuple-element.58), channel_id=1, source_target_pairs={{0,24},{2,26},{4,28},{6,30},{8,16},{10,18},{12,20},{14,22},{16,8},... | collective-permute-start | bytes 196616 | tf_op jit(solution)/shard_map/ppermute | solution.py:33
  105.3 12.1 %collective-permute-start.25 = (bf16[8,4096]{1,0:T(8,128)(2,1)S(1)}, bf16[8,4096]{1,0:T(8,128)(2,1)S(1)}, u32[]{:S(2)}, u32[]{:S(2)}) collective-permute-start(bf16[8,4096]{1,0:T(8,128)(2,1)S(1)} %get-tuple-element.59), channel_id=1, source_target_pairs={{0,28},{2,30},{4,24},{6,26},{8,20},{10,22},{12,16},{14,18},{16,12}... | collective-permute-start | bytes 196616 | tf_op jit(solution)/shard_map/ppermute | solution.py:33
  (2 other events, 1.4 us)
where the time goes:
time: 118 us
  starting transfers between devices  40.5 us (34%)
  Pallas kernels  38.3 us (32%)
  waiting for transfers between devices  23.1 us (20%)
  local copies, waits for them, and re-layouts  13.2 us (11%)
  between operations  2.18 us (2%)
    ppermute x26, starting transfers between devices, swap(): return lax.ppermute(array, axis, [(i, i ^ flip) for i in range(size)])  40.5 us
    ppermute x26, waiting for transfers between devices, swap(): return lax.ppermute(array, axis, [(i, i ^ flip) for i in range(size)])  23.1 us
    unnamed x30, local copies, waits for them, and re-layouts  13.2 us
    pallas_call x1, Pallas kernels, gu_grads(): pl.pallas_call(gu_grad_body, out_shape=(shape,) * 2, grid_spec=pltpu.Pref...  9.67 us
    pallas_call x1, Pallas kernels, d_tokens_part(): pl.pallas_call(functools.partial(d_tokens_body, others), out_shape=(jax.S...  8.03 us
    pallas_call x1, Pallas kernels, down_grads(): pl.pallas_call(down_grad_body, out_shape=jax.ShapeDtypeStruct((slots, blo...  7.7 us
    pallas_call x1, Pallas kernels, fill(): pl.pallas_call(fill_body, out_shape=(dense,) * 3, in_specs=[SCALARS] * 4...  5.83 us
    pallas_call x1, Pallas kernels, gate_up(): pl.pallas_call(gate_up_body, out_shape=(jax.ShapeDtypeStruct(shape, F32),...  3.77 us
  transfers between devices with their start and end apart: 26, of which 6 were waited for; matrix products, arithmetic and copies ran while one was open for 1% of the time, Pallas kernels for 26%

commit v1 on v0

--- a/solution.py
+++ b/solution.py
@@ -10,11 +10,10 @@
 FF = 16384
 F32 = jnp.float32
 BF16 = jnp.bfloat16
-VMEM_LIMIT = 24 * 1024 * 1024
+VMEM_LIMIT = 8 * 1024 * 1024
 
 WHOLE = pl.BlockSpec(memory_space=pltpu.VMEM)
 SCALARS = pl.BlockSpec(memory_space=pltpu.SMEM)
-ANYWHERE = pl.BlockSpec(memory_space=pl.ANY)
 
 
 def params():
@@ -27,6 +26,10 @@
 
 def resident(array):
     return pltpu.with_memory_space_constraint(array, pltpu.VMEM)
+
+
+def in_hbm(array):
+    return pltpu.with_memory_space_constraint(array, pltpu.HBM)
 
 
 def swap(array, axis, size, flip):
@@ -86,13 +89,13 @@
     return pl.pallas_call(
         fill_body,
         out_shape=(dense,) * 3,
-        in_specs=[SCALARS] * 4 + [ANYWHERE] * 3,
+        in_specs=[SCALARS] * 4 + [pl.BlockSpec(memory_space=pltpu.HBM)] * 3,
         out_specs=(WHOLE,) * 3,
         scratch_shapes=[pltpu.SemaphoreType.DMA((2,))],
         compiler_params=params(),
         cost_estimate=cost(0, 3 * gate.size * 2),
         name="fill",
-    )(gu_index, gu_count, down_index, down_count, gate, up, down)
+    )(gu_index, gu_count, down_index, down_count, in_hbm(gate), in_hbm(up), in_hbm(down))
 
 
 def gate_up_body(mine, other, gate_w, up_w, own, send):
@@ -340,40 +343,42 @@
     gu_index, down_index = gu_index[0, 0], down_index[0, 0]
     gu_count, down_count = gu_count[0], down_count[0]
 
+    same_core = [[2 * chip + core for chip in range(chips)] for core in range(2)]
+
+    def scatter(array):
+        return lax.all_to_all(
+            array, "wide", split_axis=0, concat_axis=0, axis_index_groups=same_core, tiled=True
+        )
+
     def gather(piece):
-        pieces = [piece] + [swap(piece, "wide", wide, 2 * k) for k in range(1, chips)]
-        return pieces
-
-    def share(pieces):
-        mine = jnp.concatenate(pieces, axis=0)
+        return scatter(jnp.tile(piece, (chips, 1)))
+
+    def share(mine):
         return mine, swap(mine, "wide", wide, 1)
 
     def exchange(array):
         return [swap(array, "narrow", narrow, k) for k in range(1, narrow)]
 
-    x_pieces = gather(tokens)
+    x_mine = gather(tokens)
     gate_w, up_w, down_w = fill(
         gu_index, gu_count, down_index, down_count,
         gate_vals[0, 0], up_vals[0, 0], down_vals[0, 0], f_blocks, d_blocks,
     )
-    x_pieces, cotangent = lax.optimization_barrier((x_pieces, cotangent))
-    y_pieces = gather(cotangent)
-    x_mine, x_other = share(x_pieces)
+    x_mine, cotangent = lax.optimization_barrier((x_mine, cotangent))
+    y_mine = gather(cotangent)
+    x_mine, x_other = share(x_mine)
     gu_own, gu_send = gate_up(x_mine, x_other, gate_w, up_w)
     gu_recv = exchange(gu_send)
-    y_mine, y_other = share(y_pieces)
+    y_mine, y_other = share(y_mine)
     dh_own, dh_send = d_hidden(y_mine, y_other, down_w)
     dh_recv = exchange(dh_send)
     own, send, d_pair, hidden = d_tokens_part(gu_own, dh_own, gu_recv, dh_recv, gate_w, up_w)
     own = own + swap(send, "wide", wide, 1).astype(F32)
     down_grad = down_grads(down_index, down_count, y_mine, y_other, hidden, slots)
-    parts = [own[k * rows : (k + 1) * rows] for k in range(chips)]
-    sends = [part.astype(BF16) for part in parts[1:]]
-    sends, d_pair = lax.optimization_barrier((sends, d_pair))
+    sends, d_pair = lax.optimization_barrier((own.astype(BF16), d_pair))
     gate_grad, up_grad = gu_grads(gu_index, gu_count, x_mine, x_other, d_pair, slots)
-    total = parts[0]
-    for k in range(1, chips):
-        total = total + swap(sends[k - 1], "wide", wide, 2 * k).astype(F32)
+    parts = scatter(sends).reshape(chips, rows, -1)
+    total = jnp.sum(parts.astype(F32), axis=0)
     return (
         total.astype(BF16),
         gate_grad[None, None],

time: 118 us -> 110 us (0.932)
  starting transfers between devices: 40.5 us -> 10.5 us
  blocking collectives: 0 us -> 21.6 us
  local copies, waits for them, and re-layouts: 13.2 us -> 3.9 us
  waiting for transfers between devices: 23.1 us -> 31 us
    ppermute x26 -> x5, starting transfers between devices: 40.5 us -> 2.36 us  [swap(): return lax.ppermute(array, axis, [(i, i ^ flip) for i in range(size)])]
    all_to_all x0 -> x1, blocking collectives: none -> 21.6 us  [scatter(): lax.all_to_all(array, 'wide', split_axis=0, concat_axis=0, axis_index_gro...]
    all_to_all x0 -> x2, waiting for transfers between devices: none -> 14.2 us  [scatter(): lax.all_to_all(array, 'wide', split_axis=0, concat_axis=0, axis_index_gro...]
    unnamed x30 -> x8, local copies, waits for them, and re-layouts: 13.2 us -> 1.36 us
    all_to_all x0 -> x2, starting transfers between devices: none -> 8.12 us  [scatter(): lax.all_to_all(array, 'wide', split_axis=0, concat_axis=0, axis_index_gro...]
    ppermute x26 -> x5, waiting for transfers between devices: 23.1 us -> 16.8 us  [swap(): return lax.ppermute(array, axis, [(i, i ^ flip) for i in range(size)])]
    another operation x0 -> x2, local copies, waits for them, and re-layouts: none -> 2.54 us  [gather(): return scatter(jnp.tile(piece, (chips, 1)))]
  transfers between devices with their start and end apart: 26 -> 7, of which waited for: 6 -> 4; matrix products, arithmetic and copies ran while one was open for 1% -> 0% of each run, Pallas kernels for 26% -> 28%
where the time goes in v1:
time: 110 us; the launch traced here: 109 us
  Pallas kernels  38.6 us (35%)
  waiting for transfers between devices  31 us (28%)
  blocking collectives  21.6 us (20%)
  starting transfers between devices  10.5 us (10%)
  local copies, waits for them, and re-layouts  3.9 us (4%)
  between operations  2.01 us (2%)
  other arithmetic  1.58 us (1%)
    all_to_all x1, blocking collectives, scatter(): lax.all_to_all(array, 'wide', split_axis=0, concat_axis=0, axis_index_gro...  21.6 us
    ppermute x5, waiting for transfers between devices, swap(): return lax.ppermute(array, axis, [(i, i ^ flip) for i in range(size)])  16.8 us
    all_to_all x2, waiting for transfers between devices, scatter(): lax.all_to_all(array, 'wide', split_axis=0, concat_axis=0, axis_index_gro...  14.2 us
    pallas_call x1, Pallas kernels, gu_grads(): pl.pallas_call(gu_grad_body, out_shape=(shape,) * 2, grid_spec=pltpu.Pref...  9.67 us
    all_to_all x2, starting transfers between devices, scatter(): lax.all_to_all(array, 'wide', split_axis=0, concat_axis=0, axis_index_gro...  8.12 us
    pallas_call x1, Pallas kernels, d_tokens_part(): pl.pallas_call(functools.partial(d_tokens_body, others), out_shape=(jax.S...  8.03 us
    pallas_call x1, Pallas kernels, down_grads(): pl.pallas_call(down_grad_body, out_shape=jax.ShapeDtypeStruct((slots, blo...  7.71 us
    pallas_call x1, Pallas kernels, fill(): pl.pallas_call(fill_body, out_shape=(dense,) * 3, in_specs=[SCALARS] * 4...  6.28 us
  transfers between devices with their start and end apart: 7, of which 4 were waited for; matrix products, arithmetic and copies ran while one was open for 0% of the time, Pallas kernels for 28%

profile of v1, /device:TPU:0, one launch (start us, length us, event | category | flops | bytes accessed | tf_op | source)
XLA Modules:
  0.0 109.2 jit_solution(13438774825240714136)
XLA Ops:
  0.6 0.9 tile.4
  1.5 21.6 %all_to_all.26 = bf16[8,8,4096]{2,1,0:T(8,128)(2,1)S(1)} all-to-all(bf16[8,8,4096]{2,1,0:T(8,128)(2,1)S(1)} %tile.4), channel_id=1, replica_groups={{0,4,8,12,16,20,24,28},{2,6,10,14,18,22,26,30},{1,5,9,13,17,21,25,29},{..., dimensions={0} | all-to-all | bytes 1048576 | tf_op jit(solution)/shard_map/all_to_all | solution.py:349
  23.1 1.7 %tile.5 = bf16[8,8,4096]{2,1,0:T(8,128)(2,1)} broadcast(bf16[8,4096]{1,0:T(8,128)(2,1)} %param.10), dimensions={1,2} | broadcast | bytes 589824 | tf_op jit(solution)/shard_map/tile | solution.py:354
  24.8 3.6 %all-to-all-start.1 = ((bf16[8,8,4096]{2,1,0:T(8,128)(2,1)}), bf16[8,8,4096]{2,1,0:T(8,128)(2,1)S(1)}, u32[]{:S(2)}, u32[]{:S(2)}) async-start(bf16[8,8,4096]{2,1,0:T(8,128)(2,1)} %tile.5), calls=%async_computation.1 | async-start | bytes 1048576 | tf_op jit(solution)/shard_map/all_to_all | solution.py:349
  28.4 0.0 collective-permute-start
  28.4 14.2 %all-to-all-done.1 = bf16[8,8,4096]{2,1,0:T(8,128)(2,1)S(1)} async-done(((bf16[8,8,4096]{2,1,0:T(8,128)(2,1)}), bf16[8,8,4096]{2,1,0:T(8,128)(2,1)S(1)}, u32[]{:S(2)}, u32[]{:S(2)}) %all-to-all-start.1) | async-done | bytes 524320 | tf_op jit(solution)/shard_map/all_to_all | solution.py:349
  42.6 0.0 collective-permute-start.1
  43.9 0.0 copy-start
  43.9 0.7 copy-done
  44.5 0.0 copy-start.2
  44.5 0.7 copy-done.2
  45.2 6.3 %fill.1 = (bf16[8,32,128,128]{3,2,1,0:T(8,128)(2,1)S(1)}, bf16[8,32,128,128]{3,2,1,0:T(8,128)(2,1)S(1)}, bf16[8,32,128,128]{3,2,1,0:T(8,128)(2,1)S(1)}) custom-call(s32[192]{0:T(256)S(1)} %bitcast.25, s32[1]{0:T(128)} %bitcast.13.gu_count, s32[192]{0:T(256)S(1)} %bitcast.23, s32[1]{0:T(128)} %bitcast.15.down_count, bf16[192,128,128]{2,1,0:T(8,128)(2,1)} %bitcast.27, ...), custom_call_target="tpu_custom_call" | custom-call | bytes 18874368 | tf_op jit(solution)/shard_map/fill/pallas_call | solution.py:89
  51.5 0.0 collective-permute-done.other
  51.5 3.7 %gate_up.1 = (f32[8,128,256]{2,1,0:T(8,128)S(1)}, bf16[8,128,256]{2,1,0:T(8,128)(2,1)S(1)}) custom-call(bf16[64,4096]{1,0:T(8,128)(2,1)S(1)} %bitcast.21, bf16[64,4096]{1,0:T(8,128)(2,1)S(1)} %collective-permute-done.other, bf16[8,32,128,128]{3,2,1,0:T(8,128)(2,1)S(1)} %get-tuple-element.22.gate_w.refs_4_, ...), custom_call_target="tpu_custom_call" | custom-call | flops 2147483648 | bytes 16777216 | tf_op jit(solution)/shard_map/gate_up/pallas_call | solution.py:123
  55.2 1.8 %collective-permute-start.2 = (bf16[8,128,256]{2,1,0:T(8,128)(2,1)S(1)}, bf16[8,128,256]{2,1,0:T(8,128)(2,1)S(1)}, u32[]{:S(2)}, u32[]{:S(2)}) collective-permute-start(bf16[8,128,256]{2,1,0:T(8,128)(2,1)S(1)} %get-tuple-element.28), channel_id=1, source_target_pairs={{0,1},{1,0},{2,3},{3,2},{4,5},{5,4},{6,7},{7,6},{8,9},{9,8},{10,11... | collective-permute-start | bytes 1572872 | tf_op jit(solution)/shard_map/ppermute | solution.py:36
  57.0 0.0 collective-permute-done.1.other
  57.0 3.3 %d_hidden.1 = (f32[8,128,128]{2,1,0:T(8,128)S(1)}, bf16[8,128,128]{2,1,0:T(8,128)(2,1)S(1)}) custom-call(bf16[64,4096]{1,0:T(8,128)(2,1)S(1)} %bitcast.18, bf16[64,4096]{1,0:T(8,128)(2,1)S(1)} %collective-permute-done.1.other, bf16[8,32,128,128]{3,2,1,0:T(8,128)(2,1)S(1)} %get-tuple-element.26.down_w), custom_call_target="tpu_custom_call" | custom-call | flops 1073741824 | bytes 8388608 | tf_op jit(solution)/shard_map/d_hidden/pallas_call | solution.py:160
  60.3 0.3 collective-permute-start.3
  60.6 9.4 %collective-permute-done.2.refs_2_ = bf16[8,128,256]{2,1,0:T(8,128)(2,1)S(1)} collective-permute-done((bf16[8,128,256]{2,1,0:T(8,128)(2,1)S(1)}, bf16[8,128,256]{2,1,0:T(8,128)(2,1)S(1)}, u32[]{:S(2)}, u32[]{:S(2)}) %collective-permute-start.2) | collective-permute-done | bytes 524320 | tf_op jit(solution)/shard_map/ppermute | solution.py:36
  70.0 5.6 %collective-permute-done.3.refs_3_ = bf16[8,128,128]{2,1,0:T(8,128)(2,1)S(1)} collective-permute-done((bf16[8,128,128]{2,1,0:T(8,128)(2,1)S(1)}, bf16[8,128,128]{2,1,0:T(8,128)(2,1)S(1)}, u32[]{:S(2)}, u32[]{:S(2)}) %collective-permute-start.3) | collective-permute-done | bytes 262176 | tf_op jit(solution)/shard_map/ppermute | solution.py:36
  75.7 8.0 %d_tokens.1 = (f32[64,4096]{1,0:T(8,128)S(1)}, bf16[64,4096]{1,0:T(8,128)(2,1)S(1)}, bf16[8,128,256]{2,1,0:T(8,128)(2,1)S(1)}, bf16[8,128,128]{2,1,0:T(8,128)(2,1)S(1)}) custom-call(f32[8,128,256]{2,1,0:T(8,128)S(1)} %get-tuple-element.24.refs_0_, f32[8,128,128]{2,1,0:T(8,128)S(1)} %get-tuple-element.27.refs_1_, ...), custom_call_target="tpu_custom_call" | custom-call | flops 2147483648 | bytes 16777216 | tf_op jit(solution)/shard_map/d_tokens/pallas_call | solution.py:219
  83.7 0.0 copy-start.3
  83.7 0.2 collective-permute-start.4
  83.9 1.8 %collective-permute-done.4 = bf16[64,4096]{1,0:T(8,128)(2,1)S(1)} collective-permute-done((bf16[64,4096]{1,0:T(8,128)(2,1)S(1)}, bf16[64,4096]{1,0:T(8,128)(2,1)S(1)}, u32[]{:S(2)}, u32[]{:S(2)}) %collective-permute-start.4) | collective-permute-done | bytes 524320 | tf_op jit(solution)/shard_map/ppermute | solution.py:36
  85.7 0.9 add_convert_fusion
  86.6 4.5 %all-to-all-start.2 = ((bf16[8,8,4096]{2,1,0:T(8,128)(2,1)}), bf16[8,8,4096]{2,1,0:T(8,128)(2,1)S(1)}, u32[]{:S(2)}, u32[]{:S(2)}) async-start(bf16[8,8,4096]{2,1,0:T(8,128)(2,1)} %bitcast.31), calls=%async_computation.2 | async-start | bytes 1048576 | tf_op jit(solution)/shard_map/all_to_all | solution.py:349
  91.1 0.0 copy-done.1
  91.1 7.7 %down_grads.1 = bf16[192,128,128]{2,1,0:T(8,128)(2,1)} custom-call(s32[192]{0:T(256)S(1)} %bitcast.24, s32[1]{0:T(128)} %bitcast.16.count, bf16[64,4096]{1,0:T(8,128)(2,1)S(1)} %bitcast.19, bf16[64,4096]{1,0:T(8,128)(2,1)S(1)} %collective-permute-done.1.other, bf16[8,128,128]{2,1,0:T(8,128)(2,1)S(1)} %get-tuple-element.37.hidden), custom_call_target="tpu_custom_call" | custom-call | flops 805306368 | bytes 6291456 | tf_op jit(solution)/shard_map/down_grads/pallas_call | solution.py:313
  98.8 0.0 copy-done.3
  98.8 9.7 %gu_grads.1 = (bf16[192,128,128]{2,1,0:T(8,128)(2,1)}, bf16[192,128,128]{2,1,0:T(8,128)(2,1)}) custom-call(s32[192]{0:T(256)S(1)} %bitcast.26, s32[1]{0:T(128)} %bitcast.14.count, bf16[64,4096]{1,0:T(8,128)(2,1)S(1)} %bitcast.22, bf16[64,4096]{1,0:T(8,128)(2,1)S(1)} %collective-permute-done.other, bf16[8,128,256]{2,1,0:T(8,128)(2,1)S(1)} %get-tuple-element.34.d_pair), custom_call_target="tpu_custom_call" | custom-call | flops 1610612736 | bytes 12582912 | tf_op jit(solution)/shard_map/gu_grads/pallas_call | solution.py:270
  108.5 0.0 all-to-all-done.2
  108.5 0.7 reduce_sum.12
  (1 shorter events, 0.0 us)
Async XLA Ops:
  24.8 17.8 %all-to-all-start.1 = ((bf16[8,8,4096]{2,1,0:T(8,128)(2,1)}), bf16[8,8,4096]{2,1,0:T(8,128)(2,1)S(1)}, u32[]{:S(2)}, u32[]{:S(2)}) async-start(bf16[8,8,4096]{2,1,0:T(8,128)(2,1)} %tile.5), calls=%async_computation.1 | async-start | bytes 1048576 | tf_op jit(solution)/shard_map/all_to_all | solution.py:349
  28.4 23.1 %collective-permute-start = (bf16[64,4096]{1,0:T(8,128)(2,1)S(1)}, bf16[64,4096]{1,0:T(8,128)(2,1)S(1)}, u32[]{:S(2)}, u32[]{:S(2)}) collective-permute-start(bf16[64,4096]{1,0:T(8,128)(2,1)S(1)} %bitcast.20), channel_id=1, source_target_pairs={{0,2},{2,0},{4,6},{6,4},{8,10},{10,8},{12,14},{14,12},{16,18},{18,... | collective-permute-start | bytes 1572872 | tf_op jit(solution)/shard_map/ppermute | solution.py:36
  42.6 14.5 %collective-permute-start.1 = (bf16[64,4096]{1,0:T(8,128)(2,1)S(1)}, bf16[64,4096]{1,0:T(8,128)(2,1)S(1)}, u32[]{:S(2)}, u32[]{:S(2)}) collective-permute-start(bf16[64,4096]{1,0:T(8,128)(2,1)S(1)} %bitcast.17), channel_id=1, source_target_pairs={{0,2},{2,0},{4,6},{6,4},{8,10},{10,8},{12,14},{14,12},{16,18},{18,... | collective-permute-start | bytes 1572872 | tf_op jit(solution)/shard_map/ppermute | solution.py:36
  43.9 0.7 copy-start
  44.5 0.7 copy-start.2
  55.2 14.8 %collective-permute-start.2 = (bf16[8,128,256]{2,1,0:T(8,128)(2,1)S(1)}, bf16[8,128,256]{2,1,0:T(8,128)(2,1)S(1)}, u32[]{:S(2)}, u32[]{:S(2)}) collective-permute-start(bf16[8,128,256]{2,1,0:T(8,128)(2,1)S(1)} %get-tuple-element.28), channel_id=1, source_target_pairs={{0,1},{1,0},{2,3},{3,2},{4,5},{5,4},{6,7},{7,6},{8,9},{9,8},{10,11... | collective-permute-start | bytes 1572872 | tf_op jit(solution)/shard_map/ppermute | solution.py:36
  60.3 15.3 %collective-permute-start.3 = (bf16[8,128,128]{2,1,0:T(8,128)(2,1)S(1)}, bf16[8,128,128]{2,1,0:T(8,128)(2,1)S(1)}, u32[]{:S(2)}, u32[]{:S(2)}) collective-permute-start(bf16[8,128,128]{2,1,0:T(8,128)(2,1)S(1)} %get-tuple-element.29), channel_id=1, source_target_pairs={{0,1},{1,0},{2,3},{3,2},{4,5},{5,4},{6,7},{7,6},{8,9},{9,8},{10,11... | collective-permute-start | bytes 786440 | tf_op jit(solution)/shard_map/ppermute | solution.py:36
  75.7 15.4 %copy-start.1 = (s32[1,1,192]{2,1,0:T(1,128)S(1)}, s32[1,1,192]{2,1,0:T(1,128)}, u32[]{:S(2)}) copy-start(s32[1,1,192]{2,1,0:T(1,128)} %param.16) | copy-start | bytes 2308
  83.7 15.1 %copy-start.3 = (s32[1,1,192]{2,1,0:T(1,128)S(1)}, s32[1,1,192]{2,1,0:T(1,128)}, u32[]{:S(2)}) copy-start(s32[1,1,192]{2,1,0:T(1,128)} %param.13) | copy-start | bytes 2308
  83.7 2.0 %collective-permute-start.4 = (bf16[64,4096]{1,0:T(8,128)(2,1)S(1)}, bf16[64,4096]{1,0:T(8,128)(2,1)S(1)}, u32[]{:S(2)}, u32[]{:S(2)}) collective-permute-start(bf16[64,4096]{1,0:T(8,128)(2,1)S(1)} %get-tuple-element.31), channel_id=1, source_target_pairs={{0,2},{2,0},{4,6},{6,4},{8,10},{10,8},{12,14},{14,12},{16,18},{18,... | collective-permute-start | bytes 1572872 | tf_op jit(solution)/shard_map/ppermute | solution.py:36
  86.6 21.9 %all-to-all-start.2 = ((bf16[8,8,4096]{2,1,0:T(8,128)(2,1)}), bf16[8,8,4096]{2,1,0:T(8,128)(2,1)S(1)}, u32[]{:S(2)}, u32[]{:S(2)}) async-start(bf16[8,8,4096]{2,1,0:T(8,128)(2,1)} %bitcast.31), calls=%async_computation.2 | async-start | bytes 1048576 | tf_op jit(solution)/shard_map/all_to_all | solution.py:349

commit v2 on v1

v2 whole, which is shorter than its diff:
```python
import functools

import jax
import jax.numpy as jnp
from jax import lax
from jax.experimental import pallas as pl
from jax.experimental.pallas import tpu as pltpu
from jax.sharding import PartitionSpec as P

FF = 16384
F32 = jnp.float32
BF16 = jnp.bfloat16
VMEM_LIMIT = 8 * 1024 * 1024

WHOLE = pl.BlockSpec(memory_space=pltpu.VMEM)
SCALARS = pl.BlockSpec(memory_space=pltpu.SMEM)


def params():
    return pltpu.CompilerParams(vmem_limit_bytes=VMEM_LIMIT)


def cost(flops, bytes_accessed):
    return pl.CostEstimate(flops=int(flops), bytes_accessed=int(bytes_accessed), transcendentals=0)


def resident(array):
    return pltpu.with_memory_space_constraint(array, pltpu.VMEM)


def in_hbm(array):
    return pltpu.with_memory_space_constraint(array, pltpu.HBM)


def swap(array, axis, size, flip):
    return lax.ppermute(array, axis, [(i, i ^ flip) for i in range(size)])


def reverse_bits(number, size):
    return sum(size >> (bit + 1) for bit in range(size.bit_length() - 1) if number >> bit & 1)


def fill_body(hidden_first, index, count, slots, rows, dense, rows_out, sem):
    f_blocks, d_blocks = dense.shape[:2]

    def slot_copy(s):
        place = index[0, 0, s]
        if hidden_first:
            target = dense.at[place // d_blocks, place % d_blocks]
        else:
            target = dense.at[place % f_blocks, place // f_blocks]
        return pltpu.make_async_copy(slots.at[0, 0, s], target, sem)

    rows_out[...] = rows[...]

    @pl.loop(0, f_blocks)
    def _(c):
        dense[c] = jnp.zeros(dense.shape[1:], dense.dtype)

    @pl.loop(0, count[0, 0])
    def _(s):
        slot_copy(s).start()

    @pl.loop(0, count[0, 0])
    def _(s):
        slot_copy(s).wait()


def fill(index, count, slots, rows, f_blocks, d_blocks, hidden_first):
    block = slots.shape[-1]
    return pl.pallas_call(
        functools.partial(fill_body, hidden_first),
        out_shape=(
            pltpu.VMEM((f_blocks, d_blocks, block, block), BF16),
            jax.ShapeDtypeStruct(rows.shape, rows.dtype),
        ),
        in_specs=[SCALARS] * 2 + [pl.BlockSpec(memory_space=pltpu.HBM), WHOLE],
        out_specs=(WHOLE,) * 2,
        scratch_shapes=[pltpu.SemaphoreType.DMA],
        compiler_params=params(),
        cost_estimate=cost(0, slots.size * 2),
        name="fill",
    )(index, count, in_hbm(slots), rows)


def stack(pieces):
    return jnp.concatenate([piece[...] for piece in pieces], axis=0)


def gate_up_body(*refs):
    *pieces, gate_w, up_w, own, send = refs
    f_blocks, d_blocks, block, _ = gate_w.shape
    x = stack(pieces)

    @pl.loop(0, f_blocks)
    def _(c):
        weights = jnp.concatenate(
            [
                gate_w[c].reshape(d_blocks * block, block),
                up_w[c].reshape(d_blocks * block, block),
            ],
            axis=1,
        )
        result = jnp.dot(x, weights, preferred_element_type=F32)
        own[c] = result
        send[c] = result.astype(BF16)


def gate_up(pieces, gate_w, up_w):
    f_blocks, d_blocks, block, _ = gate_w.shape
    tokens = sum(piece.shape[0] for piece in pieces)
    shape = (f_blocks, tokens, 2 * block)
    return pl.pallas_call(
        gate_up_body,
        out_shape=(jax.ShapeDtypeStruct(shape, F32), jax.ShapeDtypeStruct(shape, BF16)),
        in_specs=[WHOLE] * (len(pieces) + 2),
        out_specs=(WHOLE,) * 2,
        compiler_params=params(),
        cost_estimate=cost(4 * tokens * gate_w.size, 4 * gate_w.size),
        name="gate_up",
    )(*pieces, resident(gate_w), resident(up_w))


def d_hidden_body(*refs):
    *pieces, down_w, own, send = refs
    f_blocks, d_blocks, block, _ = down_w.shape
    y = stack(pieces)

    @pl.loop(0, f_blocks // 2)
    def _(pair):
        weights = jnp.concatenate(
            [
                down_w[pl.ds(2 * pair, 2), d].reshape(2 * block, block)
                for d in range(d_blocks)
            ],
            axis=1,
        )
        result = lax.dot_general(
            y, weights, (((1,), (1,)), ((), ())), preferred_element_type=F32
        )
        for half in range(2):
            part = result[:, half * block : (half + 1) * block]
            own[2 * pair + half] = part
            send[2 * pair + half] = part.astype(BF16)


def d_hidden(pieces, down_w):
    f_blocks, d_blocks, block, _ = down_w.shape
    tokens = sum(piece.shape[0] for piece in pieces)
    shape = (f_blocks, tokens, block)
    return pl.pallas_call(
        d_hidden_body,
        out_shape=(jax.ShapeDtypeStruct(shape, F32), jax.ShapeDtypeStruct(shape, BF16)),
        in_specs=[WHOLE] * (len(pieces) + 1),
        out_specs=(WHOLE,) * 2,
        compiler_params=params(),
        cost_estimate=cost(2 * tokens * down_w.size, 2 * down_w.size),
        name="d_hidden",
    )(*pieces, resident(down_w))


def d_tokens_body(*refs):
    coef, dh_own, *dh_recv, gate_w, up_w, own, send, d_pair, packed = refs
    f_blocks, d_blocks, block, _ = gate_w.shape
    half = own.shape[0]
    for c in range(f_blocks):
        dh = dh_own[c]
        for part in dh_recv:
            dh = dh + part[c].astype(F32)
        both = (jnp.concatenate([dh, dh], axis=1) * coef[c]).astype(BF16)
        d_pair[c] = both
        packed[:, 2 * block * c : 2 * block * (c + 1)] = both
    grads = packed[...]

    @pl.loop(0, d_blocks // 2)
    def _(pair):
        rows = pl.ds(2 * pair, 2)
        weights = jnp.concatenate(
            [
                ref[c, rows].reshape(2 * block, block)
                for c in range(f_blocks)
                for ref in (gate_w, up_w)
            ],
            axis=1,
        )
        result = lax.dot_general(
            grads, weights, (((1,), (1,)), ((), ())), preferred_element_type=F32
        )
        columns = pl.ds(pl.multiple_of(pair * 2 * block, 2 * block), 2 * block)
        own[:, columns] = result[:half]
        send[:, columns] = result[half:].astype(BF16)


def d_tokens_part(coef, dh_own, dh_recv, gate_w, up_w):
    f_blocks, d_blocks, block, _ = gate_w.shape
    tokens = dh_own.shape[1]
    width = d_blocks * block
    return pl.pallas_call(
        d_tokens_body,
        out_shape=(
            jax.ShapeDtypeStruct((tokens // 2, width), F32),
            jax.ShapeDtypeStruct((tokens // 2, width), BF16),
            jax.ShapeDtypeStruct((f_blocks, tokens, 2 * block), BF16),
        ),
        in_specs=[WHOLE] * (4 + len(dh_recv)),
        out_specs=(WHOLE,) * 3,
        scratch_shapes=[pltpu.VMEM((tokens, f_blocks * 2 * block), BF16)],
        compiler_params=params(),
        cost_estimate=cost(4 * tokens * gate_w.size, 4 * gate_w.size),
        name="d_tokens",
    )(coef, dh_own, *dh_recv, resident(gate_w), resident(up_w))


def merge_body(here, own, recv, out):
    chips = out.shape[0]
    bits = chips.bit_length() - 1
    place = sum(((here[0] >> bit) & 1) << (bits - 1 - bit) for bit in range(bits))
    for chip in range(chips):
        at = reverse_bits(chip, chips) ^ place
        out[chip] = (own[at] + recv[at].astype(F32)).astype(BF16)


def merge(chip, own, recv):
    return pl.pallas_call(
        merge_body,
        out_shape=jax.ShapeDtypeStruct(own.shape, BF16),
        in_specs=[SCALARS] + [WHOLE] * 2,
        out_specs=WHOLE,
        compiler_params=params(),
        cost_estimate=cost(own.size, 8 * own.size),
        name="merge",
    )(chip, own, recv)


def step_slots(slots):
    return max(n for n in range(1, 17) if slots % n == 0)


def gu_grad_body(index, count, *refs):
    *pieces, d_pair, gate_out, up_out, turned = refs
    f_blocks = d_pair.shape[0]
    d_blocks, block, _ = turned.shape
    step = pl.program_id(0)

    @pl.when(step == 0)
    def _():
        for d in range(d_blocks):
            columns = slice(d * block, (d + 1) * block)
            turned[d] = jnp.concatenate([piece[:, columns] for piece in pieces], axis=0).T

    for j in range(gate_out.shape[0]):
        slot = step * gate_out.shape[0] + j
        place = index[0, 0, slot]
        result = jnp.dot(
            turned[place // f_blocks], d_pair[place % f_blocks], preferred_element_type=F32
        )
        result = jnp.where(slot < count[0, 0], result, 0.0).astype(BF16)
        gate_out[j] = result[:, :block]
        up_out[j] = result[:, block:]


def gu_grads(index, count, pieces, d_pair, slots):
    f_blocks, tokens, pair = d_pair.shape
    block = pair // 2
    d_blocks = pieces[0].shape[1] // block
    chunk = step_slots(slots)
    shape = jax.ShapeDtypeStruct((slots, block, block), BF16)
    out = pl.BlockSpec((chunk, block, block), lambda i, *_: (i, 0, 0))
    return pl.pallas_call(
        gu_grad_body,
        out_shape=(shape,) * 2,
        grid_spec=pltpu.PrefetchScalarGridSpec(
            num_scalar_prefetch=2,
            grid=(slots // chunk,),
            in_specs=[WHOLE] * (len(pieces) + 1),
            out_specs=(out,) * 2,
            scratch_shapes=[pltpu.VMEM((d_blocks, block, tokens), BF16)],
        ),
        compiler_params=params(),
        cost_estimate=cost(4 * slots * block * block * tokens, 4 * slots * block * block),
        name="gu_grads",
    )(index, count, *pieces, d_pair)


def down_grad_body(pieces_count, index, count, *refs):
    pieces, gu = refs[:pieces_count], refs[pieces_count:-4]
    out, coef, turned, columns = refs[-4:]
    f_blocks = turned.shape[0]
    d_blocks, _, block = columns.shape
    step = pl.program_id(0)

    @pl.when(step == 0)
    def _():
        for f in range(f_blocks):
            both = gu[0][f]
            for part in gu[1:]:
                both = both + part[f].astype(F32)
            gate, up = both[:, :block], both[:, block:]
            sig = jax.nn.sigmoid(gate)
            silu = gate * sig
            turned[f] = (silu * up).astype(BF16).T
            coef[f, :, :block] = up * sig * (1.0 + gate * (1.0 - sig))
            coef[f, :, block:] = silu
        for d in range(d_blocks):
            at = slice(d * block, (d + 1) * block)
            columns[d] = jnp.concatenate([piece[:, at] for piece in pieces], axis=0)

    for j in range(out.shape[0]):
        slot = step * out.shape[0] + j
        place = index[0, 0, slot]
        result = jnp.dot(
            turned[place // d_blocks], columns[place % d_blocks], preferred_element_type=F32
        )
        out[j] = jnp.where(slot < count[0, 0], result, 0.0).astype(BF16)


def down_grads(index, count, pieces, gu_own, gu_recv, slots):
    f_blocks, tokens, pair = gu_own.shape
    block = pair // 2
    d_blocks = pieces[0].shape[1] // block
    chunk = step_slots(slots)
    return pl.pallas_call(
        functools.partial(down_grad_body, len(pieces)),
        out_shape=(
            jax.ShapeDtypeStruct((slots, block, block), BF16),
            jax.ShapeDtypeStruct(gu_own.shape, F32),
        ),
        grid_spec=pltpu.PrefetchScalarGridSpec(
            num_scalar_prefetch=2,
            grid=(slots // chunk,),
            in_specs=[WHOLE] * (len(pieces) + 1 + len(gu_recv)),
            out_specs=(pl.BlockSpec((chunk, block, block), lambda i, *_: (i, 0, 0)), WHOLE),
            scratch_shapes=[
                pltpu.VMEM((f_blocks, block, tokens), BF16),
                pltpu.VMEM((d_blocks, tokens, block), BF16),
            ],
        ),
        compiler_params=params(),
        cost_estimate=cost(2 * slots * block * block * tokens, 2 * slots * block * block),
        name="down_grads",
    )(index, count, *pieces, gu_own, *gu_recv)


def on_device(
    tokens, cotangent, gate_vals, up_vals, gu_index, gu_count, down_vals, down_index, down_count
):
    block = gate_vals.shape[-1]
    slots = gate_vals.shape[2]
    wide = lax.axis_size("wide")
    narrow = lax.axis_size("narrow")
    chips = wide // 2
    rows = tokens.shape[0]
    d_blocks = tokens.shape[1] // block
    f_blocks = FF // (block * wide)

    def exchange(array):
        return [swap(array, "narrow", narrow, k) for k in range(1, narrow)]

    fills = [
        functools.partial(fill, gu_index, gu_count, gate_vals, hidden_first=False),
        functools.partial(fill, gu_index, gu_count, up_vals, hidden_first=False),
        functools.partial(fill, down_index, down_count, down_vals, hidden_first=True),
    ]
    weights = []

    x, y = tokens, cotangent
    flips = [chips >> hop for hop in range(1, chips.bit_length())]
    for hop, flip in enumerate(flips):
        if hop > 0:
            x = jnp.concatenate([x, x_recv], axis=0)
            y = jnp.concatenate([y, y_recv], axis=0)
        x_recv = swap(x, "wide", wide, 2 * flip)
        y_recv = swap(y, "wide", wide, 2 * flip)
        last = hop == len(flips) - 1
        if last:
            x_across = swap(x, "wide", wide, 1)
            y_across = swap(y, "wide", wide, 1)
        while len(weights) < len(fills) and (last or len(weights) <= hop):
            dense, x = fills[len(weights)](rows=x, f_blocks=f_blocks, d_blocks=d_blocks)
            weights.append(dense)
    x_pieces = [x, x_recv, x_across, swap(x_recv, "wide", wide, 1)]
    y_pieces = [y, y_recv, y_across, swap(y_recv, "wide", wide, 1)]
    gate_w, up_w, down_w = weights

    gu_own, gu_send = gate_up(x_pieces, gate_w, up_w)
    gu_recv = exchange(gu_send)
    dh_own, dh_send = d_hidden(y_pieces, down_w)
    dh_recv = exchange(dh_send)
    down_grad, coef = down_grads(down_index, down_count, y_pieces, gu_own, gu_recv, slots)
    own, send, d_pair = d_tokens_part(coef, dh_own, dh_recv, gate_w, up_w)
    across = swap(send, "wide", wide, 1)
    chip = lax.shift_right_logical(lax.axis_index("wide"), 1)[None]
    split = (chips, rows, tokens.shape[1])
    merged = merge(chip, own.reshape(split), across.reshape(split))
    merged, d_pair = lax.optimization_barrier((merged, d_pair))
    gate_grad, up_grad = gu_grads(gu_index, gu_count, x_pieces, d_pair, slots)
    same_core = [[2 * chip + core for chip in range(chips)] for core in range(2)]
    parts = lax.all_to_all(
        merged, "wide", split_axis=0, concat_axis=0, axis_index_groups=same_core, tiled=True
    )
    total = jnp.sum(parts.astype(F32), axis=0)
    return (
        total.astype(BF16),
        gate_grad[None, None],
        up_grad[None, None],
        down_grad[None, None],
    )


def solution(mesh):
    in_specs = (
        P("wide", "narrow"),
        P("wide", "narrow"),
        P("narrow", "wide", None, None, None),
        P("narrow", "wide", None, None, None),
        P("narrow", "wide", None),
        P("narrow", "wide"),
        P("wide", "narrow", None, None, None),
        P("wide", "narrow", None),
        P("wide", "narrow"),
    )
    out_specs = (
        P("wide", "narrow"),
        P("narrow", "wide", None, None, None),
        P("narrow", "wide", None, None, None),
        P("wide", "narrow", None, None, None),
    )
    return jax.shard_map(
        on_device, mesh=mesh, in_specs=in_specs, out_specs=out_specs, check_vma=False
    )
```

time: 110 us -> 93.9 us (0.85)
  blocking collectives: 21.6 us -> 0 us
  starting transfers between devices: 10.5 us -> 17.6 us
  Pallas kernels: 38.6 us -> 42.9 us
  waiting for transfers between devices: 31 us -> 27 us
  local copies, waits for them, and re-layouts: 3.9 us -> 2.45 us
    all_to_all x1 -> x0, blocking collectives: 21.6 us -> none  [scatter(): lax.all_to_all(array, 'wide', split_axis=0, concat_axis=0, axis_index_gro...]
    ppermute x5 -> x13, starting transfers between devices: 2.36 us -> 12.3 us  [swap(): return lax.ppermute(array, axis, [(i, i ^ flip) for i in range(size)])]
    all_to_all x2 -> x1, waiting for transfers between devices: 14.2 us -> 5.1 us  [on_device(): lax.all_to_all(merged, 'wide', split_axis=0, concat_axis=0, axis_index_gr...]
    ppermute x5 -> x13, waiting for transfers between devices: 16.8 us -> 21.9 us  [swap(): return lax.ppermute(array, axis, [(i, i ^ flip) for i in range(size)])]
    pallas_call x3 -> x6, Pallas kernels: 22 us -> 26.3 us  [the longest x3 8.86 us: fill(): pl.pallas_call(functools.partial(fill_body, hidden_first), out_shape=(plt...]
    all_to_all x2 -> x1, starting transfers between devices: 8.12 us -> 5.31 us  [on_device(): lax.all_to_all(merged, 'wide', split_axis=0, concat_axis=0, axis_index_gr...]
    another operation x2 -> x0, local copies, waits for them, and re-layouts: 2.54 us -> none  [gather(): return scatter(jnp.tile(piece, (chips, 1)))]
    unnamed x8 -> x14, local copies, waits for them, and re-layouts: 1.36 us -> 2.43 us
  transfers between devices with their start and end apart: 7 -> 14, of which waited for: 4 -> 6; matrix products, arithmetic and copies ran while one was open for 0% -> 1% of each run, Pallas kernels for 28% -> 36%
where the time goes in v2:
time: 93.9 us; the launch traced here: 92.7 us
  Pallas kernels  42.9 us (46%)
  waiting for transfers between devices  27 us (29%)
  starting transfers between devices  17.6 us (19%)
  local copies, waits for them, and re-layouts  2.45 us (3%)
  between operations  2.07 us (2%)
    ppermute x13, waiting for transfers between devices, swap(): return lax.ppermute(array, axis, [(i, i ^ flip) for i in range(size)])  21.9 us
    ppermute x13, starting transfers between devices, swap(): return lax.ppermute(array, axis, [(i, i ^ flip) for i in range(size)])  12.3 us
    pallas_call x1, Pallas kernels, gu_grads(): pl.pallas_call(gu_grad_body, out_shape=(shape,) * 2, grid_spec=pltpu.Pref...  9.68 us
    pallas_call x3, Pallas kernels, fill(): pl.pallas_call(functools.partial(fill_body, hidden_first), out_shape=(plt...  8.86 us
    pallas_call x1, Pallas kernels, d_tokens_part(): pl.pallas_call(d_tokens_body, out_shape=(jax.ShapeDtypeStruct((tokens //...  8.6 us
    pallas_call x1, Pallas kernels, down_grads(): pl.pallas_call(functools.partial(down_grad_body, len(pieces)), out_shape=...  7.92 us
    all_to_all x1, starting transfers between devices, on_device(): lax.all_to_all(merged, 'wide', split_axis=0, concat_axis=0, axis_index_gr...  5.31 us
    all_to_all x1, waiting for transfers between devices, on_device(): lax.all_to_all(merged, 'wide', split_axis=0, concat_axis=0, axis_index_gr...  5.1 us
  transfers between devices with their start and end apart: 14, of which 6 were waited for; matrix products, arithmetic and copies ran while one was open for 1% of the time, Pallas kernels for 36%

profile of v2, /device:TPU:0, one launch (start us, length us, event | category | flops | bytes accessed | tf_op | source)
XLA Modules:
  0.0 92.7 jit_solution(17398664155722989451)
XLA Ops:
  0.6 0.0 copy-start.2
  0.7 4.1 %collective-permute-start.5 = (bf16[8,4096]{1,0:T(8,128)(2,1)}, bf16[8,4096]{1,0:T(8,128)(2,1)S(1)}, u32[]{:S(2)}, u32[]{:S(2)}) collective-permute-start(bf16[8,4096]{1,0:T(8,128)(2,1)} %rows.1), channel_id=1, source_target_pairs={{0,16},{2,18},{4,20},{6,22},{8,24},{10,26},{12,28},{14,30},{16,0},... | collective-permute-start | bytes 196616 | tf_op jit(solution)/shard_map/ppermute | solution.py:36
  4.8 0.1 collective-permute-start
  4.8 0.9 constant_dynamic-update-slice_fusion.2
  6.4 0.8 copy-done
  7.2 0.7 copy-done.1
  7.9 2.7 %fill.3 = (bf16[8,32,128,128]{3,2,1,0:T(8,128)(2,1)S(1)}, bf16[8,4096]{1,0:T(8,128)(2,1)S(1)}) custom-call(s32[1,1,192]{2,1,0:T(1,128)S(1)} %copy-done.1, s32[1,1]{1,0:T(1,128)S(6)} %copy.17.count, bf16[1,1,192,128,128]{4,3,2,1,0:T(8,128)(2,1)} %slots.3, bf16[8,4096]{1,0:T(8,128)(2,1)S(1)} %copy-done), custom_call_target="tpu_custom_call" | custom-call | bytes 6291456 | tf_op jit(solution)/shard_map/fill/pallas_call | solution.py:71
  10.6 0.8 collective-permute-done
  11.4 2.3 %collective-permute-start.1 = (bf16[16,4096]{1,0:T(8,128)(2,1)S(1)}, bf16[16,4096]{1,0:T(8,128)(2,1)S(1)}, u32[]{:S(2)}, u32[]{:S(2)}) collective-permute-start(bf16[16,4096]{1,0:T(8,128)(2,1)S(1)} %pad_maximum_fusion), channel_id=1, source_target_pairs={{0,8},{2,10},{4,12},{6,14},{8,0},{10,2},{12,4},{14,6},{16,24},{18,... | collective-permute-start | bytes 393224 | tf_op jit(solution)/shard_map/ppermute | solution.py:36
  13.8 0.1 collective-permute-start.6
  13.9 2.7 %fill.4 = (bf16[8,32,128,128]{3,2,1,0:T(8,128)(2,1)S(1)}, bf16[16,4096]{1,0:T(8,128)(2,1)S(1)}) custom-call(s32[1,1,192]{2,1,0:T(1,128)S(1)} %copy-done.2, s32[1,1]{1,0:T(1,128)S(6)} %copy.17.count, bf16[1,1,192,128,128]{4,3,2,1,0:T(8,128)(2,1)} %slots.4, bf16[16,4096]{1,0:T(8,128)(2,1)S(1)} %constant_dynamic-update-slice_fusion.3.rows), custom_call_target="tpu_custom_call" | custom-call | bytes 6291456 | tf_op jit(solution)/shard_map/fill/pallas_call | solution.py:71
  16.6 2.5 %collective-permute-done.6 = bf16[16,4096]{1,0:T(8,128)(2,1)S(1)} collective-permute-done((bf16[16,4096]{1,0:T(8,128)(2,1)S(1)}, bf16[16,4096]{1,0:T(8,128)(2,1)S(1)}, u32[]{:S(2)}, u32[]{:S(2)}) %collective-permute-start.6) | collective-permute-done | bytes 131104 | tf_op jit(solution)/shard_map/ppermute | solution.py:36
  19.1 2.2 %collective-permute-start.7 = (bf16[32,4096]{1,0:T(8,128)(2,1)S(1)}, bf16[32,4096]{1,0:T(8,128)(2,1)S(1)}, u32[]{:S(2)}, u32[]{:S(2)}) collective-permute-start(bf16[32,4096]{1,0:T(8,128)(2,1)S(1)} %constant_dynamic-update-slice_fusion.5.rows), channel_id=1, source_target_pairs={{0,4},{2,6},{4,0},{6,2},{8,12},{10,14},{12,8},{14,10},{16,20},{18,... | collective-permute-start | bytes 786440 | tf_op jit(solution)/shard_map/ppermute | solution.py:36
  21.4 0.1 collective-permute-start.2
  21.4 0.1 collective-permute-start.8
  21.5 7.0 %collective-permute-done.7.refs_1_ = bf16[32,4096]{1,0:T(8,128)(2,1)S(1)} collective-permute-done((bf16[32,4096]{1,0:T(8,128)(2,1)S(1)}, bf16[32,4096]{1,0:T(8,128)(2,1)S(1)}, u32[]{:S(2)}, u32[]{:S(2)}) %collective-permute-start.7) | collective-permute-done | bytes 262176 | tf_op jit(solution)/shard_map/ppermute | solution.py:36
  29.2 0.6 collective-permute-start.3
  29.8 3.5 %fill.5 = (bf16[8,32,128,128]{3,2,1,0:T(8,128)(2,1)S(1)}, bf16[32,4096]{1,0:T(8,128)(2,1)S(1)}) custom-call(s32[1,1,192]{2,1,0:T(1,128)S(1)} %copy-done.3, s32[1,1]{1,0:T(1,128)S(6)} %copy.18.count, bf16[1,1,192,128,128]{4,3,2,1,0:T(8,128)(2,1)} %slots.5, bf16[32,4096]{1,0:T(8,128)(2,1)S(1)} %constant_dynamic-update-slice_fusion.5.rows), custom_call_target="tpu_custom_call" | custom-call | bytes 6291456 | tf_op jit(solution)/shard_map/fill/pallas_call | solution.py:71
  33.3 0.6 collective-permute-start.4
  33.9 3.7 %gate_up.1 = (f32[8,128,256]{2,1,0:T(8,128)S(1)}, bf16[8,128,256]{2,1,0:T(8,128)(2,1)S(1)}) custom-call(bf16[32,4096]{1,0:T(8,128)(2,1)S(1)} %get-tuple-element.25.refs_0_, bf16[32,4096]{1,0:T(8,128)(2,1)S(1)} %collective-permute-done.7.refs_1_, bf16[32,4096]{1,0:T(8,128)(2,1)S(1)} %collective-permute-done.8.refs_2_, ...), custom_call_target="tpu_custom_call" | custom-call | flops 2147483648 | bytes 16777216 | tf_op jit(solution)/shard_map/gate_up/pallas_call | solution.py:113
  37.5 0.8 collective-permute-start.10
  38.4 3.3 %d_hidden.1 = (f32[8,128,128]{2,1,0:T(8,128)S(1)}, bf16[8,128,128]{2,1,0:T(8,128)(2,1)S(1)}) custom-call(bf16[32,4096]{1,0:T(8,128)(2,1)S(1)} %constant_dynamic-update-slice_fusion.refs_0_, bf16[32,4096]{1,0:T(8,128)(2,1)S(1)} %collective-permute-done.2.refs_1_, bf16[32,4096]{1,0:T(8,128)(2,1)S(1)} %collective-permute-done.3.refs_2_, ...), custom_call_target="tpu_custom_call" | custom-call | flops 1073741824 | bytes 8388608 | tf_op jit(solution)/shard_map/d_hidden/pallas_call | solution.py:151
  41.7 1.3 %collective-permute-start.11 = (bf16[8,128,128]{2,1,0:T(8,128)(2,1)S(1)}, bf16[8,128,128]{2,1,0:T(8,128)(2,1)S(1)}, u32[]{:S(2)}, u32[]{:S(2)}) collective-permute-start(bf16[8,128,128]{2,1,0:T(8,128)(2,1)S(1)} %get-tuple-element.33), channel_id=1, source_target_pairs={{0,1},{1,0},{2,3},{3,2},{4,5},{5,4},{6,7},{7,6},{8,9},{9,8},{10,11... | collective-permute-start | bytes 786440 | tf_op jit(solution)/shard_map/ppermute | solution.py:36
  43.0 9.4 %collective-permute-done.10.refs_5_ = bf16[8,128,256]{2,1,0:T(8,128)(2,1)S(1)} collective-permute-done((bf16[8,128,256]{2,1,0:T(8,128)(2,1)S(1)}, bf16[8,128,256]{2,1,0:T(8,128)(2,1)S(1)}, u32[]{:S(2)}, u32[]{:S(2)}) %collective-permute-start.10) | collective-permute-done | bytes 524320 | tf_op jit(solution)/shard_map/ppermute | solution.py:36
  52.4 7.9 %down_grads.1 = (bf16[192,128,128]{2,1,0:T(8,128)(2,1)}, f32[8,128,256]{2,1,0:T(8,128)S(1)}) custom-call(s32[1,1,192]{2,1,0:T(1,128)S(1)} %copy-done.3, s32[1,1]{1,0:T(1,128)S(6)} %copy.18.count, bf16[32,4096]{1,0:T(8,128)(2,1)S(1)} %constant_dynamic-update-slice_fusion.refs_0_, bf16[32,4096]{1,0:T(8,128)(2,1)S(1)} %collective-permute-done.2.refs_1_, ...), custom_call_target="tpu_custom_call" | custom-call | flops 805306368 | bytes 6291456 | tf_op jit(solution)/shard_map/down_grads/pallas_call | solution.py:322
  60.3 8.6 %d_tokens.1 = (f32[64,4096]{1,0:T(8,128)S(1)}, bf16[64,4096]{1,0:T(8,128)(2,1)}, bf16[8,128,256]{2,1,0:T(8,128)(2,1)S(1)}) custom-call(f32[8,128,256]{2,1,0:T(8,128)S(1)} %get-tuple-element.30.refs_0_, f32[8,128,128]{2,1,0:T(8,128)S(1)} %get-tuple-element.32.refs_1_, bf16[8,128,128]{2,1,0:T(8,128)(2,1)S(1)} %collective-permute-done.11.refs_2_, ...), custom_call_target="tpu_custom_call" | custom-call | flops 2147483648 | bytes 16777216 | tf_op jit(solution)/shard_map/d_tokens/pallas_call | solution.py:198
  68.9 2.1 %collective-permute-done.12 = bf16[64,4096]{1,0:T(8,128)(2,1)S(1)} collective-permute-done((bf16[64,4096]{1,0:T(8,128)(2,1)}, bf16[64,4096]{1,0:T(8,128)(2,1)S(1)}, u32[]{:S(2)}, u32[]{:S(2)}) %collective-permute-start.12) | collective-permute-done | bytes 524320 | tf_op jit(solution)/shard_map/ppermute | solution.py:36
  71.0 0.9 merge.1
  71.9 5.3 %all-to-all-start = ((bf16[8,8,4096]{2,1,0:T(8,128)(2,1)}), bf16[8,8,4096]{2,1,0:T(8,128)(2,1)S(1)}, u32[]{:S(2)}, u32[]{:S(2)}) async-start(bf16[8,8,4096]{2,1,0:T(8,128)(2,1)} %merge.1), calls=%async_computation | async-start | bytes 1048576 | tf_op jit(solution)/shard_map/all_to_all | solution.py:398
  77.2 9.7 %gu_grads.1 = (bf16[192,128,128]{2,1,0:T(8,128)(2,1)}, bf16[192,128,128]{2,1,0:T(8,128)(2,1)}) custom-call(s32[1,1,192]{2,1,0:T(1,128)S(1)} %copy-done.2, s32[1,1]{1,0:T(1,128)S(6)} %copy.17.count, bf16[32,4096]{1,0:T(8,128)(2,1)S(1)} %get-tuple-element.25.refs_0_, bf16[32,4096]{1,0:T(8,128)(2,1)S(1)} %collective-permute-done.7.refs_1_, ...), custom_call_target="tpu_custom_call" | custom-call | flops 1610612736 | bytes 12582912 | tf_op jit(solution)/shard_map/gu_grads/pallas_call | solution.py:269
  86.9 5.1 %all-to-all-done = bf16[8,8,4096]{2,1,0:T(8,128)(2,1)S(1)} async-done(((bf16[8,8,4096]{2,1,0:T(8,128)(2,1)}), bf16[8,8,4096]{2,1,0:T(8,128)(2,1)S(1)}, u32[]{:S(2)}, u32[]{:S(2)}) %all-to-all-start) | async-done | bytes 524320 | tf_op jit(solution)/shard_map/all_to_all | solution.py:398
  92.0 0.7 reduce_sum.12
  (24 shorter events, 0.1 us)
Async XLA Ops:
  0.6 10.8 %copy-start.4 = (bf16[8,4096]{1,0:T(8,128)(2,1)S(1)}, bf16[8,4096]{1,0:T(8,128)(2,1)}, u32[]{:S(2)}) copy-start(bf16[8,4096]{1,0:T(8,128)(2,1)} %param.10) | copy-start | bytes 196612
  0.6 13.3 %copy-start.2 = (s32[1,1,192]{2,1,0:T(1,128)S(1)}, s32[1,1,192]{2,1,0:T(1,128)}, u32[]{:S(2)}) copy-start(s32[1,1,192]{2,1,0:T(1,128)} %index.9) | copy-start | bytes 2308
  0.7 13.1 %collective-permute-start.5 = (bf16[8,4096]{1,0:T(8,128)(2,1)}, bf16[8,4096]{1,0:T(8,128)(2,1)S(1)}, u32[]{:S(2)}, u32[]{:S(2)}) collective-permute-start(bf16[8,4096]{1,0:T(8,128)(2,1)} %rows.1), channel_id=1, source_target_pairs={{0,16},{2,18},{4,20},{6,22},{8,24},{10,26},{12,28},{14,30},{16,0},... | collective-permute-start | bytes 196616 | tf_op jit(solution)/shard_map/ppermute | solution.py:36
  4.8 6.7 %collective-permute-start = (bf16[8,4096]{1,0:T(8,128)(2,1)}, bf16[8,4096]{1,0:T(8,128)(2,1)S(1)}, u32[]{:S(2)}, u32[]{:S(2)}) collective-permute-start(bf16[8,4096]{1,0:T(8,128)(2,1)} %param.10), channel_id=1, source_target_pairs={{0,16},{2,18},{4,20},{6,22},{8,24},{10,26},{12,28},{14,30},{16,0},... | collective-permute-start | bytes 196616 | tf_op jit(solution)/shard_map/ppermute | solution.py:36
  6.4 0.8 copy-start
  7.2 0.7 copy-start.1
  7.9 21.9 %copy-start.3 = (s32[1,1,192]{2,1,0:T(1,128)S(1)}, s32[1,1,192]{2,1,0:T(1,128)}, u32[]{:S(2)}) copy-start(s32[1,1,192]{2,1,0:T(1,128)} %index.8) | copy-start | bytes 2308
  11.4 9.9 %collective-permute-start.1 = (bf16[16,4096]{1,0:T(8,128)(2,1)S(1)}, bf16[16,4096]{1,0:T(8,128)(2,1)S(1)}, u32[]{:S(2)}, u32[]{:S(2)}) collective-permute-start(bf16[16,4096]{1,0:T(8,128)(2,1)S(1)} %pad_maximum_fusion), channel_id=1, source_target_pairs={{0,8},{2,10},{4,12},{6,14},{8,0},{10,2},{12,4},{14,6},{16,24},{18,... | collective-permute-start | bytes 393224 | tf_op jit(solution)/shard_map/ppermute | solution.py:36
  13.8 5.3 %collective-permute-start.6 = (bf16[16,4096]{1,0:T(8,128)(2,1)S(1)}, bf16[16,4096]{1,0:T(8,128)(2,1)S(1)}, u32[]{:S(2)}, u32[]{:S(2)}) collective-permute-start(bf16[16,4096]{1,0:T(8,128)(2,1)S(1)} %constant_dynamic-update-slice_fusion.3.rows), channel_id=1, source_target_pairs={{0,8},{2,10},{4,12},{6,14},{8,0},{10,2},{12,4},{14,6},{16,24},{18,... | collective-permute-start | bytes 393224 | tf_op jit(solution)/shard_map/ppermute | solution.py:36
  19.1 9.4 %collective-permute-start.7 = (bf16[32,4096]{1,0:T(8,128)(2,1)S(1)}, bf16[32,4096]{1,0:T(8,128)(2,1)S(1)}, u32[]{:S(2)}, u32[]{:S(2)}) collective-permute-start(bf16[32,4096]{1,0:T(8,128)(2,1)S(1)} %constant_dynamic-update-slice_fusion.5.rows), channel_id=1, source_target_pairs={{0,4},{2,6},{4,0},{6,2},{8,12},{10,14},{12,8},{14,10},{16,20},{18,... | collective-permute-start | bytes 786440 | tf_op jit(solution)/shard_map/ppermute | solution.py:36
  21.4 11.9 %collective-permute-start.2 = (bf16[32,4096]{1,0:T(8,128)(2,1)S(1)}, bf16[32,4096]{1,0:T(8,128)(2,1)S(1)}, u32[]{:S(2)}, u32[]{:S(2)}) collective-permute-start(bf16[32,4096]{1,0:T(8,128)(2,1)S(1)} %constant_dynamic-update-slice_fusion.refs_0_), channel_id=1, source_target_pairs={{0,4},{2,6},{4,0},{6,2},{8,12},{10,14},{12,8},{14,10},{16,20},{18,... | collective-permute-start | bytes 786440 | tf_op jit(solution)/shard_map/ppermute | solution.py:36
  21.4 12.4 %collective-permute-start.8 = (bf16[32,4096]{1,0:T(8,128)(2,1)S(1)}, bf16[32,4096]{1,0:T(8,128)(2,1)S(1)}, u32[]{:S(2)}, u32[]{:S(2)}) collective-permute-start(bf16[32,4096]{1,0:T(8,128)(2,1)S(1)} %constant_dynamic-update-slice_fusion.5.rows), channel_id=1, source_target_pairs={{0,2},{2,0},{4,6},{6,4},{8,10},{10,8},{12,14},{14,12},{16,18},{18,... | collective-permute-start | bytes 786440 | tf_op jit(solution)/shard_map/ppermute | solution.py:36
  28.6 5.3 %collective-permute-start.9 = (bf16[32,4096]{1,0:T(8,128)(2,1)S(1)}, bf16[32,4096]{1,0:T(8,128)(2,1)S(1)}, u32[]{:S(2)}, u32[]{:S(2)}) collective-permute-start(bf16[32,4096]{1,0:T(8,128)(2,1)S(1)} %collective-permute-done.7.refs_1_), channel_id=1, source_target_pairs={{0,2},{2,0},{4,6},{6,4},{8,10},{10,8},{12,14},{14,12},{16,18},{18,... | collective-permute-start | bytes 786440 | tf_op jit(solution)/shard_map/ppermute | solution.py:36
  29.2 9.2 %collective-permute-start.3 = (bf16[32,4096]{1,0:T(8,128)(2,1)S(1)}, bf16[32,4096]{1,0:T(8,128)(2,1)S(1)}, u32[]{:S(2)}, u32[]{:S(2)}) collective-permute-start(bf16[32,4096]{1,0:T(8,128)(2,1)S(1)} %constant_dynamic-update-slice_fusion.refs_0_), channel_id=1, source_target_pairs={{0,2},{2,0},{4,6},{6,4},{8,10},{10,8},{12,14},{14,12},{16,18},{18,... | collective-permute-start | bytes 786440 | tf_op jit(solution)/shard_map/ppermute | solution.py:36
  33.3 5.1 %collective-permute-start.4 = (bf16[32,4096]{1,0:T(8,128)(2,1)S(1)}, bf16[32,4096]{1,0:T(8,128)(2,1)S(1)}, u32[]{:S(2)}, u32[]{:S(2)}) collective-permute-start(bf16[32,4096]{1,0:T(8,128)(2,1)S(1)} %collective-permute-done.2.refs_1_), channel_id=1, source_target_pairs={{0,2},{2,0},{4,6},{6,4},{8,10},{10,8},{12,14},{14,12},{16,18},{18,... | collective-permute-start | bytes 786440 | tf_op jit(solution)/shard_map/ppermute | solution.py:36
  37.5 14.9 %collective-permute-start.10 = (bf16[8,128,256]{2,1,0:T(8,128)(2,1)S(1)}, bf16[8,128,256]{2,1,0:T(8,128)(2,1)S(1)}, u32[]{:S(2)}, u32[]{:S(2)}) collective-permute-start(bf16[8,128,256]{2,1,0:T(8,128)(2,1)S(1)} %get-tuple-element.29), channel_id=1, source_target_pairs={{0,1},{1,0},{2,3},{3,2},{4,5},{5,4},{6,7},{7,6},{8,9},{9,8},{10,11... | collective-permute-start | bytes 1572872 | tf_op jit(solution)/shard_map/ppermute | solution.py:36
  41.7 18.7 %collective-permute-start.11 = (bf16[8,128,128]{2,1,0:T(8,128)(2,1)S(1)}, bf16[8,128,128]{2,1,0:T(8,128)(2,1)S(1)}, u32[]{:S(2)}, u32[]{:S(2)}) collective-permute-start(bf16[8,128,128]{2,1,0:T(8,128)(2,1)S(1)} %get-tuple-element.33), channel_id=1, source_target_pairs={{0,1},{1,0},{2,3},{3,2},{4,5},{5,4},{6,7},{7,6},{8,9},{9,8},{10,11... | collective-permute-start | bytes 786440 | tf_op jit(solution)/shard_map/ppermute | solution.py:36
  68.9 2.1 %collective-permute-start.12 = (bf16[64,4096]{1,0:T(8,128)(2,1)}, bf16[64,4096]{1,0:T(8,128)(2,1)S(1)}, u32[]{:S(2)}, u32[]{:S(2)}) collective-permute-start(bf16[64,4096]{1,0:T(8,128)(2,1)} %get-tuple-element.35), channel_id=1, source_target_pairs={{0,2},{2,0},{4,6},{6,4},{8,10},{10,8},{12,14},{14,12},{16,18},{18,... | collective-permute-start | bytes 1572872 | tf_op jit(solution)/shard_map/ppermute | solution.py:36
  71.9 20.1 %all-to-all-start = ((bf16[8,8,4096]{2,1,0:T(8,128)(2,1)}), bf16[8,8,4096]{2,1,0:T(8,128)(2,1)S(1)}, u32[]{:S(2)}, u32[]{:S(2)}) async-start(bf16[8,8,4096]{2,1,0:T(8,128)(2,1)} %merge.1), calls=%async_computation | async-start | bytes 1048576 | tf_op jit(solution)/shard_map/all_to_all | solution.py:398

commit v3 on v2

v3 whole, which is shorter than its diff:
```python
import functools

import jax
import jax.numpy as jnp
from jax import lax
from jax.experimental import pallas as pl
from jax.experimental.pallas import tpu as pltpu
from jax.sharding import PartitionSpec as P

FF = 16384
F32 = jnp.float32
BF16 = jnp.bfloat16
VMEM_LIMIT = 8 * 1024 * 1024

WHOLE = pl.BlockSpec(memory_space=pltpu.VMEM)
SCALARS = pl.BlockSpec(memory_space=pltpu.SMEM)


def params():
    return pltpu.CompilerParams(vmem_limit_bytes=VMEM_LIMIT)


def cost(flops, bytes_accessed):
    return pl.CostEstimate(flops=int(flops), bytes_accessed=int(bytes_accessed), transcendentals=0)


def resident(array):
    return pltpu.with_memory_space_constraint(array, pltpu.VMEM)


def in_hbm(array):
    return pltpu.with_memory_space_constraint(array, pltpu.HBM)


def swap(array, axis, size, flip):
    return lax.ppermute(array, axis, [(i, i ^ flip) for i in range(size)])


def split_index(number, size):
    if size & (size - 1):
        return number // size, number % size
    return number >> (size.bit_length() - 1), number & (size - 1)


def reverse_bits(number, size):
    return sum(size >> (bit + 1) for bit in range(size.bit_length() - 1) if number >> bit & 1)


def fill_body(index, count, slots, dense, seen, sem):
    outer, inner = dense.shape[:2]
    live = count[0, 0]
    chunk = min(inner, 8)

    @pl.loop(0, outer * inner, unroll=8)
    def _(place):
        seen[place] = 0

    @pl.loop(0, live)
    def _(s):
        place = index[0, 0, s]
        seen[place] = 1
        high, low = split_index(place, inner)
        pltpu.make_async_copy(slots.at[0, 0, s], dense.at[high, low], sem).start()

    @pl.loop(0, outer)
    def _(high):
        for low in range(inner):

            @pl.when(seen[high * inner + low] == 0)
            def _():
                dense[high, low] = jnp.zeros(dense.shape[2:], dense.dtype)

    many, few = split_index(live, chunk)

    @pl.loop(0, many)
    def _(_):
        blocks = pl.ds(0, chunk)
        pltpu.make_async_copy(slots.at[0, 0, blocks], dense.at[0, blocks], sem).wait()

    @pl.loop(0, few)
    def _(_):
        pltpu.make_async_copy(slots.at[0, 0, 0], dense.at[0, 0], sem).wait()


def fill(index, count, slots, outer, inner):
    block = slots.shape[-1]
    return pl.pallas_call(
        fill_body,
        out_shape=pltpu.VMEM((outer, inner, block, block), BF16),
        in_specs=[SCALARS] * 2 + [pl.BlockSpec(memory_space=pltpu.HBM)],
        out_specs=WHOLE,
        scratch_shapes=[pltpu.SMEM((outer * inner,), jnp.int32), pltpu.SemaphoreType.DMA],
        compiler_params=params(),
        cost_estimate=cost(0, slots.size * 2),
        name="fill",
    )(index, count, in_hbm(slots))


def stack(pieces):
    return jnp.concatenate([piece[...] for piece in pieces], axis=0)


def gate_up_body(*refs):
    *pieces, gate_w, up_w, own, send = refs
    d_blocks, f_blocks, block, _ = gate_w.shape
    x = stack(pieces)

    @pl.loop(0, f_blocks)
    def _(c):
        weights = jnp.concatenate(
            [
                gate_w[:, c].reshape(d_blocks * block, block),
                up_w[:, c].reshape(d_blocks * block, block),
            ],
            axis=1,
        )
        result = jnp.dot(x, weights, preferred_element_type=F32)
        own[c] = result
        send[c] = result.astype(BF16)


def gate_up(pieces, gate_w, up_w):
    d_blocks, f_blocks, block, _ = gate_w.shape
    tokens = sum(piece.shape[0] for piece in pieces)
    shape = (f_blocks, tokens, 2 * block)
    return pl.pallas_call(
        gate_up_body,
        out_shape=(jax.ShapeDtypeStruct(shape, F32), jax.ShapeDtypeStruct(shape, BF16)),
        in_specs=[WHOLE] * (len(pieces) + 2),
        out_specs=(WHOLE,) * 2,
        compiler_params=params(),
        cost_estimate=cost(4 * tokens * gate_w.size, 4 * gate_w.size),
        name="gate_up",
    )(*pieces, resident(gate_w), resident(up_w))


def d_hidden_body(pieces_count, *refs):
    y_pieces, x_pieces = refs[:pieces_count], refs[pieces_count : 2 * pieces_count]
    down_w, own, send, turned = refs[2 * pieces_count :]
    f_blocks, d_blocks, block, _ = down_w.shape
    y = stack(y_pieces)

    @pl.loop(0, f_blocks // 2)
    def _(pair):
        weights = jnp.concatenate(
            [
                down_w[pl.ds(2 * pair, 2), d].reshape(2 * block, block)
                for d in range(d_blocks)
            ],
            axis=1,
        )
        result = lax.dot_general(
            y, weights, (((1,), (1,)), ((), ())), preferred_element_type=F32
        )
        for half in range(2):
            part = result[:, half * block : (half + 1) * block]
            own[2 * pair + half] = part
            send[2 * pair + half] = part.astype(BF16)

    for d in range(d_blocks):
        columns = slice(d * block, (d + 1) * block)
        turned[d] = jnp.concatenate([piece[:, columns] for piece in x_pieces], axis=0).T


def d_hidden(y_pieces, x_pieces, down_w):
    f_blocks, d_blocks, block, _ = down_w.shape
    tokens = sum(piece.shape[0] for piece in y_pieces)
    shape = (f_blocks, tokens, block)
    return pl.pallas_call(
        functools.partial(d_hidden_body, len(y_pieces)),
        out_shape=(
            jax.ShapeDtypeStruct(shape, F32),
            jax.ShapeDtypeStruct(shape, BF16),
            jax.ShapeDtypeStruct((d_blocks, block, tokens), BF16),
        ),
        in_specs=[WHOLE] * (2 * len(y_pieces) + 1),
        out_specs=(WHOLE,) * 3,
        compiler_params=params(),
        cost_estimate=cost(2 * tokens * down_w.size, 2 * down_w.size),
        name="d_hidden",
    )(*y_pieces, *x_pieces, resident(down_w))


def d_tokens_body(group, *refs):
    coef, dh_own, *dh_recv, gate_w, up_w, own, send, d_pair, turned = refs
    d_blocks, f_blocks, block, _ = gate_w.shape
    half = own.shape[0]
    for c in range(f_blocks):
        dh = dh_own[c]
        for part in dh_recv:
            dh = dh + part[c].astype(F32)
        both = (jnp.concatenate([dh, dh], axis=1) * coef[c]).astype(BF16)
        d_pair[c] = both
        for side in range(2):
            turned[pl.ds((2 * c + side) * block, block), :] = both[
                :, side * block : (side + 1) * block
            ].T
    grads = turned[...]

    @pl.loop(0, d_blocks // group)
    def _(at):
        rows = pl.ds(at * group, group)
        weights = jnp.concatenate(
            [
                ref[rows, c].reshape(group * block, block)
                for c in range(f_blocks)
                for ref in (gate_w, up_w)
            ],
            axis=1,
        )
        result = jnp.dot(weights, grads, preferred_element_type=F32).T
        columns = pl.ds(pl.multiple_of(at * group * block, group * block), group * block)
        own[:, columns] = result[:half]
        send[:, columns] = result[half:].astype(BF16)


def d_tokens_part(coef, dh_own, dh_recv, gate_w, up_w):
    d_blocks, f_blocks, block, _ = gate_w.shape
    tokens = dh_own.shape[1]
    width = d_blocks * block
    group = max(n for n in (1, 2, 4) if d_blocks % n == 0)
    return pl.pallas_call(
        functools.partial(d_tokens_body, group),
        out_shape=(
            jax.ShapeDtypeStruct((tokens // 2, width), F32),
            jax.ShapeDtypeStruct((tokens // 2, width), BF16),
            jax.ShapeDtypeStruct((f_blocks, tokens, 2 * block), BF16),
        ),
        in_specs=[WHOLE] * (4 + len(dh_recv)),
        out_specs=(WHOLE,) * 3,
        scratch_shapes=[pltpu.VMEM((f_blocks * 2 * block, tokens), BF16)],
        compiler_params=params(),
        cost_estimate=cost(4 * tokens * gate_w.size, 4 * gate_w.size),
        name="d_tokens",
    )(coef, dh_own, *dh_recv, resident(gate_w), resident(up_w))


def step_slots(slots):
    return max(n for n in range(1, 17) if slots % n == 0)


def gu_grad_body(first, index, count, d_pair, turned, *refs):
    gate_out, up_out = refs[-2:]
    f_blocks = d_pair.shape[0]
    block = turned.shape[1]
    step = pl.program_id(0) + first

    for j in range(gate_out.shape[0]):
        slot = step * gate_out.shape[0] + j
        d, f = split_index(index[0, 0, slot], f_blocks)
        result = jnp.dot(turned[d], d_pair[f], preferred_element_type=F32)
        result = jnp.where(slot < count[0, 0], result, 0.0).astype(BF16)
        gate_out[j] = result[:, :block]
        up_out[j] = result[:, block:]


def gu_grads(index, count, d_pair, turned, slots, part, parts, before):
    block, tokens = turned.shape[1:]
    chunk = step_slots(slots // parts)
    steps = slots // parts // chunk
    first = part * steps
    shape = jax.ShapeDtypeStruct((slots, block, block), BF16)
    out = pl.BlockSpec((chunk, block, block), lambda i, *_: (i + first, 0, 0))
    flops = 4 * slots * block * block * tokens
    return pl.pallas_call(
        functools.partial(gu_grad_body, first),
        out_shape=(shape,) * 2,
        grid_spec=pltpu.PrefetchScalarGridSpec(
            num_scalar_prefetch=2,
            grid=(steps,),
            in_specs=[WHOLE] * 2 + [pl.BlockSpec(memory_space=pl.ANY)] * len(before),
            out_specs=(out,) * 2,
        ),
        input_output_aliases={4 + at: at for at in range(len(before))},
        compiler_params=params(),
        cost_estimate=cost(flops // parts, 4 * slots * block * block // parts),
        name="gu_grads",
    )(index, count, d_pair, turned, *before)


def down_grad_body(pieces_count, index, count, *refs):
    pieces, gu = refs[:pieces_count], refs[pieces_count:-4]
    out, coef, turned, columns = refs[-4:]
    f_blocks = turned.shape[0]
    d_blocks, _, block = columns.shape
    step = pl.program_id(0)

    @pl.when(step == 0)
    def _():
        for f in range(f_blocks):
            both = gu[0][f]
            for part in gu[1:]:
                both = both + part[f].astype(F32)
            gate, up = both[:, :block], both[:, block:]
            sig = jax.nn.sigmoid(gate)
            silu = gate * sig
            turned[f] = (silu * up).astype(BF16).T
            coef[f, :, :block] = up * sig * (1.0 + gate * (1.0 - sig))
            coef[f, :, block:] = silu
        for d in range(d_blocks):
            at = slice(d * block, (d + 1) * block)
            columns[d] = jnp.concatenate([piece[:, at] for piece in pieces], axis=0)

    for j in range(out.shape[0]):
        slot = step * out.shape[0] + j
        f, d = split_index(index[0, 0, slot], d_blocks)
        result = jnp.dot(turned[f], columns[d], preferred_element_type=F32)
        out[j] = jnp.where(slot < count[0, 0], result, 0.0).astype(BF16)


def down_grads(index, count, pieces, gu_own, gu_recv, slots):
    f_blocks, tokens, pair = gu_own.shape
    block = pair // 2
    d_blocks = pieces[0].shape[1] // block
    chunk = step_slots(slots)
    return pl.pallas_call(
        functools.partial(down_grad_body, len(pieces)),
        out_shape=(
            jax.ShapeDtypeStruct((slots, block, block), BF16),
            jax.ShapeDtypeStruct(gu_own.shape, F32),
        ),
        grid_spec=pltpu.PrefetchScalarGridSpec(
            num_scalar_prefetch=2,
            grid=(slots // chunk,),
            in_specs=[WHOLE] * (len(pieces) + 1 + len(gu_recv)),
            out_specs=(pl.BlockSpec((chunk, block, block), lambda i, *_: (i, 0, 0)), WHOLE),
            scratch_shapes=[
                pltpu.VMEM((f_blocks, block, tokens), BF16),
                pltpu.VMEM((d_blocks, tokens, block), BF16),
            ],
        ),
        compiler_params=params(),
        cost_estimate=cost(2 * slots * block * block * tokens, 2 * slots * block * block),
        name="down_grads",
    )(index, count, *pieces, gu_own, *gu_recv)


def on_device(
    tokens, cotangent, gate_vals, up_vals, gu_index, gu_count, down_vals, down_index, down_count
):
    block = gate_vals.shape[-1]
    slots = gate_vals.shape[2]
    wide = lax.axis_size("wide")
    narrow = lax.axis_size("narrow")
    chips = wide // 2
    rows = tokens.shape[0]
    d_blocks = tokens.shape[1] // block
    f_blocks = FF // (block * wide)

    def exchange(array):
        return [swap(array, "narrow", narrow, k) for k in range(1, narrow)]

    x, y = tokens, cotangent
    weights = []
    index = gu_index
    flips = [chips >> hop for hop in range(1, chips.bit_length())]
    for hop, flip in enumerate(flips):
        if hop > 0:
            x = jnp.concatenate([x, x_recv], axis=0)
            y = jnp.concatenate([y, y_recv], axis=0)
            x, weights, index = lax.optimization_barrier((x, weights, index))
        x_recv = swap(x, "wide", wide, 2 * flip)
        if hop == len(flips) - 1:
            x_across = swap(x, "wide", wide, 1)
        if len(weights) < 2:
            slots_of = (gate_vals, up_vals)[hop]
            weights.append(fill(index, gu_count, slots_of, d_blocks, f_blocks))
        y, _ = lax.optimization_barrier((y, x_recv))
        y_recv = swap(y, "wide", wide, 2 * flip)
    x_pieces = [x, x_recv, x_across, swap(x_recv, "wide", wide, 1)]
    gate_w, up_w = weights

    gu_own, gu_send = gate_up(x_pieces, gate_w, up_w)
    gu_recv = exchange(gu_send)
    late_index, y, y_recv, _ = lax.optimization_barrier((down_index, y, y_recv, gu_send))
    y_across = swap(y, "wide", wide, 1)
    down_w = fill(late_index, down_count, down_vals, f_blocks, d_blocks)
    y_pieces = [y, y_recv, y_across, swap(y_recv, "wide", wide, 1)]
    dh_own, dh_send, turned = d_hidden(y_pieces, x_pieces, down_w)
    dh_recv = exchange(dh_send)
    down_grad, coef = down_grads(down_index, down_count, y_pieces, gu_own, gu_recv, slots)
    own, send, d_pair = d_tokens_part(coef, dh_own, dh_recv, gate_w, up_w)

    own = own + swap(send, "wide", wide, 1).astype(F32)
    kept = chips // 2 * rows
    far = own[kept:].astype(BF16)
    own = own[:kept]
    parts = 2 if slots % 2 == 0 else 1
    far, d_pair = lax.optimization_barrier((far, d_pair))
    grads = gu_grads(gu_index, gu_count, d_pair, turned, slots, 0, parts, ())
    own = own + swap(far, "wide", wide, 2).astype(F32)
    sends = [own[p * rows : (p + 1) * rows].astype(BF16) for p in range(1, chips // 2)]
    if parts == 2:
        sends, d_pair = lax.optimization_barrier((sends, d_pair))
        grads = gu_grads(gu_index, gu_count, d_pair, turned, slots, 1, parts, grads)
    gate_grad, up_grad = grads
    total = own[:rows]
    for p, part in enumerate(sends, 1):
        total = total + swap(part, "wide", wide, 2 * reverse_bits(p, chips)).astype(F32)
    return (
        total.astype(BF16),
        gate_grad[None, None],
        up_grad[None, None],
        down_grad[None, None],
    )


def solution(mesh):
    in_specs = (
        P("wide", "narrow"),
        P("wide", "narrow"),
        P("narrow", "wide", None, None, None),
        P("narrow", "wide", None, None, None),
        P("narrow", "wide", None),
        P("narrow", "wide"),
        P("wide", "narrow", None, None, None),
        P("wide", "narrow", None),
        P("wide", "narrow"),
    )
    out_specs = (
        P("wide", "narrow"),
        P("narrow", "wide", None, None, None),
        P("narrow", "wide", None, None, None),
        P("wide", "narrow", None, None, None),
    )
    return jax.shard_map(
        on_device, mesh=mesh, in_specs=in_specs, out_specs=out_specs, check_vma=False
    )
```

time: 93.9 us -> 84 us (0.89); the launches traced: 92.7 us -> 83.8 us
  waiting for transfers between devices: 27 us -> 16.9 us
  starting transfers between devices: 17.6 us -> 19.6 us
  local copies, waits for them, and re-layouts: 2.45 us -> 0.73 us
    ppermute x13 -> x17, starting transfers between devices: 12.3 us -> 19.6 us  [swap(): return lax.ppermute(array, axis, [(i, i ^ flip) for i in range(size)])]
    all_to_all x1 -> x0, starting transfers between devices: 5.31 us -> none  [on_device(): lax.all_to_all(merged, 'wide', split_axis=0, concat_axis=0, axis_index_gr...]
    all_to_all x1 -> x0, waiting for transfers between devices: 5.1 us -> none  [on_device(): lax.all_to_all(merged, 'wide', split_axis=0, concat_axis=0, axis_index_gr...]
    ppermute x13 -> x17, waiting for transfers between devices: 21.9 us -> 16.9 us  [swap(): return lax.ppermute(array, axis, [(i, i ^ flip) for i in range(size)])]
    unnamed x14 -> x10, local copies, waits for them, and re-layouts: 2.43 us -> 0.69 us
  transfers between devices with their start and end apart: 14 -> 17, of which waited for: 6 -> 6; matrix products, arithmetic and copies ran while one was open for 1% -> 0% of each run, Pallas kernels for 36% -> 44%
where the time goes in v3:
time: 84 us; the launch traced here: 83.8 us
  Pallas kernels  43.6 us (52%)
  starting transfers between devices  19.6 us (23%)
  waiting for transfers between devices  16.9 us (20%)
  between operations  2.12 us (3%)
  other arithmetic  0.88 us (1%)
    ppermute x17, starting transfers between devices, swap(): return lax.ppermute(array, axis, [(i, i ^ flip) for i in range(size)])  19.6 us
    ppermute x17, waiting for transfers between devices, swap(): return lax.ppermute(array, axis, [(i, i ^ flip) for i in range(size)])  16.9 us
    pallas_call x3, Pallas kernels, fill(): pl.pallas_call(fill_body, out_shape=pltpu.VMEM((outer, inner, block, bloc...  11.6 us
    pallas_call x2, Pallas kernels, gu_grads(): pl.pallas_call(functools.partial(gu_grad_body, first), out_shape=(shape,)...  10.4 us
    pallas_call x1, Pallas kernels, down_grads(): pl.pallas_call(functools.partial(down_grad_body, len(pieces)), out_shape=...  7.84 us
    pallas_call x1, Pallas kernels, d_tokens_part(): pl.pallas_call(functools.partial(d_tokens_body, group), out_shape=(jax.Sh...  6.49 us
    pallas_call x1, Pallas kernels, gate_up(): pl.pallas_call(gate_up_body, out_shape=(jax.ShapeDtypeStruct(shape, F32),...  3.66 us
    pallas_call x1, Pallas kernels, d_hidden(): pl.pallas_call(functools.partial(d_hidden_body, len(y_pieces)), out_shape...  3.59 us
  transfers between devices with their start and end apart: 17, of which 6 were waited for; matrix products, arithmetic and copies ran while one was open for 0% of the time, Pallas kernels for 44%

profile of v3, /device:TPU:0, one launch (start us, length us, event | category | flops | bytes accessed | tf_op | source)
XLA Modules:
  0.0 83.8 jit_solution(7269147583235235830)
XLA Ops:
  0.6 4.1 %collective-permute-start = (bf16[8,4096]{1,0:T(8,128)(2,1)}, bf16[8,4096]{1,0:T(8,128)(2,1)S(1)}, u32[]{:S(2)}, u32[]{:S(2)}) collective-permute-start(bf16[8,4096]{1,0:T(8,128)(2,1)} %param.9), channel_id=1, source_target_pairs={{0,16},{2,18},{4,20},{6,22},{8,24},{10,26},{12,28},{14,30},{16,0},... | collective-permute-start | bytes 196616 | tf_op jit(solution)/shard_map/ppermute | solution.py:36
  5.4 0.7 copy-done
  6.1 4.0 %fill.3.refs_4_.refs_3_ = bf16[32,8,128,128]{3,2,1,0:T(8,128)(2,1)S(1)} custom-call(s32[1,1,192]{2,1,0:T(1,128)S(1)} %copy-done, s32[1,1]{1,0:T(1,128)S(6)} %copy.17.count, bf16[1,1,192,128,128]{4,3,2,1,0:T(8,128)(2,1)} %slots.3), custom_call_target="tpu_custom_call" | custom-call | bytes 6291456 | tf_op jit(solution)/shard_map/fill/pallas_call | solution.py:87
  10.2 1.5 %collective-permute-start.2 = (bf16[16,4096]{1,0:T(8,128)(2,1)S(1)}, bf16[16,4096]{1,0:T(8,128)(2,1)S(1)}, u32[]{:S(2)}, u32[]{:S(2)}) collective-permute-start(bf16[16,4096]{1,0:T(8,128)(2,1)S(1)} %pad_maximum_fusion.3), channel_id=1, source_target_pairs={{0,8},{2,10},{4,12},{6,14},{8,0},{10,2},{12,4},{14,6},{16,24},{18,... | collective-permute-start | bytes 393224 | tf_op jit(solution)/shard_map/ppermute | solution.py:36
  11.6 1.0 %collective-permute-start.1 = (bf16[8,4096]{1,0:T(8,128)(2,1)S(1)}, bf16[8,4096]{1,0:T(8,128)(2,1)S(1)}, u32[]{:S(2)}, u32[]{:S(2)}) collective-permute-start(bf16[8,4096]{1,0:T(8,128)(2,1)S(1)} %copy-done.4), channel_id=1, source_target_pairs={{0,16},{2,18},{4,20},{6,22},{8,24},{10,26},{12,28},{14,30},{16,0},... | collective-permute-start | bytes 196616 | tf_op jit(solution)/shard_map/ppermute | solution.py:36
  12.6 4.0 %fill.4.refs_5_.refs_4_ = bf16[32,8,128,128]{3,2,1,0:T(8,128)(2,1)S(1)} custom-call(s32[1,1,192]{2,1,0:T(1,128)S(1)} %copy-done.1, s32[1,1]{1,0:T(1,128)S(6)} %copy.17.count, bf16[1,1,192,128,128]{4,3,2,1,0:T(8,128)(2,1)} %slots.4), custom_call_target="tpu_custom_call" | custom-call | bytes 6291456 | tf_op jit(solution)/shard_map/fill/pallas_call | solution.py:87
  16.7 1.6 %collective-permute-start.4 = (bf16[32,4096]{1,0:T(8,128)(2,1)S(1)}, bf16[32,4096]{1,0:T(8,128)(2,1)S(1)}, u32[]{:S(2)}, u32[]{:S(2)}) collective-permute-start(bf16[32,4096]{1,0:T(8,128)(2,1)S(1)} %pad_maximum_fusion.1.refs_0_.refs_4_), channel_id=1, source_target_pairs={{0,4},{2,6},{4,0},{6,2},{8,12},{10,14},{12,8},{14,10},{16,20},{18,... | collective-permute-start | bytes 786440 | tf_op jit(solution)/shard_map/ppermute | solution.py:36
  18.4 1.4 %collective-permute-start.3 = (bf16[16,4096]{1,0:T(8,128)(2,1)S(1)}, bf16[16,4096]{1,0:T(8,128)(2,1)S(1)}, u32[]{:S(2)}, u32[]{:S(2)}) collective-permute-start(bf16[16,4096]{1,0:T(8,128)(2,1)S(1)} %pad_maximum_fusion.2), channel_id=1, source_target_pairs={{0,8},{2,10},{4,12},{6,14},{8,0},{10,2},{12,4},{14,6},{16,24},{18,... | collective-permute-start | bytes 393224 | tf_op jit(solution)/shard_map/ppermute | solution.py:36
  19.7 4.7 %collective-permute-done.4.refs_1_.refs_5_ = bf16[32,4096]{1,0:T(8,128)(2,1)S(1)} collective-permute-done((bf16[32,4096]{1,0:T(8,128)(2,1)S(1)}, bf16[32,4096]{1,0:T(8,128)(2,1)S(1)}, u32[]{:S(2)}, u32[]{:S(2)}) %collective-permute-start.4) | collective-permute-done | bytes 262176 | tf_op jit(solution)/shard_map/ppermute | solution.py:36
  24.5 1.3 %collective-permute-start.5 = (bf16[32,4096]{1,0:T(8,128)(2,1)S(1)}, bf16[32,4096]{1,0:T(8,128)(2,1)S(1)}, u32[]{:S(2)}, u32[]{:S(2)}) collective-permute-start(bf16[32,4096]{1,0:T(8,128)(2,1)S(1)} %pad_maximum_fusion.refs_0_), channel_id=1, source_target_pairs={{0,4},{2,6},{4,0},{6,2},{8,12},{10,14},{12,8},{14,10},{16,20},{18,... | collective-permute-start | bytes 786440 | tf_op jit(solution)/shard_map/ppermute | solution.py:36
  25.8 0.2 collective-permute-done.7.refs_3_.refs_7_
  26.0 3.7 %gate_up.1 = (f32[8,128,256]{2,1,0:T(8,128)S(1)}, bf16[8,128,256]{2,1,0:T(8,128)(2,1)S(1)}) custom-call(bf16[32,4096]{1,0:T(8,128)(2,1)S(1)} %pad_maximum_fusion.1.refs_0_.refs_4_, bf16[32,4096]{1,0:T(8,128)(2,1)S(1)} %collective-permute-done.4.refs_1_.refs_5_, bf16[32,4096]{1,0:T(8,128)(2,1)S(1)} %collective-permute-done.6.refs_2_.refs_6_, ...), custom_call_target="tpu_custom_call" | custom-call | flops 2147483648 | bytes 16777216 | tf_op jit(solution)/shard_map/gate_up/pallas_call | solution.py:126
  29.6 3.6 %collective-permute-done.5.refs_1_ = bf16[32,4096]{1,0:T(8,128)(2,1)S(1)} collective-permute-done((bf16[32,4096]{1,0:T(8,128)(2,1)S(1)}, bf16[32,4096]{1,0:T(8,128)(2,1)S(1)}, u32[]{:S(2)}, u32[]{:S(2)}) %collective-permute-start.5) | collective-permute-done | bytes 262176 | tf_op jit(solution)/shard_map/ppermute | solution.py:36
  33.3 0.5 collective-permute-start.9
  33.8 1.2 %collective-permute-start.10 = (bf16[8,128,256]{2,1,0:T(8,128)(2,1)S(1)}, bf16[8,128,256]{2,1,0:T(8,128)(2,1)S(1)}, u32[]{:S(2)}, u32[]{:S(2)}) collective-permute-start(bf16[8,128,256]{2,1,0:T(8,128)(2,1)S(1)} %get-tuple-element.45), channel_id=1, source_target_pairs={{0,1},{1,0},{2,3},{3,2},{4,5},{5,4},{6,7},{7,6},{8,9},{9,8},{10,11... | collective-permute-start | bytes 1572872 | tf_op jit(solution)/shard_map/ppermute | solution.py:36
  35.6 3.5 %fill.5.refs_8_ = bf16[8,32,128,128]{3,2,1,0:T(8,128)(2,1)S(1)} custom-call(s32[1,1,192]{2,1,0:T(1,128)S(1)} %copy-done.2, s32[1,1]{1,0:T(1,128)S(6)} %copy.18.count, bf16[1,1,192,128,128]{4,3,2,1,0:T(8,128)(2,1)} %slots.5), custom_call_target="tpu_custom_call" | custom-call | bytes 6291456 | tf_op jit(solution)/shard_map/fill/pallas_call | solution.py:87
  39.2 3.6 %d_hidden.1 = (f32[8,128,128]{2,1,0:T(8,128)S(1)}, bf16[8,128,128]{2,1,0:T(8,128)(2,1)S(1)}, bf16[32,128,128]{2,1,0:T(8,128)(2,1)S(1)}) custom-call(bf16[32,4096]{1,0:T(8,128)(2,1)S(1)} %pad_maximum_fusion.refs_0_, bf16[32,4096]{1,0:T(8,128)(2,1)S(1)} %collective-permute-done.5.refs_1_, bf16[32,4096]{1,0:T(8,128)(2,1)S(1)} %collective-permute-done.8.refs_2_, ...), custom_call_target="tpu_custom_call" | custom-call | flops 1073741824 | bytes 8388608 | tf_op jit(solution)/shard_map/d_hidden/pallas_call | solution.py:169
  42.8 1.2 %collective-permute-start.11 = (bf16[8,128,128]{2,1,0:T(8,128)(2,1)S(1)}, bf16[8,128,128]{2,1,0:T(8,128)(2,1)S(1)}, u32[]{:S(2)}, u32[]{:S(2)}) collective-permute-start(bf16[8,128,128]{2,1,0:T(8,128)(2,1)S(1)} %get-tuple-element.52), channel_id=1, source_target_pairs={{0,1},{1,0},{2,3},{3,2},{4,5},{5,4},{6,7},{7,6},{8,9},{9,8},{10,11... | collective-permute-start | bytes 786440 | tf_op jit(solution)/shard_map/ppermute | solution.py:36
  44.0 4.6 %collective-permute-done.10.refs_5_ = bf16[8,128,256]{2,1,0:T(8,128)(2,1)S(1)} collective-permute-done((bf16[8,128,256]{2,1,0:T(8,128)(2,1)S(1)}, bf16[8,128,256]{2,1,0:T(8,128)(2,1)S(1)}, u32[]{:S(2)}, u32[]{:S(2)}) %collective-permute-start.10) | collective-permute-done | bytes 524320 | tf_op jit(solution)/shard_map/ppermute | solution.py:36
  48.6 7.8 %down_grads.1 = (bf16[192,128,128]{2,1,0:T(8,128)(2,1)}, f32[8,128,256]{2,1,0:T(8,128)S(1)}) custom-call(s32[1,1,192]{2,1,0:T(1,128)S(1)} %copy-done.2, s32[1,1]{1,0:T(1,128)S(6)} %copy.18.count, bf16[32,4096]{1,0:T(8,128)(2,1)S(1)} %pad_maximum_fusion.refs_0_, bf16[32,4096]{1,0:T(8,128)(2,1)S(1)} %collective-permute-done.5.refs_1_, ...), custom_call_target="tpu_custom_call" | custom-call | flops 805306368 | bytes 6291456 | tf_op jit(solution)/shard_map/down_grads/pallas_call | solution.py:316
  56.4 6.5 %d_tokens.1 = (f32[64,4096]{1,0:T(8,128)S(1)}, bf16[64,4096]{1,0:T(8,128)(2,1)S(1)}, bf16[8,128,256]{2,1,0:T(8,128)(2,1)S(1)}) custom-call(f32[8,128,256]{2,1,0:T(8,128)S(1)} %get-tuple-element.49.refs_0_, f32[8,128,128]{2,1,0:T(8,128)S(1)} %get-tuple-element.51.refs_1_, bf16[8,128,128]{2,1,0:T(8,128)(2,1)S(1)} %collective-permute-done.11.refs_2_, ...), custom_call_target="tpu_custom_call" | custom-call | flops 2147483648 | bytes 16777216 | tf_op jit(solution)/shard_map/d_tokens/pallas_call | solution.py:222
  62.9 0.1 collective-permute-start.12
  63.0 1.9 %collective-permute-done.12 = bf16[64,4096]{1,0:T(8,128)(2,1)S(1)} collective-permute-done((bf16[64,4096]{1,0:T(8,128)(2,1)S(1)}, bf16[64,4096]{1,0:T(8,128)(2,1)S(1)}, u32[]{:S(2)}, u32[]{:S(2)}) %collective-permute-start.12) | collective-permute-done | bytes 524320 | tf_op jit(solution)/shard_map/ppermute | solution.py:36
  64.9 0.1 convert_add_fusion
  65.0 1.3 %collective-permute-start.13 = (bf16[32,4096]{1,0:T(8,128)(2,1)S(1)}, bf16[32,4096]{1,0:T(8,128)(2,1)S(1)}, u32[]{:S(2)}, u32[]{:S(2)}) collective-permute-start(bf16[32,4096]{1,0:T(8,128)(2,1)S(1)} %slice.43), channel_id=1, source_target_pairs={{0,4},{2,6},{4,0},{6,2},{8,12},{10,14},{12,8},{14,10},{16,20},{18,... | collective-permute-start | bytes 786440 | tf_op jit(solution)/shard_map/ppermute | solution.py:36
  66.3 5.2 %gu_grads.2 = (bf16[192,128,128]{2,1,0:T(8,128)(2,1)}, bf16[192,128,128]{2,1,0:T(8,128)(2,1)}) custom-call(s32[1,1,192]{2,1,0:T(1,128)S(1)} %copy-done.1, s32[1,1]{1,0:T(1,128)S(6)} %copy.17.count, bf16[8,128,256]{2,1,0:T(8,128)(2,1)S(1)} %get-tuple-element.61.d_pair, bf16[32,128,128]{2,1,0:T(8,128)(2,1)S(1)} %get-tuple-element.62.turned), custom_call_target="tpu_custom_call" | custom-call | flops 805306368 | bytes 6291456 | tf_op jit(solution)/shard_map/gu_grads/pallas_call | solution.py:265
  71.5 1.9 %collective-permute-done.13 = bf16[32,4096]{1,0:T(8,128)(2,1)S(1)} collective-permute-done((bf16[32,4096]{1,0:T(8,128)(2,1)S(1)}, bf16[32,4096]{1,0:T(8,128)(2,1)S(1)}, u32[]{:S(2)}, u32[]{:S(2)}) %collective-permute-start.13) | collective-permute-done | bytes 262176 | tf_op jit(solution)/shard_map/ppermute | solution.py:36
  73.4 0.1 fusion.3
  73.5 2.7 %collective-permute-start.14 = (bf16[8,4096]{1,0:T(8,128)(2,1)S(1)}, bf16[8,4096]{1,0:T(8,128)(2,1)S(1)}, u32[]{:S(2)}, u32[]{:S(2)}) collective-permute-start(bf16[8,4096]{1,0:T(8,128)(2,1)S(1)} %get-tuple-element.58), channel_id=1, source_target_pairs={{0,16},{2,18},{4,20},{6,22},{8,24},{10,26},{12,28},{14,30},{16,0},... | collective-permute-start | bytes 196616 | tf_op jit(solution)/shard_map/ppermute | solution.py:36
  76.2 1.7 %collective-permute-start.16 = (bf16[8,4096]{1,0:T(8,128)(2,1)S(1)}, bf16[8,4096]{1,0:T(8,128)(2,1)S(1)}, u32[]{:S(2)}, u32[]{:S(2)}) collective-permute-start(bf16[8,4096]{1,0:T(8,128)(2,1)S(1)} %get-tuple-element.60), channel_id=1, source_target_pairs={{0,24},{2,26},{4,28},{6,30},{8,16},{10,18},{12,20},{14,22},{16,8},... | collective-permute-start | bytes 196616 | tf_op jit(solution)/shard_map/ppermute | solution.py:36
  78.0 5.2 %gu_grads.3 = (bf16[192,128,128]{2,1,0:T(8,128)(2,1)}, bf16[192,128,128]{2,1,0:T(8,128)(2,1)}) custom-call(s32[1,1,192]{2,1,0:T(1,128)S(1)} %copy-done.1, s32[1,1]{1,0:T(1,128)S(6)} %copy.17.count, bf16[8,128,256]{2,1,0:T(8,128)(2,1)S(1)} %get-tuple-element.61.d_pair, ...), custom_call_target="tpu_custom_call", output_to_operand_aliasing={{0}: (4, {}), {1}: (5, {})} | custom-call | flops 805306368 | bytes 6291456 | tf_op jit(solution)/shard_map/gu_grads/pallas_call | solution.py:265
  83.2 0.7 fusion.2
  (30 shorter events, 0.2 us)
Async XLA Ops:
  0.6 9.5 %collective-permute-start = (bf16[8,4096]{1,0:T(8,128)(2,1)}, bf16[8,4096]{1,0:T(8,128)(2,1)S(1)}, u32[]{:S(2)}, u32[]{:S(2)}) collective-permute-start(bf16[8,4096]{1,0:T(8,128)(2,1)} %param.9), channel_id=1, source_target_pairs={{0,16},{2,18},{4,20},{6,22},{8,24},{10,26},{12,28},{14,30},{16,0},... | collective-permute-start | bytes 196616 | tf_op jit(solution)/shard_map/ppermute | solution.py:36
  5.4 0.7 copy-start
  6.1 4.1 %copy-start.3 = (bf16[8,4096]{1,0:T(8,128)(2,1)S(1)}, bf16[8,4096]{1,0:T(8,128)(2,1)}, u32[]{:S(2)}) copy-start(bf16[8,4096]{1,0:T(8,128)(2,1)} %param.9) | copy-start | bytes 196612
  6.1 5.6 %copy-start.4 = (bf16[8,4096]{1,0:T(8,128)(2,1)S(1)}, bf16[8,4096]{1,0:T(8,128)(2,1)}, u32[]{:S(2)}) copy-start(bf16[8,4096]{1,0:T(8,128)(2,1)} %param.10) | copy-start | bytes 196612
  6.1 6.6 %copy-start.1 = (s32[1,1,192]{2,1,0:T(1,128)S(1)}, s32[1,1,192]{2,1,0:T(1,128)}, u32[]{:S(2)}) copy-start(s32[1,1,192]{2,1,0:T(1,128)} %index.9) | copy-start | bytes 2308
  10.2 6.5 %collective-permute-start.2 = (bf16[16,4096]{1,0:T(8,128)(2,1)S(1)}, bf16[16,4096]{1,0:T(8,128)(2,1)S(1)}, u32[]{:S(2)}, u32[]{:S(2)}) collective-permute-start(bf16[16,4096]{1,0:T(8,128)(2,1)S(1)} %pad_maximum_fusion.3), channel_id=1, source_target_pairs={{0,8},{2,10},{4,12},{6,14},{8,0},{10,2},{12,4},{14,6},{16,24},{18,... | collective-permute-start | bytes 393224 | tf_op jit(solution)/shard_map/ppermute | solution.py:36
  11.6 6.7 %collective-permute-start.1 = (bf16[8,4096]{1,0:T(8,128)(2,1)S(1)}, bf16[8,4096]{1,0:T(8,128)(2,1)S(1)}, u32[]{:S(2)}, u32[]{:S(2)}) collective-permute-start(bf16[8,4096]{1,0:T(8,128)(2,1)S(1)} %copy-done.4), channel_id=1, source_target_pairs={{0,16},{2,18},{4,20},{6,22},{8,24},{10,26},{12,28},{14,30},{16,0},... | collective-permute-start | bytes 196616 | tf_op jit(solution)/shard_map/ppermute | solution.py:36
  16.7 7.7 %collective-permute-start.4 = (bf16[32,4096]{1,0:T(8,128)(2,1)S(1)}, bf16[32,4096]{1,0:T(8,128)(2,1)S(1)}, u32[]{:S(2)}, u32[]{:S(2)}) collective-permute-start(bf16[32,4096]{1,0:T(8,128)(2,1)S(1)} %pad_maximum_fusion.1.refs_0_.refs_4_), channel_id=1, source_target_pairs={{0,4},{2,6},{4,0},{6,2},{8,12},{10,14},{12,8},{14,10},{16,20},{18,... | collective-permute-start | bytes 786440 | tf_op jit(solution)/shard_map/ppermute | solution.py:36
  18.4 6.1 %collective-permute-start.3 = (bf16[16,4096]{1,0:T(8,128)(2,1)S(1)}, bf16[16,4096]{1,0:T(8,128)(2,1)S(1)}, u32[]{:S(2)}, u32[]{:S(2)}) collective-permute-start(bf16[16,4096]{1,0:T(8,128)(2,1)S(1)} %pad_maximum_fusion.2), channel_id=1, source_target_pairs={{0,8},{2,10},{4,12},{6,14},{8,0},{10,2},{12,4},{14,6},{16,24},{18,... | collective-permute-start | bytes 393224 | tf_op jit(solution)/shard_map/ppermute | solution.py:36
  19.7 6.1 %collective-permute-start.6 = (bf16[32,4096]{1,0:T(8,128)(2,1)S(1)}, bf16[32,4096]{1,0:T(8,128)(2,1)S(1)}, u32[]{:S(2)}, u32[]{:S(2)}) collective-permute-start(bf16[32,4096]{1,0:T(8,128)(2,1)S(1)} %pad_maximum_fusion.1.refs_0_.refs_4_), channel_id=1, source_target_pairs={{0,2},{2,0},{4,6},{6,4},{8,10},{10,8},{12,14},{14,12},{16,18},{18,... | collective-permute-start | bytes 786440 | tf_op jit(solution)/shard_map/ppermute | solution.py:36
  24.4 1.5 %collective-permute-start.7 = (bf16[32,4096]{1,0:T(8,128)(2,1)S(1)}, bf16[32,4096]{1,0:T(8,128)(2,1)S(1)}, u32[]{:S(2)}, u32[]{:S(2)}) collective-permute-start(bf16[32,4096]{1,0:T(8,128)(2,1)S(1)} %collective-permute-done.4.refs_1_.refs_5_), channel_id=1, source_target_pairs={{0,2},{2,0},{4,6},{6,4},{8,10},{10,8},{12,14},{14,12},{16,18},{18,... | collective-permute-start | bytes 786440 | tf_op jit(solution)/shard_map/ppermute | solution.py:36
  24.5 11.2 %copy-start.2 = (s32[1,1,192]{2,1,0:T(1,128)S(1)}, s32[1,1,192]{2,1,0:T(1,128)}, u32[]{:S(2)}) copy-start(s32[1,1,192]{2,1,0:T(1,128)} %index.7) | copy-start | bytes 2308
  24.5 8.8 %collective-permute-start.5 = (bf16[32,4096]{1,0:T(8,128)(2,1)S(1)}, bf16[32,4096]{1,0:T(8,128)(2,1)S(1)}, u32[]{:S(2)}, u32[]{:S(2)}) collective-permute-start(bf16[32,4096]{1,0:T(8,128)(2,1)S(1)} %pad_maximum_fusion.refs_0_), channel_id=1, source_target_pairs={{0,4},{2,6},{4,0},{6,2},{8,12},{10,14},{12,8},{14,10},{16,20},{18,... | collective-permute-start | bytes 786440 | tf_op jit(solution)/shard_map/ppermute | solution.py:36
  33.3 5.9 %collective-permute-start.8 = (bf16[32,4096]{1,0:T(8,128)(2,1)S(1)}, bf16[32,4096]{1,0:T(8,128)(2,1)S(1)}, u32[]{:S(2)}, u32[]{:S(2)}) collective-permute-start(bf16[32,4096]{1,0:T(8,128)(2,1)S(1)} %pad_maximum_fusion.refs_0_), channel_id=1, source_target_pairs={{0,2},{2,0},{4,6},{6,4},{8,10},{10,8},{12,14},{14,12},{16,18},{18,... | collective-permute-start | bytes 786440 | tf_op jit(solution)/shard_map/ppermute | solution.py:36
  33.3 5.9 %collective-permute-start.9 = (bf16[32,4096]{1,0:T(8,128)(2,1)S(1)}, bf16[32,4096]{1,0:T(8,128)(2,1)S(1)}, u32[]{:S(2)}, u32[]{:S(2)}) collective-permute-start(bf16[32,4096]{1,0:T(8,128)(2,1)S(1)} %collective-permute-done.5.refs_1_), channel_id=1, source_target_pairs={{0,2},{2,0},{4,6},{6,4},{8,10},{10,8},{12,14},{14,12},{16,18},{18,... | collective-permute-start | bytes 786440 | tf_op jit(solution)/shard_map/ppermute | solution.py:36
  33.8 14.8 %collective-permute-start.10 = (bf16[8,128,256]{2,1,0:T(8,128)(2,1)S(1)}, bf16[8,128,256]{2,1,0:T(8,128)(2,1)S(1)}, u32[]{:S(2)}, u32[]{:S(2)}) collective-permute-start(bf16[8,128,256]{2,1,0:T(8,128)(2,1)S(1)} %get-tuple-element.45), channel_id=1, source_target_pairs={{0,1},{1,0},{2,3},{3,2},{4,5},{5,4},{6,7},{7,6},{8,9},{9,8},{10,11... | collective-permute-start | bytes 1572872 | tf_op jit(solution)/shard_map/ppermute | solution.py:36
  42.8 13.6 %collective-permute-start.11 = (bf16[8,128,128]{2,1,0:T(8,128)(2,1)S(1)}, bf16[8,128,128]{2,1,0:T(8,128)(2,1)S(1)}, u32[]{:S(2)}, u32[]{:S(2)}) collective-permute-start(bf16[8,128,128]{2,1,0:T(8,128)(2,1)S(1)} %get-tuple-element.52), channel_id=1, source_target_pairs={{0,1},{1,0},{2,3},{3,2},{4,5},{5,4},{6,7},{7,6},{8,9},{9,8},{10,11... | collective-permute-start | bytes 786440 | tf_op jit(solution)/shard_map/ppermute | solution.py:36
  62.9 2.0 %collective-permute-start.12 = (bf16[64,4096]{1,0:T(8,128)(2,1)S(1)}, bf16[64,4096]{1,0:T(8,128)(2,1)S(1)}, u32[]{:S(2)}, u32[]{:S(2)}) collective-permute-start(bf16[64,4096]{1,0:T(8,128)(2,1)S(1)} %get-tuple-element.54), channel_id=1, source_target_pairs={{0,2},{2,0},{4,6},{6,4},{8,10},{10,8},{12,14},{14,12},{16,18},{18,... | collective-permute-start | bytes 1572872 | tf_op jit(solution)/shard_map/ppermute | solution.py:36
  65.0 8.4 %collective-permute-start.13 = (bf16[32,4096]{1,0:T(8,128)(2,1)S(1)}, bf16[32,4096]{1,0:T(8,128)(2,1)S(1)}, u32[]{:S(2)}, u32[]{:S(2)}) collective-permute-start(bf16[32,4096]{1,0:T(8,128)(2,1)S(1)} %slice.43), channel_id=1, source_target_pairs={{0,4},{2,6},{4,0},{6,2},{8,12},{10,14},{12,8},{14,10},{16,20},{18,... | collective-permute-start | bytes 786440 | tf_op jit(solution)/shard_map/ppermute | solution.py:36
  73.5 9.6 %collective-permute-start.14 = (bf16[8,4096]{1,0:T(8,128)(2,1)S(1)}, bf16[8,4096]{1,0:T(8,128)(2,1)S(1)}, u32[]{:S(2)}, u32[]{:S(2)}) collective-permute-start(bf16[8,4096]{1,0:T(8,128)(2,1)S(1)} %get-tuple-element.58), channel_id=1, source_target_pairs={{0,16},{2,18},{4,20},{6,22},{8,24},{10,26},{12,28},{14,30},{16,0},... | collective-permute-start | bytes 196616 | tf_op jit(solution)/shard_map/ppermute | solution.py:36
  76.2 6.9 %collective-permute-start.15 = (bf16[8,4096]{1,0:T(8,128)(2,1)S(1)}, bf16[8,4096]{1,0:T(8,128)(2,1)S(1)}, u32[]{:S(2)}, u32[]{:S(2)}) collective-permute-start(bf16[8,4096]{1,0:T(8,128)(2,1)S(1)} %get-tuple-element.59), channel_id=1, source_target_pairs={{0,8},{2,10},{4,12},{6,14},{8,0},{10,2},{12,4},{14,6},{16,24},{18,... | collective-permute-start | bytes 196616 | tf_op jit(solution)/shard_map/ppermute | solution.py:36
  76.2 6.9 %collective-permute-start.16 = (bf16[8,4096]{1,0:T(8,128)(2,1)S(1)}, bf16[8,4096]{1,0:T(8,128)(2,1)S(1)}, u32[]{:S(2)}, u32[]{:S(2)}) collective-permute-start(bf16[8,4096]{1,0:T(8,128)(2,1)S(1)} %get-tuple-element.60), channel_id=1, source_target_pairs={{0,24},{2,26},{4,28},{6,30},{8,16},{10,18},{12,20},{14,22},{16,8},... | collective-permute-start | bytes 196616 | tf_op jit(solution)/shard_map/ppermute | solution.py:36

commit v4 on v3

--- a/solution.py
+++ b/solution.py
@@ -46,54 +46,49 @@
     return sum(size >> (bit + 1) for bit in range(size.bit_length() - 1) if number >> bit & 1)
 
 
-def fill_body(index, count, slots, dense, seen, sem):
-    outer, inner = dense.shape[:2]
+def fill_body(arrays, index, count, *refs):
+    slots, dense, sem = refs[:arrays], refs[arrays : 2 * arrays], refs[2 * arrays]
+    outer, inner = dense[0].shape[:2]
     live = count[0, 0]
     chunk = min(inner, 8)
 
-    @pl.loop(0, outer * inner, unroll=8)
-    def _(place):
-        seen[place] = 0
-
-    @pl.loop(0, live)
-    def _(s):
-        place = index[0, 0, s]
-        seen[place] = 1
-        high, low = split_index(place, inner)
-        pltpu.make_async_copy(slots.at[0, 0, s], dense.at[high, low], sem).start()
-
-    @pl.loop(0, outer)
-    def _(high):
-        for low in range(inner):
-
-            @pl.when(seen[high * inner + low] == 0)
-            def _():
-                dense[high, low] = jnp.zeros(dense.shape[2:], dense.dtype)
+    for source, target in zip(slots, dense):
+
+        @pl.loop(0, outer)
+        def _(high):
+            target[high] = jnp.zeros(target.shape[1:], target.dtype)
+
+        @pl.loop(0, live)
+        def _(s):
+            high, low = split_index(index[0, 0, s], inner)
+            pltpu.make_async_copy(source.at[0, 0, s], target.at[high, low], sem).start()
 
     many, few = split_index(live, chunk)
-
-    @pl.loop(0, many)
-    def _(_):
-        blocks = pl.ds(0, chunk)
-        pltpu.make_async_copy(slots.at[0, 0, blocks], dense.at[0, blocks], sem).wait()
-
-    @pl.loop(0, few)
-    def _(_):
-        pltpu.make_async_copy(slots.at[0, 0, 0], dense.at[0, 0], sem).wait()
+    for source, target in zip(slots, dense):
+
+        @pl.loop(0, many)
+        def _(_):
+            blocks = pl.ds(0, chunk)
+            pltpu.make_async_copy(source.at[0, 0, blocks], target.at[0, blocks], sem).wait()
+
+        @pl.loop(0, few)
+        def _(_):
+            pltpu.make_async_copy(source.at[0, 0, 0], target.at[0, 0], sem).wait()
 
 
 def fill(index, count, slots, outer, inner):
-    block = slots.shape[-1]
-    return pl.pallas_call(
-        fill_body,
-        out_shape=pltpu.VMEM((outer, inner, block, block), BF16),
-        in_specs=[SCALARS] * 2 + [pl.BlockSpec(memory_space=pltpu.HBM)],
-        out_specs=WHOLE,
-        scratch_shapes=[pltpu.SMEM((outer * inner,), jnp.int32), pltpu.SemaphoreType.DMA],
-        compiler_params=params(),
-        cost_estimate=cost(0, slots.size * 2),
+    arrays = len(slots)
+    block = slots[0].shape[-1]
+    return pl.pallas_call(
+        functools.partial(fill_body, arrays),
+        out_shape=(pltpu.VMEM((outer, inner, block, block), BF16),) * arrays,
+        in_specs=[SCALARS] * 2 + [pl.BlockSpec(memory_space=pltpu.HBM)] * arrays,
+        out_specs=(WHOLE,) * arrays,
+        scratch_shapes=[pltpu.SemaphoreType.DMA],
+        compiler_params=params(),
+        cost_estimate=cost(0, arrays * slots[0].size * 2),
         name="fill",
-    )(index, count, in_hbm(slots))
+    )(index, count, *(in_hbm(array) for array in slots))
 
 
 def stack(pieces):
@@ -184,7 +179,7 @@
 def d_tokens_body(group, *refs):
     coef, dh_own, *dh_recv, gate_w, up_w, own, send, d_pair, turned = refs
     d_blocks, f_blocks, block, _ = gate_w.shape
-    half = own.shape[0]
+    piece = own.shape[0] // 2
     for c in range(f_blocks):
         dh = dh_own[c]
         for part in dh_recv:
@@ -210,8 +205,11 @@
         )
         result = jnp.dot(weights, grads, preferred_element_type=F32).T
         columns = pl.ds(pl.multiple_of(at * group * block, group * block), group * block)
-        own[:, columns] = result[:half]
-        send[:, columns] = result[half:].astype(BF16)
+        for at_piece in range(2):
+            rows = slice(at_piece * piece, (at_piece + 1) * piece)
+            start = 2 * at_piece * piece
+            own[rows, columns] = result[start : start + piece]
+            send[rows, columns] = result[start + piece : start + 2 * piece].astype(BF16)
 
 
 def d_tokens_part(coef, dh_own, dh_recv, gate_w, up_w):
@@ -280,6 +278,7 @@
 
 def down_grad_body(pieces_count, index, count, *refs):
     pieces, gu = refs[:pieces_count], refs[pieces_count:-4]
+    halves = gu[: len(gu) // 2], gu[len(gu) // 2 :]
     out, coef, turned, columns = refs[-4:]
     f_blocks = turned.shape[0]
     d_blocks, _, block = columns.shape
@@ -288,9 +287,13 @@
     @pl.when(step == 0)
     def _():
         for f in range(f_blocks):
-            both = gu[0][f]
-            for part in gu[1:]:
-                both = both + part[f].astype(F32)
+            both = jnp.concatenate(
+                [
+                    sum((part[f].astype(F32) for part in half[1:]), half[0][f])
+                    for half in halves
+                ],
+                axis=0,
+            )
             gate, up = both[:, :block], both[:, block:]
             sig = jax.nn.sigmoid(gate)
             silu = gate * sig
@@ -308,8 +311,9 @@
         out[j] = jnp.where(slot < count[0, 0], result, 0.0).astype(BF16)
 
 
-def down_grads(index, count, pieces, gu_own, gu_recv, slots):
-    f_blocks, tokens, pair = gu_own.shape
+def down_grads(index, count, pieces, halves, slots):
+    f_blocks, half_tokens, pair = halves[0][0].shape
+    tokens = 2 * half_tokens
     block = pair // 2
     d_blocks = pieces[0].shape[1] // block
     chunk = step_slots(slots)
@@ -317,12 +321,12 @@
         functools.partial(down_grad_body, len(pieces)),
         out_shape=(
             jax.ShapeDtypeStruct((slots, block, block), BF16),
-            jax.ShapeDtypeStruct(gu_own.shape, F32),
+            jax.ShapeDtypeStruct((f_blocks, tokens, pair), F32),
         ),
         grid_spec=pltpu.PrefetchScalarGridSpec(
             num_scalar_prefetch=2,
             grid=(slots // chunk,),
-            in_specs=[WHOLE] * (len(pieces) + 1 + len(gu_recv)),
+            in_specs=[WHOLE] * (len(pieces) + 2 * len(halves[0])),
             out_specs=(pl.BlockSpec((chunk, block, block), lambda i, *_: (i, 0, 0)), WHOLE),
             scratch_shapes=[
                 pltpu.VMEM((f_blocks, block, tokens), BF16),
@@ -332,7 +336,7 @@
         compiler_params=params(),
         cost_estimate=cost(2 * slots * block * block * tokens, 2 * slots * block * block),
         name="down_grads",
-    )(index, count, *pieces, gu_own, *gu_recv)
+    )(index, count, *pieces, *halves[0], *halves[1])
 
 
 def on_device(
@@ -350,35 +354,43 @@
     def exchange(array):
         return [swap(array, "narrow", narrow, k) for k in range(1, narrow)]
 
+    flips = [chips >> hop for hop in range(1, chips.bit_length())]
     x, y = tokens, cotangent
-    weights = []
-    index = gu_index
-    flips = [chips >> hop for hop in range(1, chips.bit_length())]
-    for hop, flip in enumerate(flips):
-        if hop > 0:
-            x = jnp.concatenate([x, x_recv], axis=0)
-            y = jnp.concatenate([y, y_recv], axis=0)
-            x, weights, index = lax.optimization_barrier((x, weights, index))
+    x_recv = swap(x, "wide", wide, 2 * flips[0])
+    gate_w, up_w = fill(gu_index, gu_count, (gate_vals, up_vals), d_blocks, f_blocks)
+    y, _ = lax.optimization_barrier((y, x_recv))
+    y_recv = swap(y, "wide", wide, 2 * flips[0])
+    for hop, flip in enumerate(flips[1:-1]):
+        x = jnp.concatenate([x, x_recv], axis=0)
+        if hop == 0:
+            x, gate_w, up_w, index = lax.optimization_barrier((x, gate_w, up_w, down_index))
+            (down_w,) = fill(index, down_count, (down_vals,), f_blocks, d_blocks)
         x_recv = swap(x, "wide", wide, 2 * flip)
-        if hop == len(flips) - 1:
-            x_across = swap(x, "wide", wide, 1)
-        if len(weights) < 2:
-            slots_of = (gate_vals, up_vals)[hop]
-            weights.append(fill(index, gu_count, slots_of, d_blocks, f_blocks))
+        y = jnp.concatenate([y, y_recv], axis=0)
         y, _ = lax.optimization_barrier((y, x_recv))
         y_recv = swap(y, "wide", wide, 2 * flip)
-    x_pieces = [x, x_recv, x_across, swap(x_recv, "wide", wide, 1)]
-    gate_w, up_w = weights
-
-    gu_own, gu_send = gate_up(x_pieces, gate_w, up_w)
-    gu_recv = exchange(gu_send)
-    late_index, y, y_recv, _ = lax.optimization_barrier((down_index, y, y_recv, gu_send))
-    y_across = swap(y, "wide", wide, 1)
-    down_w = fill(late_index, down_count, down_vals, f_blocks, d_blocks)
-    y_pieces = [y, y_recv, y_across, swap(y_recv, "wide", wide, 1)]
+    x = jnp.concatenate([x, x_recv], axis=0)
+    x, down_w = lax.optimization_barrier((x, down_w))
+
+    x_near = [x, swap(x, "wide", wide, 1)]
+    x_far = swap(x, "wide", wide, 2 * flips[-1])
+    near_own, near_send = gate_up(x_near, gate_w, up_w)
+    near_recv = exchange(near_send)
+    y = jnp.concatenate([y, y_recv], axis=0)
+    x_far, y, _ = lax.optimization_barrier((x_far, y, near_send))
+    y_far = swap(y, "wide", wide, 2 * flips[-1])
+    y_near = [y, swap(y, "wide", wide, 1)]
+    x_far = [x_far, swap(x_far, "wide", wide, 1)]
+    far_own, far_send = gate_up(x_far, gate_w, up_w)
+    far_recv = exchange(far_send)
+    y_far, _ = lax.optimization_barrier((y_far, far_send))
+    y_far = [y_far, swap(y_far, "wide", wide, 1)]
+    x_pieces = x_near + x_far
+    y_pieces = y_near + y_far
     dh_own, dh_send, turned = d_hidden(y_pieces, x_pieces, down_w)
     dh_recv = exchange(dh_send)
-    down_grad, coef = down_grads(down_index, down_count, y_pieces, gu_own, gu_recv, slots)
+    halves = (near_own, *near_recv), (far_own, *far_recv)
+    down_grad, coef = down_grads(down_index, down_count, y_pieces, halves, slots)
     own, send, d_pair = d_tokens_part(coef, dh_own, dh_recv, gate_w, up_w)
 
     own = own + swap(send, "wide", wide, 1).astype(F32)

time: 84 us -> 87.6 us (1.043)
  starting transfers between devices: 19.6 us -> 21.3 us
  waiting for transfers between devices: 16.9 us -> 18.1 us
    pallas_call x1 -> x2, Pallas kernels: 3.66 us -> 7.79 us  [gate_up(): pl.pallas_call(gate_up_body, out_shape=(jax.ShapeDtypeStruct(shape, F32),...]
    pallas_call x3 -> x2, Pallas kernels: 11.6 us -> 7.99 us  [fill(): pl.pallas_call(functools.partial(fill_body, arrays), out_shape=(pltpu.VME...]
    ppermute x17 -> x18, starting transfers between devices: 19.6 us -> 21.3 us  [swap(): return lax.ppermute(array, axis, [(i, i ^ flip) for i in range(size)])]
    ppermute x17 -> x18, waiting for transfers between devices: 16.9 us -> 18.1 us  [swap(): return lax.ppermute(array, axis, [(i, i ^ flip) for i in range(size)])]
  transfers between devices with their start and end apart: 17 -> 18, of which waited for: 6 -> 8; matrix products, arithmetic and copies ran while one was open for 0% -> 0% of each run, Pallas kernels for 44% -> 43%
where the time goes in v4:
time: 87.6 us; the launch traced here: 87.2 us
  Pallas kernels  44.1 us (50%)
  starting transfers between devices  21.3 us (24%)
  waiting for transfers between devices  18.1 us (21%)
  between operations  2.1 us (2%)
    ppermute x18, starting transfers between devices, swap(): return lax.ppermute(array, axis, [(i, i ^ flip) for i in range(size)])  21.3 us
    ppermute x18, waiting for transfers between devices, swap(): return lax.ppermute(array, axis, [(i, i ^ flip) for i in range(size)])  18.1 us
    pallas_call x2, Pallas kernels, gu_grads(): pl.pallas_call(functools.partial(gu_grad_body, first), out_shape=(shape,)...  10.4 us
    pallas_call x2, Pallas kernels, fill(): pl.pallas_call(functools.partial(fill_body, arrays), out_shape=(pltpu.VME...  7.99 us
    pallas_call x1, Pallas kernels, down_grads(): pl.pallas_call(functools.partial(down_grad_body, len(pieces)), out_shape=...  7.84 us
    pallas_call x2, Pallas kernels, gate_up(): pl.pallas_call(gate_up_body, out_shape=(jax.ShapeDtypeStruct(shape, F32),...  7.79 us
    pallas_call x1, Pallas kernels, d_tokens_part(): pl.pallas_call(functools.partial(d_tokens_body, group), out_shape=(jax.Sh...  6.49 us
    pallas_call x1, Pallas kernels, d_hidden(): pl.pallas_call(functools.partial(d_hidden_body, len(y_pieces)), out_shape...  3.59 us
  transfers between devices with their start and end apart: 18, of which 8 were waited for; matrix products, arithmetic and copies ran while one was open for 0% of the time, Pallas kernels for 43%

profile of v4, /device:TPU:0, one launch (start us, length us, event | category | flops | bytes accessed | tf_op | source)
XLA Modules:
  0.0 87.2 jit_solution(2184805074089851332)
XLA Ops:
  0.6 4.1 %collective-permute-start = (bf16[8,4096]{1,0:T(8,128)(2,1)}, bf16[8,4096]{1,0:T(8,128)(2,1)S(1)}, u32[]{:S(2)}, u32[]{:S(2)}) collective-permute-start(bf16[8,4096]{1,0:T(8,128)(2,1)} %param.9), channel_id=1, source_target_pairs={{0,16},{2,18},{4,20},{6,22},{8,24},{10,26},{12,28},{14,30},{16,0},... | collective-permute-start | bytes 196616 | tf_op jit(solution)/shard_map/ppermute | solution.py:36
  6.0 0.7 copy-done
  6.7 4.5 %fill.2 = (bf16[32,8,128,128]{3,2,1,0:T(8,128)(2,1)S(1)}, bf16[32,8,128,128]{3,2,1,0:T(8,128)(2,1)S(1)}) custom-call(s32[1,1,192]{2,1,0:T(1,128)S(1)} %copy-done, s32[1,1]{1,0:T(1,128)S(6)} %copy.17.count, bf16[1,1,192,128,128]{4,3,2,1,0:T(8,128)(2,1)} %refs_0_.2, bf16[1,1,192,128,128]{4,3,2,1,0:T(8,128)(2,1)} %refs_1_.1), custom_call_target="tpu_custom_call" | custom-call | bytes 12582912 | tf_op jit(solution)/shard_map/fill/pallas_call | solution.py:82
  11.3 1.5 %collective-permute-start.3 = (bf16[8,4096]{1,0:T(8,128)(2,1)S(1)}, bf16[8,4096]{1,0:T(8,128)(2,1)S(1)}, u32[]{:S(2)}, u32[]{:S(2)}) collective-permute-start(bf16[8,4096]{1,0:T(8,128)(2,1)S(1)} %copy-done.4), channel_id=1, source_target_pairs={{0,16},{2,18},{4,20},{6,22},{8,24},{10,26},{12,28},{14,30},{16,0},... | collective-permute-start | bytes 196616 | tf_op jit(solution)/shard_map/ppermute | solution.py:36
  12.9 3.4 %fill.3.refs_8_ = bf16[8,32,128,128]{3,2,1,0:T(8,128)(2,1)S(1)} custom-call(s32[1,1,192]{2,1,0:T(1,128)S(1)} %copy-done.2, s32[1,1]{1,0:T(1,128)S(6)} %copy.18.count, bf16[1,1,192,128,128]{4,3,2,1,0:T(8,128)(2,1)} %refs_0_.3), custom_call_target="tpu_custom_call" | custom-call | bytes 6291456 | tf_op jit(solution)/shard_map/fill/pallas_call | solution.py:82
  16.3 1.6 %collective-permute-done.3 = bf16[8,4096]{1,0:T(8,128)(2,1)S(1)} collective-permute-done((bf16[8,4096]{1,0:T(8,128)(2,1)S(1)}, bf16[8,4096]{1,0:T(8,128)(2,1)S(1)}, u32[]{:S(2)}, u32[]{:S(2)}) %collective-permute-start.3) | collective-permute-done | bytes 65568 | tf_op jit(solution)/shard_map/ppermute | solution.py:36
  18.0 1.6 %collective-permute-start.4 = (bf16[16,4096]{1,0:T(8,128)(2,1)S(1)}, bf16[16,4096]{1,0:T(8,128)(2,1)S(1)}, u32[]{:S(2)}, u32[]{:S(2)}) collective-permute-start(bf16[16,4096]{1,0:T(8,128)(2,1)S(1)} %pad_maximum_fusion.3), channel_id=1, source_target_pairs={{0,8},{2,10},{4,12},{6,14},{8,0},{10,2},{12,4},{14,6},{16,24},{18,... | collective-permute-start | bytes 393224 | tf_op jit(solution)/shard_map/ppermute | solution.py:36
  19.7 1.7 %collective-permute-start.2 = (bf16[32,4096]{1,0:T(8,128)(2,1)S(1)}, bf16[32,4096]{1,0:T(8,128)(2,1)S(1)}, u32[]{:S(2)}, u32[]{:S(2)}) collective-permute-start(bf16[32,4096]{1,0:T(8,128)(2,1)S(1)} %pad_maximum_fusion.refs_0_.refs_4_), channel_id=1, source_target_pairs={{0,4},{2,6},{4,0},{6,2},{8,12},{10,14},{12,8},{14,10},{16,20},{18,... | collective-permute-start | bytes 786440 | tf_op jit(solution)/shard_map/ppermute | solution.py:36
  21.4 1.6 %collective-permute-done.4 = bf16[16,4096]{1,0:T(8,128)(2,1)S(1)} collective-permute-done((bf16[16,4096]{1,0:T(8,128)(2,1)S(1)}, bf16[16,4096]{1,0:T(8,128)(2,1)S(1)}, u32[]{:S(2)}, u32[]{:S(2)}) %collective-permute-start.4) | collective-permute-done | bytes 131104 | tf_op jit(solution)/shard_map/ppermute | solution.py:36
  23.1 3.9 %gate_up.2 = (f32[8,64,256]{2,1,0:T(8,128)S(1)}, bf16[8,64,256]{2,1,0:T(8,128)(2,1)S(1)}) custom-call(bf16[32,4096]{1,0:T(8,128)(2,1)S(1)} %pad_maximum_fusion.refs_0_.refs_4_, bf16[32,4096]{1,0:T(8,128)(2,1)S(1)} %collective-permute-done.5.refs_1_.refs_5_, bf16[32,8,128,128]{3,2,1,0:T(8,128)(2,1)S(1)} %get-tuple-element.46.refs_2_.refs_3_, ...), custom_call_target="tpu_custom_call" | custom-call | flops 1073741824 | bytes 16777216 | tf_op jit(solution)/shard_map/gate_up/pallas_call | solution.py:121
  27.0 1.4 %collective-permute-done.2.refs_0_.refs_6_ = bf16[32,4096]{1,0:T(8,128)(2,1)S(1)} collective-permute-done((bf16[32,4096]{1,0:T(8,128)(2,1)S(1)}, bf16[32,4096]{1,0:T(8,128)(2,1)S(1)}, u32[]{:S(2)}, u32[]{:S(2)}) %collective-permute-start.2) | collective-permute-done | bytes 262176 | tf_op jit(solution)/shard_map/ppermute | solution.py:36
  28.4 1.7 %collective-permute-start.7 = (bf16[32,4096]{1,0:T(8,128)(2,1)S(1)}, bf16[32,4096]{1,0:T(8,128)(2,1)S(1)}, u32[]{:S(2)}, u32[]{:S(2)}) collective-permute-start(bf16[32,4096]{1,0:T(8,128)(2,1)S(1)} %pad_maximum_fusion.1.refs_0_), channel_id=1, source_target_pairs={{0,4},{2,6},{4,0},{6,2},{8,12},{10,14},{12,8},{14,10},{16,20},{18,... | collective-permute-start | bytes 786440 | tf_op jit(solution)/shard_map/ppermute | solution.py:36
  30.1 0.2 collective-permute-start.6
  30.3 3.9 %gate_up.3 = (f32[8,64,256]{2,1,0:T(8,128)S(1)}, bf16[8,64,256]{2,1,0:T(8,128)(2,1)S(1)}) custom-call(bf16[32,4096]{1,0:T(8,128)(2,1)S(1)} %collective-permute-done.2.refs_0_.refs_6_, bf16[32,4096]{1,0:T(8,128)(2,1)S(1)} %collective-permute-done.8.refs_1_.refs_7_, bf16[32,8,128,128]{3,2,1,0:T(8,128)(2,1)S(1)} %get-tuple-element.46.refs_2_.refs_3_, ...), custom_call_target="tpu_custom_call" | custom-call | flops 1073741824 | bytes 16777216 | tf_op jit(solution)/shard_map/gate_up/pallas_call | solution.py:121
  34.2 2.9 %collective-permute-done.7.refs_2_ = bf16[32,4096]{1,0:T(8,128)(2,1)S(1)} collective-permute-done((bf16[32,4096]{1,0:T(8,128)(2,1)S(1)}, bf16[32,4096]{1,0:T(8,128)(2,1)S(1)}, u32[]{:S(2)}, u32[]{:S(2)}) %collective-permute-start.7) | collective-permute-done | bytes 262176 | tf_op jit(solution)/shard_map/ppermute | solution.py:36
  37.1 2.0 %collective-permute-start.10 = (bf16[8,64,256]{2,1,0:T(8,128)(2,1)S(1)}, bf16[8,64,256]{2,1,0:T(8,128)(2,1)S(1)}, u32[]{:S(2)}, u32[]{:S(2)}) collective-permute-start(bf16[8,64,256]{2,1,0:T(8,128)(2,1)S(1)} %get-tuple-element.48), channel_id=1, source_target_pairs={{0,1},{1,0},{2,3},{3,2},{4,5},{5,4},{6,7},{7,6},{8,9},{9,8},{10,11... | collective-permute-start | bytes 786440 | tf_op jit(solution)/shard_map/ppermute | solution.py:36
  39.2 3.6 %d_hidden.1 = (f32[8,128,128]{2,1,0:T(8,128)S(1)}, bf16[8,128,128]{2,1,0:T(8,128)(2,1)S(1)}, bf16[32,128,128]{2,1,0:T(8,128)(2,1)S(1)}) custom-call(bf16[32,4096]{1,0:T(8,128)(2,1)S(1)} %pad_maximum_fusion.1.refs_0_, bf16[32,4096]{1,0:T(8,128)(2,1)S(1)} %collective-permute-done.6.refs_1_, bf16[32,4096]{1,0:T(8,128)(2,1)S(1)} %collective-permute-done.7.refs_2_, ...), custom_call_target="tpu_custom_call" | custom-call | flops 1073741824 | bytes 8388608 | tf_op jit(solution)/shard_map/d_hidden/pallas_call | solution.py:164
  42.8 2.1 %collective-permute-start.12 = (bf16[8,128,128]{2,1,0:T(8,128)(2,1)S(1)}, bf16[8,128,128]{2,1,0:T(8,128)(2,1)S(1)}, u32[]{:S(2)}, u32[]{:S(2)}) collective-permute-start(bf16[8,128,128]{2,1,0:T(8,128)(2,1)S(1)} %get-tuple-element.58), channel_id=1, source_target_pairs={{0,1},{1,0},{2,3},{3,2},{4,5},{5,4},{6,7},{7,6},{8,9},{9,8},{10,11... | collective-permute-start | bytes 786440 | tf_op jit(solution)/shard_map/ppermute | solution.py:36
  44.8 1.5 %collective-permute-done.10.refs_5_ = bf16[8,64,256]{2,1,0:T(8,128)(2,1)S(1)} collective-permute-done((bf16[8,64,256]{2,1,0:T(8,128)(2,1)S(1)}, bf16[8,64,256]{2,1,0:T(8,128)(2,1)S(1)}, u32[]{:S(2)}, u32[]{:S(2)}) %collective-permute-start.10) | collective-permute-done | bytes 262176 | tf_op jit(solution)/shard_map/ppermute | solution.py:36
  46.3 5.6 %collective-permute-done.11.refs_7_ = bf16[8,64,256]{2,1,0:T(8,128)(2,1)S(1)} collective-permute-done((bf16[8,64,256]{2,1,0:T(8,128)(2,1)S(1)}, bf16[8,64,256]{2,1,0:T(8,128)(2,1)S(1)}, u32[]{:S(2)}, u32[]{:S(2)}) %collective-permute-start.11) | collective-permute-done | bytes 262176 | tf_op jit(solution)/shard_map/ppermute | solution.py:36
  51.9 7.8 %down_grads.1 = (bf16[192,128,128]{2,1,0:T(8,128)(2,1)}, f32[8,128,256]{2,1,0:T(8,128)S(1)}) custom-call(s32[1,1,192]{2,1,0:T(1,128)S(1)} %copy-done.2, s32[1,1]{1,0:T(1,128)S(6)} %copy.18.count, bf16[32,4096]{1,0:T(8,128)(2,1)S(1)} %pad_maximum_fusion.1.refs_0_, bf16[32,4096]{1,0:T(8,128)(2,1)S(1)} %collective-permute-done.6.refs_1_, ...), custom_call_target="tpu_custom_call" | custom-call | flops 805306368 | bytes 6291456 | tf_op jit(solution)/shard_map/down_grads/pallas_call | solution.py:320
  59.8 6.5 %d_tokens.1 = (f32[64,4096]{1,0:T(8,128)S(1)}, bf16[64,4096]{1,0:T(8,128)(2,1)S(1)}, bf16[8,128,256]{2,1,0:T(8,128)(2,1)S(1)}) custom-call(f32[8,128,256]{2,1,0:T(8,128)S(1)} %get-tuple-element.55.refs_0_, f32[8,128,128]{2,1,0:T(8,128)S(1)} %get-tuple-element.57.refs_1_, bf16[8,128,128]{2,1,0:T(8,128)(2,1)S(1)} %collective-permute-done.12.refs_2_, ...), custom_call_target="tpu_custom_call" | custom-call | flops 2147483648 | bytes 16777216 | tf_op jit(solution)/shard_map/d_tokens/pallas_call | solution.py:220
  66.3 1.9 %collective-permute-done.13 = bf16[64,4096]{1,0:T(8,128)(2,1)S(1)} collective-permute-done((bf16[64,4096]{1,0:T(8,128)(2,1)S(1)}, bf16[64,4096]{1,0:T(8,128)(2,1)S(1)}, u32[]{:S(2)}, u32[]{:S(2)}) %collective-permute-start.13) | collective-permute-done | bytes 524320 | tf_op jit(solution)/shard_map/ppermute | solution.py:36
  68.2 0.1 convert_add_fusion
  68.4 1.8 %collective-permute-start.14 = (bf16[32,4096]{1,0:T(8,128)(2,1)S(1)}, bf16[32,4096]{1,0:T(8,128)(2,1)S(1)}, u32[]{:S(2)}, u32[]{:S(2)}) collective-permute-start(bf16[32,4096]{1,0:T(8,128)(2,1)S(1)} %slice.43), channel_id=1, source_target_pairs={{0,4},{2,6},{4,0},{6,2},{8,12},{10,14},{12,8},{14,10},{16,20},{18,... | collective-permute-start | bytes 786440 | tf_op jit(solution)/shard_map/ppermute | solution.py:36
  70.2 5.2 %gu_grads.2 = (bf16[192,128,128]{2,1,0:T(8,128)(2,1)}, bf16[192,128,128]{2,1,0:T(8,128)(2,1)}) custom-call(s32[1,1,192]{2,1,0:T(1,128)S(1)} %copy-done.1, s32[1,1]{1,0:T(1,128)S(6)} %copy.17.count, bf16[8,128,256]{2,1,0:T(8,128)(2,1)S(1)} %get-tuple-element.67.d_pair, bf16[32,128,128]{2,1,0:T(8,128)(2,1)S(1)} %get-tuple-element.68.turned), custom_call_target="tpu_custom_call" | custom-call | flops 805306368 | bytes 6291456 | tf_op jit(solution)/shard_map/gu_grads/pallas_call | solution.py:263
  75.3 1.4 %collective-permute-done.14 = bf16[32,4096]{1,0:T(8,128)(2,1)S(1)} collective-permute-done((bf16[32,4096]{1,0:T(8,128)(2,1)S(1)}, bf16[32,4096]{1,0:T(8,128)(2,1)S(1)}, u32[]{:S(2)}, u32[]{:S(2)}) %collective-permute-start.14) | collective-permute-done | bytes 262176 | tf_op jit(solution)/shard_map/ppermute | solution.py:36
  76.9 2.1 %collective-permute-start.15 = (bf16[8,4096]{1,0:T(8,128)(2,1)S(1)}, bf16[8,4096]{1,0:T(8,128)(2,1)S(1)}, u32[]{:S(2)}, u32[]{:S(2)}) collective-permute-start(bf16[8,4096]{1,0:T(8,128)(2,1)S(1)} %get-tuple-element.64), channel_id=1, source_target_pairs={{0,16},{2,18},{4,20},{6,22},{8,24},{10,26},{12,28},{14,30},{16,0},... | collective-permute-start | bytes 196616 | tf_op jit(solution)/shard_map/ppermute | solution.py:36
  79.0 1.4 %collective-permute-start.16 = (bf16[8,4096]{1,0:T(8,128)(2,1)S(1)}, bf16[8,4096]{1,0:T(8,128)(2,1)S(1)}, u32[]{:S(2)}, u32[]{:S(2)}) collective-permute-start(bf16[8,4096]{1,0:T(8,128)(2,1)S(1)} %get-tuple-element.65), channel_id=1, source_target_pairs={{0,8},{2,10},{4,12},{6,14},{8,0},{10,2},{12,4},{14,6},{16,24},{18,... | collective-permute-start | bytes 196616 | tf_op jit(solution)/shard_map/ppermute | solution.py:36
  80.4 0.9 %collective-permute-start.17 = (bf16[8,4096]{1,0:T(8,128)(2,1)S(1)}, bf16[8,4096]{1,0:T(8,128)(2,1)S(1)}, u32[]{:S(2)}, u32[]{:S(2)}) collective-permute-start(bf16[8,4096]{1,0:T(8,128)(2,1)S(1)} %get-tuple-element.66), channel_id=1, source_target_pairs={{0,24},{2,26},{4,28},{6,30},{8,16},{10,18},{12,20},{14,22},{16,8},... | collective-permute-start | bytes 196616 | tf_op jit(solution)/shard_map/ppermute | solution.py:36
  81.3 5.2 %gu_grads.3 = (bf16[192,128,128]{2,1,0:T(8,128)(2,1)}, bf16[192,128,128]{2,1,0:T(8,128)(2,1)}) custom-call(s32[1,1,192]{2,1,0:T(1,128)S(1)} %copy-done.1, s32[1,1]{1,0:T(1,128)S(6)} %copy.17.count, bf16[8,128,256]{2,1,0:T(8,128)(2,1)S(1)} %get-tuple-element.67.d_pair, ...), custom_call_target="tpu_custom_call", output_to_operand_aliasing={{0}: (4, {}), {1}: (5, {})} | custom-call | flops 805306368 | bytes 6291456 | tf_op jit(solution)/shard_map/gu_grads/pallas_call | solution.py:263
  86.5 0.7 fusion.2
  (32 shorter events, 0.5 us)
Async XLA Ops:
  0.6 10.6 %collective-permute-start = (bf16[8,4096]{1,0:T(8,128)(2,1)}, bf16[8,4096]{1,0:T(8,128)(2,1)S(1)}, u32[]{:S(2)}, u32[]{:S(2)}) collective-permute-start(bf16[8,4096]{1,0:T(8,128)(2,1)} %param.9), channel_id=1, source_target_pairs={{0,16},{2,18},{4,20},{6,22},{8,24},{10,26},{12,28},{14,30},{16,0},... | collective-permute-start | bytes 196616 | tf_op jit(solution)/shard_map/ppermute | solution.py:36
  6.0 0.7 copy-start
  6.7 4.6 %copy-start.4 = (bf16[8,4096]{1,0:T(8,128)(2,1)S(1)}, bf16[8,4096]{1,0:T(8,128)(2,1)}, u32[]{:S(2)}) copy-start(bf16[8,4096]{1,0:T(8,128)(2,1)} %param.10) | copy-start | bytes 196612
  6.7 6.1 %copy-start.3 = (bf16[8,4096]{1,0:T(8,128)(2,1)S(1)}, bf16[8,4096]{1,0:T(8,128)(2,1)}, u32[]{:S(2)}) copy-start(bf16[8,4096]{1,0:T(8,128)(2,1)} %param.9) | copy-start | bytes 196612
  6.7 6.2 %copy-start.2 = (s32[1,1,192]{2,1,0:T(1,128)S(1)}, s32[1,1,192]{2,1,0:T(1,128)}, u32[]{:S(2)}) copy-start(s32[1,1,192]{2,1,0:T(1,128)} %index.6) | copy-start | bytes 2308
  11.3 6.7 %collective-permute-start.3 = (bf16[8,4096]{1,0:T(8,128)(2,1)S(1)}, bf16[8,4096]{1,0:T(8,128)(2,1)S(1)}, u32[]{:S(2)}, u32[]{:S(2)}) collective-permute-start(bf16[8,4096]{1,0:T(8,128)(2,1)S(1)} %copy-done.4), channel_id=1, source_target_pairs={{0,16},{2,18},{4,20},{6,22},{8,24},{10,26},{12,28},{14,30},{16,0},... | collective-permute-start | bytes 196616 | tf_op jit(solution)/shard_map/ppermute | solution.py:36
  12.8 5.2 %collective-permute-start.1 = (bf16[16,4096]{1,0:T(8,128)(2,1)S(1)}, bf16[16,4096]{1,0:T(8,128)(2,1)S(1)}, u32[]{:S(2)}, u32[]{:S(2)}) collective-permute-start(bf16[16,4096]{1,0:T(8,128)(2,1)S(1)} %pad_maximum_fusion.2), channel_id=1, source_target_pairs={{0,8},{2,10},{4,12},{6,14},{8,0},{10,2},{12,4},{14,6},{16,24},{18,... | collective-permute-start | bytes 393224 | tf_op jit(solution)/shard_map/ppermute | solution.py:36
  18.0 5.0 %collective-permute-start.4 = (bf16[16,4096]{1,0:T(8,128)(2,1)S(1)}, bf16[16,4096]{1,0:T(8,128)(2,1)S(1)}, u32[]{:S(2)}, u32[]{:S(2)}) collective-permute-start(bf16[16,4096]{1,0:T(8,128)(2,1)S(1)} %pad_maximum_fusion.3), channel_id=1, source_target_pairs={{0,8},{2,10},{4,12},{6,14},{8,0},{10,2},{12,4},{14,6},{16,24},{18,... | collective-permute-start | bytes 393224 | tf_op jit(solution)/shard_map/ppermute | solution.py:36
  19.6 3.5 %collective-permute-start.5 = (bf16[32,4096]{1,0:T(8,128)(2,1)S(1)}, bf16[32,4096]{1,0:T(8,128)(2,1)S(1)}, u32[]{:S(2)}, u32[]{:S(2)}) collective-permute-start(bf16[32,4096]{1,0:T(8,128)(2,1)S(1)} %pad_maximum_fusion.refs_0_.refs_4_), channel_id=1, source_target_pairs={{0,2},{2,0},{4,6},{6,4},{8,10},{10,8},{12,14},{14,12},{16,18},{18,... | collective-permute-start | bytes 786440 | tf_op jit(solution)/shard_map/ppermute | solution.py:36
  19.7 8.7 %collective-permute-start.2 = (bf16[32,4096]{1,0:T(8,128)(2,1)S(1)}, bf16[32,4096]{1,0:T(8,128)(2,1)S(1)}, u32[]{:S(2)}, u32[]{:S(2)}) collective-permute-start(bf16[32,4096]{1,0:T(8,128)(2,1)S(1)} %pad_maximum_fusion.refs_0_.refs_4_), channel_id=1, source_target_pairs={{0,4},{2,6},{4,0},{6,2},{8,12},{10,14},{12,8},{14,10},{16,20},{18,... | collective-permute-start | bytes 786440 | tf_op jit(solution)/shard_map/ppermute | solution.py:36
  28.4 1.9 %collective-permute-start.8 = (bf16[32,4096]{1,0:T(8,128)(2,1)S(1)}, bf16[32,4096]{1,0:T(8,128)(2,1)S(1)}, u32[]{:S(2)}, u32[]{:S(2)}) collective-permute-start(bf16[32,4096]{1,0:T(8,128)(2,1)S(1)} %collective-permute-done.2.refs_0_.refs_6_), channel_id=1, source_target_pairs={{0,2},{2,0},{4,6},{6,4},{8,10},{10,8},{12,14},{14,12},{16,18},{18,... | collective-permute-start | bytes 786440 | tf_op jit(solution)/shard_map/ppermute | solution.py:36
  28.4 8.7 %collective-permute-start.7 = (bf16[32,4096]{1,0:T(8,128)(2,1)S(1)}, bf16[32,4096]{1,0:T(8,128)(2,1)S(1)}, u32[]{:S(2)}, u32[]{:S(2)}) collective-permute-start(bf16[32,4096]{1,0:T(8,128)(2,1)S(1)} %pad_maximum_fusion.1.refs_0_), channel_id=1, source_target_pairs={{0,4},{2,6},{4,0},{6,2},{8,12},{10,14},{12,8},{14,10},{16,20},{18,... | collective-permute-start | bytes 786440 | tf_op jit(solution)/shard_map/ppermute | solution.py:36
  30.1 9.1 %collective-permute-start.6 = (bf16[32,4096]{1,0:T(8,128)(2,1)S(1)}, bf16[32,4096]{1,0:T(8,128)(2,1)S(1)}, u32[]{:S(2)}, u32[]{:S(2)}) collective-permute-start(bf16[32,4096]{1,0:T(8,128)(2,1)S(1)} %pad_maximum_fusion.1.refs_0_), channel_id=1, source_target_pairs={{0,2},{2,0},{4,6},{6,4},{8,10},{10,8},{12,14},{14,12},{16,18},{18,... | collective-permute-start | bytes 786440 | tf_op jit(solution)/shard_map/ppermute | solution.py:36
  37.1 2.1 %collective-permute-start.9 = (bf16[32,4096]{1,0:T(8,128)(2,1)S(1)}, bf16[32,4096]{1,0:T(8,128)(2,1)S(1)}, u32[]{:S(2)}, u32[]{:S(2)}) collective-permute-start(bf16[32,4096]{1,0:T(8,128)(2,1)S(1)} %collective-permute-done.7.refs_2_), channel_id=1, source_target_pairs={{0,2},{2,0},{4,6},{6,4},{8,10},{10,8},{12,14},{14,12},{16,18},{18,... | collective-permute-start | bytes 786440 | tf_op jit(solution)/shard_map/ppermute | solution.py:36
  37.1 9.2 %collective-permute-start.10 = (bf16[8,64,256]{2,1,0:T(8,128)(2,1)S(1)}, bf16[8,64,256]{2,1,0:T(8,128)(2,1)S(1)}, u32[]{:S(2)}, u32[]{:S(2)}) collective-permute-start(bf16[8,64,256]{2,1,0:T(8,128)(2,1)S(1)} %get-tuple-element.48), channel_id=1, source_target_pairs={{0,1},{1,0},{2,3},{3,2},{4,5},{5,4},{6,7},{7,6},{8,9},{9,8},{10,11... | collective-permute-start | bytes 786440 | tf_op jit(solution)/shard_map/ppermute | solution.py:36
  39.1 12.8 %collective-permute-start.11 = (bf16[8,64,256]{2,1,0:T(8,128)(2,1)S(1)}, bf16[8,64,256]{2,1,0:T(8,128)(2,1)S(1)}, u32[]{:S(2)}, u32[]{:S(2)}) collective-permute-start(bf16[8,64,256]{2,1,0:T(8,128)(2,1)S(1)} %get-tuple-element.51), channel_id=1, source_target_pairs={{0,1},{1,0},{2,3},{3,2},{4,5},{5,4},{6,7},{7,6},{8,9},{9,8},{10,11... | collective-permute-start | bytes 786440 | tf_op jit(solution)/shard_map/ppermute | solution.py:36
  42.8 17.0 %collective-permute-start.12 = (bf16[8,128,128]{2,1,0:T(8,128)(2,1)S(1)}, bf16[8,128,128]{2,1,0:T(8,128)(2,1)S(1)}, u32[]{:S(2)}, u32[]{:S(2)}) collective-permute-start(bf16[8,128,128]{2,1,0:T(8,128)(2,1)S(1)} %get-tuple-element.58), channel_id=1, source_target_pairs={{0,1},{1,0},{2,3},{3,2},{4,5},{5,4},{6,7},{7,6},{8,9},{9,8},{10,11... | collective-permute-start | bytes 786440 | tf_op jit(solution)/shard_map/ppermute | solution.py:36
  59.8 10.4 %copy-start.1 = (s32[1,1,192]{2,1,0:T(1,128)S(1)}, s32[1,1,192]{2,1,0:T(1,128)}, u32[]{:S(2)}) copy-start(s32[1,1,192]{2,1,0:T(1,128)} %index.8) | copy-start | bytes 2308
  66.2 2.0 %collective-permute-start.13 = (bf16[64,4096]{1,0:T(8,128)(2,1)S(1)}, bf16[64,4096]{1,0:T(8,128)(2,1)S(1)}, u32[]{:S(2)}, u32[]{:S(2)}) collective-permute-start(bf16[64,4096]{1,0:T(8,128)(2,1)S(1)} %get-tuple-element.60), channel_id=1, source_target_pairs={{0,2},{2,0},{4,6},{6,4},{8,10},{10,8},{12,14},{14,12},{16,18},{18,... | collective-permute-start | bytes 1572872 | tf_op jit(solution)/shard_map/ppermute | solution.py:36
  68.4 8.4 %collective-permute-start.14 = (bf16[32,4096]{1,0:T(8,128)(2,1)S(1)}, bf16[32,4096]{1,0:T(8,128)(2,1)S(1)}, u32[]{:S(2)}, u32[]{:S(2)}) collective-permute-start(bf16[32,4096]{1,0:T(8,128)(2,1)S(1)} %slice.43), channel_id=1, source_target_pairs={{0,4},{2,6},{4,0},{6,2},{8,12},{10,14},{12,8},{14,10},{16,20},{18,... | collective-permute-start | bytes 786440 | tf_op jit(solution)/shard_map/ppermute | solution.py:36
  76.9 9.6 %collective-permute-start.15 = (bf16[8,4096]{1,0:T(8,128)(2,1)S(1)}, bf16[8,4096]{1,0:T(8,128)(2,1)S(1)}, u32[]{:S(2)}, u32[]{:S(2)}) collective-permute-start(bf16[8,4096]{1,0:T(8,128)(2,1)S(1)} %get-tuple-element.64), channel_id=1, source_target_pairs={{0,16},{2,18},{4,20},{6,22},{8,24},{10,26},{12,28},{14,30},{16,0},... | collective-permute-start | bytes 196616 | tf_op jit(solution)/shard_map/ppermute | solution.py:36
  79.0 7.5 %collective-permute-start.16 = (bf16[8,4096]{1,0:T(8,128)(2,1)S(1)}, bf16[8,4096]{1,0:T(8,128)(2,1)S(1)}, u32[]{:S(2)}, u32[]{:S(2)}) collective-permute-start(bf16[8,4096]{1,0:T(8,128)(2,1)S(1)} %get-tuple-element.65), channel_id=1, source_target_pairs={{0,8},{2,10},{4,12},{6,14},{8,0},{10,2},{12,4},{14,6},{16,24},{18,... | collective-permute-start | bytes 196616 | tf_op jit(solution)/shard_map/ppermute | solution.py:36
  80.4 6.1 %collective-permute-start.17 = (bf16[8,4096]{1,0:T(8,128)(2,1)S(1)}, bf16[8,4096]{1,0:T(8,128)(2,1)S(1)}, u32[]{:S(2)}, u32[]{:S(2)}) collective-permute-start(bf16[8,4096]{1,0:T(8,128)(2,1)S(1)} %get-tuple-element.66), channel_id=1, source_target_pairs={{0,24},{2,26},{4,28},{6,30},{8,16},{10,18},{12,20},{14,22},{16,8},... | collective-permute-start | bytes 196616 | tf_op jit(solution)/shard_map/ppermute | solution.py:36

commit v5 on v4

--- a/solution.py
+++ b/solution.py
@@ -16,8 +16,8 @@
 SCALARS = pl.BlockSpec(memory_space=pltpu.SMEM)
 
 
-def params():
-    return pltpu.CompilerParams(vmem_limit_bytes=VMEM_LIMIT)
+def params(vmem=VMEM_LIMIT):
+    return pltpu.CompilerParams(vmem_limit_bytes=vmem)
 
 
 def cost(flops, bytes_accessed):
@@ -177,14 +177,15 @@
 
 
 def d_tokens_body(group, *refs):
-    coef, dh_own, *dh_recv, gate_w, up_w, own, send, d_pair, turned = refs
+    near, far, dh_own, *dh_recv, gate_w, up_w, own, send, d_pair, turned = refs
     d_blocks, f_blocks, block, _ = gate_w.shape
     piece = own.shape[0] // 2
     for c in range(f_blocks):
         dh = dh_own[c]
         for part in dh_recv:
             dh = dh + part[c].astype(F32)
-        both = (jnp.concatenate([dh, dh], axis=1) * coef[c]).astype(BF16)
+        coef = jnp.concatenate([near[c], far[c]], axis=0)
+        both = (jnp.concatenate([dh, dh], axis=1) * coef).astype(BF16)
         d_pair[c] = both
         for side in range(2):
             turned[pl.ds((2 * c + side) * block, block), :] = both[
@@ -212,7 +213,7 @@
             send[rows, columns] = result[start + piece : start + 2 * piece].astype(BF16)
 
 
-def d_tokens_part(coef, dh_own, dh_recv, gate_w, up_w):
+def d_tokens_part(near, far, dh_own, dh_recv, gate_w, up_w):
     d_blocks, f_blocks, block, _ = gate_w.shape
     tokens = dh_own.shape[1]
     width = d_blocks * block
@@ -224,13 +225,13 @@
             jax.ShapeDtypeStruct((tokens // 2, width), BF16),
             jax.ShapeDtypeStruct((f_blocks, tokens, 2 * block), BF16),
         ),
-        in_specs=[WHOLE] * (4 + len(dh_recv)),
+        in_specs=[WHOLE] * (5 + len(dh_recv)),
         out_specs=(WHOLE,) * 3,
         scratch_shapes=[pltpu.VMEM((f_blocks * 2 * block, tokens), BF16)],
         compiler_params=params(),
         cost_estimate=cost(4 * tokens * gate_w.size, 4 * gate_w.size),
         name="d_tokens",
-    )(coef, dh_own, *dh_recv, resident(gate_w), resident(up_w))
+    )(near, far, dh_own, *dh_recv, resident(gate_w), resident(up_w))
 
 
 def step_slots(slots):
@@ -276,67 +277,85 @@
     )(index, count, d_pair, turned, *before)
 
 
-def down_grad_body(pieces_count, index, count, *refs):
-    pieces, gu = refs[:pieces_count], refs[pieces_count:-4]
-    halves = gu[: len(gu) // 2], gu[len(gu) // 2 :]
-    out, coef, turned, columns = refs[-4:]
-    f_blocks = turned.shape[0]
-    d_blocks, _, block = columns.shape
-    step = pl.program_id(0)
-
-    @pl.when(step == 0)
-    def _():
-        for f in range(f_blocks):
-            both = jnp.concatenate(
-                [
-                    sum((part[f].astype(F32) for part in half[1:]), half[0][f])
-                    for half in halves
-                ],
-                axis=0,
-            )
-            gate, up = both[:, :block], both[:, block:]
-            sig = jax.nn.sigmoid(gate)
-            silu = gate * sig
-            turned[f] = (silu * up).astype(BF16).T
-            coef[f, :, :block] = up * sig * (1.0 + gate * (1.0 - sig))
-            coef[f, :, block:] = silu
-        for d in range(d_blocks):
-            at = slice(d * block, (d + 1) * block)
-            columns[d] = jnp.concatenate([piece[:, at] for piece in pieces], axis=0)
-
-    for j in range(out.shape[0]):
-        slot = step * out.shape[0] + j
-        f, d = split_index(index[0, 0, slot], d_blocks)
-        result = jnp.dot(turned[f], columns[d], preferred_element_type=F32)
-        out[j] = jnp.where(slot < count[0, 0], result, 0.0).astype(BF16)
-
-
-def down_grads(index, count, pieces, halves, slots):
-    f_blocks, half_tokens, pair = halves[0][0].shape
-    tokens = 2 * half_tokens
-    block = pair // 2
+def activate_body(*refs):
+    own, *recv, hidden, coef = refs
+    block = hidden.shape[2]
+    for f in range(hidden.shape[0]):
+        both = own[f]
+        for part in recv:
+            both = both + part[f].astype(F32)
+        gate, up = both[:, :block], both[:, block:]
+        sig = jax.nn.sigmoid(gate)
+        silu = gate * sig
+        hidden[f] = (silu * up).astype(BF16)
+        coef[f, :, :block] = up * sig * (1.0 + gate * (1.0 - sig))
+        coef[f, :, block:] = silu
+
+
+def activate(own, recv):
+    f_blocks, tokens, pair = own.shape
+    return pl.pallas_call(
+        activate_body,
+        out_shape=(
+            jax.ShapeDtypeStruct((f_blocks, tokens, pair // 2), BF16),
+            jax.ShapeDtypeStruct(own.shape, F32),
+        ),
+        in_specs=[WHOLE] * (1 + len(recv)),
+        out_specs=(WHOLE,) * 2,
+        compiler_params=params(),
+        cost_estimate=cost(20 * own.size, 8 * own.size),
+        name="activate",
+    )(own, *recv)
+
+
+def down_grad_body(index, count, near, far, *refs):
+    *pieces, out, turned, dense, zero, sem = refs
+    f_blocks, d_blocks, block, _ = dense.shape
+    live = count[0, 0]
+    for f in range(f_blocks):
+        turned[pl.ds(f * block, block), :] = jnp.concatenate([near[f], far[f]], axis=0).T
+    zero[...] = jnp.zeros(zero.shape, zero.dtype)
+
+    @pl.loop(live, out.shape[0])
+    def _(s):
+        pltpu.make_async_copy(zero, out.at[s], sem).start()
+
+    @pl.loop(0, d_blocks // 2)
+    def _(pair):
+        columns = pl.ds(pl.multiple_of(pair * 2 * block, 2 * block), 2 * block)
+        y = jnp.concatenate([piece[:, columns] for piece in pieces], axis=0)
+        result = jnp.dot(turned[...], y, preferred_element_type=F32).astype(BF16)
+        for side in range(2):
+            part = result[:, side * block : (side + 1) * block]
+            dense[:, 2 * pair + side] = part.reshape(f_blocks, block, block)
+
+    @pl.loop(0, live)
+    def _(s):
+        f, d = split_index(index[0, 0, s], d_blocks)
+        pltpu.make_async_copy(dense.at[f, d], out.at[s], sem).start()
+
+    pltpu.make_async_copy(out, out, sem).wait()
+
+
+def down_grads(index, count, pieces, near, far, slots):
+    f_blocks, _, block = near.shape
+    tokens = sum(piece.shape[0] for piece in pieces)
     d_blocks = pieces[0].shape[1] // block
-    chunk = step_slots(slots)
-    return pl.pallas_call(
-        functools.partial(down_grad_body, len(pieces)),
-        out_shape=(
-            jax.ShapeDtypeStruct((slots, block, block), BF16),
-            jax.ShapeDtypeStruct((f_blocks, tokens, pair), F32),
-        ),
-        grid_spec=pltpu.PrefetchScalarGridSpec(
-            num_scalar_prefetch=2,
-            grid=(slots // chunk,),
-            in_specs=[WHOLE] * (len(pieces) + 2 * len(halves[0])),
-            out_specs=(pl.BlockSpec((chunk, block, block), lambda i, *_: (i, 0, 0)), WHOLE),
-            scratch_shapes=[
-                pltpu.VMEM((f_blocks, block, tokens), BF16),
-                pltpu.VMEM((d_blocks, tokens, block), BF16),
-            ],
-        ),
-        compiler_params=params(),
+    return pl.pallas_call(
+        down_grad_body,
+        out_shape=jax.ShapeDtypeStruct((slots, block, block), BF16),
+        in_specs=[SCALARS] * 2 + [WHOLE] * (2 + len(pieces)),
+        out_specs=pl.BlockSpec(memory_space=pltpu.HBM),
+        scratch_shapes=[
+            pltpu.VMEM((f_blocks * block, tokens), BF16),
+            pltpu.VMEM((f_blocks, d_blocks, block, block), BF16),
+            pltpu.VMEM((block, block), BF16),
+            pltpu.SemaphoreType.DMA,
+        ],
+        compiler_params=params(VMEM_LIMIT + 2 * f_blocks * d_blocks * block * block),
         cost_estimate=cost(2 * slots * block * block * tokens, 2 * slots * block * block),
         name="down_grads",
-    )(index, count, *pieces, *halves[0], *halves[1])
+    )(index, count, near, far, *pieces)
 
 
 def on_device(
@@ -383,15 +402,20 @@
     x_far = [x_far, swap(x_far, "wide", wide, 1)]
     far_own, far_send = gate_up(x_far, gate_w, up_w)
     far_recv = exchange(far_send)
+    near_hidden, near_coef = activate(near_own, near_recv)
     y_far, _ = lax.optimization_barrier((y_far, far_send))
     y_far = [y_far, swap(y_far, "wide", wide, 1)]
     x_pieces = x_near + x_far
     y_pieces = y_near + y_far
+    down_w, near_hidden = lax.optimization_barrier((down_w, near_hidden))
     dh_own, dh_send, turned = d_hidden(y_pieces, x_pieces, down_w)
     dh_recv = exchange(dh_send)
-    halves = (near_own, *near_recv), (far_own, *far_recv)
-    down_grad, coef = down_grads(down_index, down_count, y_pieces, halves, slots)
-    own, send, d_pair = d_tokens_part(coef, dh_own, dh_recv, gate_w, up_w)
+    far_hidden, far_coef = activate(far_own, far_recv)
+    down_grad = down_grads(down_index, down_count, y_pieces, near_hidden, far_hidden, slots)
+    down_grad, far_coef = lax.optimization_barrier((down_grad, far_coef))
+    own, send, d_pair = d_tokens_part(
+        near_coef, far_coef, dh_own, dh_recv, gate_w, up_w
+    )
 
     own = own + swap(send, "wide", wide, 1).astype(F32)
     kept = chips // 2 * rows

time: 87.6 us -> 82.1 us (0.937)
  waiting for transfers between devices: 18.1 us -> 8.9 us
  starting transfers between devices: 21.3 us -> 24 us
  Pallas kernels: 44.1 us -> 45.1 us
    ppermute x18, waiting for transfers between devices: 18.1 us -> 8.9 us  [swap(): return lax.ppermute(array, axis, [(i, i ^ flip) for i in range(size)])]
    ppermute x18, starting transfers between devices: 21.3 us -> 24 us  [swap(): return lax.ppermute(array, axis, [(i, i ^ flip) for i in range(size)])]
    pallas_call x2, Pallas kernels: 7.99 us -> 9.07 us  [fill(): pl.pallas_call(functools.partial(fill_body, arrays), out_shape=(pltpu.VME...]
    pallas_call x1 -> x3, Pallas kernels: 7.84 us -> 7.75 us  [the longest x1 7.51 us: down_grads(): pl.pallas_call(down_grad_body, out_shape=jax.ShapeDtypeStruct((slots, blo...]
  transfers between devices with their start and end apart: 18 -> 18, of which waited for: 8 -> 8; matrix products, arithmetic and copies ran while one was open for 0% -> 0% of each run, Pallas kernels for 43% -> 47%
where the time goes in v5:
time: 82.1 us; the launch traced here: 81.8 us
  Pallas kernels  45.1 us (55%)
  starting transfers between devices  24 us (29%)
  waiting for transfers between devices  8.9 us (11%)
  between operations  2.15 us (3%)
  other arithmetic  0.87 us (1%)
    ppermute x18, starting transfers between devices, swap(): return lax.ppermute(array, axis, [(i, i ^ flip) for i in range(size)])  24 us
    pallas_call x2, Pallas kernels, gu_grads(): pl.pallas_call(functools.partial(gu_grad_body, first), out_shape=(shape,)...  10.4 us
    pallas_call x2, Pallas kernels, fill(): pl.pallas_call(functools.partial(fill_body, arrays), out_shape=(pltpu.VME...  9.07 us
    ppermute x18, waiting for transfers between devices, swap(): return lax.ppermute(array, axis, [(i, i ^ flip) for i in range(size)])  8.9 us
    pallas_call x2, Pallas kernels, gate_up(): pl.pallas_call(gate_up_body, out_shape=(jax.ShapeDtypeStruct(shape, F32),...  7.79 us
    pallas_call x1, Pallas kernels, down_grads(): pl.pallas_call(down_grad_body, out_shape=jax.ShapeDtypeStruct((slots, blo...  7.51 us
    pallas_call x1, Pallas kernels, d_tokens_part(): pl.pallas_call(functools.partial(d_tokens_body, group), out_shape=(jax.Sh...  6.48 us
    pallas_call x1, Pallas kernels, d_hidden(): pl.pallas_call(functools.partial(d_hidden_body, len(y_pieces)), out_shape...  3.6 us
  transfers between devices with their start and end apart: 18, of which 8 were waited for; matrix products, arithmetic and copies ran while one was open for 0% of the time, Pallas kernels for 47%

profile of v5, /device:TPU:0, one launch (start us, length us, event | category | flops | bytes accessed | tf_op | source)
XLA Modules:
  0.0 81.8 jit_solution(10787019981013395753)
XLA Ops:
  0.6 4.1 %collective-permute-start = (bf16[8,4096]{1,0:T(8,128)(2,1)}, bf16[8,4096]{1,0:T(8,128)(2,1)S(1)}, u32[]{:S(2)}, u32[]{:S(2)}) collective-permute-start(bf16[8,4096]{1,0:T(8,128)(2,1)} %param.9), channel_id=1, source_target_pairs={{0,16},{2,18},{4,20},{6,22},{8,24},{10,26},{12,28},{14,30},{16,0},... | collective-permute-start | bytes 196616 | tf_op jit(solution)/shard_map/ppermute | solution.py:36
  6.0 0.7 copy-done.1
  6.7 5.6 %fill.2 = (bf16[32,8,128,128]{3,2,1,0:T(8,128)(2,1)S(1)}, bf16[32,8,128,128]{3,2,1,0:T(8,128)(2,1)S(1)}) custom-call(s32[1,1,192]{2,1,0:T(1,128)S(1)} %copy-done.1, s32[1,1]{1,0:T(1,128)S(6)} %copy.17.count, bf16[1,1,192,128,128]{4,3,2,1,0:T(8,128)(2,1)} %refs_0_.2, bf16[1,1,192,128,128]{4,3,2,1,0:T(8,128)(2,1)} %refs_1_.1), custom_call_target="tpu_custom_call" | custom-call | bytes 12582912 | tf_op jit(solution)/shard_map/fill/pallas_call | solution.py:82
  12.5 0.7 collective-permute-start.1
  13.2 3.5 %fill.3.refs_8_ = bf16[8,32,128,128]{3,2,1,0:T(8,128)(2,1)S(1)} custom-call(s32[1,1,192]{2,1,0:T(1,128)S(1)} %copy-done, s32[1,1]{1,0:T(1,128)S(6)} %copy.18.count, bf16[1,1,192,128,128]{4,3,2,1,0:T(8,128)(2,1)} %refs_0_.3), custom_call_target="tpu_custom_call" | custom-call | bytes 6291456 | tf_op jit(solution)/shard_map/fill/pallas_call | solution.py:82
  16.6 1.6 %collective-permute-done.5 = bf16[8,4096]{1,0:T(8,128)(2,1)S(1)} collective-permute-done((bf16[8,4096]{1,0:T(8,128)(2,1)S(1)}, bf16[8,4096]{1,0:T(8,128)(2,1)S(1)}, u32[]{:S(2)}, u32[]{:S(2)}) %collective-permute-start.5) | collective-permute-done | bytes 65568 | tf_op jit(solution)/shard_map/ppermute | solution.py:36
  18.2 0.1 collective-permute-done.1
  18.4 1.0 %collective-permute-start.6 = (bf16[16,4096]{1,0:T(8,128)(2,1)S(1)}, bf16[16,4096]{1,0:T(8,128)(2,1)S(1)}, u32[]{:S(2)}, u32[]{:S(2)}) collective-permute-start(bf16[16,4096]{1,0:T(8,128)(2,1)S(1)} %pad_maximum_fusion.3), channel_id=1, source_target_pairs={{0,8},{2,10},{4,12},{6,14},{8,0},{10,2},{12,4},{14,6},{16,24},{18,... | collective-permute-start | bytes 393224 | tf_op jit(solution)/shard_map/ppermute | solution.py:36
  19.4 2.1 %collective-permute-start.4 = (bf16[32,4096]{1,0:T(8,128)(2,1)S(1)}, bf16[32,4096]{1,0:T(8,128)(2,1)S(1)}, u32[]{:S(2)}, u32[]{:S(2)}) collective-permute-start(bf16[32,4096]{1,0:T(8,128)(2,1)S(1)} %pad_maximum_fusion.refs_0_.refs_4_), channel_id=1, source_target_pairs={{0,4},{2,6},{4,0},{6,2},{8,12},{10,14},{12,8},{14,10},{16,20},{18,... | collective-permute-start | bytes 786440 | tf_op jit(solution)/shard_map/ppermute | solution.py:36
  21.6 1.8 %collective-permute-done.6 = bf16[16,4096]{1,0:T(8,128)(2,1)S(1)} collective-permute-done((bf16[16,4096]{1,0:T(8,128)(2,1)S(1)}, bf16[16,4096]{1,0:T(8,128)(2,1)S(1)}, u32[]{:S(2)}, u32[]{:S(2)}) %collective-permute-start.6) | collective-permute-done | bytes 131104 | tf_op jit(solution)/shard_map/ppermute | solution.py:36
  23.4 3.9 %gate_up.2 = (f32[8,64,256]{2,1,0:T(8,128)S(1)}, bf16[8,64,256]{2,1,0:T(8,128)(2,1)S(1)}) custom-call(bf16[32,4096]{1,0:T(8,128)(2,1)S(1)} %pad_maximum_fusion.refs_0_.refs_4_, bf16[32,4096]{1,0:T(8,128)(2,1)S(1)} %collective-permute-done.2.refs_1_.refs_5_, bf16[32,8,128,128]{3,2,1,0:T(8,128)(2,1)S(1)} %get-tuple-element.50.refs_2_.refs_4_, ...), custom_call_target="tpu_custom_call" | custom-call | flops 1073741824 | bytes 16777216 | tf_op jit(solution)/shard_map/gate_up/pallas_call | solution.py:121
  27.4 2.3 %collective-permute-start.10 = (bf16[32,4096]{1,0:T(8,128)(2,1)S(1)}, bf16[32,4096]{1,0:T(8,128)(2,1)S(1)}, u32[]{:S(2)}, u32[]{:S(2)}) collective-permute-start(bf16[32,4096]{1,0:T(8,128)(2,1)S(1)} %pad_maximum_fusion.1.refs_0_), channel_id=1, source_target_pairs={{0,4},{2,6},{4,0},{6,2},{8,12},{10,14},{12,8},{14,10},{16,20},{18,... | collective-permute-start | bytes 786440 | tf_op jit(solution)/shard_map/ppermute | solution.py:36
  29.6 0.2 collective-permute-start.9
  29.8 2.5 %collective-permute-start.3 = (bf16[8,64,256]{2,1,0:T(8,128)(2,1)S(1)}, bf16[8,64,256]{2,1,0:T(8,128)(2,1)S(1)}, u32[]{:S(2)}, u32[]{:S(2)}) collective-permute-start(bf16[8,64,256]{2,1,0:T(8,128)(2,1)S(1)} %get-tuple-element.53), channel_id=1, source_target_pairs={{0,1},{1,0},{2,3},{3,2},{4,5},{5,4},{6,7},{7,6},{8,9},{9,8},{10,11... | collective-permute-start | bytes 786440 | tf_op jit(solution)/shard_map/ppermute | solution.py:36
  32.3 3.9 %gate_up.3 = (f32[8,64,256]{2,1,0:T(8,128)S(1)}, bf16[8,64,256]{2,1,0:T(8,128)(2,1)S(1)}) custom-call(bf16[32,4096]{1,0:T(8,128)(2,1)S(1)} %collective-permute-done.4.refs_0_.refs_6_, bf16[32,4096]{1,0:T(8,128)(2,1)S(1)} %collective-permute-done.7.refs_1_.refs_7_, bf16[32,8,128,128]{3,2,1,0:T(8,128)(2,1)S(1)} %get-tuple-element.50.refs_2_.refs_4_, ...), custom_call_target="tpu_custom_call" | custom-call | flops 1073741824 | bytes 16777216 | tf_op jit(solution)/shard_map/gate_up/pallas_call | solution.py:121
  36.2 0.3 collective-permute-done.10.refs_2_
  36.5 2.5 %collective-permute-start.8 = (bf16[8,64,256]{2,1,0:T(8,128)(2,1)S(1)}, bf16[8,64,256]{2,1,0:T(8,128)(2,1)S(1)}, u32[]{:S(2)}, u32[]{:S(2)}) collective-permute-start(bf16[8,64,256]{2,1,0:T(8,128)(2,1)S(1)} %get-tuple-element.62), channel_id=1, source_target_pairs={{0,1},{1,0},{2,3},{3,2},{4,5},{5,4},{6,7},{7,6},{8,9},{9,8},{10,11... | collective-permute-start | bytes 786440 | tf_op jit(solution)/shard_map/ppermute | solution.py:36
  39.1 0.1 activate.2
  39.3 3.6 %d_hidden.1 = (f32[8,128,128]{2,1,0:T(8,128)S(1)}, bf16[8,128,128]{2,1,0:T(8,128)(2,1)S(1)}, bf16[32,128,128]{2,1,0:T(8,128)(2,1)S(1)}) custom-call(bf16[32,4096]{1,0:T(8,128)(2,1)S(1)} %pad_maximum_fusion.1.refs_0_, bf16[32,4096]{1,0:T(8,128)(2,1)S(1)} %collective-permute-done.9.refs_1_, bf16[32,4096]{1,0:T(8,128)(2,1)S(1)} %collective-permute-done.10.refs_2_, ...), custom_call_target="tpu_custom_call" | custom-call | flops 1073741824 | bytes 8388608 | tf_op jit(solution)/shard_map/d_hidden/pallas_call | solution.py:164
  42.9 1.8 %collective-permute-start.12 = (bf16[8,128,128]{2,1,0:T(8,128)(2,1)S(1)}, bf16[8,128,128]{2,1,0:T(8,128)(2,1)S(1)}, u32[]{:S(2)}, u32[]{:S(2)}) collective-permute-start(bf16[8,128,128]{2,1,0:T(8,128)(2,1)S(1)} %get-tuple-element.70), channel_id=1, source_target_pairs={{0,1},{1,0},{2,3},{3,2},{4,5},{5,4},{6,7},{7,6},{8,9},{9,8},{10,11... | collective-permute-start | bytes 786440 | tf_op jit(solution)/shard_map/ppermute | solution.py:36
  44.7 1.5 %collective-permute-done.8.refs_1_ = bf16[8,64,256]{2,1,0:T(8,128)(2,1)S(1)} collective-permute-done((bf16[8,64,256]{2,1,0:T(8,128)(2,1)S(1)}, bf16[8,64,256]{2,1,0:T(8,128)(2,1)S(1)}, u32[]{:S(2)}, u32[]{:S(2)}) %collective-permute-start.8) | collective-permute-done | bytes 262176 | tf_op jit(solution)/shard_map/ppermute | solution.py:36
  46.2 0.1 activate.3
  46.3 7.5 %down_grads.1 = bf16[192,128,128]{2,1,0:T(8,128)(2,1)} custom-call(s32[1,1,192]{2,1,0:T(1,128)S(1)} %copy-done, s32[1,1]{1,0:T(1,128)S(6)} %copy.18.count, bf16[8,64,128]{2,1,0:T(8,128)(2,1)S(1)} %get-tuple-element.57.near, bf16[8,64,128]{2,1,0:T(8,128)(2,1)S(1)} %get-tuple-element.63.far, bf16[32,4096]{1,0:T(8,128)(2,1)S(1)} %pad_maximum_fusion.1.refs_0_, ...), custom_call_target="tpu_custom_call" | custom-call | flops 805306368 | bytes 6291456 | tf_op jit(solution)/shard_map/down_grads/pallas_call | solution.py:344
  53.9 6.5 %d_tokens.1 = (f32[64,4096]{1,0:T(8,128)S(1)}, bf16[64,4096]{1,0:T(8,128)(2,1)S(1)}, bf16[8,128,256]{2,1,0:T(8,128)(2,1)S(1)}) custom-call(f32[8,64,256]{2,1,0:T(8,128)S(1)} %get-tuple-element.54.refs_0_, f32[8,64,256]{2,1,0:T(8,128)S(1)} %get-tuple-element.67.refs_1_, f32[8,128,128]{2,1,0:T(8,128)S(1)} %get-tuple-element.69.refs_2_, ...), custom_call_target="tpu_custom_call" | custom-call | flops 2147483648 | bytes 16777216 | tf_op jit(solution)/shard_map/d_tokens/pallas_call | solution.py:221
  60.4 1.9 %collective-permute-done.13 = bf16[64,4096]{1,0:T(8,128)(2,1)S(1)} collective-permute-done((bf16[64,4096]{1,0:T(8,128)(2,1)S(1)}, bf16[64,4096]{1,0:T(8,128)(2,1)S(1)}, u32[]{:S(2)}, u32[]{:S(2)}) %collective-permute-start.13) | collective-permute-done | bytes 524320 | tf_op jit(solution)/shard_map/ppermute | solution.py:36
  62.5 1.7 %collective-permute-start.14 = (bf16[32,4096]{1,0:T(8,128)(2,1)S(1)}, bf16[32,4096]{1,0:T(8,128)(2,1)S(1)}, u32[]{:S(2)}, u32[]{:S(2)}) collective-permute-start(bf16[32,4096]{1,0:T(8,128)(2,1)S(1)} %slice.43), channel_id=1, source_target_pairs={{0,4},{2,6},{4,0},{6,2},{8,12},{10,14},{12,8},{14,10},{16,20},{18,... | collective-permute-start | bytes 786440 | tf_op jit(solution)/shard_map/ppermute | solution.py:36
  64.1 5.2 %gu_grads.2 = (bf16[192,128,128]{2,1,0:T(8,128)(2,1)}, bf16[192,128,128]{2,1,0:T(8,128)(2,1)}) custom-call(s32[1,1,192]{2,1,0:T(1,128)S(1)} %copy-done.2, s32[1,1]{1,0:T(1,128)S(6)} %copy.17.count, bf16[8,128,256]{2,1,0:T(8,128)(2,1)S(1)} %get-tuple-element.79.d_pair, bf16[32,128,128]{2,1,0:T(8,128)(2,1)S(1)} %get-tuple-element.80.turned), custom_call_target="tpu_custom_call" | custom-call | flops 805306368 | bytes 6291456 | tf_op jit(solution)/shard_map/gu_grads/pallas_call | solution.py:264
  69.3 1.6 %collective-permute-done.14 = bf16[32,4096]{1,0:T(8,128)(2,1)S(1)} collective-permute-done((bf16[32,4096]{1,0:T(8,128)(2,1)S(1)}, bf16[32,4096]{1,0:T(8,128)(2,1)S(1)}, u32[]{:S(2)}, u32[]{:S(2)}) %collective-permute-start.14) | collective-permute-done | bytes 262176 | tf_op jit(solution)/shard_map/ppermute | solution.py:36
  71.0 3.4 %collective-permute-start.15 = (bf16[8,4096]{1,0:T(8,128)(2,1)S(1)}, bf16[8,4096]{1,0:T(8,128)(2,1)S(1)}, u32[]{:S(2)}, u32[]{:S(2)}) collective-permute-start(bf16[8,4096]{1,0:T(8,128)(2,1)S(1)} %get-tuple-element.76), channel_id=1, source_target_pairs={{0,16},{2,18},{4,20},{6,22},{8,24},{10,26},{12,28},{14,30},{16,0},... | collective-permute-start | bytes 196616 | tf_op jit(solution)/shard_map/ppermute | solution.py:36
  74.4 1.5 %collective-permute-start.17 = (bf16[8,4096]{1,0:T(8,128)(2,1)S(1)}, bf16[8,4096]{1,0:T(8,128)(2,1)S(1)}, u32[]{:S(2)}, u32[]{:S(2)}) collective-permute-start(bf16[8,4096]{1,0:T(8,128)(2,1)S(1)} %get-tuple-element.78), channel_id=1, source_target_pairs={{0,24},{2,26},{4,28},{6,30},{8,16},{10,18},{12,20},{14,22},{16,8},... | collective-permute-start | bytes 196616 | tf_op jit(solution)/shard_map/ppermute | solution.py:36
  75.9 5.2 %gu_grads.3 = (bf16[192,128,128]{2,1,0:T(8,128)(2,1)}, bf16[192,128,128]{2,1,0:T(8,128)(2,1)}) custom-call(s32[1,1,192]{2,1,0:T(1,128)S(1)} %copy-done.2, s32[1,1]{1,0:T(1,128)S(6)} %copy.17.count, bf16[8,128,256]{2,1,0:T(8,128)(2,1)S(1)} %get-tuple-element.79.d_pair, ...), custom_call_target="tpu_custom_call", output_to_operand_aliasing={{0}: (4, {}), {1}: (5, {})} | custom-call | flops 805306368 | bytes 6291456 | tf_op jit(solution)/shard_map/gu_grads/pallas_call | solution.py:264
  81.1 0.7 fusion.2
  (34 shorter events, 0.7 us)
Async XLA Ops:
  0.6 11.7 %collective-permute-start = (bf16[8,4096]{1,0:T(8,128)(2,1)}, bf16[8,4096]{1,0:T(8,128)(2,1)S(1)}, u32[]{:S(2)}, u32[]{:S(2)}) collective-permute-start(bf16[8,4096]{1,0:T(8,128)(2,1)} %param.9), channel_id=1, source_target_pairs={{0,16},{2,18},{4,20},{6,22},{8,24},{10,26},{12,28},{14,30},{16,0},... | collective-permute-start | bytes 196616 | tf_op jit(solution)/shard_map/ppermute | solution.py:36
  6.0 0.7 copy-start.1
  6.7 5.6 %copy-start.4 = (bf16[8,4096]{1,0:T(8,128)(2,1)S(1)}, bf16[8,4096]{1,0:T(8,128)(2,1)}, u32[]{:S(2)}) copy-start(bf16[8,4096]{1,0:T(8,128)(2,1)} %param.10) | copy-start | bytes 196612
  6.7 5.7 %copy-start.3 = (bf16[8,4096]{1,0:T(8,128)(2,1)S(1)}, bf16[8,4096]{1,0:T(8,128)(2,1)}, u32[]{:S(2)}) copy-start(bf16[8,4096]{1,0:T(8,128)(2,1)} %param.9) | copy-start | bytes 196612
  6.7 6.4 %copy-start = (s32[1,1,192]{2,1,0:T(1,128)S(1)}, s32[1,1,192]{2,1,0:T(1,128)}, u32[]{:S(2)}) copy-start(s32[1,1,192]{2,1,0:T(1,128)} %index.6) | copy-start | bytes 2308
  12.3 5.9 %collective-permute-start.5 = (bf16[8,4096]{1,0:T(8,128)(2,1)S(1)}, bf16[8,4096]{1,0:T(8,128)(2,1)S(1)}, u32[]{:S(2)}, u32[]{:S(2)}) collective-permute-start(bf16[8,4096]{1,0:T(8,128)(2,1)S(1)} %copy-done.4), channel_id=1, source_target_pairs={{0,16},{2,18},{4,20},{6,22},{8,24},{10,26},{12,28},{14,30},{16,0},... | collective-permute-start | bytes 196616 | tf_op jit(solution)/shard_map/ppermute | solution.py:36
  12.5 5.9 %collective-permute-start.1 = (bf16[16,4096]{1,0:T(8,128)(2,1)S(1)}, bf16[16,4096]{1,0:T(8,128)(2,1)S(1)}, u32[]{:S(2)}, u32[]{:S(2)}) collective-permute-start(bf16[16,4096]{1,0:T(8,128)(2,1)S(1)} %pad_maximum_fusion.2), channel_id=1, source_target_pairs={{0,8},{2,10},{4,12},{6,14},{8,0},{10,2},{12,4},{14,6},{16,24},{18,... | collective-permute-start | bytes 393224 | tf_op jit(solution)/shard_map/ppermute | solution.py:36
  18.4 5.0 %collective-permute-start.6 = (bf16[16,4096]{1,0:T(8,128)(2,1)S(1)}, bf16[16,4096]{1,0:T(8,128)(2,1)S(1)}, u32[]{:S(2)}, u32[]{:S(2)}) collective-permute-start(bf16[16,4096]{1,0:T(8,128)(2,1)S(1)} %pad_maximum_fusion.3), channel_id=1, source_target_pairs={{0,8},{2,10},{4,12},{6,14},{8,0},{10,2},{12,4},{14,6},{16,24},{18,... | collective-permute-start | bytes 393224 | tf_op jit(solution)/shard_map/ppermute | solution.py:36
  19.4 7.8 %collective-permute-start.4 = (bf16[32,4096]{1,0:T(8,128)(2,1)S(1)}, bf16[32,4096]{1,0:T(8,128)(2,1)S(1)}, u32[]{:S(2)}, u32[]{:S(2)}) collective-permute-start(bf16[32,4096]{1,0:T(8,128)(2,1)S(1)} %pad_maximum_fusion.refs_0_.refs_4_), channel_id=1, source_target_pairs={{0,4},{2,6},{4,0},{6,2},{8,12},{10,14},{12,8},{14,10},{16,20},{18,... | collective-permute-start | bytes 786440 | tf_op jit(solution)/shard_map/ppermute | solution.py:36
  21.6 1.8 %collective-permute-start.2 = (bf16[32,4096]{1,0:T(8,128)(2,1)S(1)}, bf16[32,4096]{1,0:T(8,128)(2,1)S(1)}, u32[]{:S(2)}, u32[]{:S(2)}) collective-permute-start(bf16[32,4096]{1,0:T(8,128)(2,1)S(1)} %pad_maximum_fusion.refs_0_.refs_4_), channel_id=1, source_target_pairs={{0,2},{2,0},{4,6},{6,4},{8,10},{10,8},{12,14},{14,12},{16,18},{18,... | collective-permute-start | bytes 786440 | tf_op jit(solution)/shard_map/ppermute | solution.py:36
  27.3 5.0 %collective-permute-start.7 = (bf16[32,4096]{1,0:T(8,128)(2,1)S(1)}, bf16[32,4096]{1,0:T(8,128)(2,1)S(1)}, u32[]{:S(2)}, u32[]{:S(2)}) collective-permute-start(bf16[32,4096]{1,0:T(8,128)(2,1)S(1)} %collective-permute-done.4.refs_0_.refs_6_), channel_id=1, source_target_pairs={{0,2},{2,0},{4,6},{6,4},{8,10},{10,8},{12,14},{14,12},{16,18},{18,... | collective-permute-start | bytes 786440 | tf_op jit(solution)/shard_map/ppermute | solution.py:36
  27.4 9.2 %collective-permute-start.10 = (bf16[32,4096]{1,0:T(8,128)(2,1)S(1)}, bf16[32,4096]{1,0:T(8,128)(2,1)S(1)}, u32[]{:S(2)}, u32[]{:S(2)}) collective-permute-start(bf16[32,4096]{1,0:T(8,128)(2,1)S(1)} %pad_maximum_fusion.1.refs_0_), channel_id=1, source_target_pairs={{0,4},{2,6},{4,0},{6,2},{8,12},{10,14},{12,8},{14,10},{16,20},{18,... | collective-permute-start | bytes 786440 | tf_op jit(solution)/shard_map/ppermute | solution.py:36
  29.6 9.6 %collective-permute-start.9 = (bf16[32,4096]{1,0:T(8,128)(2,1)S(1)}, bf16[32,4096]{1,0:T(8,128)(2,1)S(1)}, u32[]{:S(2)}, u32[]{:S(2)}) collective-permute-start(bf16[32,4096]{1,0:T(8,128)(2,1)S(1)} %pad_maximum_fusion.1.refs_0_), channel_id=1, source_target_pairs={{0,2},{2,0},{4,6},{6,4},{8,10},{10,8},{12,14},{14,12},{16,18},{18,... | collective-permute-start | bytes 786440 | tf_op jit(solution)/shard_map/ppermute | solution.py:36
  29.8 9.3 %collective-permute-start.3 = (bf16[8,64,256]{2,1,0:T(8,128)(2,1)S(1)}, bf16[8,64,256]{2,1,0:T(8,128)(2,1)S(1)}, u32[]{:S(2)}, u32[]{:S(2)}) collective-permute-start(bf16[8,64,256]{2,1,0:T(8,128)(2,1)S(1)} %get-tuple-element.53), channel_id=1, source_target_pairs={{0,1},{1,0},{2,3},{3,2},{4,5},{5,4},{6,7},{7,6},{8,9},{9,8},{10,11... | collective-permute-start | bytes 786440 | tf_op jit(solution)/shard_map/ppermute | solution.py:36
  36.5 2.7 %collective-permute-start.11 = (bf16[32,4096]{1,0:T(8,128)(2,1)S(1)}, bf16[32,4096]{1,0:T(8,128)(2,1)S(1)}, u32[]{:S(2)}, u32[]{:S(2)}) collective-permute-start(bf16[32,4096]{1,0:T(8,128)(2,1)S(1)} %collective-permute-done.10.refs_2_), channel_id=1, source_target_pairs={{0,2},{2,0},{4,6},{6,4},{8,10},{10,8},{12,14},{14,12},{16,18},{18,... | collective-permute-start | bytes 786440 | tf_op jit(solution)/shard_map/ppermute | solution.py:36
  36.5 9.7 %collective-permute-start.8 = (bf16[8,64,256]{2,1,0:T(8,128)(2,1)S(1)}, bf16[8,64,256]{2,1,0:T(8,128)(2,1)S(1)}, u32[]{:S(2)}, u32[]{:S(2)}) collective-permute-start(bf16[8,64,256]{2,1,0:T(8,128)(2,1)S(1)} %get-tuple-element.62), channel_id=1, source_target_pairs={{0,1},{1,0},{2,3},{3,2},{4,5},{5,4},{6,7},{7,6},{8,9},{9,8},{10,11... | collective-permute-start | bytes 786440 | tf_op jit(solution)/shard_map/ppermute | solution.py:36
  42.9 11.0 %collective-permute-start.12 = (bf16[8,128,128]{2,1,0:T(8,128)(2,1)S(1)}, bf16[8,128,128]{2,1,0:T(8,128)(2,1)S(1)}, u32[]{:S(2)}, u32[]{:S(2)}) collective-permute-start(bf16[8,128,128]{2,1,0:T(8,128)(2,1)S(1)} %get-tuple-element.70), channel_id=1, source_target_pairs={{0,1},{1,0},{2,3},{3,2},{4,5},{5,4},{6,7},{7,6},{8,9},{9,8},{10,11... | collective-permute-start | bytes 786440 | tf_op jit(solution)/shard_map/ppermute | solution.py:36
  53.9 10.3 %copy-start.2 = (s32[1,1,192]{2,1,0:T(1,128)S(1)}, s32[1,1,192]{2,1,0:T(1,128)}, u32[]{:S(2)}) copy-start(s32[1,1,192]{2,1,0:T(1,128)} %index.8) | copy-start | bytes 2308
  60.4 2.0 %collective-permute-start.13 = (bf16[64,4096]{1,0:T(8,128)(2,1)S(1)}, bf16[64,4096]{1,0:T(8,128)(2,1)S(1)}, u32[]{:S(2)}, u32[]{:S(2)}) collective-permute-start(bf16[64,4096]{1,0:T(8,128)(2,1)S(1)} %get-tuple-element.72), channel_id=1, source_target_pairs={{0,2},{2,0},{4,6},{6,4},{8,10},{10,8},{12,14},{14,12},{16,18},{18,... | collective-permute-start | bytes 1572872 | tf_op jit(solution)/shard_map/ppermute | solution.py:36
  62.5 8.4 %collective-permute-start.14 = (bf16[32,4096]{1,0:T(8,128)(2,1)S(1)}, bf16[32,4096]{1,0:T(8,128)(2,1)S(1)}, u32[]{:S(2)}, u32[]{:S(2)}) collective-permute-start(bf16[32,4096]{1,0:T(8,128)(2,1)S(1)} %slice.43), channel_id=1, source_target_pairs={{0,4},{2,6},{4,0},{6,2},{8,12},{10,14},{12,8},{14,10},{16,20},{18,... | collective-permute-start | bytes 786440 | tf_op jit(solution)/shard_map/ppermute | solution.py:36
  71.0 10.1 %collective-permute-start.15 = (bf16[8,4096]{1,0:T(8,128)(2,1)S(1)}, bf16[8,4096]{1,0:T(8,128)(2,1)S(1)}, u32[]{:S(2)}, u32[]{:S(2)}) collective-permute-start(bf16[8,4096]{1,0:T(8,128)(2,1)S(1)} %get-tuple-element.76), channel_id=1, source_target_pairs={{0,16},{2,18},{4,20},{6,22},{8,24},{10,26},{12,28},{14,30},{16,0},... | collective-permute-start | bytes 196616 | tf_op jit(solution)/shard_map/ppermute | solution.py:36
  74.4 6.7 %collective-permute-start.16 = (bf16[8,4096]{1,0:T(8,128)(2,1)S(1)}, bf16[8,4096]{1,0:T(8,128)(2,1)S(1)}, u32[]{:S(2)}, u32[]{:S(2)}) collective-permute-start(bf16[8,4096]{1,0:T(8,128)(2,1)S(1)} %get-tuple-element.77), channel_id=1, source_target_pairs={{0,8},{2,10},{4,12},{6,14},{8,0},{10,2},{12,4},{14,6},{16,24},{18,... | collective-permute-start | bytes 196616 | tf_op jit(solution)/shard_map/ppermute | solution.py:36
  74.4 6.7 %collective-permute-start.17 = (bf16[8,4096]{1,0:T(8,128)(2,1)S(1)}, bf16[8,4096]{1,0:T(8,128)(2,1)S(1)}, u32[]{:S(2)}, u32[]{:S(2)}) collective-permute-start(bf16[8,4096]{1,0:T(8,128)(2,1)S(1)} %get-tuple-element.78), channel_id=1, source_target_pairs={{0,24},{2,26},{4,28},{6,30},{8,16},{10,18},{12,20},{14,22},{16,8},... | collective-permute-start | bytes 196616 | tf_op jit(solution)/shard_map/ppermute | solution.py:36

commit v6 on v5

v6 whole, which is shorter than its diff:
```python
import functools
import math

import jax
import jax.numpy as jnp
from jax import lax
from jax.experimental import pallas as pl
from jax.experimental.pallas import tpu as pltpu
from jax.sharding import PartitionSpec as P

FF = 16384
F32 = jnp.float32
BF16 = jnp.bfloat16
VMEM_LIMIT = 8 * 1024 * 1024

WHOLE = pl.BlockSpec(memory_space=pltpu.VMEM)
SCALARS = pl.BlockSpec(memory_space=pltpu.SMEM)
IN_HBM = pl.BlockSpec(memory_space=pltpu.HBM)


def params(vmem=VMEM_LIMIT):
    return pltpu.CompilerParams(vmem_limit_bytes=vmem)


def cost(flops, bytes_accessed):
    return pl.CostEstimate(flops=int(flops), bytes_accessed=int(bytes_accessed), transcendentals=0)


def resident(array):
    return pltpu.with_memory_space_constraint(array, pltpu.VMEM)


def in_hbm(array):
    return pltpu.with_memory_space_constraint(array, pltpu.HBM)


def swap(array, axis, size, flip):
    return lax.ppermute(array, axis, [(i, i ^ flip) for i in range(size)])


def split_index(number, size):
    if size & (size - 1):
        return number // size, number % size
    return number >> (size.bit_length() - 1), number & (size - 1)


class Slots:
    def __init__(self, index_from, count, index, sem):
        self.copy = pltpu.make_async_copy(index_from, index, sem)
        self.index, self.live = index, count[0, 0]

    @staticmethod
    def scratch(index):
        return [pltpu.SMEM(index.shape, index.dtype), pltpu.SemaphoreType.DMA]

    def place(self, slot, size):
        return split_index(self.index[0, 0, slot], size)


def fill_body(index, count, source, target, index_here, slots_sem, sem):
    slots = Slots(index, count, index_here, slots_sem)
    slots.copy.start()
    outer, inner = target.shape[:2]
    chunk = min(inner, 8)

    @pl.loop(0, outer)
    def _(high):
        target[high] = jnp.zeros(target.shape[1:], target.dtype)

    slots.copy.wait()

    @pl.loop(0, slots.live)
    def _(s):
        high, low = slots.place(s, inner)
        pltpu.make_async_copy(source.at[0, 0, s], target.at[high, low], sem).start()

    many, few = split_index(slots.live, chunk)

    @pl.loop(0, many)
    def _(_):
        blocks = pl.ds(0, chunk)
        pltpu.make_async_copy(source.at[0, 0, blocks], target.at[0, blocks], sem).wait()

    @pl.loop(0, few)
    def _(_):
        pltpu.make_async_copy(source.at[0, 0, 0], target.at[0, 0], sem).wait()


def fill(index, count, slots, outer, inner):
    block = slots.shape[-1]
    return pl.pallas_call(
        fill_body,
        out_shape=pltpu.VMEM((outer, inner, block, block), BF16),
        in_specs=[IN_HBM, SCALARS, IN_HBM],
        out_specs=WHOLE,
        scratch_shapes=[*Slots.scratch(index), pltpu.SemaphoreType.DMA],
        compiler_params=params(),
        cost_estimate=cost(0, slots.size * 2),
        name="fill",
    )(in_hbm(index), count, in_hbm(slots))


def stack(pieces):
    return jnp.concatenate([piece[...] for piece in pieces], axis=0)


def gate_up_body(first, *refs):
    *pieces, gate_w, up_w, own, send = refs
    d_blocks, _, block, _ = gate_w.shape
    x = stack(pieces)

    @pl.loop(0, own.shape[0])
    def _(c):
        weights = jnp.concatenate(
            [
                gate_w[:, first + c].reshape(d_blocks * block, block),
                up_w[:, first + c].reshape(d_blocks * block, block),
            ],
            axis=1,
        )
        result = jnp.dot(x, weights, preferred_element_type=F32)
        own[c] = result
        send[c] = result.astype(BF16)


def gate_up(pieces, gate_w, up_w, half):
    d_blocks, f_blocks, block, _ = gate_w.shape
    tokens = sum(piece.shape[0] for piece in pieces)
    shape = (f_blocks // 2, tokens, 2 * block)
    return pl.pallas_call(
        functools.partial(gate_up_body, half * f_blocks // 2),
        out_shape=(jax.ShapeDtypeStruct(shape, F32), jax.ShapeDtypeStruct(shape, BF16)),
        in_specs=[WHOLE] * (len(pieces) + 2),
        out_specs=(WHOLE,) * 2,
        compiler_params=params(),
        cost_estimate=cost(2 * tokens * gate_w.size, 2 * gate_w.size),
        name="gate_up",
    )(*pieces, resident(gate_w), resident(up_w))


def d_hidden_body(pieces_count, *refs):
    y_pieces, x_pieces = refs[:pieces_count], refs[pieces_count : 2 * pieces_count]
    down_w, own, send, turned = refs[2 * pieces_count :]
    f_blocks, d_blocks, block, _ = down_w.shape
    y = stack(y_pieces)

    @pl.loop(0, f_blocks // 2)
    def _(pair):
        weights = jnp.concatenate(
            [
                down_w[pl.ds(2 * pair, 2), d].reshape(2 * block, block)
                for d in range(d_blocks)
            ],
            axis=1,
        )
        result = lax.dot_general(
            y, weights, (((1,), (1,)), ((), ())), preferred_element_type=F32
        )
        for half in range(2):
            part = result[:, half * block : (half + 1) * block]
            own[2 * pair + half] = part
            send[2 * pair + half] = part.astype(BF16)

    for d in range(d_blocks):
        columns = slice(d * block, (d + 1) * block)
        turned[d] = jnp.concatenate([piece[:, columns] for piece in x_pieces], axis=0).T


def d_hidden(y_pieces, x_pieces, down_w):
    f_blocks, d_blocks, block, _ = down_w.shape
    tokens = sum(piece.shape[0] for piece in y_pieces)
    shape = (f_blocks, tokens, block)
    return pl.pallas_call(
        functools.partial(d_hidden_body, len(y_pieces)),
        out_shape=(
            jax.ShapeDtypeStruct(shape, F32),
            jax.ShapeDtypeStruct(shape, BF16),
            jax.ShapeDtypeStruct((d_blocks, block, tokens), BF16),
        ),
        in_specs=[WHOLE] * (2 * len(y_pieces) + 1),
        out_specs=(WHOLE,) * 3,
        compiler_params=params(),
        cost_estimate=cost(2 * tokens * down_w.size, 2 * down_w.size),
        name="d_hidden",
    )(*y_pieces, *x_pieces, resident(down_w))


def d_tokens_body(group, *refs):
    *coef, dh_own = refs[:3]
    *dh_recv, gate_w, up_w, own, send, d_pair, turned = refs[3:]
    d_blocks, f_blocks, block, _ = gate_w.shape
    half = own.shape[0]
    for c in range(f_blocks):
        dh = dh_own[c]
        for part in dh_recv:
            dh = dh + part[c].astype(F32)
        side, at = divmod(c, f_blocks // 2)
        both = (jnp.concatenate([dh, dh], axis=1) * coef[side][at]).astype(BF16)
        d_pair[c] = both
        for side in range(2):
            turned[pl.ds((2 * c + side) * block, block), :] = both[
                :, side * block : (side + 1) * block
            ].T
    grads = turned[...]

    for at in range(d_blocks // group):
        weights = jnp.concatenate(
            [
                ref[at * group : (at + 1) * group, c].reshape(group * block, block)
                for c in range(f_blocks)
                for ref in (gate_w, up_w)
            ],
            axis=1,
        )
        result = jnp.dot(weights, grads, preferred_element_type=F32).T
        columns = slice(at * group * block, (at + 1) * group * block)
        own[:, columns] = result[:half]
        send[:, columns] = result[half:].astype(BF16)


def d_tokens_part(coef, dh_own, dh_recv, gate_w, up_w):
    d_blocks, f_blocks, block, _ = gate_w.shape
    tokens = dh_own.shape[1]
    width = d_blocks * block
    group = max(n for n in (1, 2, 4) if d_blocks % n == 0)
    return pl.pallas_call(
        functools.partial(d_tokens_body, group),
        out_shape=(
            jax.ShapeDtypeStruct((tokens // 2, width), F32),
            jax.ShapeDtypeStruct((tokens // 2, width), BF16),
            jax.ShapeDtypeStruct((f_blocks, tokens, 2 * block), BF16),
        ),
        in_specs=[WHOLE] * (5 + len(dh_recv)),
        out_specs=(WHOLE,) * 3,
        scratch_shapes=[pltpu.VMEM((f_blocks * 2 * block, tokens), BF16)],
        compiler_params=params(),
        cost_estimate=cost(4 * tokens * gate_w.size, 4 * gate_w.size),
        name="d_tokens",
    )(*coef, dh_own, *dh_recv, resident(gate_w), resident(up_w))


def step_slots(slots):
    return max(n for n in range(1, 17) if slots % n == 0)


def gu_grad_body(first, given, index, count, d_pair, turned, *refs):
    gate_out, up_out, *scalars = refs[given:]
    slots = Slots(index, count, *scalars)
    f_blocks = d_pair.shape[0]
    block = turned.shape[1]
    step = pl.program_id(0)

    @pl.when(step == 0)
    def _():
        slots.copy.start()
        slots.copy.wait()

    for j in range(gate_out.shape[0]):
        slot = (step + first) * gate_out.shape[0] + j
        d, f = slots.place(slot, f_blocks)
        result = jnp.dot(turned[d], d_pair[f], preferred_element_type=F32)
        result = jnp.where(slot < slots.live, result, 0.0).astype(BF16)
        gate_out[j] = result[:, :block]
        up_out[j] = result[:, block:]


def gu_grads(index, count, d_pair, turned, total, begin, end, before):
    block, tokens = turned.shape[1:]
    chunk = step_slots(math.gcd(begin, end))
    first = begin // chunk
    shape = jax.ShapeDtypeStruct((total, block, block), BF16)
    out = pl.BlockSpec((chunk, block, block), lambda i: (i + first, 0, 0))
    size = (end - begin) * block * block
    return pl.pallas_call(
        functools.partial(gu_grad_body, first, len(before)),
        out_shape=(shape,) * 2,
        grid=((end - begin) // chunk,),
        in_specs=[IN_HBM, SCALARS] + [WHOLE] * 2 + [pl.BlockSpec(memory_space=pl.ANY)] * len(before),
        out_specs=(out,) * 2,
        scratch_shapes=Slots.scratch(index),
        input_output_aliases={4 + at: at for at in range(len(before))},
        compiler_params=params(),
        cost_estimate=cost(4 * size * tokens, 4 * size),
        name="gu_grads",
    )(in_hbm(index), count, d_pair, turned, *before)


def activate_body(*refs):
    own, *recv, hidden, coef = refs
    block = hidden.shape[2]
    for f in range(hidden.shape[0]):
        both = own[f]
        for part in recv:
            both = both + part[f].astype(F32)
        gate, up = both[:, :block], both[:, block:]
        sig = jax.nn.sigmoid(gate)
        silu = gate * sig
        hidden[f] = (silu * up).astype(BF16)
        coef[f, :, :block] = up * sig * (1.0 + gate * (1.0 - sig))
        coef[f, :, block:] = silu


def activate(own, recv):
    f_blocks, tokens, pair = own.shape
    return pl.pallas_call(
        activate_body,
        out_shape=(
            jax.ShapeDtypeStruct((f_blocks, tokens, pair // 2), BF16),
            jax.ShapeDtypeStruct(own.shape, F32),
        ),
        in_specs=[WHOLE] * (1 + len(recv)),
        out_specs=(WHOLE,) * 2,
        compiler_params=params(),
        cost_estimate=cost(20 * own.size, 8 * own.size),
        name="activate",
    )(own, *recv)


def down_grad_body(index, count, near, far, *refs):
    *pieces, out, index_here, slots_sem, turned, dense, zero, sem = refs
    slots = Slots(index, count, index_here, slots_sem)
    slots.copy.start()
    f_blocks, d_blocks, block, _ = dense.shape
    total = out.shape[0]
    halves = 2 if d_blocks % 4 == 0 else 1
    width = d_blocks // halves
    for f in range(f_blocks):
        half = (near, far)[f * 2 // f_blocks]
        turned[pl.ds(f * block, block), :] = half[f % (f_blocks // 2)].T
    zero[...] = jnp.zeros(zero.shape, zero.dtype)
    slots.copy.wait()

    @pl.loop(slots.live, total)
    def _(s):
        pltpu.make_async_copy(zero, out.at[s], sem).start()

    for part in range(halves):

        @pl.loop(0, width // 2)
        def _(pair):
            d = part * width + 2 * pair
            columns = pl.ds(pl.multiple_of(d * block, 2 * block), 2 * block)
            y = jnp.concatenate([piece[:, columns] for piece in pieces], axis=0)
            for f in range(0, f_blocks, 2):
                rows = turned[pl.ds(f * block, 2 * block), :]
                result = jnp.dot(rows, y, preferred_element_type=F32).astype(BF16)
                for side in range(2):
                    at = result[:, side * block : (side + 1) * block]
                    dense[pl.ds(f, 2), d + side] = at.reshape(2, block, block)

        @pl.loop(0, slots.live)
        def _(s):
            f, d = slots.place(s, d_blocks)

            @pl.when((d >= part * width) & (d < (part + 1) * width))
            def _():
                pltpu.make_async_copy(dense.at[f, d], out.at[s], sem).start()

    pltpu.make_async_copy(out, out, sem).wait()


def down_grads(index, count, pieces, near, far, slots):
    f_blocks, tokens, block = near.shape
    f_blocks = 2 * f_blocks
    d_blocks = pieces[0].shape[1] // block
    return pl.pallas_call(
        down_grad_body,
        out_shape=jax.ShapeDtypeStruct((slots, block, block), BF16),
        in_specs=[IN_HBM, SCALARS] + [WHOLE] * (2 + len(pieces)),
        out_specs=IN_HBM,
        scratch_shapes=[
            *Slots.scratch(index),
            pltpu.VMEM((f_blocks * block, tokens), BF16),
            pltpu.VMEM((f_blocks, d_blocks, block, block), BF16),
            pltpu.VMEM((block, block), BF16),
            pltpu.SemaphoreType.DMA,
        ],
        compiler_params=params(VMEM_LIMIT + 2 * f_blocks * d_blocks * block * block),
        cost_estimate=cost(2 * slots * block * block * tokens, 2 * slots * block * block),
        name="down_grads",
    )(in_hbm(index), count, near, far, *pieces)


def on_device(
    tokens, cotangent, gate_vals, up_vals, gu_index, gu_count, down_vals, down_index, down_count
):
    block = gate_vals.shape[-1]
    slots = gate_vals.shape[2]
    wide = lax.axis_size("wide")
    narrow = lax.axis_size("narrow")
    chips = wide // 2
    rows = tokens.shape[0]
    d_blocks = tokens.shape[1] // block
    f_blocks = FF // (block * wide)

    def exchange(array):
        return [swap(array, "narrow", narrow, k) for k in range(1, narrow)]

    flips = [chips >> hop for hop in range(1, chips.bit_length())]
    vals = (gate_vals, up_vals)
    x, y, index = tokens, cotangent, gu_index
    weights = []
    for hop, flip in enumerate(flips):
        if hop > 0:
            x = jnp.concatenate([x, x_recv], axis=0)
            y = jnp.concatenate([y, y_recv], axis=0)
            x, weights, index = lax.optimization_barrier((x, weights, index))
        x_recv = swap(x, "wide", wide, 2 * flip)
        if hop < 2:
            weights.append(fill(index, gu_count, vals[hop], d_blocks, f_blocks))
        y, _ = lax.optimization_barrier((y, x_recv))
        y_recv = swap(y, "wide", wide, 2 * flip)
    x_pieces = [x, x_recv, swap(x, "wide", wide, 1), swap(x_recv, "wide", wide, 1)]

    near_own, near_send = gate_up(x_pieces, *weights, 0)
    near_recv = exchange(near_send)
    late, _ = lax.optimization_barrier((x, near_send))
    far_own, far_send = gate_up([late, *x_pieces[1:]], *weights, 1)
    far_recv = exchange(far_send)
    index, _ = lax.optimization_barrier((down_index, far_send))
    down_w = fill(index, down_count, down_vals, f_blocks, d_blocks)
    y, y_recv, down_w = lax.optimization_barrier((y, y_recv, down_w))
    y_pieces = [y, y_recv, swap(y, "wide", wide, 1), swap(y_recv, "wide", wide, 1)]
    near_hidden, near_coef = activate(near_own, near_recv)
    down_w, near_hidden = lax.optimization_barrier((down_w, near_hidden))
    dh_own, dh_send, turned = d_hidden(y_pieces, x_pieces, down_w)
    dh_recv = exchange(dh_send)
    far_hidden, far_coef = activate(far_own, far_recv)
    down_grad = down_grads(down_index, down_count, y_pieces, near_hidden, far_hidden, slots)
    down_grad, far_coef = lax.optimization_barrier((down_grad, far_coef))
    own, send, d_pair = d_tokens_part((near_coef, far_coef), dh_own, dh_recv, *weights)

    own = own + swap(send, "wide", wide, 1).astype(F32)
    cuts = [0, slots // 2, slots * 3 // 4, slots]
    if slots % 4:
        cuts = [0, slots]
    grads = ()
    for hop, flip in enumerate(reversed(flips)):
        kept = own.shape[0] // 2
        far = own[kept:].astype(BF16)
        own = own[:kept]
        if hop + 1 < len(cuts):
            far, d_pair, grads = lax.optimization_barrier((far, d_pair, grads))
            grads = gu_grads(
                gu_index, gu_count, d_pair, turned, slots, cuts[hop], cuts[hop + 1], grads
            )
        own = own + swap(far, "wide", wide, 2 * flip).astype(F32)
    gate_grad, up_grad = grads
    return (
        own.astype(BF16),
        gate_grad[None, None],
        up_grad[None, None],
        down_grad[None, None],
    )


def solution(mesh):
    in_specs = (
        P("wide", "narrow"),
        P("wide", "narrow"),
        P("narrow", "wide", None, None, None),
        P("narrow", "wide", None, None, None),
        P("narrow", "wide", None),
        P("narrow", "wide"),
        P("wide", "narrow", None, None, None),
        P("wide", "narrow", None),
        P("wide", "narrow"),
    )
    out_specs = (
        P("wide", "narrow"),
        P("narrow", "wide", None, None, None),
        P("narrow", "wide", None, None, None),
        P("wide", "narrow", None, None, None),
    )
    return jax.shard_map(
        on_device, mesh=mesh, in_specs=in_specs, out_specs=out_specs, check_vma=False
    )
```

time: 82.1 us -> 78 us (0.950)
  Pallas kernels: 45.1 us -> 41.7 us
  waiting for transfers between devices: 8.9 us -> 11.6 us
  starting transfers between devices: 24 us -> 21.4 us
    ppermute x18 -> x17, waiting for transfers between devices: 8.9 us -> 11.6 us  [swap(): return lax.ppermute(array, axis, [(i, i ^ flip) for i in range(size)])]
    ppermute x18 -> x17, starting transfers between devices: 24 us -> 21.4 us  [swap(): return lax.ppermute(array, axis, [(i, i ^ flip) for i in range(size)])]
    pallas_call x6 -> x8, Pallas kernels: 27.2 us -> 25.3 us  [the longest x3 12.3 us: gu_grads(): pl.pallas_call(functools.partial(gu_grad_body, first, len(before)), out_s...]
    pallas_call x1, Pallas kernels: 6.48 us -> 4.7 us  [d_tokens_part(): pl.pallas_call(functools.partial(d_tokens_body, group), out_shape=(jax.Sh...]
  transfers between devices with their start and end apart: 18 -> 17, of which waited for: 8 -> 5; matrix products, arithmetic and copies ran while one was open for 0% -> 0% of each run, Pallas kernels for 47% -> 47%
where the time goes in v6:
time: 78 us; the launch traced here: 77.9 us
  Pallas kernels  41.7 us (53%)
  starting transfers between devices  21.4 us (27%)
  waiting for transfers between devices  11.6 us (15%)
  between operations  2.23 us (3%)
  other arithmetic  0.86 us (1%)
    ppermute x17, starting transfers between devices, swap(): return lax.ppermute(array, axis, [(i, i ^ flip) for i in range(size)])  21.4 us
    pallas_call x3, Pallas kernels, gu_grads(): pl.pallas_call(functools.partial(gu_grad_body, first, len(before)), out_s...  12.3 us
    ppermute x17, waiting for transfers between devices, swap(): return lax.ppermute(array, axis, [(i, i ^ flip) for i in range(size)])  11.6 us
    pallas_call x3, Pallas kernels, fill(): pl.pallas_call(fill_body, out_shape=pltpu.VMEM((outer, inner, block, bloc...  9.36 us
    pallas_call x1, Pallas kernels, down_grads(): pl.pallas_call(down_grad_body, out_shape=jax.ShapeDtypeStruct((slots, blo...  7.78 us
    pallas_call x1, Pallas kernels, d_tokens_part(): pl.pallas_call(functools.partial(d_tokens_body, group), out_shape=(jax.Sh...  4.7 us
    pallas_call x2, Pallas kernels, gate_up(): pl.pallas_call(functools.partial(gate_up_body, half * f_blocks // 2), out...  3.73 us
    pallas_call x1, Pallas kernels, d_hidden(): pl.pallas_call(functools.partial(d_hidden_body, len(y_pieces)), out_shape...  3.59 us
  transfers between devices with their start and end apart: 17, of which 5 were waited for; matrix products, arithmetic and copies ran while one was open for 0% of the time, Pallas kernels for 47%

profile of v6, /device:TPU:0, one launch (start us, length us, event | category | flops | bytes accessed | tf_op | source)
XLA Modules:
  0.0 77.9 jit_solution(1414767874865454273)
XLA Ops:
  0.6 4.1 %collective-permute-start = (bf16[8,4096]{1,0:T(8,128)(2,1)}, bf16[8,4096]{1,0:T(8,128)(2,1)S(1)}, u32[]{:S(2)}, u32[]{:S(2)}) collective-permute-start(bf16[8,4096]{1,0:T(8,128)(2,1)} %param.9), channel_id=1, source_target_pairs={{0,16},{2,18},{4,20},{6,22},{8,24},{10,26},{12,28},{14,30},{16,0},... | collective-permute-start | bytes 196616 | tf_op jit(solution)/shard_map/ppermute | solution.py:38
  5.4 3.3 %fill.3.refs_4_ = bf16[32,8,128,128]{3,2,1,0:T(8,128)(2,1)S(1)} custom-call(s32[1,1,192]{2,1,0:T(1,128)} %index.11, s32[1,1]{1,0:T(1,128)S(6)} %copy.21.count, bf16[1,1,192,128,128]{4,3,2,1,0:T(8,128)(2,1)} %source.3), custom_call_target="tpu_custom_call" | custom-call | bytes 6291456 | tf_op jit(solution)/shard_map/fill/pallas_call | solution.py:91
  8.8 1.2 %collective-permute-start.1 = (bf16[16,4096]{1,0:T(8,128)(2,1)S(1)}, bf16[16,4096]{1,0:T(8,128)(2,1)S(1)}, u32[]{:S(2)}, u32[]{:S(2)}) collective-permute-start(bf16[16,4096]{1,0:T(8,128)(2,1)S(1)} %pad_maximum_fusion.2), channel_id=1, source_target_pairs={{0,8},{2,10},{4,12},{6,14},{8,0},{10,2},{12,4},{14,6},{16,24},{18,... | collective-permute-start | bytes 393224 | tf_op jit(solution)/shard_map/ppermute | solution.py:38
  10.0 2.7 %collective-permute-start.6 = (bf16[8,4096]{1,0:T(8,128)(2,1)S(1)}, bf16[8,4096]{1,0:T(8,128)(2,1)S(1)}, u32[]{:S(2)}, u32[]{:S(2)}) collective-permute-start(bf16[8,4096]{1,0:T(8,128)(2,1)S(1)} %copy-done.1), channel_id=1, source_target_pairs={{0,16},{2,18},{4,20},{6,22},{8,24},{10,26},{12,28},{14,30},{16,0},... | collective-permute-start | bytes 196616 | tf_op jit(solution)/shard_map/ppermute | solution.py:38
  12.6 3.3 %fill.4.refs_5_ = bf16[32,8,128,128]{3,2,1,0:T(8,128)(2,1)S(1)} custom-call(s32[1,1,192]{2,1,0:T(1,128)} %index.11, s32[1,1]{1,0:T(1,128)S(6)} %copy.21.count, bf16[1,1,192,128,128]{4,3,2,1,0:T(8,128)(2,1)} %source.4), custom_call_target="tpu_custom_call" | custom-call | bytes 6291456 | tf_op jit(solution)/shard_map/fill/pallas_call | solution.py:91
  16.0 1.5 %collective-permute-start.2 = (bf16[32,4096]{1,0:T(8,128)(2,1)S(1)}, bf16[32,4096]{1,0:T(8,128)(2,1)S(1)}, u32[]{:S(2)}, u32[]{:S(2)}) collective-permute-start(bf16[32,4096]{1,0:T(8,128)(2,1)S(1)} %pad_maximum_fusion.refs_0_.refs_4_), channel_id=1, source_target_pairs={{0,4},{2,6},{4,0},{6,2},{8,12},{10,14},{12,8},{14,10},{16,20},{18,... | collective-permute-start | bytes 786440 | tf_op jit(solution)/shard_map/ppermute | solution.py:38
  17.7 5.4 %collective-permute-done.2.refs_1_.refs_5_ = bf16[32,4096]{1,0:T(8,128)(2,1)S(1)} collective-permute-done((bf16[32,4096]{1,0:T(8,128)(2,1)S(1)}, bf16[32,4096]{1,0:T(8,128)(2,1)S(1)}, u32[]{:S(2)}, u32[]{:S(2)}) %collective-permute-start.2) | collective-permute-done | bytes 262176 | tf_op jit(solution)/shard_map/ppermute | solution.py:38
  23.1 1.8 %collective-permute-start.8 = (bf16[32,4096]{1,0:T(8,128)(2,1)S(1)}, bf16[32,4096]{1,0:T(8,128)(2,1)S(1)}, u32[]{:S(2)}, u32[]{:S(2)}) collective-permute-start(bf16[32,4096]{1,0:T(8,128)(2,1)S(1)} %pad_maximum_fusion.1.refs_0_), channel_id=1, source_target_pairs={{0,4},{2,6},{4,0},{6,2},{8,12},{10,14},{12,8},{14,10},{16,20},{18,... | collective-permute-start | bytes 786440 | tf_op jit(solution)/shard_map/ppermute | solution.py:38
  25.6 1.9 %gate_up.2 = (f32[4,128,256]{2,1,0:T(8,128)S(1)}, bf16[4,128,256]{2,1,0:T(8,128)(2,1)S(1)}) custom-call(bf16[32,4096]{1,0:T(8,128)(2,1)S(1)} %pad_maximum_fusion.refs_0_.refs_4_, bf16[32,4096]{1,0:T(8,128)(2,1)S(1)} %collective-permute-done.2.refs_1_.refs_5_, bf16[32,4096]{1,0:T(8,128)(2,1)S(1)} %collective-permute-done.3.refs_2_.refs_6_, ...), custom_call_target="tpu_custom_call" | custom-call | flops 1073741824 | bytes 8388608 | tf_op jit(solution)/shard_map/gate_up/pallas_call | solution.py:130
  27.5 0.6 collective-permute-start.5
  28.0 1.9 %gate_up.3 = (f32[4,128,256]{2,1,0:T(8,128)S(1)}, bf16[4,128,256]{2,1,0:T(8,128)(2,1)S(1)}) custom-call(bf16[32,4096]{1,0:T(8,128)(2,1)S(1)} %pad_maximum_fusion.refs_0_.refs_4_, bf16[32,4096]{1,0:T(8,128)(2,1)S(1)} %collective-permute-done.2.refs_1_.refs_5_, bf16[32,4096]{1,0:T(8,128)(2,1)S(1)} %collective-permute-done.3.refs_2_.refs_6_, ...), custom_call_target="tpu_custom_call" | custom-call | flops 1073741824 | bytes 8388608 | tf_op jit(solution)/shard_map/gate_up/pallas_call | solution.py:130
  29.9 2.7 %fill.5.refs_8_ = bf16[8,32,128,128]{3,2,1,0:T(8,128)(2,1)S(1)} custom-call(s32[1,1,192]{2,1,0:T(1,128)} %index.8, s32[1,1]{1,0:T(1,128)S(6)} %copy.22.count, bf16[1,1,192,128,128]{4,3,2,1,0:T(8,128)(2,1)} %source.5), custom_call_target="tpu_custom_call" | custom-call | bytes 6291456 | tf_op jit(solution)/shard_map/fill/pallas_call | solution.py:91
  32.6 0.2 collective-permute-start.10
  32.9 0.3 collective-permute-start.11
  33.2 1.1 %collective-permute-start.9 = (bf16[4,128,256]{2,1,0:T(8,128)(2,1)S(1)}, bf16[4,128,256]{2,1,0:T(8,128)(2,1)S(1)}, u32[]{:S(2)}, u32[]{:S(2)}) collective-permute-start(bf16[4,128,256]{2,1,0:T(8,128)(2,1)S(1)} %get-tuple-element.65), channel_id=1, source_target_pairs={{0,1},{1,0},{2,3},{3,2},{4,5},{5,4},{6,7},{7,6},{8,9},{9,8},{10,11... | collective-permute-start | bytes 786440 | tf_op jit(solution)/shard_map/ppermute | solution.py:38
  34.3 1.7 %collective-permute-done.5.refs_1_ = bf16[4,128,256]{2,1,0:T(8,128)(2,1)S(1)} collective-permute-done((bf16[4,128,256]{2,1,0:T(8,128)(2,1)S(1)}, bf16[4,128,256]{2,1,0:T(8,128)(2,1)S(1)}, u32[]{:S(2)}, u32[]{:S(2)}) %collective-permute-start.5) | collective-permute-done | bytes 262176 | tf_op jit(solution)/shard_map/ppermute | solution.py:38
  36.0 0.1 activate.2
  36.1 3.6 %d_hidden.1 = (f32[8,128,128]{2,1,0:T(8,128)S(1)}, bf16[8,128,128]{2,1,0:T(8,128)(2,1)S(1)}, bf16[32,128,128]{2,1,0:T(8,128)(2,1)S(1)}) custom-call(bf16[32,4096]{1,0:T(8,128)(2,1)S(1)} %pad_maximum_fusion.1.refs_0_, bf16[32,4096]{1,0:T(8,128)(2,1)S(1)} %collective-permute-done.8.refs_1_, bf16[32,4096]{1,0:T(8,128)(2,1)S(1)} %collective-permute-done.10.refs_2_, ...), custom_call_target="tpu_custom_call" | custom-call | flops 1073741824 | bytes 8388608 | tf_op jit(solution)/shard_map/d_hidden/pallas_call | solution.py:173
  39.7 0.6 collective-permute-start.12
  40.3 1.3 %collective-permute-done.9.refs_1_ = bf16[4,128,256]{2,1,0:T(8,128)(2,1)S(1)} collective-permute-done((bf16[4,128,256]{2,1,0:T(8,128)(2,1)S(1)}, bf16[4,128,256]{2,1,0:T(8,128)(2,1)S(1)}, u32[]{:S(2)}, u32[]{:S(2)}) %collective-permute-start.9) | collective-permute-done | bytes 262176 | tf_op jit(solution)/shard_map/ppermute | solution.py:38
  41.6 0.1 activate.3
  41.7 7.8 %down_grads.1 = bf16[192,128,128]{2,1,0:T(8,128)(2,1)} custom-call(s32[1,1,192]{2,1,0:T(1,128)} %index.8, s32[1,1]{1,0:T(1,128)S(6)} %copy.22.count, bf16[4,128,128]{2,1,0:T(8,128)(2,1)S(1)} %get-tuple-element.69.near, bf16[4,128,128]{2,1,0:T(8,128)(2,1)S(1)} %get-tuple-element.71.far, bf16[32,4096]{1,0:T(8,128)(2,1)S(1)} %pad_maximum_fusion.1.refs_0_, ...), custom_call_target="tpu_custom_call" | custom-call | flops 805306368 | bytes 6291456 | tf_op jit(solution)/shard_map/down_grads/pallas_call | solution.py:366
  49.5 4.7 %d_tokens.1 = (f32[64,4096]{1,0:T(8,128)S(1)}, bf16[64,4096]{1,0:T(8,128)(2,1)S(1)}, bf16[8,128,256]{2,1,0:T(8,128)(2,1)S(1)}) custom-call(f32[4,128,256]{2,1,0:T(8,128)S(1)} %get-tuple-element.60.refs_0_, f32[4,128,256]{2,1,0:T(8,128)S(1)} %get-tuple-element.75.refs_1_, f32[8,128,128]{2,1,0:T(8,128)S(1)} %get-tuple-element.77.refs_2_, ...), custom_call_target="tpu_custom_call" | custom-call | flops 2147483648 | bytes 16777216 | tf_op jit(solution)/shard_map/d_tokens/pallas_call | solution.py:226
  54.3 1.9 %collective-permute-done.13 = bf16[64,4096]{1,0:T(8,128)(2,1)S(1)} collective-permute-done((bf16[64,4096]{1,0:T(8,128)(2,1)S(1)}, bf16[64,4096]{1,0:T(8,128)(2,1)S(1)}, u32[]{:S(2)}, u32[]{:S(2)}) %collective-permute-start.13) | collective-permute-done | bytes 524320 | tf_op jit(solution)/shard_map/ppermute | solution.py:38
  56.3 1.8 %collective-permute-start.14 = (bf16[32,4096]{1,0:T(8,128)(2,1)S(1)}, bf16[32,4096]{1,0:T(8,128)(2,1)S(1)}, u32[]{:S(2)}, u32[]{:S(2)}) collective-permute-start(bf16[32,4096]{1,0:T(8,128)(2,1)S(1)} %slice.41), channel_id=1, source_target_pairs={{0,4},{2,6},{4,0},{6,2},{8,12},{10,14},{12,8},{14,10},{16,20},{18,... | collective-permute-start | bytes 786440 | tf_op jit(solution)/shard_map/ppermute | solution.py:38
  58.1 5.3 %gu_grads.3 = (bf16[192,128,128]{2,1,0:T(8,128)(2,1)}, bf16[192,128,128]{2,1,0:T(8,128)(2,1)}) custom-call(s32[1,1,192]{2,1,0:T(1,128)} %index.11, s32[1,1]{1,0:T(1,128)S(6)} %copy.21.count, bf16[8,128,256]{2,1,0:T(8,128)(2,1)S(1)} %get-tuple-element.94.d_pair, bf16[32,128,128]{2,1,0:T(8,128)(2,1)S(1)} %get-tuple-element.84.turned), custom_call_target="tpu_custom_call" | custom-call | flops 805306368 | bytes 6291456 | tf_op jit(solution)/shard_map/gu_grads/pallas_call | solution.py:274
  63.4 1.3 %collective-permute-done.14 = bf16[32,4096]{1,0:T(8,128)(2,1)S(1)} collective-permute-done((bf16[32,4096]{1,0:T(8,128)(2,1)S(1)}, bf16[32,4096]{1,0:T(8,128)(2,1)S(1)}, u32[]{:S(2)}, u32[]{:S(2)}) %collective-permute-start.14) | collective-permute-done | bytes 262176 | tf_op jit(solution)/shard_map/ppermute | solution.py:38
  64.8 2.2 %collective-permute-start.15 = (bf16[16,4096]{1,0:T(8,128)(2,1)S(1)}, bf16[16,4096]{1,0:T(8,128)(2,1)S(1)}, u32[]{:S(2)}, u32[]{:S(2)}) collective-permute-start(bf16[16,4096]{1,0:T(8,128)(2,1)S(1)} %slice.42), channel_id=1, source_target_pairs={{0,8},{2,10},{4,12},{6,14},{8,0},{10,2},{12,4},{14,6},{16,24},{18,... | collective-permute-start | bytes 393224 | tf_op jit(solution)/shard_map/ppermute | solution.py:38
  67.1 3.5 %gu_grads.4 = (bf16[192,128,128]{2,1,0:T(8,128)(2,1)}, bf16[192,128,128]{2,1,0:T(8,128)(2,1)}) custom-call(s32[1,1,192]{2,1,0:T(1,128)} %index.11, s32[1,1]{1,0:T(1,128)S(6)} %copy.21.count, bf16[8,128,256]{2,1,0:T(8,128)(2,1)S(1)} %get-tuple-element.94.d_pair, ...), custom_call_target="tpu_custom_call", output_to_operand_aliasing={{0}: (4, {}), {1}: (5, {})} | custom-call | flops 402653184 | bytes 3145728 | tf_op jit(solution)/shard_map/gu_grads/pallas_call | solution.py:274
  70.6 3.1 %collective-permute-start.16 = (bf16[8,4096]{1,0:T(8,128)(2,1)S(1)}, bf16[8,4096]{1,0:T(8,128)(2,1)S(1)}, u32[]{:S(2)}, u32[]{:S(2)}) collective-permute-start(bf16[8,4096]{1,0:T(8,128)(2,1)S(1)} %slice.43), channel_id=1, source_target_pairs={{0,16},{2,18},{4,20},{6,22},{8,24},{10,26},{12,28},{14,30},{16,0},... | collective-permute-start | bytes 196616 | tf_op jit(solution)/shard_map/ppermute | solution.py:38
  73.7 3.5 %gu_grads.5 = (bf16[192,128,128]{2,1,0:T(8,128)(2,1)}, bf16[192,128,128]{2,1,0:T(8,128)(2,1)}) custom-call(s32[1,1,192]{2,1,0:T(1,128)} %index.11, s32[1,1]{1,0:T(1,128)S(6)} %copy.21.count, bf16[8,128,256]{2,1,0:T(8,128)(2,1)S(1)} %get-tuple-element.94.d_pair, ...), custom_call_target="tpu_custom_call", output_to_operand_aliasing={{0}: (4, {}), {1}: (5, {})} | custom-call | flops 402653184 | bytes 3145728 | tf_op jit(solution)/shard_map/gu_grads/pallas_call | solution.py:274
  77.2 0.6 fusion
  (30 shorter events, 0.5 us)
Async XLA Ops:
  0.6 8.1 %collective-permute-start = (bf16[8,4096]{1,0:T(8,128)(2,1)}, bf16[8,4096]{1,0:T(8,128)(2,1)S(1)}, u32[]{:S(2)}, u32[]{:S(2)}) collective-permute-start(bf16[8,4096]{1,0:T(8,128)(2,1)} %param.9), channel_id=1, source_target_pairs={{0,16},{2,18},{4,20},{6,22},{8,24},{10,26},{12,28},{14,30},{16,0},... | collective-permute-start | bytes 196616 | tf_op jit(solution)/shard_map/ppermute | solution.py:38
  5.4 3.4 %copy-start = (bf16[8,4096]{1,0:T(8,128)(2,1)S(1)}, bf16[8,4096]{1,0:T(8,128)(2,1)}, u32[]{:S(2)}) copy-start(bf16[8,4096]{1,0:T(8,128)(2,1)} %param.9) | copy-start | bytes 196612
  5.4 4.6 %copy-start.1 = (bf16[8,4096]{1,0:T(8,128)(2,1)S(1)}, bf16[8,4096]{1,0:T(8,128)(2,1)}, u32[]{:S(2)}) copy-start(bf16[8,4096]{1,0:T(8,128)(2,1)} %param.10) | copy-start | bytes 196612
  8.8 7.2 %collective-permute-start.1 = (bf16[16,4096]{1,0:T(8,128)(2,1)S(1)}, bf16[16,4096]{1,0:T(8,128)(2,1)S(1)}, u32[]{:S(2)}, u32[]{:S(2)}) collective-permute-start(bf16[16,4096]{1,0:T(8,128)(2,1)S(1)} %pad_maximum_fusion.2), channel_id=1, source_target_pairs={{0,8},{2,10},{4,12},{6,14},{8,0},{10,2},{12,4},{14,6},{16,24},{18,... | collective-permute-start | bytes 393224 | tf_op jit(solution)/shard_map/ppermute | solution.py:38
  10.0 7.6 %collective-permute-start.6 = (bf16[8,4096]{1,0:T(8,128)(2,1)S(1)}, bf16[8,4096]{1,0:T(8,128)(2,1)S(1)}, u32[]{:S(2)}, u32[]{:S(2)}) collective-permute-start(bf16[8,4096]{1,0:T(8,128)(2,1)S(1)} %copy-done.1), channel_id=1, source_target_pairs={{0,16},{2,18},{4,20},{6,22},{8,24},{10,26},{12,28},{14,30},{16,0},... | collective-permute-start | bytes 196616 | tf_op jit(solution)/shard_map/ppermute | solution.py:38
  16.0 7.1 %collective-permute-start.2 = (bf16[32,4096]{1,0:T(8,128)(2,1)S(1)}, bf16[32,4096]{1,0:T(8,128)(2,1)S(1)}, u32[]{:S(2)}, u32[]{:S(2)}) collective-permute-start(bf16[32,4096]{1,0:T(8,128)(2,1)S(1)} %pad_maximum_fusion.refs_0_.refs_4_), channel_id=1, source_target_pairs={{0,4},{2,6},{4,0},{6,2},{8,12},{10,14},{12,8},{14,10},{16,20},{18,... | collective-permute-start | bytes 786440 | tf_op jit(solution)/shard_map/ppermute | solution.py:38
  17.6 5.5 %collective-permute-start.7 = (bf16[16,4096]{1,0:T(8,128)(2,1)S(1)}, bf16[16,4096]{1,0:T(8,128)(2,1)S(1)}, u32[]{:S(2)}, u32[]{:S(2)}) collective-permute-start(bf16[16,4096]{1,0:T(8,128)(2,1)S(1)} %pad_maximum_fusion.3), channel_id=1, source_target_pairs={{0,8},{2,10},{4,12},{6,14},{8,0},{10,2},{12,4},{14,6},{16,24},{18,... | collective-permute-start | bytes 393224 | tf_op jit(solution)/shard_map/ppermute | solution.py:38
  17.6 7.9 %collective-permute-start.3 = (bf16[32,4096]{1,0:T(8,128)(2,1)S(1)}, bf16[32,4096]{1,0:T(8,128)(2,1)S(1)}, u32[]{:S(2)}, u32[]{:S(2)}) collective-permute-start(bf16[32,4096]{1,0:T(8,128)(2,1)S(1)} %pad_maximum_fusion.refs_0_.refs_4_), channel_id=1, source_target_pairs={{0,2},{2,0},{4,6},{6,4},{8,10},{10,8},{12,14},{14,12},{16,18},{18,... | collective-permute-start | bytes 786440 | tf_op jit(solution)/shard_map/ppermute | solution.py:38
  23.1 2.5 %collective-permute-start.4 = (bf16[32,4096]{1,0:T(8,128)(2,1)S(1)}, bf16[32,4096]{1,0:T(8,128)(2,1)S(1)}, u32[]{:S(2)}, u32[]{:S(2)}) collective-permute-start(bf16[32,4096]{1,0:T(8,128)(2,1)S(1)} %collective-permute-done.2.refs_1_.refs_5_), channel_id=1, source_target_pairs={{0,2},{2,0},{4,6},{6,4},{8,10},{10,8},{12,14},{14,12},{16,18},{18,... | collective-permute-start | bytes 786440 | tf_op jit(solution)/shard_map/ppermute | solution.py:38
  23.1 9.5 %collective-permute-start.8 = (bf16[32,4096]{1,0:T(8,128)(2,1)S(1)}, bf16[32,4096]{1,0:T(8,128)(2,1)S(1)}, u32[]{:S(2)}, u32[]{:S(2)}) collective-permute-start(bf16[32,4096]{1,0:T(8,128)(2,1)S(1)} %pad_maximum_fusion.1.refs_0_), channel_id=1, source_target_pairs={{0,4},{2,6},{4,0},{6,2},{8,12},{10,14},{12,8},{14,10},{16,20},{18,... | collective-permute-start | bytes 786440 | tf_op jit(solution)/shard_map/ppermute | solution.py:38
  27.5 8.5 %collective-permute-start.5 = (bf16[4,128,256]{2,1,0:T(8,128)(2,1)S(1)}, bf16[4,128,256]{2,1,0:T(8,128)(2,1)S(1)}, u32[]{:S(2)}, u32[]{:S(2)}) collective-permute-start(bf16[4,128,256]{2,1,0:T(8,128)(2,1)S(1)} %get-tuple-element.59), channel_id=1, source_target_pairs={{0,1},{1,0},{2,3},{3,2},{4,5},{5,4},{6,7},{7,6},{8,9},{9,8},{10,11... | collective-permute-start | bytes 786440 | tf_op jit(solution)/shard_map/ppermute | solution.py:38
  32.6 3.5 %collective-permute-start.10 = (bf16[32,4096]{1,0:T(8,128)(2,1)S(1)}, bf16[32,4096]{1,0:T(8,128)(2,1)S(1)}, u32[]{:S(2)}, u32[]{:S(2)}) collective-permute-start(bf16[32,4096]{1,0:T(8,128)(2,1)S(1)} %pad_maximum_fusion.1.refs_0_), channel_id=1, source_target_pairs={{0,2},{2,0},{4,6},{6,4},{8,10},{10,8},{12,14},{14,12},{16,18},{18,... | collective-permute-start | bytes 786440 | tf_op jit(solution)/shard_map/ppermute | solution.py:38
  32.9 3.2 %collective-permute-start.11 = (bf16[32,4096]{1,0:T(8,128)(2,1)S(1)}, bf16[32,4096]{1,0:T(8,128)(2,1)S(1)}, u32[]{:S(2)}, u32[]{:S(2)}) collective-permute-start(bf16[32,4096]{1,0:T(8,128)(2,1)S(1)} %collective-permute-done.8.refs_1_), channel_id=1, source_target_pairs={{0,2},{2,0},{4,6},{6,4},{8,10},{10,8},{12,14},{14,12},{16,18},{18,... | collective-permute-start | bytes 786440 | tf_op jit(solution)/shard_map/ppermute | solution.py:38
  33.2 8.4 %collective-permute-start.9 = (bf16[4,128,256]{2,1,0:T(8,128)(2,1)S(1)}, bf16[4,128,256]{2,1,0:T(8,128)(2,1)S(1)}, u32[]{:S(2)}, u32[]{:S(2)}) collective-permute-start(bf16[4,128,256]{2,1,0:T(8,128)(2,1)S(1)} %get-tuple-element.65), channel_id=1, source_target_pairs={{0,1},{1,0},{2,3},{3,2},{4,5},{5,4},{6,7},{7,6},{8,9},{9,8},{10,11... | collective-permute-start | bytes 786440 | tf_op jit(solution)/shard_map/ppermute | solution.py:38
  39.7 9.8 %collective-permute-start.12 = (bf16[8,128,128]{2,1,0:T(8,128)(2,1)S(1)}, bf16[8,128,128]{2,1,0:T(8,128)(2,1)S(1)}, u32[]{:S(2)}, u32[]{:S(2)}) collective-permute-start(bf16[8,128,128]{2,1,0:T(8,128)(2,1)S(1)} %get-tuple-element.78), channel_id=1, source_target_pairs={{0,1},{1,0},{2,3},{3,2},{4,5},{5,4},{6,7},{7,6},{8,9},{9,8},{10,11... | collective-permute-start | bytes 786440 | tf_op jit(solution)/shard_map/ppermute | solution.py:38
  54.2 2.0 %collective-permute-start.13 = (bf16[64,4096]{1,0:T(8,128)(2,1)S(1)}, bf16[64,4096]{1,0:T(8,128)(2,1)S(1)}, u32[]{:S(2)}, u32[]{:S(2)}) collective-permute-start(bf16[64,4096]{1,0:T(8,128)(2,1)S(1)} %get-tuple-element.80), channel_id=1, source_target_pairs={{0,2},{2,0},{4,6},{6,4},{8,10},{10,8},{12,14},{14,12},{16,18},{18,... | collective-permute-start | bytes 1572872 | tf_op jit(solution)/shard_map/ppermute | solution.py:38
  56.3 8.4 %collective-permute-start.14 = (bf16[32,4096]{1,0:T(8,128)(2,1)S(1)}, bf16[32,4096]{1,0:T(8,128)(2,1)S(1)}, u32[]{:S(2)}, u32[]{:S(2)}) collective-permute-start(bf16[32,4096]{1,0:T(8,128)(2,1)S(1)} %slice.41), channel_id=1, source_target_pairs={{0,4},{2,6},{4,0},{6,2},{8,12},{10,14},{12,8},{14,10},{16,20},{18,... | collective-permute-start | bytes 786440 | tf_op jit(solution)/shard_map/ppermute | solution.py:38
  64.8 5.7 %collective-permute-start.15 = (bf16[16,4096]{1,0:T(8,128)(2,1)S(1)}, bf16[16,4096]{1,0:T(8,128)(2,1)S(1)}, u32[]{:S(2)}, u32[]{:S(2)}) collective-permute-start(bf16[16,4096]{1,0:T(8,128)(2,1)S(1)} %slice.42), channel_id=1, source_target_pairs={{0,8},{2,10},{4,12},{6,14},{8,0},{10,2},{12,4},{14,6},{16,24},{18,... | collective-permute-start | bytes 393224 | tf_op jit(solution)/shard_map/ppermute | solution.py:38
  70.6 6.6 %collective-permute-start.16 = (bf16[8,4096]{1,0:T(8,128)(2,1)S(1)}, bf16[8,4096]{1,0:T(8,128)(2,1)S(1)}, u32[]{:S(2)}, u32[]{:S(2)}) collective-permute-start(bf16[8,4096]{1,0:T(8,128)(2,1)S(1)} %slice.43), channel_id=1, source_target_pairs={{0,16},{2,18},{4,20},{6,22},{8,24},{10,26},{12,28},{14,30},{16,0},... | collective-permute-start | bytes 196616 | tf_op jit(solution)/shard_map/ppermute | solution.py:38

commit v7 on v6

--- a/solution.py
+++ b/solution.py
@@ -317,44 +317,34 @@
 
 
 def down_grad_body(index, count, near, far, *refs):
-    *pieces, out, index_here, slots_sem, turned, dense, zero, sem = refs
+    *pieces, out, index_here, slots_sem, turned, dense, sem = refs
     slots = Slots(index, count, index_here, slots_sem)
     slots.copy.start()
-    f_blocks, d_blocks, block, _ = dense.shape
-    total = out.shape[0]
-    halves = 2 if d_blocks % 4 == 0 else 1
-    width = d_blocks // halves
+    block = dense.shape[1]
+    f_blocks = turned.shape[0] // block
+    d_blocks = (dense.shape[0] - 1) // f_blocks
+    zeros = f_blocks * d_blocks
+    dense[zeros] = jnp.zeros(dense.shape[1:], dense.dtype)
     for f in range(f_blocks):
         half = (near, far)[f * 2 // f_blocks]
-        turned[pl.ds(f * block, block), :] = half[f % (f_blocks // 2)].T
-    zero[...] = jnp.zeros(zero.shape, zero.dtype)
+        turned[f * block : (f + 1) * block, :] = half[f % (f_blocks // 2)].T
+    for d in range(0, d_blocks, 2):
+        y = jnp.concatenate([piece[:, d * block : (d + 2) * block] for piece in pieces], axis=0)
+        for f in range(0, f_blocks, 2):
+            rows = turned[f * block : (f + 2) * block, :]
+            result = jnp.dot(rows, y, preferred_element_type=F32).astype(BF16)
+            for row in range(2):
+                for side in range(2):
+                    dense[(f + row) * d_blocks + d + side] = result[
+                        row * block : (row + 1) * block, side * block : (side + 1) * block
+                    ]
     slots.copy.wait()
-
-    @pl.loop(slots.live, total)
+    total = out.shape[0]
+
+    @pl.loop(0, total, unroll=max(n for n in (1, 2, 4, 8) if total % n == 0))
     def _(s):
-        pltpu.make_async_copy(zero, out.at[s], sem).start()
-
-    for part in range(halves):
-
-        @pl.loop(0, width // 2)
-        def _(pair):
-            d = part * width + 2 * pair
-            columns = pl.ds(pl.multiple_of(d * block, 2 * block), 2 * block)
-            y = jnp.concatenate([piece[:, columns] for piece in pieces], axis=0)
-            for f in range(0, f_blocks, 2):
-                rows = turned[pl.ds(f * block, 2 * block), :]
-                result = jnp.dot(rows, y, preferred_element_type=F32).astype(BF16)
-                for side in range(2):
-                    at = result[:, side * block : (side + 1) * block]
-                    dense[pl.ds(f, 2), d + side] = at.reshape(2, block, block)
-
-        @pl.loop(0, slots.live)
-        def _(s):
-            f, d = slots.place(s, d_blocks)
-
-            @pl.when((d >= part * width) & (d < (part + 1) * width))
-            def _():
-                pltpu.make_async_copy(dense.at[f, d], out.at[s], sem).start()
+        place = jnp.where(s < slots.live, slots.index[0, 0, s], zeros)
+        pltpu.make_async_copy(dense.at[place], out.at[s], sem).start()
 
     pltpu.make_async_copy(out, out, sem).wait()
 
@@ -363,6 +353,7 @@
     f_blocks, tokens, block = near.shape
     f_blocks = 2 * f_blocks
     d_blocks = pieces[0].shape[1] // block
+    blocks = f_blocks * d_blocks + 1
     return pl.pallas_call(
         down_grad_body,
         out_shape=jax.ShapeDtypeStruct((slots, block, block), BF16),
@@ -371,11 +362,10 @@
         scratch_shapes=[
             *Slots.scratch(index),
             pltpu.VMEM((f_blocks * block, tokens), BF16),
-            pltpu.VMEM((f_blocks, d_blocks, block, block), BF16),
-            pltpu.VMEM((block, block), BF16),
+            pltpu.VMEM((blocks, block, block), BF16),
             pltpu.SemaphoreType.DMA,
         ],
-        compiler_params=params(VMEM_LIMIT + 2 * f_blocks * d_blocks * block * block),
+        compiler_params=params(VMEM_LIMIT + 2 * blocks * block * block),
         cost_estimate=cost(2 * slots * block * block * tokens, 2 * slots * block * block),
         name="down_grads",
     )(in_hbm(index), count, near, far, *pieces)
@@ -398,28 +388,30 @@
 
     flips = [chips >> hop for hop in range(1, chips.bit_length())]
     vals = (gate_vals, up_vals)
-    x, y, index = tokens, cotangent, gu_index
+    x, index = tokens, gu_index
     weights = []
     for hop, flip in enumerate(flips):
         if hop > 0:
             x = jnp.concatenate([x, x_recv], axis=0)
-            y = jnp.concatenate([y, y_recv], axis=0)
             x, weights, index = lax.optimization_barrier((x, weights, index))
         x_recv = swap(x, "wide", wide, 2 * flip)
         if hop < 2:
             weights.append(fill(index, gu_count, vals[hop], d_blocks, f_blocks))
-        y, _ = lax.optimization_barrier((y, x_recv))
-        y_recv = swap(y, "wide", wide, 2 * flip)
+    y, index, _ = lax.optimization_barrier((cotangent, down_index, x))
+    down_w = fill(index, down_count, down_vals, f_blocks, d_blocks)
+    for flip in flips[:-1]:
+        y = jnp.concatenate([y, swap(y, "wide", wide, 2 * flip)], axis=0)
+        y, down_w = lax.optimization_barrier((y, down_w))
     x_pieces = [x, x_recv, swap(x, "wide", wide, 1), swap(x_recv, "wide", wide, 1)]
+    y, _ = lax.optimization_barrier((y, x_recv))
+    y_recv = swap(y, "wide", wide, 2 * flips[-1])
 
     near_own, near_send = gate_up(x_pieces, *weights, 0)
     near_recv = exchange(near_send)
     late, _ = lax.optimization_barrier((x, near_send))
     far_own, far_send = gate_up([late, *x_pieces[1:]], *weights, 1)
     far_recv = exchange(far_send)
-    index, _ = lax.optimization_barrier((down_index, far_send))
-    down_w = fill(index, down_count, down_vals, f_blocks, d_blocks)
-    y, y_recv, down_w = lax.optimization_barrier((y, y_recv, down_w))
+    y, y_recv, _ = lax.optimization_barrier((y, y_recv, far_send))
     y_pieces = [y, y_recv, swap(y, "wide", wide, 1), swap(y_recv, "wide", wide, 1)]
     near_hidden, near_coef = activate(near_own, near_recv)
     down_w, near_hidden = lax.optimization_barrier((down_w, near_hidden))
@@ -431,20 +423,21 @@
     own, send, d_pair = d_tokens_part((near_coef, far_coef), dh_own, dh_recv, *weights)
 
     own = own + swap(send, "wide", wide, 1).astype(F32)
-    cuts = [0, slots // 2, slots * 3 // 4, slots]
-    if slots % 4:
-        cuts = [0, slots]
-    grads = ()
-    for hop, flip in enumerate(reversed(flips)):
-        kept = own.shape[0] // 2
-        far = own[kept:].astype(BF16)
-        own = own[:kept]
-        if hop + 1 < len(cuts):
-            far, d_pair, grads = lax.optimization_barrier((far, d_pair, grads))
-            grads = gu_grads(
-                gu_index, gu_count, d_pair, turned, slots, cuts[hop], cuts[hop + 1], grads
-            )
-        own = own + swap(far, "wide", wide, 2 * flip).astype(F32)
+    kept = own.shape[0] // 2
+    far = own[kept:].astype(BF16)
+    own = own[:kept]
+    cut = slots * 2 // 3 if slots % 3 == 0 else slots
+    far, d_pair = lax.optimization_barrier((far, d_pair))
+    grads = gu_grads(gu_index, gu_count, d_pair, turned, slots, 0, cut, ())
+    own = own + swap(far, "wide", wide, 2 * flips[-1]).astype(F32)
+    sends = [own[p * rows : (p + 1) * rows].astype(BF16) for p in range(1, chips // 2)]
+    if cut < slots:
+        sends, d_pair, grads = lax.optimization_barrier((sends, d_pair, grads))
+        grads = gu_grads(gu_index, gu_count, d_pair, turned, slots, cut, slots, grads)
+    own = own[:rows]
+    for p, part in enumerate(sends, 1):
+        flip = sum(flips[bit] for bit in range(len(flips)) if p >> bit & 1)
+        own = own + swap(part, "wide", wide, 2 * flip).astype(F32)
     gate_grad, up_grad = grads
     return (
         own.astype(BF16),

time: 78 us -> 73.2 us (0.938)
  Pallas kernels: 41.7 us -> 37.6 us
  waiting for transfers between devices: 11.6 us -> 10.2 us
    pallas_call x1, Pallas kernels: 7.78 us -> 5.35 us  [down_grads(): pl.pallas_call(down_grad_body, out_shape=jax.ShapeDtypeStruct((slots, blo...]
    pallas_call x3 -> x2, Pallas kernels: 12.3 us -> 10.6 us  [gu_grads(): pl.pallas_call(functools.partial(gu_grad_body, first, len(before)), out_s...]
    ppermute x17 -> x18, waiting for transfers between devices: 11.6 us -> 10.2 us  [swap(): return lax.ppermute(array, axis, [(i, i ^ flip) for i in range(size)])]
    ppermute x17 -> x18, starting transfers between devices: 21.4 us -> 21.5 us  [swap(): return lax.ppermute(array, axis, [(i, i ^ flip) for i in range(size)])]
  transfers between devices with their start and end apart: 17 -> 18, of which waited for: 5 -> 9; matrix products, arithmetic and copies ran while one was open for 0% -> 0% of each run, Pallas kernels for 47% -> 45%
where the time goes in v7:
time: 73.2 us; the launch traced here: 72.4 us
  Pallas kernels  37.6 us (51%)
  starting transfers between devices  21.5 us (29%)
  waiting for transfers between devices  10.2 us (14%)
  between operations  2.15 us (3%)
  other arithmetic  0.86 us (1%)
    ppermute x18, starting transfers between devices, swap(): return lax.ppermute(array, axis, [(i, i ^ flip) for i in range(size)])  21.5 us
    pallas_call x2, Pallas kernels, gu_grads(): pl.pallas_call(functools.partial(gu_grad_body, first, len(before)), out_s...  10.6 us
    ppermute x18, waiting for transfers between devices, swap(): return lax.ppermute(array, axis, [(i, i ^ flip) for i in range(size)])  10.2 us
    pallas_call x3, Pallas kernels, fill(): pl.pallas_call(fill_body, out_shape=pltpu.VMEM((outer, inner, block, bloc...  9.35 us
    pallas_call x1, Pallas kernels, down_grads(): pl.pallas_call(down_grad_body, out_shape=jax.ShapeDtypeStruct((slots, blo...  5.35 us
    pallas_call x1, Pallas kernels, d_tokens_part(): pl.pallas_call(functools.partial(d_tokens_body, group), out_shape=(jax.Sh...  4.7 us
    pallas_call x2, Pallas kernels, gate_up(): pl.pallas_call(functools.partial(gate_up_body, half * f_blocks // 2), out...  3.72 us
    pallas_call x1, Pallas kernels, d_hidden(): pl.pallas_call(functools.partial(d_hidden_body, len(y_pieces)), out_shape...  3.59 us
  transfers between devices with their start and end apart: 18, of which 9 were waited for; matrix products, arithmetic and copies ran while one was open for 0% of the time, Pallas kernels for 45%

profile of v7, /device:TPU:0, one launch (start us, length us, event | category | flops | bytes accessed | tf_op | source)
XLA Modules:
  0.0 72.4 jit_solution(9603810332421103776)
XLA Ops:
  0.6 4.1 %collective-permute-start = (bf16[8,4096]{1,0:T(8,128)(2,1)}, bf16[8,4096]{1,0:T(8,128)(2,1)S(1)}, u32[]{:S(2)}, u32[]{:S(2)}) collective-permute-start(bf16[8,4096]{1,0:T(8,128)(2,1)} %param.9), channel_id=1, source_target_pairs={{0,16},{2,18},{4,20},{6,22},{8,24},{10,26},{12,28},{14,30},{16,0},... | collective-permute-start | bytes 196616 | tf_op jit(solution)/shard_map/ppermute | solution.py:38
  5.4 3.2 %fill.3.refs_4_ = bf16[32,8,128,128]{3,2,1,0:T(8,128)(2,1)S(1)} custom-call(s32[1,1,192]{2,1,0:T(1,128)} %index.9, s32[1,1]{1,0:T(1,128)S(6)} %copy.17.count, bf16[1,1,192,128,128]{4,3,2,1,0:T(8,128)(2,1)} %source.3), custom_call_target="tpu_custom_call" | custom-call | bytes 6291456 | tf_op jit(solution)/shard_map/fill/pallas_call | solution.py:91
  8.6 0.7 %collective-permute-start.1 = (bf16[16,4096]{1,0:T(8,128)(2,1)S(1)}, bf16[16,4096]{1,0:T(8,128)(2,1)S(1)}, u32[]{:S(2)}, u32[]{:S(2)}) collective-permute-start(bf16[16,4096]{1,0:T(8,128)(2,1)S(1)} %pad_maximum_fusion.2), channel_id=1, source_target_pairs={{0,8},{2,10},{4,12},{6,14},{8,0},{10,2},{12,4},{14,6},{16,24},{18,... | collective-permute-start | bytes 393224 | tf_op jit(solution)/shard_map/ppermute | solution.py:38
  9.4 3.2 %fill.4.refs_5_ = bf16[32,8,128,128]{3,2,1,0:T(8,128)(2,1)S(1)} custom-call(s32[1,1,192]{2,1,0:T(1,128)} %index.9, s32[1,1]{1,0:T(1,128)S(6)} %copy.17.count, bf16[1,1,192,128,128]{4,3,2,1,0:T(8,128)(2,1)} %source.4), custom_call_target="tpu_custom_call" | custom-call | bytes 6291456 | tf_op jit(solution)/shard_map/fill/pallas_call | solution.py:91
  12.5 1.1 %collective-permute-done.1 = bf16[16,4096]{1,0:T(8,128)(2,1)S(1)} collective-permute-done((bf16[16,4096]{1,0:T(8,128)(2,1)S(1)}, bf16[16,4096]{1,0:T(8,128)(2,1)S(1)}, u32[]{:S(2)}, u32[]{:S(2)}) %collective-permute-start.1) | collective-permute-done | bytes 131104 | tf_op jit(solution)/shard_map/ppermute | solution.py:38
  13.7 2.4 %collective-permute-start.6 = (bf16[8,4096]{1,0:T(8,128)(2,1)S(1)}, bf16[8,4096]{1,0:T(8,128)(2,1)S(1)}, u32[]{:S(2)}, u32[]{:S(2)}) collective-permute-start(bf16[8,4096]{1,0:T(8,128)(2,1)S(1)} %copy-done.1), channel_id=1, source_target_pairs={{0,16},{2,18},{4,20},{6,22},{8,24},{10,26},{12,28},{14,30},{16,0},... | collective-permute-start | bytes 196616 | tf_op jit(solution)/shard_map/ppermute | solution.py:38
  16.7 1.6 %collective-permute-start.2 = (bf16[32,4096]{1,0:T(8,128)(2,1)S(1)}, bf16[32,4096]{1,0:T(8,128)(2,1)S(1)}, u32[]{:S(2)}, u32[]{:S(2)}) collective-permute-start(bf16[32,4096]{1,0:T(8,128)(2,1)S(1)} %pad_maximum_fusion.refs_0_.refs_4_), channel_id=1, source_target_pairs={{0,4},{2,6},{4,0},{6,2},{8,12},{10,14},{12,8},{14,10},{16,20},{18,... | collective-permute-start | bytes 786440 | tf_op jit(solution)/shard_map/ppermute | solution.py:38
  18.3 3.0 %fill.5.refs_8_ = bf16[8,32,128,128]{3,2,1,0:T(8,128)(2,1)S(1)} custom-call(s32[1,1,192]{2,1,0:T(1,128)} %index.7, s32[1,1]{1,0:T(1,128)S(6)} %copy.18.count, bf16[1,1,192,128,128]{4,3,2,1,0:T(8,128)(2,1)} %source.5), custom_call_target="tpu_custom_call" | custom-call | bytes 6291456 | tf_op jit(solution)/shard_map/fill/pallas_call | solution.py:91
  21.4 1.6 %collective-permute-start.7 = (bf16[16,4096]{1,0:T(8,128)(2,1)S(1)}, bf16[16,4096]{1,0:T(8,128)(2,1)S(1)}, u32[]{:S(2)}, u32[]{:S(2)}) collective-permute-start(bf16[16,4096]{1,0:T(8,128)(2,1)S(1)} %pad_maximum_fusion.3), channel_id=1, source_target_pairs={{0,8},{2,10},{4,12},{6,14},{8,0},{10,2},{12,4},{14,6},{16,24},{18,... | collective-permute-start | bytes 393224 | tf_op jit(solution)/shard_map/ppermute | solution.py:38
  23.0 0.9 %collective-permute-done.2.refs_1_.refs_5_ = bf16[32,4096]{1,0:T(8,128)(2,1)S(1)} collective-permute-done((bf16[32,4096]{1,0:T(8,128)(2,1)S(1)}, bf16[32,4096]{1,0:T(8,128)(2,1)S(1)}, u32[]{:S(2)}, u32[]{:S(2)}) %collective-permute-start.2) | collective-permute-done | bytes 262176 | tf_op jit(solution)/shard_map/ppermute | solution.py:38
  23.9 2.5 %collective-permute-done.7 = bf16[16,4096]{1,0:T(8,128)(2,1)S(1)} collective-permute-done((bf16[16,4096]{1,0:T(8,128)(2,1)S(1)}, bf16[16,4096]{1,0:T(8,128)(2,1)S(1)}, u32[]{:S(2)}, u32[]{:S(2)}) %collective-permute-start.7) | collective-permute-done | bytes 131104 | tf_op jit(solution)/shard_map/ppermute | solution.py:38
  26.8 1.9 %gate_up.2 = (f32[4,128,256]{2,1,0:T(8,128)S(1)}, bf16[4,128,256]{2,1,0:T(8,128)(2,1)S(1)}) custom-call(bf16[32,4096]{1,0:T(8,128)(2,1)S(1)} %pad_maximum_fusion.refs_0_.refs_4_, bf16[32,4096]{1,0:T(8,128)(2,1)S(1)} %collective-permute-done.2.refs_1_.refs_5_, bf16[32,4096]{1,0:T(8,128)(2,1)S(1)} %collective-permute-done.3.refs_2_.refs_6_, ...), custom_call_target="tpu_custom_call" | custom-call | flops 1073741824 | bytes 8388608 | tf_op jit(solution)/shard_map/gate_up/pallas_call | solution.py:130
  28.6 1.4 %collective-permute-start.5 = (bf16[4,128,256]{2,1,0:T(8,128)(2,1)S(1)}, bf16[4,128,256]{2,1,0:T(8,128)(2,1)S(1)}, u32[]{:S(2)}, u32[]{:S(2)}) collective-permute-start(bf16[4,128,256]{2,1,0:T(8,128)(2,1)S(1)} %get-tuple-element.57), channel_id=1, source_target_pairs={{0,1},{1,0},{2,3},{3,2},{4,5},{5,4},{6,7},{7,6},{8,9},{9,8},{10,11... | collective-permute-start | bytes 786440 | tf_op jit(solution)/shard_map/ppermute | solution.py:38
  30.1 1.9 %gate_up.3 = (f32[4,128,256]{2,1,0:T(8,128)S(1)}, bf16[4,128,256]{2,1,0:T(8,128)(2,1)S(1)}) custom-call(bf16[32,4096]{1,0:T(8,128)(2,1)S(1)} %pad_maximum_fusion.refs_0_.refs_4_, bf16[32,4096]{1,0:T(8,128)(2,1)S(1)} %collective-permute-done.2.refs_1_.refs_5_, bf16[32,4096]{1,0:T(8,128)(2,1)S(1)} %collective-permute-done.3.refs_2_.refs_6_, ...), custom_call_target="tpu_custom_call" | custom-call | flops 1073741824 | bytes 8388608 | tf_op jit(solution)/shard_map/gate_up/pallas_call | solution.py:130
  31.9 0.9 %collective-permute-done.9.refs_1_ = bf16[32,4096]{1,0:T(8,128)(2,1)S(1)} collective-permute-done((bf16[32,4096]{1,0:T(8,128)(2,1)S(1)}, bf16[32,4096]{1,0:T(8,128)(2,1)S(1)}, u32[]{:S(2)}, u32[]{:S(2)}) %collective-permute-start.9) | collective-permute-done | bytes 262176 | tf_op jit(solution)/shard_map/ppermute | solution.py:38
  32.9 0.5 collective-permute-start.11
  33.4 1.4 %collective-permute-start.8 = (bf16[4,128,256]{2,1,0:T(8,128)(2,1)S(1)}, bf16[4,128,256]{2,1,0:T(8,128)(2,1)S(1)}, u32[]{:S(2)}, u32[]{:S(2)}) collective-permute-start(bf16[4,128,256]{2,1,0:T(8,128)(2,1)S(1)} %get-tuple-element.68), channel_id=1, source_target_pairs={{0,1},{1,0},{2,3},{3,2},{4,5},{5,4},{6,7},{7,6},{8,9},{9,8},{10,11... | collective-permute-start | bytes 786440 | tf_op jit(solution)/shard_map/ppermute | solution.py:38
  34.8 1.1 %collective-permute-done.5.refs_1_ = bf16[4,128,256]{2,1,0:T(8,128)(2,1)S(1)} collective-permute-done((bf16[4,128,256]{2,1,0:T(8,128)(2,1)S(1)}, bf16[4,128,256]{2,1,0:T(8,128)(2,1)S(1)}, u32[]{:S(2)}, u32[]{:S(2)}) %collective-permute-start.5) | collective-permute-done | bytes 262176 | tf_op jit(solution)/shard_map/ppermute | solution.py:38
  36.1 3.6 %d_hidden.1 = (f32[8,128,128]{2,1,0:T(8,128)S(1)}, bf16[8,128,128]{2,1,0:T(8,128)(2,1)S(1)}, bf16[32,128,128]{2,1,0:T(8,128)(2,1)S(1)}) custom-call(bf16[32,4096]{1,0:T(8,128)(2,1)S(1)} %pad_maximum_fusion.1.refs_0_, bf16[32,4096]{1,0:T(8,128)(2,1)S(1)} %collective-permute-done.9.refs_1_, bf16[32,4096]{1,0:T(8,128)(2,1)S(1)} %collective-permute-done.10.refs_2_, ...), custom_call_target="tpu_custom_call" | custom-call | flops 1073741824 | bytes 8388608 | tf_op jit(solution)/shard_map/d_hidden/pallas_call | solution.py:173
  39.7 1.4 %collective-permute-start.12 = (bf16[8,128,128]{2,1,0:T(8,128)(2,1)S(1)}, bf16[8,128,128]{2,1,0:T(8,128)(2,1)S(1)}, u32[]{:S(2)}, u32[]{:S(2)}) collective-permute-start(bf16[8,128,128]{2,1,0:T(8,128)(2,1)S(1)} %get-tuple-element.78), channel_id=1, source_target_pairs={{0,1},{1,0},{2,3},{3,2},{4,5},{5,4},{6,7},{7,6},{8,9},{9,8},{10,11... | collective-permute-start | bytes 786440 | tf_op jit(solution)/shard_map/ppermute | solution.py:38
  41.1 0.8 %collective-permute-done.8.refs_1_ = bf16[4,128,256]{2,1,0:T(8,128)(2,1)S(1)} collective-permute-done((bf16[4,128,256]{2,1,0:T(8,128)(2,1)S(1)}, bf16[4,128,256]{2,1,0:T(8,128)(2,1)S(1)}, u32[]{:S(2)}, u32[]{:S(2)}) %collective-permute-start.8) | collective-permute-done | bytes 262176 | tf_op jit(solution)/shard_map/ppermute | solution.py:38
  42.1 5.3 %down_grads.1 = bf16[192,128,128]{2,1,0:T(8,128)(2,1)} custom-call(s32[1,1,192]{2,1,0:T(1,128)} %index.7, s32[1,1]{1,0:T(1,128)S(6)} %copy.18.count, bf16[4,128,128]{2,1,0:T(8,128)(2,1)S(1)} %get-tuple-element.65.near, bf16[4,128,128]{2,1,0:T(8,128)(2,1)S(1)} %get-tuple-element.69.far, bf16[32,4096]{1,0:T(8,128)(2,1)S(1)} %pad_maximum_fusion.1.refs_0_, ...), custom_call_target="tpu_custom_call" | custom-call | flops 805306368 | bytes 6291456 | tf_op jit(solution)/shard_map/down_grads/pallas_call | solution.py:357
  47.4 4.7 %d_tokens.1 = (f32[64,4096]{1,0:T(8,128)S(1)}, bf16[64,4096]{1,0:T(8,128)(2,1)S(1)}, bf16[8,128,256]{2,1,0:T(8,128)(2,1)S(1)}) custom-call(f32[4,128,256]{2,1,0:T(8,128)S(1)} %get-tuple-element.58.refs_0_, f32[4,128,256]{2,1,0:T(8,128)S(1)} %get-tuple-element.75.refs_1_, f32[8,128,128]{2,1,0:T(8,128)S(1)} %get-tuple-element.77.refs_2_, ...), custom_call_target="tpu_custom_call" | custom-call | flops 2147483648 | bytes 16777216 | tf_op jit(solution)/shard_map/d_tokens/pallas_call | solution.py:226
  52.2 1.9 %collective-permute-done.13 = bf16[64,4096]{1,0:T(8,128)(2,1)S(1)} collective-permute-done((bf16[64,4096]{1,0:T(8,128)(2,1)S(1)}, bf16[64,4096]{1,0:T(8,128)(2,1)S(1)}, u32[]{:S(2)}, u32[]{:S(2)}) %collective-permute-start.13) | collective-permute-done | bytes 524320 | tf_op jit(solution)/shard_map/ppermute | solution.py:38
  54.2 1.5 %collective-permute-start.14 = (bf16[32,4096]{1,0:T(8,128)(2,1)S(1)}, bf16[32,4096]{1,0:T(8,128)(2,1)S(1)}, u32[]{:S(2)}, u32[]{:S(2)}) collective-permute-start(bf16[32,4096]{1,0:T(8,128)(2,1)S(1)} %slice.43), channel_id=1, source_target_pairs={{0,4},{2,6},{4,0},{6,2},{8,12},{10,14},{12,8},{14,10},{16,20},{18,... | collective-permute-start | bytes 786440 | tf_op jit(solution)/shard_map/ppermute | solution.py:38
  55.7 6.7 %gu_grads.2 = (bf16[192,128,128]{2,1,0:T(8,128)(2,1)}, bf16[192,128,128]{2,1,0:T(8,128)(2,1)}) custom-call(s32[1,1,192]{2,1,0:T(1,128)} %index.9, s32[1,1]{1,0:T(1,128)S(6)} %copy.17.count, bf16[8,128,256]{2,1,0:T(8,128)(2,1)S(1)} %get-tuple-element.90.d_pair, bf16[32,128,128]{2,1,0:T(8,128)(2,1)S(1)} %get-tuple-element.84.turned), custom_call_target="tpu_custom_call" | custom-call | flops 1073741824 | bytes 8388608 | tf_op jit(solution)/shard_map/gu_grads/pallas_call | solution.py:274
  62.7 0.8 %collective-permute-start.15 = (bf16[8,4096]{1,0:T(8,128)(2,1)S(1)}, bf16[8,4096]{1,0:T(8,128)(2,1)S(1)}, u32[]{:S(2)}, u32[]{:S(2)}) collective-permute-start(bf16[8,4096]{1,0:T(8,128)(2,1)S(1)} %get-tuple-element.87), channel_id=1, source_target_pairs={{0,16},{2,18},{4,20},{6,22},{8,24},{10,26},{12,28},{14,30},{16,0},... | collective-permute-start | bytes 196616 | tf_op jit(solution)/shard_map/ppermute | solution.py:38
  63.5 2.0 %collective-permute-start.16 = (bf16[8,4096]{1,0:T(8,128)(2,1)S(1)}, bf16[8,4096]{1,0:T(8,128)(2,1)S(1)}, u32[]{:S(2)}, u32[]{:S(2)}) collective-permute-start(bf16[8,4096]{1,0:T(8,128)(2,1)S(1)} %get-tuple-element.88), channel_id=1, source_target_pairs={{0,8},{2,10},{4,12},{6,14},{8,0},{10,2},{12,4},{14,6},{16,24},{18,... | collective-permute-start | bytes 196616 | tf_op jit(solution)/shard_map/ppermute | solution.py:38
  65.5 1.7 %collective-permute-start.17 = (bf16[8,4096]{1,0:T(8,128)(2,1)S(1)}, bf16[8,4096]{1,0:T(8,128)(2,1)S(1)}, u32[]{:S(2)}, u32[]{:S(2)}) collective-permute-start(bf16[8,4096]{1,0:T(8,128)(2,1)S(1)} %get-tuple-element.89), channel_id=1, source_target_pairs={{0,24},{2,26},{4,28},{6,30},{8,16},{10,18},{12,20},{14,22},{16,8},... | collective-permute-start | bytes 196616 | tf_op jit(solution)/shard_map/ppermute | solution.py:38
  67.2 3.9 %gu_grads.3 = (bf16[192,128,128]{2,1,0:T(8,128)(2,1)}, bf16[192,128,128]{2,1,0:T(8,128)(2,1)}) custom-call(s32[1,1,192]{2,1,0:T(1,128)} %index.9, s32[1,1]{1,0:T(1,128)S(6)} %copy.17.count, bf16[8,128,256]{2,1,0:T(8,128)(2,1)S(1)} %get-tuple-element.90.d_pair, ...), custom_call_target="tpu_custom_call", output_to_operand_aliasing={{0}: (4, {}), {1}: (5, {})} | custom-call | flops 536870912 | bytes 4194304 | tf_op jit(solution)/shard_map/gu_grads/pallas_call | solution.py:274
  71.2 0.5 collective-permute-done.17
  71.7 0.7 fusion.2
  (29 shorter events, 1.2 us)
Async XLA Ops:
  0.6 8.0 %collective-permute-start = (bf16[8,4096]{1,0:T(8,128)(2,1)}, bf16[8,4096]{1,0:T(8,128)(2,1)S(1)}, u32[]{:S(2)}, u32[]{:S(2)}) collective-permute-start(bf16[8,4096]{1,0:T(8,128)(2,1)} %param.9), channel_id=1, source_target_pairs={{0,16},{2,18},{4,20},{6,22},{8,24},{10,26},{12,28},{14,30},{16,0},... | collective-permute-start | bytes 196616 | tf_op jit(solution)/shard_map/ppermute | solution.py:38
  5.4 3.2 %copy-start = (bf16[8,4096]{1,0:T(8,128)(2,1)S(1)}, bf16[8,4096]{1,0:T(8,128)(2,1)}, u32[]{:S(2)}) copy-start(bf16[8,4096]{1,0:T(8,128)(2,1)} %param.9) | copy-start | bytes 196612
  8.6 5.1 %copy-start.1 = (bf16[8,4096]{1,0:T(8,128)(2,1)S(1)}, bf16[8,4096]{1,0:T(8,128)(2,1)}, u32[]{:S(2)}) copy-start(bf16[8,4096]{1,0:T(8,128)(2,1)} %param.10) | copy-start | bytes 196612
  8.6 5.0 %collective-permute-start.1 = (bf16[16,4096]{1,0:T(8,128)(2,1)S(1)}, bf16[16,4096]{1,0:T(8,128)(2,1)S(1)}, u32[]{:S(2)}, u32[]{:S(2)}) collective-permute-start(bf16[16,4096]{1,0:T(8,128)(2,1)S(1)} %pad_maximum_fusion.2), channel_id=1, source_target_pairs={{0,8},{2,10},{4,12},{6,14},{8,0},{10,2},{12,4},{14,6},{16,24},{18,... | collective-permute-start | bytes 393224 | tf_op jit(solution)/shard_map/ppermute | solution.py:38
  13.7 7.7 %collective-permute-start.6 = (bf16[8,4096]{1,0:T(8,128)(2,1)S(1)}, bf16[8,4096]{1,0:T(8,128)(2,1)S(1)}, u32[]{:S(2)}, u32[]{:S(2)}) collective-permute-start(bf16[8,4096]{1,0:T(8,128)(2,1)S(1)} %copy-done.1), channel_id=1, source_target_pairs={{0,16},{2,18},{4,20},{6,22},{8,24},{10,26},{12,28},{14,30},{16,0},... | collective-permute-start | bytes 196616 | tf_op jit(solution)/shard_map/ppermute | solution.py:38
  16.7 7.2 %collective-permute-start.2 = (bf16[32,4096]{1,0:T(8,128)(2,1)S(1)}, bf16[32,4096]{1,0:T(8,128)(2,1)S(1)}, u32[]{:S(2)}, u32[]{:S(2)}) collective-permute-start(bf16[32,4096]{1,0:T(8,128)(2,1)S(1)} %pad_maximum_fusion.refs_0_.refs_4_), channel_id=1, source_target_pairs={{0,4},{2,6},{4,0},{6,2},{8,12},{10,14},{12,8},{14,10},{16,20},{18,... | collective-permute-start | bytes 786440 | tf_op jit(solution)/shard_map/ppermute | solution.py:38
  21.4 5.0 %collective-permute-start.7 = (bf16[16,4096]{1,0:T(8,128)(2,1)S(1)}, bf16[16,4096]{1,0:T(8,128)(2,1)S(1)}, u32[]{:S(2)}, u32[]{:S(2)}) collective-permute-start(bf16[16,4096]{1,0:T(8,128)(2,1)S(1)} %pad_maximum_fusion.3), channel_id=1, source_target_pairs={{0,8},{2,10},{4,12},{6,14},{8,0},{10,2},{12,4},{14,6},{16,24},{18,... | collective-permute-start | bytes 393224 | tf_op jit(solution)/shard_map/ppermute | solution.py:38
  23.0 3.8 %collective-permute-start.3 = (bf16[32,4096]{1,0:T(8,128)(2,1)S(1)}, bf16[32,4096]{1,0:T(8,128)(2,1)S(1)}, u32[]{:S(2)}, u32[]{:S(2)}) collective-permute-start(bf16[32,4096]{1,0:T(8,128)(2,1)S(1)} %pad_maximum_fusion.refs_0_.refs_4_), channel_id=1, source_target_pairs={{0,2},{2,0},{4,6},{6,4},{8,10},{10,8},{12,14},{14,12},{16,18},{18,... | collective-permute-start | bytes 786440 | tf_op jit(solution)/shard_map/ppermute | solution.py:38
  23.9 2.9 %collective-permute-start.4 = (bf16[32,4096]{1,0:T(8,128)(2,1)S(1)}, bf16[32,4096]{1,0:T(8,128)(2,1)S(1)}, u32[]{:S(2)}, u32[]{:S(2)}) collective-permute-start(bf16[32,4096]{1,0:T(8,128)(2,1)S(1)} %collective-permute-done.2.refs_1_.refs_5_), channel_id=1, source_target_pairs={{0,2},{2,0},{4,6},{6,4},{8,10},{10,8},{12,14},{14,12},{16,18},{18,... | collective-permute-start | bytes 786440 | tf_op jit(solution)/shard_map/ppermute | solution.py:38
  26.4 6.4 %collective-permute-start.9 = (bf16[32,4096]{1,0:T(8,128)(2,1)S(1)}, bf16[32,4096]{1,0:T(8,128)(2,1)S(1)}, u32[]{:S(2)}, u32[]{:S(2)}) collective-permute-start(bf16[32,4096]{1,0:T(8,128)(2,1)S(1)} %pad_maximum_fusion.1.refs_0_), channel_id=1, source_target_pairs={{0,4},{2,6},{4,0},{6,2},{8,12},{10,14},{12,8},{14,10},{16,20},{18,... | collective-permute-start | bytes 786440 | tf_op jit(solution)/shard_map/ppermute | solution.py:38
  28.6 7.3 %collective-permute-start.5 = (bf16[4,128,256]{2,1,0:T(8,128)(2,1)S(1)}, bf16[4,128,256]{2,1,0:T(8,128)(2,1)S(1)}, u32[]{:S(2)}, u32[]{:S(2)}) collective-permute-start(bf16[4,128,256]{2,1,0:T(8,128)(2,1)S(1)} %get-tuple-element.57), channel_id=1, source_target_pairs={{0,1},{1,0},{2,3},{3,2},{4,5},{5,4},{6,7},{7,6},{8,9},{9,8},{10,11... | collective-permute-start | bytes 786440 | tf_op jit(solution)/shard_map/ppermute | solution.py:38
  32.9 3.2 %collective-permute-start.10 = (bf16[32,4096]{1,0:T(8,128)(2,1)S(1)}, bf16[32,4096]{1,0:T(8,128)(2,1)S(1)}, u32[]{:S(2)}, u32[]{:S(2)}) collective-permute-start(bf16[32,4096]{1,0:T(8,128)(2,1)S(1)} %pad_maximum_fusion.1.refs_0_), channel_id=1, source_target_pairs={{0,2},{2,0},{4,6},{6,4},{8,10},{10,8},{12,14},{14,12},{16,18},{18,... | collective-permute-start | bytes 786440 | tf_op jit(solution)/shard_map/ppermute | solution.py:38
  32.9 3.2 %collective-permute-start.11 = (bf16[32,4096]{1,0:T(8,128)(2,1)S(1)}, bf16[32,4096]{1,0:T(8,128)(2,1)S(1)}, u32[]{:S(2)}, u32[]{:S(2)}) collective-permute-start(bf16[32,4096]{1,0:T(8,128)(2,1)S(1)} %collective-permute-done.9.refs_1_), channel_id=1, source_target_pairs={{0,2},{2,0},{4,6},{6,4},{8,10},{10,8},{12,14},{14,12},{16,18},{18,... | collective-permute-start | bytes 786440 | tf_op jit(solution)/shard_map/ppermute | solution.py:38
  33.4 8.6 %collective-permute-start.8 = (bf16[4,128,256]{2,1,0:T(8,128)(2,1)S(1)}, bf16[4,128,256]{2,1,0:T(8,128)(2,1)S(1)}, u32[]{:S(2)}, u32[]{:S(2)}) collective-permute-start(bf16[4,128,256]{2,1,0:T(8,128)(2,1)S(1)} %get-tuple-element.68), channel_id=1, source_target_pairs={{0,1},{1,0},{2,3},{3,2},{4,5},{5,4},{6,7},{7,6},{8,9},{9,8},{10,11... | collective-permute-start | bytes 786440 | tf_op jit(solution)/shard_map/ppermute | solution.py:38
  39.7 7.7 %collective-permute-start.12 = (bf16[8,128,128]{2,1,0:T(8,128)(2,1)S(1)}, bf16[8,128,128]{2,1,0:T(8,128)(2,1)S(1)}, u32[]{:S(2)}, u32[]{:S(2)}) collective-permute-start(bf16[8,128,128]{2,1,0:T(8,128)(2,1)S(1)} %get-tuple-element.78), channel_id=1, source_target_pairs={{0,1},{1,0},{2,3},{3,2},{4,5},{5,4},{6,7},{7,6},{8,9},{9,8},{10,11... | collective-permute-start | bytes 786440 | tf_op jit(solution)/shard_map/ppermute | solution.py:38
  52.1 2.0 %collective-permute-start.13 = (bf16[64,4096]{1,0:T(8,128)(2,1)S(1)}, bf16[64,4096]{1,0:T(8,128)(2,1)S(1)}, u32[]{:S(2)}, u32[]{:S(2)}) collective-permute-start(bf16[64,4096]{1,0:T(8,128)(2,1)S(1)} %get-tuple-element.80), channel_id=1, source_target_pairs={{0,2},{2,0},{4,6},{6,4},{8,10},{10,8},{12,14},{14,12},{16,18},{18,... | collective-permute-start | bytes 1572872 | tf_op jit(solution)/shard_map/ppermute | solution.py:38
  54.2 8.4 %collective-permute-start.14 = (bf16[32,4096]{1,0:T(8,128)(2,1)S(1)}, bf16[32,4096]{1,0:T(8,128)(2,1)S(1)}, u32[]{:S(2)}, u32[]{:S(2)}) collective-permute-start(bf16[32,4096]{1,0:T(8,128)(2,1)S(1)} %slice.43), channel_id=1, source_target_pairs={{0,4},{2,6},{4,0},{6,2},{8,12},{10,14},{12,8},{14,10},{16,20},{18,... | collective-permute-start | bytes 786440 | tf_op jit(solution)/shard_map/ppermute | solution.py:38
  62.7 8.4 %collective-permute-start.15 = (bf16[8,4096]{1,0:T(8,128)(2,1)S(1)}, bf16[8,4096]{1,0:T(8,128)(2,1)S(1)}, u32[]{:S(2)}, u32[]{:S(2)}) collective-permute-start(bf16[8,4096]{1,0:T(8,128)(2,1)S(1)} %get-tuple-element.87), channel_id=1, source_target_pairs={{0,16},{2,18},{4,20},{6,22},{8,24},{10,26},{12,28},{14,30},{16,0},... | collective-permute-start | bytes 196616 | tf_op jit(solution)/shard_map/ppermute | solution.py:38
  63.5 7.7 %collective-permute-start.16 = (bf16[8,4096]{1,0:T(8,128)(2,1)S(1)}, bf16[8,4096]{1,0:T(8,128)(2,1)S(1)}, u32[]{:S(2)}, u32[]{:S(2)}) collective-permute-start(bf16[8,4096]{1,0:T(8,128)(2,1)S(1)} %get-tuple-element.88), channel_id=1, source_target_pairs={{0,8},{2,10},{4,12},{6,14},{8,0},{10,2},{12,4},{14,6},{16,24},{18,... | collective-permute-start | bytes 196616 | tf_op jit(solution)/shard_map/ppermute | solution.py:38
  65.5 6.2 %collective-permute-start.17 = (bf16[8,4096]{1,0:T(8,128)(2,1)S(1)}, bf16[8,4096]{1,0:T(8,128)(2,1)S(1)}, u32[]{:S(2)}, u32[]{:S(2)}) collective-permute-start(bf16[8,4096]{1,0:T(8,128)(2,1)S(1)} %get-tuple-element.89), channel_id=1, source_target_pairs={{0,24},{2,26},{4,28},{6,30},{8,16},{10,18},{12,20},{14,22},{16,8},... | collective-permute-start | bytes 196616 | tf_op jit(solution)/shard_map/ppermute | solution.py:38

commit v8 on v7

--- a/solution.py
+++ b/solution.py
@@ -57,7 +57,8 @@
         return split_index(self.index[0, 0, slot], size)
 
 
-def fill_body(index, count, source, target, index_here, slots_sem, sem):
+def fill_body(index, count, source, *refs):
+    target, index_here, slots_sem, sem = refs[-4:]
     slots = Slots(index, count, index_here, slots_sem)
     slots.copy.start()
     outer, inner = target.shape[:2]
@@ -86,18 +87,18 @@
         pltpu.make_async_copy(source.at[0, 0, 0], target.at[0, 0], sem).wait()
 
 
-def fill(index, count, slots, outer, inner):
+def fill(index, count, slots, outer, inner, early=()):
     block = slots.shape[-1]
     return pl.pallas_call(
         fill_body,
         out_shape=pltpu.VMEM((outer, inner, block, block), BF16),
-        in_specs=[IN_HBM, SCALARS, IN_HBM],
+        in_specs=[IN_HBM, SCALARS, IN_HBM] + [SCALARS] * len(early),
         out_specs=WHOLE,
         scratch_shapes=[*Slots.scratch(index), pltpu.SemaphoreType.DMA],
         compiler_params=params(),
         cost_estimate=cost(0, slots.size * 2),
         name="fill",
-    )(in_hbm(index), count, in_hbm(slots))
+    )(in_hbm(index), count, in_hbm(slots), *early)
 
 
 def stack(pieces):
@@ -396,12 +397,15 @@
             x, weights, index = lax.optimization_barrier((x, weights, index))
         x_recv = swap(x, "wide", wide, 2 * flip)
         if hop < 2:
-            weights.append(fill(index, gu_count, vals[hop], d_blocks, f_blocks))
-    y, index, _ = lax.optimization_barrier((cotangent, down_index, x))
+            early = (down_count,) if hop == 1 else ()
+            weights.append(fill(index, gu_count, vals[hop], d_blocks, f_blocks, early))
+        if hop == 1:
+            y, _ = lax.optimization_barrier((cotangent, weights[1]))
+    index, _ = lax.optimization_barrier((down_index, x))
     down_w = fill(index, down_count, down_vals, f_blocks, d_blocks)
     for flip in flips[:-1]:
         y = jnp.concatenate([y, swap(y, "wide", wide, 2 * flip)], axis=0)
-        y, down_w = lax.optimization_barrier((y, down_w))
+    x, down_w = lax.optimization_barrier((x, down_w))
     x_pieces = [x, x_recv, swap(x, "wide", wide, 1), swap(x_recv, "wide", wide, 1)]
     y, _ = lax.optimization_barrier((y, x_recv))
     y_recv = swap(y, "wide", wide, 2 * flips[-1])

time: 73.2 us -> 73.6 us (level)
  starting transfers between devices: 21.5 us -> 23.1 us
  Pallas kernels: 37.6 us -> 36.4 us
    ppermute x18, starting transfers between devices: 21.5 us -> 23.1 us  [swap(): return lax.ppermute(array, axis, [(i, i ^ flip) for i in range(size)])]
    pallas_call x3, Pallas kernels: 9.35 us -> 8.18 us  [fill(): pl.pallas_call(fill_body, out_shape=pltpu.VMEM((outer, inner, block, bloc...]
  transfers between devices with their start and end apart: 18 -> 18, of which waited for: 9 -> 10; matrix products, arithmetic and copies ran while one was open for 0% -> 0% of each run, Pallas kernels for 45% -> 43%
where the time goes in v8:
time: 73.6 us; the launch traced here: 73.2 us
  Pallas kernels  36.4 us (49%)
  starting transfers between devices  23.1 us (31%)
  waiting for transfers between devices  10.7 us (15%)
  between operations  2.16 us (3%)
  other arithmetic  0.86 us (1%)
    ppermute x18, starting transfers between devices, swap(): return lax.ppermute(array, axis, [(i, i ^ flip) for i in range(size)])  23.1 us
    ppermute x18, waiting for transfers between devices, swap(): return lax.ppermute(array, axis, [(i, i ^ flip) for i in range(size)])  10.7 us
    pallas_call x2, Pallas kernels, gu_grads(): pl.pallas_call(functools.partial(gu_grad_body, first, len(before)), out_s...  10.6 us
    pallas_call x3, Pallas kernels, fill(): pl.pallas_call(fill_body, out_shape=pltpu.VMEM((outer, inner, block, bloc...  8.18 us
    pallas_call x1, Pallas kernels, down_grads(): pl.pallas_call(down_grad_body, out_shape=jax.ShapeDtypeStruct((slots, blo...  5.34 us
    pallas_call x1, Pallas kernels, d_tokens_part(): pl.pallas_call(functools.partial(d_tokens_body, group), out_shape=(jax.Sh...  4.7 us
    pallas_call x2, Pallas kernels, gate_up(): pl.pallas_call(functools.partial(gate_up_body, half * f_blocks // 2), out...  3.73 us
    pallas_call x1, Pallas kernels, d_hidden(): pl.pallas_call(functools.partial(d_hidden_body, len(y_pieces)), out_shape...  3.6 us
  transfers between devices with their start and end apart: 18, of which 10 were waited for; matrix products, arithmetic and copies ran while one was open for 0% of the time, Pallas kernels for 43%

profile of v8, /device:TPU:0, one launch (start us, length us, event | category | flops | bytes accessed | tf_op | source)
XLA Modules:
  0.0 73.2 jit_solution(17051125139985976837)
XLA Ops:
  0.6 4.1 %collective-permute-start = (bf16[8,4096]{1,0:T(8,128)(2,1)}, bf16[8,4096]{1,0:T(8,128)(2,1)S(1)}, u32[]{:S(2)}, u32[]{:S(2)}) collective-permute-start(bf16[8,4096]{1,0:T(8,128)(2,1)} %param.9), channel_id=1, source_target_pairs={{0,16},{2,18},{4,20},{6,22},{8,24},{10,26},{12,28},{14,30},{16,0},... | collective-permute-start | bytes 196616 | tf_op jit(solution)/shard_map/ppermute | solution.py:38
  5.4 2.4 %fill.3.refs_4_ = bf16[32,8,128,128]{3,2,1,0:T(8,128)(2,1)S(1)} custom-call(s32[1,1,192]{2,1,0:T(1,128)} %index.9, s32[1,1]{1,0:T(1,128)S(6)} %copy.17.count, bf16[1,1,192,128,128]{4,3,2,1,0:T(8,128)(2,1)} %source.3), custom_call_target="tpu_custom_call" | custom-call | bytes 6291456 | tf_op jit(solution)/shard_map/fill/pallas_call | solution.py:92
  7.8 0.8 %collective-permute-done = bf16[8,4096]{1,0:T(8,128)(2,1)S(1)} collective-permute-done((bf16[8,4096]{1,0:T(8,128)(2,1)}, bf16[8,4096]{1,0:T(8,128)(2,1)S(1)}, u32[]{:S(2)}, u32[]{:S(2)}) %collective-permute-start) | collective-permute-done | bytes 65568 | tf_op jit(solution)/shard_map/ppermute | solution.py:38
  8.6 1.2 %collective-permute-start.1 = (bf16[16,4096]{1,0:T(8,128)(2,1)S(1)}, bf16[16,4096]{1,0:T(8,128)(2,1)S(1)}, u32[]{:S(2)}, u32[]{:S(2)}) collective-permute-start(bf16[16,4096]{1,0:T(8,128)(2,1)S(1)} %pad_maximum_fusion.2), channel_id=1, source_target_pairs={{0,8},{2,10},{4,12},{6,14},{8,0},{10,2},{12,4},{14,6},{16,24},{18,... | collective-permute-start | bytes 393224 | tf_op jit(solution)/shard_map/ppermute | solution.py:38
  10.5 2.4 %fill.4.refs_5_ = bf16[32,8,128,128]{3,2,1,0:T(8,128)(2,1)S(1)} custom-call(s32[1,1,192]{2,1,0:T(1,128)} %index.9, s32[1,1]{1,0:T(1,128)S(6)} %copy.17.count, bf16[1,1,192,128,128]{4,3,2,1,0:T(8,128)(2,1)} %source.4, s32[1,1]{1,0:T(1,128)S(6)} %copy.18.refs_0_.count), custom_call_target="tpu_custom_call" | custom-call | bytes 6291456 | tf_op jit(solution)/shard_map/fill/pallas_call | solution.py:92
  13.0 3.8 %collective-permute-start.7 = (bf16[8,4096]{1,0:T(8,128)(2,1)S(1)}, bf16[8,4096]{1,0:T(8,128)(2,1)S(1)}, u32[]{:S(2)}, u32[]{:S(2)}) collective-permute-start(bf16[8,4096]{1,0:T(8,128)(2,1)S(1)} %copy-done), channel_id=1, source_target_pairs={{0,16},{2,18},{4,20},{6,22},{8,24},{10,26},{12,28},{14,30},{16,0},... | collective-permute-start | bytes 196616 | tf_op jit(solution)/shard_map/ppermute | solution.py:38
  16.7 1.1 %collective-permute-start.2 = (bf16[32,4096]{1,0:T(8,128)(2,1)S(1)}, bf16[32,4096]{1,0:T(8,128)(2,1)S(1)}, u32[]{:S(2)}, u32[]{:S(2)}) collective-permute-start(bf16[32,4096]{1,0:T(8,128)(2,1)S(1)} %pad_maximum_fusion.refs_0_.refs_4_), channel_id=1, source_target_pairs={{0,4},{2,6},{4,0},{6,2},{8,12},{10,14},{12,8},{14,10},{16,20},{18,... | collective-permute-start | bytes 786440 | tf_op jit(solution)/shard_map/ppermute | solution.py:38
  17.8 1.8 %collective-permute-done.7 = bf16[8,4096]{1,0:T(8,128)(2,1)S(1)} collective-permute-done((bf16[8,4096]{1,0:T(8,128)(2,1)S(1)}, bf16[8,4096]{1,0:T(8,128)(2,1)S(1)}, u32[]{:S(2)}, u32[]{:S(2)}) %collective-permute-start.7) | collective-permute-done | bytes 65568 | tf_op jit(solution)/shard_map/ppermute | solution.py:38
  19.7 3.3 %fill.5.refs_8_ = bf16[8,32,128,128]{3,2,1,0:T(8,128)(2,1)S(1)} custom-call(s32[1,1,192]{2,1,0:T(1,128)} %index.7, s32[1,1]{1,0:T(1,128)S(6)} %copy.18.refs_0_.count, bf16[1,1,192,128,128]{4,3,2,1,0:T(8,128)(2,1)} %source.5), custom_call_target="tpu_custom_call" | custom-call | bytes 6291456 | tf_op jit(solution)/shard_map/fill/pallas_call | solution.py:92
  23.1 0.8 %collective-permute-done.2.refs_1_.refs_5_ = bf16[32,4096]{1,0:T(8,128)(2,1)S(1)} collective-permute-done((bf16[32,4096]{1,0:T(8,128)(2,1)S(1)}, bf16[32,4096]{1,0:T(8,128)(2,1)S(1)}, u32[]{:S(2)}, u32[]{:S(2)}) %collective-permute-start.2) | collective-permute-done | bytes 262176 | tf_op jit(solution)/shard_map/ppermute | solution.py:38
  23.9 0.7 collective-permute-done.8
  24.7 1.2 %collective-permute-start.9 = (bf16[32,4096]{1,0:T(8,128)(2,1)S(1)}, bf16[32,4096]{1,0:T(8,128)(2,1)S(1)}, u32[]{:S(2)}, u32[]{:S(2)}) collective-permute-start(bf16[32,4096]{1,0:T(8,128)(2,1)S(1)} %pad_maximum_fusion.1.refs_0_), channel_id=1, source_target_pairs={{0,4},{2,6},{4,0},{6,2},{8,12},{10,14},{12,8},{14,10},{16,20},{18,... | collective-permute-start | bytes 786440 | tf_op jit(solution)/shard_map/ppermute | solution.py:38
  25.8 1.9 %gate_up.2 = (f32[4,128,256]{2,1,0:T(8,128)S(1)}, bf16[4,128,256]{2,1,0:T(8,128)(2,1)S(1)}) custom-call(bf16[32,4096]{1,0:T(8,128)(2,1)S(1)} %pad_maximum_fusion.refs_0_.refs_4_, bf16[32,4096]{1,0:T(8,128)(2,1)S(1)} %collective-permute-done.2.refs_1_.refs_5_, bf16[32,4096]{1,0:T(8,128)(2,1)S(1)} %collective-permute-done.3.refs_2_.refs_6_, ...), custom_call_target="tpu_custom_call" | custom-call | flops 1073741824 | bytes 8388608 | tf_op jit(solution)/shard_map/gate_up/pallas_call | solution.py:131
  27.7 1.9 %collective-permute-start.5 = (bf16[4,128,256]{2,1,0:T(8,128)(2,1)S(1)}, bf16[4,128,256]{2,1,0:T(8,128)(2,1)S(1)}, u32[]{:S(2)}, u32[]{:S(2)}) collective-permute-start(bf16[4,128,256]{2,1,0:T(8,128)(2,1)S(1)} %get-tuple-element.57), channel_id=1, source_target_pairs={{0,1},{1,0},{2,3},{3,2},{4,5},{5,4},{6,7},{7,6},{8,9},{9,8},{10,11... | collective-permute-start | bytes 786440 | tf_op jit(solution)/shard_map/ppermute | solution.py:38
  29.6 1.9 %gate_up.3 = (f32[4,128,256]{2,1,0:T(8,128)S(1)}, bf16[4,128,256]{2,1,0:T(8,128)(2,1)S(1)}) custom-call(bf16[32,4096]{1,0:T(8,128)(2,1)S(1)} %pad_maximum_fusion.refs_0_.refs_4_, bf16[32,4096]{1,0:T(8,128)(2,1)S(1)} %collective-permute-done.2.refs_1_.refs_5_, bf16[32,4096]{1,0:T(8,128)(2,1)S(1)} %collective-permute-done.3.refs_2_.refs_6_, ...), custom_call_target="tpu_custom_call" | custom-call | flops 1073741824 | bytes 8388608 | tf_op jit(solution)/shard_map/gate_up/pallas_call | solution.py:131
  31.4 1.3 %collective-permute-done.9.refs_1_ = bf16[32,4096]{1,0:T(8,128)(2,1)S(1)} collective-permute-done((bf16[32,4096]{1,0:T(8,128)(2,1)S(1)}, bf16[32,4096]{1,0:T(8,128)(2,1)S(1)}, u32[]{:S(2)}, u32[]{:S(2)}) %collective-permute-start.9) | collective-permute-done | bytes 262176 | tf_op jit(solution)/shard_map/ppermute | solution.py:38
  32.8 0.5 collective-permute-start.11
  33.3 1.3 %collective-permute-start.6 = (bf16[4,128,256]{2,1,0:T(8,128)(2,1)S(1)}, bf16[4,128,256]{2,1,0:T(8,128)(2,1)S(1)}, u32[]{:S(2)}, u32[]{:S(2)}) collective-permute-start(bf16[4,128,256]{2,1,0:T(8,128)(2,1)S(1)} %get-tuple-element.64), channel_id=1, source_target_pairs={{0,1},{1,0},{2,3},{3,2},{4,5},{5,4},{6,7},{7,6},{8,9},{9,8},{10,11... | collective-permute-start | bytes 786440 | tf_op jit(solution)/shard_map/ppermute | solution.py:38
  34.6 1.2 %collective-permute-done.5.refs_1_ = bf16[4,128,256]{2,1,0:T(8,128)(2,1)S(1)} collective-permute-done((bf16[4,128,256]{2,1,0:T(8,128)(2,1)S(1)}, bf16[4,128,256]{2,1,0:T(8,128)(2,1)S(1)}, u32[]{:S(2)}, u32[]{:S(2)}) %collective-permute-start.5) | collective-permute-done | bytes 262176 | tf_op jit(solution)/shard_map/ppermute | solution.py:38
  35.9 3.6 %d_hidden.1 = (f32[8,128,128]{2,1,0:T(8,128)S(1)}, bf16[8,128,128]{2,1,0:T(8,128)(2,1)S(1)}, bf16[32,128,128]{2,1,0:T(8,128)(2,1)S(1)}) custom-call(bf16[32,4096]{1,0:T(8,128)(2,1)S(1)} %pad_maximum_fusion.1.refs_0_, bf16[32,4096]{1,0:T(8,128)(2,1)S(1)} %collective-permute-done.9.refs_1_, bf16[32,4096]{1,0:T(8,128)(2,1)S(1)} %collective-permute-done.10.refs_2_, ...), custom_call_target="tpu_custom_call" | custom-call | flops 1073741824 | bytes 8388608 | tf_op jit(solution)/shard_map/d_hidden/pallas_call | solution.py:174
  39.5 2.0 %collective-permute-start.12 = (bf16[8,128,128]{2,1,0:T(8,128)(2,1)S(1)}, bf16[8,128,128]{2,1,0:T(8,128)(2,1)S(1)}, u32[]{:S(2)}, u32[]{:S(2)}) collective-permute-start(bf16[8,128,128]{2,1,0:T(8,128)(2,1)S(1)} %get-tuple-element.74), channel_id=1, source_target_pairs={{0,1},{1,0},{2,3},{3,2},{4,5},{5,4},{6,7},{7,6},{8,9},{9,8},{10,11... | collective-permute-start | bytes 786440 | tf_op jit(solution)/shard_map/ppermute | solution.py:38
  41.9 5.3 %down_grads.1 = bf16[192,128,128]{2,1,0:T(8,128)(2,1)} custom-call(s32[1,1,192]{2,1,0:T(1,128)} %index.7, s32[1,1]{1,0:T(1,128)S(6)} %copy.18.refs_0_.count, bf16[4,128,128]{2,1,0:T(8,128)(2,1)S(1)} %get-tuple-element.61.near, bf16[4,128,128]{2,1,0:T(8,128)(2,1)S(1)} %get-tuple-element.65.far, bf16[32,4096]{1,0:T(8,128)(2,1)S(1)} %pad_maximum_fusion.1.refs_0_, ...), custom_call_target="tpu_custom_call" | custom-call | flops 805306368 | bytes 6291456 | tf_op jit(solution)/shard_map/down_grads/pallas_call | solution.py:358
  47.3 4.7 %d_tokens.1 = (f32[64,4096]{1,0:T(8,128)S(1)}, bf16[64,4096]{1,0:T(8,128)(2,1)S(1)}, bf16[8,128,256]{2,1,0:T(8,128)(2,1)S(1)}) custom-call(f32[4,128,256]{2,1,0:T(8,128)S(1)} %get-tuple-element.58.refs_0_, f32[4,128,256]{2,1,0:T(8,128)S(1)} %get-tuple-element.71.refs_1_, f32[8,128,128]{2,1,0:T(8,128)S(1)} %get-tuple-element.73.refs_2_, ...), custom_call_target="tpu_custom_call" | custom-call | flops 2147483648 | bytes 16777216 | tf_op jit(solution)/shard_map/d_tokens/pallas_call | solution.py:227
  52.1 1.9 %collective-permute-done.13 = bf16[64,4096]{1,0:T(8,128)(2,1)S(1)} collective-permute-done((bf16[64,4096]{1,0:T(8,128)(2,1)S(1)}, bf16[64,4096]{1,0:T(8,128)(2,1)S(1)}, u32[]{:S(2)}, u32[]{:S(2)}) %collective-permute-start.13) | collective-permute-done | bytes 524320 | tf_op jit(solution)/shard_map/ppermute | solution.py:38
  54.1 1.2 %collective-permute-start.14 = (bf16[32,4096]{1,0:T(8,128)(2,1)S(1)}, bf16[32,4096]{1,0:T(8,128)(2,1)S(1)}, u32[]{:S(2)}, u32[]{:S(2)}) collective-permute-start(bf16[32,4096]{1,0:T(8,128)(2,1)S(1)} %slice.43), channel_id=1, source_target_pairs={{0,4},{2,6},{4,0},{6,2},{8,12},{10,14},{12,8},{14,10},{16,20},{18,... | collective-permute-start | bytes 786440 | tf_op jit(solution)/shard_map/ppermute | solution.py:38
  55.4 6.7 %gu_grads.2 = (bf16[192,128,128]{2,1,0:T(8,128)(2,1)}, bf16[192,128,128]{2,1,0:T(8,128)(2,1)}) custom-call(s32[1,1,192]{2,1,0:T(1,128)} %index.9, s32[1,1]{1,0:T(1,128)S(6)} %copy.17.count, bf16[8,128,256]{2,1,0:T(8,128)(2,1)S(1)} %get-tuple-element.86.d_pair, bf16[32,128,128]{2,1,0:T(8,128)(2,1)S(1)} %get-tuple-element.80.turned), custom_call_target="tpu_custom_call" | custom-call | flops 1073741824 | bytes 8388608 | tf_op jit(solution)/shard_map/gu_grads/pallas_call | solution.py:275
  62.6 3.0 %collective-permute-start.15 = (bf16[8,4096]{1,0:T(8,128)(2,1)S(1)}, bf16[8,4096]{1,0:T(8,128)(2,1)S(1)}, u32[]{:S(2)}, u32[]{:S(2)}) collective-permute-start(bf16[8,4096]{1,0:T(8,128)(2,1)S(1)} %get-tuple-element.83), channel_id=1, source_target_pairs={{0,16},{2,18},{4,20},{6,22},{8,24},{10,26},{12,28},{14,30},{16,0},... | collective-permute-start | bytes 196616 | tf_op jit(solution)/shard_map/ppermute | solution.py:38
  65.6 0.9 %collective-permute-start.16 = (bf16[8,4096]{1,0:T(8,128)(2,1)S(1)}, bf16[8,4096]{1,0:T(8,128)(2,1)S(1)}, u32[]{:S(2)}, u32[]{:S(2)}) collective-permute-start(bf16[8,4096]{1,0:T(8,128)(2,1)S(1)} %get-tuple-element.84), channel_id=1, source_target_pairs={{0,8},{2,10},{4,12},{6,14},{8,0},{10,2},{12,4},{14,6},{16,24},{18,... | collective-permute-start | bytes 196616 | tf_op jit(solution)/shard_map/ppermute | solution.py:38
  66.5 0.6 collective-permute-start.17
  67.1 3.9 %gu_grads.3 = (bf16[192,128,128]{2,1,0:T(8,128)(2,1)}, bf16[192,128,128]{2,1,0:T(8,128)(2,1)}) custom-call(s32[1,1,192]{2,1,0:T(1,128)} %index.9, s32[1,1]{1,0:T(1,128)S(6)} %copy.17.count, bf16[8,128,256]{2,1,0:T(8,128)(2,1)S(1)} %get-tuple-element.86.d_pair, ...), custom_call_target="tpu_custom_call", output_to_operand_aliasing={{0}: (4, {}), {1}: (5, {})} | custom-call | flops 536870912 | bytes 4194304 | tf_op jit(solution)/shard_map/gu_grads/pallas_call | solution.py:275
  71.1 1.5 %collective-permute-done.17 = bf16[8,4096]{1,0:T(8,128)(2,1)S(1)} collective-permute-done((bf16[8,4096]{1,0:T(8,128)(2,1)S(1)}, bf16[8,4096]{1,0:T(8,128)(2,1)S(1)}, u32[]{:S(2)}, u32[]{:S(2)}) %collective-permute-start.17) | collective-permute-done | bytes 65568 | tf_op jit(solution)/shard_map/ppermute | solution.py:38
  72.6 0.7 fusion.2
  (29 shorter events, 1.5 us)
Async XLA Ops:
  0.6 8.0 %collective-permute-start = (bf16[8,4096]{1,0:T(8,128)(2,1)}, bf16[8,4096]{1,0:T(8,128)(2,1)S(1)}, u32[]{:S(2)}, u32[]{:S(2)}) collective-permute-start(bf16[8,4096]{1,0:T(8,128)(2,1)} %param.9), channel_id=1, source_target_pairs={{0,16},{2,18},{4,20},{6,22},{8,24},{10,26},{12,28},{14,30},{16,0},... | collective-permute-start | bytes 196616 | tf_op jit(solution)/shard_map/ppermute | solution.py:38
  5.4 3.2 %copy-start.1 = (bf16[8,4096]{1,0:T(8,128)(2,1)S(1)}, bf16[8,4096]{1,0:T(8,128)(2,1)}, u32[]{:S(2)}) copy-start(bf16[8,4096]{1,0:T(8,128)(2,1)} %param.9) | copy-start | bytes 196612
  8.6 8.1 %collective-permute-start.1 = (bf16[16,4096]{1,0:T(8,128)(2,1)S(1)}, bf16[16,4096]{1,0:T(8,128)(2,1)S(1)}, u32[]{:S(2)}, u32[]{:S(2)}) collective-permute-start(bf16[16,4096]{1,0:T(8,128)(2,1)S(1)} %pad_maximum_fusion.2), channel_id=1, source_target_pairs={{0,8},{2,10},{4,12},{6,14},{8,0},{10,2},{12,4},{14,6},{16,24},{18,... | collective-permute-start | bytes 393224 | tf_op jit(solution)/shard_map/ppermute | solution.py:38
  10.5 2.4 %copy-start = (bf16[8,4096]{1,0:T(8,128)(2,1)S(1)}, bf16[8,4096]{1,0:T(8,128)(2,1)}, u32[]{:S(2)}) copy-start(bf16[8,4096]{1,0:T(8,128)(2,1)} %param.10) | copy-start | bytes 196612
  13.0 6.6 %collective-permute-start.7 = (bf16[8,4096]{1,0:T(8,128)(2,1)S(1)}, bf16[8,4096]{1,0:T(8,128)(2,1)S(1)}, u32[]{:S(2)}, u32[]{:S(2)}) collective-permute-start(bf16[8,4096]{1,0:T(8,128)(2,1)S(1)} %copy-done), channel_id=1, source_target_pairs={{0,16},{2,18},{4,20},{6,22},{8,24},{10,26},{12,28},{14,30},{16,0},... | collective-permute-start | bytes 196616 | tf_op jit(solution)/shard_map/ppermute | solution.py:38
  16.7 7.2 %collective-permute-start.2 = (bf16[32,4096]{1,0:T(8,128)(2,1)S(1)}, bf16[32,4096]{1,0:T(8,128)(2,1)S(1)}, u32[]{:S(2)}, u32[]{:S(2)}) collective-permute-start(bf16[32,4096]{1,0:T(8,128)(2,1)S(1)} %pad_maximum_fusion.refs_0_.refs_4_), channel_id=1, source_target_pairs={{0,4},{2,6},{4,0},{6,2},{8,12},{10,14},{12,8},{14,10},{16,20},{18,... | collective-permute-start | bytes 786440 | tf_op jit(solution)/shard_map/ppermute | solution.py:38
  19.6 5.0 %collective-permute-start.8 = (bf16[16,4096]{1,0:T(8,128)(2,1)S(1)}, bf16[16,4096]{1,0:T(8,128)(2,1)S(1)}, u32[]{:S(2)}, u32[]{:S(2)}) collective-permute-start(bf16[16,4096]{1,0:T(8,128)(2,1)S(1)} %pad_maximum_fusion.3), channel_id=1, source_target_pairs={{0,8},{2,10},{4,12},{6,14},{8,0},{10,2},{12,4},{14,6},{16,24},{18,... | collective-permute-start | bytes 393224 | tf_op jit(solution)/shard_map/ppermute | solution.py:38
  23.0 2.8 %collective-permute-start.3 = (bf16[32,4096]{1,0:T(8,128)(2,1)S(1)}, bf16[32,4096]{1,0:T(8,128)(2,1)S(1)}, u32[]{:S(2)}, u32[]{:S(2)}) collective-permute-start(bf16[32,4096]{1,0:T(8,128)(2,1)S(1)} %pad_maximum_fusion.refs_0_.refs_4_), channel_id=1, source_target_pairs={{0,2},{2,0},{4,6},{6,4},{8,10},{10,8},{12,14},{14,12},{16,18},{18,... | collective-permute-start | bytes 786440 | tf_op jit(solution)/shard_map/ppermute | solution.py:38
  23.9 1.9 %collective-permute-start.4 = (bf16[32,4096]{1,0:T(8,128)(2,1)S(1)}, bf16[32,4096]{1,0:T(8,128)(2,1)S(1)}, u32[]{:S(2)}, u32[]{:S(2)}) collective-permute-start(bf16[32,4096]{1,0:T(8,128)(2,1)S(1)} %collective-permute-done.2.refs_1_.refs_5_), channel_id=1, source_target_pairs={{0,2},{2,0},{4,6},{6,4},{8,10},{10,8},{12,14},{14,12},{16,18},{18,... | collective-permute-start | bytes 786440 | tf_op jit(solution)/shard_map/ppermute | solution.py:38
  24.7 8.1 %collective-permute-start.9 = (bf16[32,4096]{1,0:T(8,128)(2,1)S(1)}, bf16[32,4096]{1,0:T(8,128)(2,1)S(1)}, u32[]{:S(2)}, u32[]{:S(2)}) collective-permute-start(bf16[32,4096]{1,0:T(8,128)(2,1)S(1)} %pad_maximum_fusion.1.refs_0_), channel_id=1, source_target_pairs={{0,4},{2,6},{4,0},{6,2},{8,12},{10,14},{12,8},{14,10},{16,20},{18,... | collective-permute-start | bytes 786440 | tf_op jit(solution)/shard_map/ppermute | solution.py:38
  27.7 8.1 %collective-permute-start.5 = (bf16[4,128,256]{2,1,0:T(8,128)(2,1)S(1)}, bf16[4,128,256]{2,1,0:T(8,128)(2,1)S(1)}, u32[]{:S(2)}, u32[]{:S(2)}) collective-permute-start(bf16[4,128,256]{2,1,0:T(8,128)(2,1)S(1)} %get-tuple-element.57), channel_id=1, source_target_pairs={{0,1},{1,0},{2,3},{3,2},{4,5},{5,4},{6,7},{7,6},{8,9},{9,8},{10,11... | collective-permute-start | bytes 786440 | tf_op jit(solution)/shard_map/ppermute | solution.py:38
  32.8 3.1 %collective-permute-start.10 = (bf16[32,4096]{1,0:T(8,128)(2,1)S(1)}, bf16[32,4096]{1,0:T(8,128)(2,1)S(1)}, u32[]{:S(2)}, u32[]{:S(2)}) collective-permute-start(bf16[32,4096]{1,0:T(8,128)(2,1)S(1)} %pad_maximum_fusion.1.refs_0_), channel_id=1, source_target_pairs={{0,2},{2,0},{4,6},{6,4},{8,10},{10,8},{12,14},{14,12},{16,18},{18,... | collective-permute-start | bytes 786440 | tf_op jit(solution)/shard_map/ppermute | solution.py:38
  32.8 3.1 %collective-permute-start.11 = (bf16[32,4096]{1,0:T(8,128)(2,1)S(1)}, bf16[32,4096]{1,0:T(8,128)(2,1)S(1)}, u32[]{:S(2)}, u32[]{:S(2)}) collective-permute-start(bf16[32,4096]{1,0:T(8,128)(2,1)S(1)} %collective-permute-done.9.refs_1_), channel_id=1, source_target_pairs={{0,2},{2,0},{4,6},{6,4},{8,10},{10,8},{12,14},{14,12},{16,18},{18,... | collective-permute-start | bytes 786440 | tf_op jit(solution)/shard_map/ppermute | solution.py:38
  33.3 8.5 %collective-permute-start.6 = (bf16[4,128,256]{2,1,0:T(8,128)(2,1)S(1)}, bf16[4,128,256]{2,1,0:T(8,128)(2,1)S(1)}, u32[]{:S(2)}, u32[]{:S(2)}) collective-permute-start(bf16[4,128,256]{2,1,0:T(8,128)(2,1)S(1)} %get-tuple-element.64), channel_id=1, source_target_pairs={{0,1},{1,0},{2,3},{3,2},{4,5},{5,4},{6,7},{7,6},{8,9},{9,8},{10,11... | collective-permute-start | bytes 786440 | tf_op jit(solution)/shard_map/ppermute | solution.py:38
  39.5 7.8 %collective-permute-start.12 = (bf16[8,128,128]{2,1,0:T(8,128)(2,1)S(1)}, bf16[8,128,128]{2,1,0:T(8,128)(2,1)S(1)}, u32[]{:S(2)}, u32[]{:S(2)}) collective-permute-start(bf16[8,128,128]{2,1,0:T(8,128)(2,1)S(1)} %get-tuple-element.74), channel_id=1, source_target_pairs={{0,1},{1,0},{2,3},{3,2},{4,5},{5,4},{6,7},{7,6},{8,9},{9,8},{10,11... | collective-permute-start | bytes 786440 | tf_op jit(solution)/shard_map/ppermute | solution.py:38
  52.0 2.0 %collective-permute-start.13 = (bf16[64,4096]{1,0:T(8,128)(2,1)S(1)}, bf16[64,4096]{1,0:T(8,128)(2,1)S(1)}, u32[]{:S(2)}, u32[]{:S(2)}) collective-permute-start(bf16[64,4096]{1,0:T(8,128)(2,1)S(1)} %get-tuple-element.76), channel_id=1, source_target_pairs={{0,2},{2,0},{4,6},{6,4},{8,10},{10,8},{12,14},{14,12},{16,18},{18,... | collective-permute-start | bytes 1572872 | tf_op jit(solution)/shard_map/ppermute | solution.py:38
  54.1 8.4 %collective-permute-start.14 = (bf16[32,4096]{1,0:T(8,128)(2,1)S(1)}, bf16[32,4096]{1,0:T(8,128)(2,1)S(1)}, u32[]{:S(2)}, u32[]{:S(2)}) collective-permute-start(bf16[32,4096]{1,0:T(8,128)(2,1)S(1)} %slice.43), channel_id=1, source_target_pairs={{0,4},{2,6},{4,0},{6,2},{8,12},{10,14},{12,8},{14,10},{16,20},{18,... | collective-permute-start | bytes 786440 | tf_op jit(solution)/shard_map/ppermute | solution.py:38
  62.6 8.5 %collective-permute-start.15 = (bf16[8,4096]{1,0:T(8,128)(2,1)S(1)}, bf16[8,4096]{1,0:T(8,128)(2,1)S(1)}, u32[]{:S(2)}, u32[]{:S(2)}) collective-permute-start(bf16[8,4096]{1,0:T(8,128)(2,1)S(1)} %get-tuple-element.83), channel_id=1, source_target_pairs={{0,16},{2,18},{4,20},{6,22},{8,24},{10,26},{12,28},{14,30},{16,0},... | collective-permute-start | bytes 196616 | tf_op jit(solution)/shard_map/ppermute | solution.py:38
  65.6 5.5 %collective-permute-start.16 = (bf16[8,4096]{1,0:T(8,128)(2,1)S(1)}, bf16[8,4096]{1,0:T(8,128)(2,1)S(1)}, u32[]{:S(2)}, u32[]{:S(2)}) collective-permute-start(bf16[8,4096]{1,0:T(8,128)(2,1)S(1)} %get-tuple-element.84), channel_id=1, source_target_pairs={{0,8},{2,10},{4,12},{6,14},{8,0},{10,2},{12,4},{14,6},{16,24},{18,... | collective-permute-start | bytes 196616 | tf_op jit(solution)/shard_map/ppermute | solution.py:38
  66.5 6.1 %collective-permute-start.17 = (bf16[8,4096]{1,0:T(8,128)(2,1)S(1)}, bf16[8,4096]{1,0:T(8,128)(2,1)S(1)}, u32[]{:S(2)}, u32[]{:S(2)}) collective-permute-start(bf16[8,4096]{1,0:T(8,128)(2,1)S(1)} %get-tuple-element.85), channel_id=1, source_target_pairs={{0,24},{2,26},{4,28},{6,30},{8,16},{10,18},{12,20},{14,22},{16,8},... | collective-permute-start | bytes 196616 | tf_op jit(solution)/shard_map/ppermute | solution.py:38

commit v9 on v8

--- a/solution.py
+++ b/solution.py
@@ -109,9 +109,7 @@
     *pieces, gate_w, up_w, own, send = refs
     d_blocks, _, block, _ = gate_w.shape
     x = stack(pieces)
-
-    @pl.loop(0, own.shape[0])
-    def _(c):
+    for c in range(own.shape[0]):
         weights = jnp.concatenate(
             [
                 gate_w[:, first + c].reshape(d_blocks * block, block),
@@ -139,51 +137,65 @@
     )(*pieces, resident(gate_w), resident(up_w))
 
 
-def d_hidden_body(pieces_count, *refs):
-    y_pieces, x_pieces = refs[:pieces_count], refs[pieces_count : 2 * pieces_count]
-    down_w, own, send, turned = refs[2 * pieces_count :]
+def d_hidden_body(group, *refs):
+    *pieces, down_w, own, send, turned = refs
     f_blocks, d_blocks, block, _ = down_w.shape
-    y = stack(y_pieces)
-
-    @pl.loop(0, f_blocks // 2)
-    def _(pair):
+    for d in range(d_blocks):
+        at = slice(d * block, (d + 1) * block)
+        turned[at, :] = jnp.concatenate([piece[:, at] for piece in pieces], axis=0).T
+    y = turned[...]
+    for f in range(0, f_blocks, group):
         weights = jnp.concatenate(
             [
-                down_w[pl.ds(2 * pair, 2), d].reshape(2 * block, block)
+                down_w[f : f + group, d].reshape(group * block, block)
                 for d in range(d_blocks)
             ],
             axis=1,
         )
-        result = lax.dot_general(
-            y, weights, (((1,), (1,)), ((), ())), preferred_element_type=F32
-        )
-        for half in range(2):
-            part = result[:, half * block : (half + 1) * block]
-            own[2 * pair + half] = part
-            send[2 * pair + half] = part.astype(BF16)
-
-    for d in range(d_blocks):
-        columns = slice(d * block, (d + 1) * block)
-        turned[d] = jnp.concatenate([piece[:, columns] for piece in x_pieces], axis=0).T
-
-
-def d_hidden(y_pieces, x_pieces, down_w):
+        result = jnp.dot(weights, y, preferred_element_type=F32).T
+        for side in range(group):
+            part = result[:, side * block : (side + 1) * block]
+            own[f + side] = part
+            send[f + side] = part.astype(BF16)
+
+
+def d_hidden(pieces, down_w):
     f_blocks, d_blocks, block, _ = down_w.shape
-    tokens = sum(piece.shape[0] for piece in y_pieces)
+    tokens = sum(piece.shape[0] for piece in pieces)
     shape = (f_blocks, tokens, block)
-    return pl.pallas_call(
-        functools.partial(d_hidden_body, len(y_pieces)),
-        out_shape=(
-            jax.ShapeDtypeStruct(shape, F32),
-            jax.ShapeDtypeStruct(shape, BF16),
-            jax.ShapeDtypeStruct((d_blocks, block, tokens), BF16),
-        ),
-        in_specs=[WHOLE] * (2 * len(y_pieces) + 1),
-        out_specs=(WHOLE,) * 3,
+    group = max(n for n in (1, 2, 4) if f_blocks % n == 0)
+    return pl.pallas_call(
+        functools.partial(d_hidden_body, group),
+        out_shape=(jax.ShapeDtypeStruct(shape, F32), jax.ShapeDtypeStruct(shape, BF16)),
+        in_specs=[WHOLE] * (len(pieces) + 1),
+        out_specs=(WHOLE,) * 2,
+        scratch_shapes=[pltpu.VMEM((d_blocks * block, tokens), BF16)],
         compiler_params=params(),
         cost_estimate=cost(2 * tokens * down_w.size, 2 * down_w.size),
         name="d_hidden",
-    )(*y_pieces, *x_pieces, resident(down_w))
+    )(*pieces, resident(down_w))
+
+
+def turn_body(*refs):
+    *pieces, turned = refs
+    block = turned.shape[1]
+    for d in range(turned.shape[0]):
+        columns = slice(d * block, (d + 1) * block)
+        turned[d] = jnp.concatenate([piece[:, columns] for piece in pieces], axis=0).T
+
+
+def turn(pieces, block):
+    tokens = sum(piece.shape[0] for piece in pieces)
+    width = pieces[0].shape[1]
+    return pl.pallas_call(
+        turn_body,
+        out_shape=jax.ShapeDtypeStruct((width // block, block, tokens), BF16),
+        in_specs=[WHOLE] * len(pieces),
+        out_specs=WHOLE,
+        compiler_params=params(),
+        cost_estimate=cost(0, 4 * tokens * width),
+        name="turn",
+    )(*pieces)
 
 
 def d_tokens_body(group, *refs):
@@ -389,37 +401,38 @@
 
     flips = [chips >> hop for hop in range(1, chips.bit_length())]
     vals = (gate_vals, up_vals)
-    x, index = tokens, gu_index
+    x, y, index = tokens, cotangent, gu_index
     weights = []
     for hop, flip in enumerate(flips):
         if hop > 0:
             x = jnp.concatenate([x, x_recv], axis=0)
+            y = jnp.concatenate([y, y_recv], axis=0)
             x, weights, index = lax.optimization_barrier((x, weights, index))
         x_recv = swap(x, "wide", wide, 2 * flip)
         if hop < 2:
             early = (down_count,) if hop == 1 else ()
             weights.append(fill(index, gu_count, vals[hop], d_blocks, f_blocks, early))
-        if hop == 1:
-            y, _ = lax.optimization_barrier((cotangent, weights[1]))
+        if hop < len(flips) - 1:
+            y, _ = lax.optimization_barrier((y, x_recv))
+            y_recv = swap(y, "wide", wide, 2 * flip)
     index, _ = lax.optimization_barrier((down_index, x))
     down_w = fill(index, down_count, down_vals, f_blocks, d_blocks)
-    for flip in flips[:-1]:
-        y = jnp.concatenate([y, swap(y, "wide", wide, 2 * flip)], axis=0)
     x, down_w = lax.optimization_barrier((x, down_w))
     x_pieces = [x, x_recv, swap(x, "wide", wide, 1), swap(x_recv, "wide", wide, 1)]
-    y, _ = lax.optimization_barrier((y, x_recv))
-    y_recv = swap(y, "wide", wide, 2 * flips[-1])
 
     near_own, near_send = gate_up(x_pieces, *weights, 0)
     near_recv = exchange(near_send)
-    late, _ = lax.optimization_barrier((x, near_send))
-    far_own, far_send = gate_up([late, *x_pieces[1:]], *weights, 1)
+    late, y, _ = lax.optimization_barrier((x_pieces, y, near_send))
+    y_recv = swap(y, "wide", wide, 2 * flips[-1])
+    far_own, far_send = gate_up(late, *weights, 1)
     far_recv = exchange(far_send)
-    y, y_recv, _ = lax.optimization_barrier((y, y_recv, far_send))
-    y_pieces = [y, y_recv, swap(y, "wide", wide, 1), swap(y_recv, "wide", wide, 1)]
+    late, _ = lax.optimization_barrier((x_pieces, far_send))
+    turned = turn(late, block)
     near_hidden, near_coef = activate(near_own, near_recv)
-    down_w, near_hidden = lax.optimization_barrier((down_w, near_hidden))
-    dh_own, dh_send, turned = d_hidden(y_pieces, x_pieces, down_w)
+    y = jnp.concatenate([y, y_recv], axis=0)
+    y, turned, near_hidden = lax.optimization_barrier((y, turned, near_hidden))
+    y_pieces = [y, swap(y, "wide", wide, 1)]
+    dh_own, dh_send = d_hidden(y_pieces, down_w)
     dh_recv = exchange(dh_send)
     far_hidden, far_coef = activate(far_own, far_recv)
     down_grad = down_grads(down_index, down_count, y_pieces, near_hidden, far_hidden, slots)

time: 73.6 us -> 76.3 us (1.037)
  waiting for transfers between devices: 10.7 us -> 14.6 us
  starting transfers between devices: 23.1 us -> 22.2 us
    ppermute x18 -> x17, waiting for transfers between devices: 10.7 us -> 14.6 us  [swap(): return lax.ppermute(array, axis, [(i, i ^ flip) for i in range(size)])]
    pallas_call x2, Pallas kernels: 3.73 us -> 2.5 us  [gate_up(): pl.pallas_call(functools.partial(gate_up_body, half * f_blocks // 2), out...]
    pallas_call x3, Pallas kernels: 8.18 us -> 9.32 us  [fill(): pl.pallas_call(fill_body, out_shape=pltpu.VMEM((outer, inner, block, bloc...]
    ppermute x18 -> x17, starting transfers between devices: 23.1 us -> 22.2 us  [swap(): return lax.ppermute(array, axis, [(i, i ^ flip) for i in range(size)])]
    pallas_call x1 -> x2, Pallas kernels: 3.6 us -> 2.94 us  [the longest x1 2.62 us: d_hidden(): pl.pallas_call(functools.partial(d_hidden_body, group), out_shape=(jax.Sh...]
  transfers between devices with their start and end apart: 18 -> 17, of which waited for: 10 -> 8; matrix products, arithmetic and copies ran while one was open for 0% -> 0% of each run, Pallas kernels for 43% -> 39%
where the time goes in v9:
time: 76.3 us; the launch traced here: 75.8 us
  Pallas kernels  35.8 us (47%)
  starting transfers between devices  22.2 us (29%)
  waiting for transfers between devices  14.6 us (19%)
  between operations  2.21 us (3%)
  other arithmetic  0.9 us (1%)
    ppermute x17, starting transfers between devices, swap(): return lax.ppermute(array, axis, [(i, i ^ flip) for i in range(size)])  22.2 us
    ppermute x17, waiting for transfers between devices, swap(): return lax.ppermute(array, axis, [(i, i ^ flip) for i in range(size)])  14.6 us
    pallas_call x2, Pallas kernels, gu_grads(): pl.pallas_call(functools.partial(gu_grad_body, first, len(before)), out_s...  10.6 us
    pallas_call x3, Pallas kernels, fill(): pl.pallas_call(fill_body, out_shape=pltpu.VMEM((outer, inner, block, bloc...  9.32 us
    pallas_call x1, Pallas kernels, down_grads(): pl.pallas_call(down_grad_body, out_shape=jax.ShapeDtypeStruct((slots, blo...  5.52 us
    pallas_call x1, Pallas kernels, d_tokens_part(): pl.pallas_call(functools.partial(d_tokens_body, group), out_shape=(jax.Sh...  4.7 us
    pallas_call x1, Pallas kernels, d_hidden(): pl.pallas_call(functools.partial(d_hidden_body, group), out_shape=(jax.Sh...  2.62 us
    pallas_call x2, Pallas kernels, gate_up(): pl.pallas_call(functools.partial(gate_up_body, half * f_blocks // 2), out...  2.5 us
  transfers between devices with their start and end apart: 17, of which 8 were waited for; matrix products, arithmetic and copies ran while one was open for 0% of the time, Pallas kernels for 39%

profile of v9, /device:TPU:0, one launch (start us, length us, event | category | flops | bytes accessed | tf_op | source)
XLA Modules:
  0.0 75.8 jit_solution(14476576686848744748)
XLA Ops:
  0.6 4.1 %collective-permute-start = (bf16[8,4096]{1,0:T(8,128)(2,1)}, bf16[8,4096]{1,0:T(8,128)(2,1)S(1)}, u32[]{:S(2)}, u32[]{:S(2)}) collective-permute-start(bf16[8,4096]{1,0:T(8,128)(2,1)} %param.9), channel_id=1, source_target_pairs={{0,16},{2,18},{4,20},{6,22},{8,24},{10,26},{12,28},{14,30},{16,0},... | collective-permute-start | bytes 196616 | tf_op jit(solution)/shard_map/ppermute | solution.py:38
  5.4 3.2 %fill.3.refs_4_ = bf16[32,8,128,128]{3,2,1,0:T(8,128)(2,1)S(1)} custom-call(s32[1,1,192]{2,1,0:T(1,128)} %index.9, s32[1,1]{1,0:T(1,128)S(6)} %copy.17.count, bf16[1,1,192,128,128]{4,3,2,1,0:T(8,128)(2,1)} %source.3), custom_call_target="tpu_custom_call" | custom-call | bytes 6291456 | tf_op jit(solution)/shard_map/fill/pallas_call | solution.py:92
  8.7 1.3 %collective-permute-start.1 = (bf16[16,4096]{1,0:T(8,128)(2,1)S(1)}, bf16[16,4096]{1,0:T(8,128)(2,1)S(1)}, u32[]{:S(2)}, u32[]{:S(2)}) collective-permute-start(bf16[16,4096]{1,0:T(8,128)(2,1)S(1)} %pad_maximum_fusion.3), channel_id=1, source_target_pairs={{0,8},{2,10},{4,12},{6,14},{8,0},{10,2},{12,4},{14,6},{16,24},{18,... | collective-permute-start | bytes 393224 | tf_op jit(solution)/shard_map/ppermute | solution.py:38
  10.6 2.7 %collective-permute-start.6 = (bf16[8,4096]{1,0:T(8,128)(2,1)S(1)}, bf16[8,4096]{1,0:T(8,128)(2,1)S(1)}, u32[]{:S(2)}, u32[]{:S(2)}) collective-permute-start(bf16[8,4096]{1,0:T(8,128)(2,1)S(1)} %copy-done.1), channel_id=1, source_target_pairs={{0,16},{2,18},{4,20},{6,22},{8,24},{10,26},{12,28},{14,30},{16,0},... | collective-permute-start | bytes 196616 | tf_op jit(solution)/shard_map/ppermute | solution.py:38
  13.4 3.2 %fill.4.refs_5_ = bf16[32,8,128,128]{3,2,1,0:T(8,128)(2,1)S(1)} custom-call(s32[1,1,192]{2,1,0:T(1,128)} %index.9, s32[1,1]{1,0:T(1,128)S(6)} %copy.17.count, bf16[1,1,192,128,128]{4,3,2,1,0:T(8,128)(2,1)} %source.4, s32[1,1]{1,0:T(1,128)S(6)} %copy.18.refs_0_.count), custom_call_target="tpu_custom_call" | custom-call | bytes 6291456 | tf_op jit(solution)/shard_map/fill/pallas_call | solution.py:92
  16.6 1.6 %collective-permute-start.2 = (bf16[32,4096]{1,0:T(8,128)(2,1)S(1)}, bf16[32,4096]{1,0:T(8,128)(2,1)S(1)}, u32[]{:S(2)}, u32[]{:S(2)}) collective-permute-start(bf16[32,4096]{1,0:T(8,128)(2,1)S(1)} %pad_maximum_fusion.1.refs_0_), channel_id=1, source_target_pairs={{0,4},{2,6},{4,0},{6,2},{8,12},{10,14},{12,8},{14,10},{16,20},{18,... | collective-permute-start | bytes 786440 | tf_op jit(solution)/shard_map/ppermute | solution.py:38
  18.3 2.9 %fill.5.refs_2_ = bf16[8,32,128,128]{3,2,1,0:T(8,128)(2,1)S(1)} custom-call(s32[1,1,192]{2,1,0:T(1,128)} %index.7, s32[1,1]{1,0:T(1,128)S(6)} %copy.18.refs_0_.count, bf16[1,1,192,128,128]{4,3,2,1,0:T(8,128)(2,1)} %source.5), custom_call_target="tpu_custom_call" | custom-call | bytes 6291456 | tf_op jit(solution)/shard_map/fill/pallas_call | solution.py:92
  21.3 2.2 %collective-permute-done.2.refs_1_ = bf16[32,4096]{1,0:T(8,128)(2,1)S(1)} collective-permute-done((bf16[32,4096]{1,0:T(8,128)(2,1)S(1)}, bf16[32,4096]{1,0:T(8,128)(2,1)S(1)}, u32[]{:S(2)}, u32[]{:S(2)}) %collective-permute-start.2) | collective-permute-done | bytes 262176 | tf_op jit(solution)/shard_map/ppermute | solution.py:38
  23.5 1.5 %collective-permute-done.4.refs_3_ = bf16[32,4096]{1,0:T(8,128)(2,1)S(1)} collective-permute-done((bf16[32,4096]{1,0:T(8,128)(2,1)S(1)}, bf16[32,4096]{1,0:T(8,128)(2,1)S(1)}, u32[]{:S(2)}, u32[]{:S(2)}) %collective-permute-start.4) | collective-permute-done | bytes 262176 | tf_op jit(solution)/shard_map/ppermute | solution.py:38
  25.0 1.3 %gate_up.2 = (f32[4,128,256]{2,1,0:T(8,128)S(1)}, bf16[4,128,256]{2,1,0:T(8,128)(2,1)S(1)}) custom-call(bf16[32,4096]{1,0:T(8,128)(2,1)S(1)} %pad_maximum_fusion.1.refs_0_, bf16[32,4096]{1,0:T(8,128)(2,1)S(1)} %collective-permute-done.2.refs_1_, bf16[32,4096]{1,0:T(8,128)(2,1)S(1)} %collective-permute-done.3.refs_2_, ...), custom_call_target="tpu_custom_call" | custom-call | flops 1073741824 | bytes 8388608 | tf_op jit(solution)/shard_map/gate_up/pallas_call | solution.py:129
  26.3 1.8 %collective-permute-start.8 = (bf16[32,4096]{1,0:T(8,128)(2,1)S(1)}, bf16[32,4096]{1,0:T(8,128)(2,1)S(1)}, u32[]{:S(2)}, u32[]{:S(2)}) collective-permute-start(bf16[32,4096]{1,0:T(8,128)(2,1)S(1)} %pad_maximum_fusion.2), channel_id=1, source_target_pairs={{0,4},{2,6},{4,0},{6,2},{8,12},{10,14},{12,8},{14,10},{16,20},{18,... | collective-permute-start | bytes 786440 | tf_op jit(solution)/shard_map/ppermute | solution.py:38
  28.1 1.9 %collective-permute-start.5 = (bf16[4,128,256]{2,1,0:T(8,128)(2,1)S(1)}, bf16[4,128,256]{2,1,0:T(8,128)(2,1)S(1)}, u32[]{:S(2)}, u32[]{:S(2)}) collective-permute-start(bf16[4,128,256]{2,1,0:T(8,128)(2,1)S(1)} %get-tuple-element.63), channel_id=1, source_target_pairs={{0,1},{1,0},{2,3},{3,2},{4,5},{5,4},{6,7},{7,6},{8,9},{9,8},{10,11... | collective-permute-start | bytes 786440 | tf_op jit(solution)/shard_map/ppermute | solution.py:38
  30.0 1.3 %gate_up.3 = (f32[4,128,256]{2,1,0:T(8,128)S(1)}, bf16[4,128,256]{2,1,0:T(8,128)(2,1)S(1)}) custom-call(bf16[32,4096]{1,0:T(8,128)(2,1)S(1)} %pad_maximum_fusion.1.refs_0_, bf16[32,4096]{1,0:T(8,128)(2,1)S(1)} %collective-permute-done.2.refs_1_, bf16[32,4096]{1,0:T(8,128)(2,1)S(1)} %collective-permute-done.3.refs_2_, ...), custom_call_target="tpu_custom_call" | custom-call | flops 1073741824 | bytes 8388608 | tf_op jit(solution)/shard_map/gate_up/pallas_call | solution.py:129
  31.3 0.3 turn.1.turned
  31.6 3.1 %collective-permute-done.8 = bf16[32,4096]{1,0:T(8,128)(2,1)S(1)} collective-permute-done((bf16[32,4096]{1,0:T(8,128)(2,1)S(1)}, bf16[32,4096]{1,0:T(8,128)(2,1)S(1)}, u32[]{:S(2)}, u32[]{:S(2)}) %collective-permute-start.8) | collective-permute-done | bytes 262176 | tf_op jit(solution)/shard_map/ppermute | solution.py:38
  34.8 1.6 %collective-permute-done.5.refs_1_ = bf16[4,128,256]{2,1,0:T(8,128)(2,1)S(1)} collective-permute-done((bf16[4,128,256]{2,1,0:T(8,128)(2,1)S(1)}, bf16[4,128,256]{2,1,0:T(8,128)(2,1)S(1)}, u32[]{:S(2)}, u32[]{:S(2)}) %collective-permute-start.5) | collective-permute-done | bytes 262176 | tf_op jit(solution)/shard_map/ppermute | solution.py:38
  36.3 0.1 activate.2
  36.5 1.8 %collective-permute-start.9 = (bf16[4,128,256]{2,1,0:T(8,128)(2,1)S(1)}, bf16[4,128,256]{2,1,0:T(8,128)(2,1)S(1)}, u32[]{:S(2)}, u32[]{:S(2)}) collective-permute-start(bf16[4,128,256]{2,1,0:T(8,128)(2,1)S(1)} %get-tuple-element.72), channel_id=1, source_target_pairs={{0,1},{1,0},{2,3},{3,2},{4,5},{5,4},{6,7},{7,6},{8,9},{9,8},{10,11... | collective-permute-start | bytes 786440 | tf_op jit(solution)/shard_map/ppermute | solution.py:38
  38.4 2.6 %d_hidden.1 = (f32[8,128,128]{2,1,0:T(8,128)S(1)}, bf16[8,128,128]{2,1,0:T(8,128)(2,1)S(1)}) custom-call(bf16[64,4096]{1,0:T(8,128)(2,1)S(1)} %pad_maximum_fusion.refs_0_, bf16[64,4096]{1,0:T(8,128)(2,1)S(1)} %collective-permute-done.10.refs_1_, bf16[8,32,128,128]{3,2,1,0:T(8,128)(2,1)S(1)} %fill.5.refs_2_), custom_call_target="tpu_custom_call" | custom-call | flops 1073741824 | bytes 8388608 | tf_op jit(solution)/shard_map/d_hidden/pallas_call | solution.py:167
  41.0 1.8 %collective-permute-start.11 = (bf16[8,128,128]{2,1,0:T(8,128)(2,1)S(1)}, bf16[8,128,128]{2,1,0:T(8,128)(2,1)S(1)}, u32[]{:S(2)}, u32[]{:S(2)}) collective-permute-start(bf16[8,128,128]{2,1,0:T(8,128)(2,1)S(1)} %get-tuple-element.86), channel_id=1, source_target_pairs={{0,1},{1,0},{2,3},{3,2},{4,5},{5,4},{6,7},{7,6},{8,9},{9,8},{10,11... | collective-permute-start | bytes 786440 | tf_op jit(solution)/shard_map/ppermute | solution.py:38
  42.8 2.9 %collective-permute-done.9.refs_1_ = bf16[4,128,256]{2,1,0:T(8,128)(2,1)S(1)} collective-permute-done((bf16[4,128,256]{2,1,0:T(8,128)(2,1)S(1)}, bf16[4,128,256]{2,1,0:T(8,128)(2,1)S(1)}, u32[]{:S(2)}, u32[]{:S(2)}) %collective-permute-start.9) | collective-permute-done | bytes 262176 | tf_op jit(solution)/shard_map/ppermute | solution.py:38
  45.7 0.1 activate.3
  45.8 5.5 %down_grads.1 = bf16[192,128,128]{2,1,0:T(8,128)(2,1)} custom-call(s32[1,1,192]{2,1,0:T(1,128)} %index.7, s32[1,1]{1,0:T(1,128)S(6)} %copy.18.refs_0_.count, bf16[4,128,128]{2,1,0:T(8,128)(2,1)S(1)} %get-tuple-element.78.near, bf16[4,128,128]{2,1,0:T(8,128)(2,1)S(1)} %get-tuple-element.80.far, bf16[64,4096]{1,0:T(8,128)(2,1)S(1)} %pad_maximum_fusion.refs_0_, ...), custom_call_target="tpu_custom_call" | custom-call | flops 805306368 | bytes 6291456 | tf_op jit(solution)/shard_map/down_grads/pallas_call | solution.py:370
  51.4 4.7 %d_tokens.1 = (f32[64,4096]{1,0:T(8,128)S(1)}, bf16[64,4096]{1,0:T(8,128)(2,1)S(1)}, bf16[8,128,256]{2,1,0:T(8,128)(2,1)S(1)}) custom-call(f32[4,128,256]{2,1,0:T(8,128)S(1)} %get-tuple-element.64.refs_0_, f32[4,128,256]{2,1,0:T(8,128)S(1)} %get-tuple-element.83.refs_1_, f32[8,128,128]{2,1,0:T(8,128)S(1)} %get-tuple-element.85.refs_2_, ...), custom_call_target="tpu_custom_call" | custom-call | flops 2147483648 | bytes 16777216 | tf_op jit(solution)/shard_map/d_tokens/pallas_call | solution.py:239
  56.2 1.9 %collective-permute-done.12 = bf16[64,4096]{1,0:T(8,128)(2,1)S(1)} collective-permute-done((bf16[64,4096]{1,0:T(8,128)(2,1)S(1)}, bf16[64,4096]{1,0:T(8,128)(2,1)S(1)}, u32[]{:S(2)}, u32[]{:S(2)}) %collective-permute-start.12) | collective-permute-done | bytes 524320 | tf_op jit(solution)/shard_map/ppermute | solution.py:38
  58.2 0.4 collective-permute-start.13
  58.6 6.7 %gu_grads.2 = (bf16[192,128,128]{2,1,0:T(8,128)(2,1)}, bf16[192,128,128]{2,1,0:T(8,128)(2,1)}) custom-call(s32[1,1,192]{2,1,0:T(1,128)} %index.9, s32[1,1]{1,0:T(1,128)S(6)} %copy.17.count, bf16[8,128,256]{2,1,0:T(8,128)(2,1)S(1)} %get-tuple-element.98.d_pair, bf16[32,128,128]{2,1,0:T(8,128)(2,1)S(1)} %turn.1.turned), custom_call_target="tpu_custom_call" | custom-call | flops 1073741824 | bytes 8388608 | tf_op jit(solution)/shard_map/gu_grads/pallas_call | solution.py:287
  65.3 1.3 %collective-permute-done.13 = bf16[32,4096]{1,0:T(8,128)(2,1)S(1)} collective-permute-done((bf16[32,4096]{1,0:T(8,128)(2,1)S(1)}, bf16[32,4096]{1,0:T(8,128)(2,1)S(1)}, u32[]{:S(2)}, u32[]{:S(2)}) %collective-permute-start.13) | collective-permute-done | bytes 262176 | tf_op jit(solution)/shard_map/ppermute | solution.py:38
  66.8 1.0 %collective-permute-start.15 = (bf16[8,4096]{1,0:T(8,128)(2,1)S(1)}, bf16[8,4096]{1,0:T(8,128)(2,1)S(1)}, u32[]{:S(2)}, u32[]{:S(2)}) collective-permute-start(bf16[8,4096]{1,0:T(8,128)(2,1)S(1)} %get-tuple-element.96), channel_id=1, source_target_pairs={{0,8},{2,10},{4,12},{6,14},{8,0},{10,2},{12,4},{14,6},{16,24},{18,... | collective-permute-start | bytes 196616 | tf_op jit(solution)/shard_map/ppermute | solution.py:38
  67.8 3.3 %collective-permute-start.16 = (bf16[8,4096]{1,0:T(8,128)(2,1)S(1)}, bf16[8,4096]{1,0:T(8,128)(2,1)S(1)}, u32[]{:S(2)}, u32[]{:S(2)}) collective-permute-start(bf16[8,4096]{1,0:T(8,128)(2,1)S(1)} %get-tuple-element.97), channel_id=1, source_target_pairs={{0,24},{2,26},{4,28},{6,30},{8,16},{10,18},{12,20},{14,22},{16,8},... | collective-permute-start | bytes 196616 | tf_op jit(solution)/shard_map/ppermute | solution.py:38
  71.1 3.9 %gu_grads.3 = (bf16[192,128,128]{2,1,0:T(8,128)(2,1)}, bf16[192,128,128]{2,1,0:T(8,128)(2,1)}) custom-call(s32[1,1,192]{2,1,0:T(1,128)} %index.9, s32[1,1]{1,0:T(1,128)S(6)} %copy.17.count, bf16[8,128,256]{2,1,0:T(8,128)(2,1)S(1)} %get-tuple-element.98.d_pair, bf16[32,128,128]{2,1,0:T(8,128)(2,1)S(1)} %turn.1.turned, ...), custom_call_target="tpu_custom_call", output_to_operand_aliasing={{0}: (4, {}), {1}: (5, {})} | custom-call | flops 536870912 | bytes 4194304 | tf_op jit(solution)/shard_map/gu_grads/pallas_call | solution.py:287
  75.1 0.7 fusion.2
  (29 shorter events, 0.8 us)
Async XLA Ops:
  0.6 8.0 %collective-permute-start = (bf16[8,4096]{1,0:T(8,128)(2,1)}, bf16[8,4096]{1,0:T(8,128)(2,1)S(1)}, u32[]{:S(2)}, u32[]{:S(2)}) collective-permute-start(bf16[8,4096]{1,0:T(8,128)(2,1)} %param.9), channel_id=1, source_target_pairs={{0,16},{2,18},{4,20},{6,22},{8,24},{10,26},{12,28},{14,30},{16,0},... | collective-permute-start | bytes 196616 | tf_op jit(solution)/shard_map/ppermute | solution.py:38
  5.4 3.3 %copy-start = (bf16[8,4096]{1,0:T(8,128)(2,1)S(1)}, bf16[8,4096]{1,0:T(8,128)(2,1)}, u32[]{:S(2)}) copy-start(bf16[8,4096]{1,0:T(8,128)(2,1)} %param.9) | copy-start | bytes 196612
  5.4 5.2 %copy-start.1 = (bf16[8,4096]{1,0:T(8,128)(2,1)S(1)}, bf16[8,4096]{1,0:T(8,128)(2,1)}, u32[]{:S(2)}) copy-start(bf16[8,4096]{1,0:T(8,128)(2,1)} %param.10) | copy-start | bytes 196612
  8.7 7.9 %collective-permute-start.1 = (bf16[16,4096]{1,0:T(8,128)(2,1)S(1)}, bf16[16,4096]{1,0:T(8,128)(2,1)S(1)}, u32[]{:S(2)}, u32[]{:S(2)}) collective-permute-start(bf16[16,4096]{1,0:T(8,128)(2,1)S(1)} %pad_maximum_fusion.3), channel_id=1, source_target_pairs={{0,8},{2,10},{4,12},{6,14},{8,0},{10,2},{12,4},{14,6},{16,24},{18,... | collective-permute-start | bytes 393224 | tf_op jit(solution)/shard_map/ppermute | solution.py:38
  10.6 7.6 %collective-permute-start.6 = (bf16[8,4096]{1,0:T(8,128)(2,1)S(1)}, bf16[8,4096]{1,0:T(8,128)(2,1)S(1)}, u32[]{:S(2)}, u32[]{:S(2)}) collective-permute-start(bf16[8,4096]{1,0:T(8,128)(2,1)S(1)} %copy-done.1), channel_id=1, source_target_pairs={{0,16},{2,18},{4,20},{6,22},{8,24},{10,26},{12,28},{14,30},{16,0},... | collective-permute-start | bytes 196616 | tf_op jit(solution)/shard_map/ppermute | solution.py:38
  16.6 6.9 %collective-permute-start.2 = (bf16[32,4096]{1,0:T(8,128)(2,1)S(1)}, bf16[32,4096]{1,0:T(8,128)(2,1)S(1)}, u32[]{:S(2)}, u32[]{:S(2)}) collective-permute-start(bf16[32,4096]{1,0:T(8,128)(2,1)S(1)} %pad_maximum_fusion.1.refs_0_), channel_id=1, source_target_pairs={{0,4},{2,6},{4,0},{6,2},{8,12},{10,14},{12,8},{14,10},{16,20},{18,... | collective-permute-start | bytes 786440 | tf_op jit(solution)/shard_map/ppermute | solution.py:38
  18.2 5.3 %collective-permute-start.7 = (bf16[16,4096]{1,0:T(8,128)(2,1)S(1)}, bf16[16,4096]{1,0:T(8,128)(2,1)S(1)}, u32[]{:S(2)}, u32[]{:S(2)}) collective-permute-start(bf16[16,4096]{1,0:T(8,128)(2,1)S(1)} %pad_maximum_fusion.4), channel_id=1, source_target_pairs={{0,8},{2,10},{4,12},{6,14},{8,0},{10,2},{12,4},{14,6},{16,24},{18,... | collective-permute-start | bytes 393224 | tf_op jit(solution)/shard_map/ppermute | solution.py:38
  21.2 2.3 %collective-permute-start.3 = (bf16[32,4096]{1,0:T(8,128)(2,1)S(1)}, bf16[32,4096]{1,0:T(8,128)(2,1)S(1)}, u32[]{:S(2)}, u32[]{:S(2)}) collective-permute-start(bf16[32,4096]{1,0:T(8,128)(2,1)S(1)} %pad_maximum_fusion.1.refs_0_), channel_id=1, source_target_pairs={{0,2},{2,0},{4,6},{6,4},{8,10},{10,8},{12,14},{14,12},{16,18},{18,... | collective-permute-start | bytes 786440 | tf_op jit(solution)/shard_map/ppermute | solution.py:38
  23.5 1.5 %collective-permute-start.4 = (bf16[32,4096]{1,0:T(8,128)(2,1)S(1)}, bf16[32,4096]{1,0:T(8,128)(2,1)S(1)}, u32[]{:S(2)}, u32[]{:S(2)}) collective-permute-start(bf16[32,4096]{1,0:T(8,128)(2,1)S(1)} %collective-permute-done.2.refs_1_), channel_id=1, source_target_pairs={{0,2},{2,0},{4,6},{6,4},{8,10},{10,8},{12,14},{14,12},{16,18},{18,... | collective-permute-start | bytes 786440 | tf_op jit(solution)/shard_map/ppermute | solution.py:38
  26.3 8.4 %collective-permute-start.8 = (bf16[32,4096]{1,0:T(8,128)(2,1)S(1)}, bf16[32,4096]{1,0:T(8,128)(2,1)S(1)}, u32[]{:S(2)}, u32[]{:S(2)}) collective-permute-start(bf16[32,4096]{1,0:T(8,128)(2,1)S(1)} %pad_maximum_fusion.2), channel_id=1, source_target_pairs={{0,4},{2,6},{4,0},{6,2},{8,12},{10,14},{12,8},{14,10},{16,20},{18,... | collective-permute-start | bytes 786440 | tf_op jit(solution)/shard_map/ppermute | solution.py:38
  28.1 8.2 %collective-permute-start.5 = (bf16[4,128,256]{2,1,0:T(8,128)(2,1)S(1)}, bf16[4,128,256]{2,1,0:T(8,128)(2,1)S(1)}, u32[]{:S(2)}, u32[]{:S(2)}) collective-permute-start(bf16[4,128,256]{2,1,0:T(8,128)(2,1)S(1)} %get-tuple-element.63), channel_id=1, source_target_pairs={{0,1},{1,0},{2,3},{3,2},{4,5},{5,4},{6,7},{7,6},{8,9},{9,8},{10,11... | collective-permute-start | bytes 786440 | tf_op jit(solution)/shard_map/ppermute | solution.py:38
  36.4 2.0 %collective-permute-start.10 = (bf16[64,4096]{1,0:T(8,128)(2,1)S(1)}, bf16[64,4096]{1,0:T(8,128)(2,1)S(1)}, u32[]{:S(2)}, u32[]{:S(2)}) collective-permute-start(bf16[64,4096]{1,0:T(8,128)(2,1)S(1)} %pad_maximum_fusion.refs_0_), channel_id=1, source_target_pairs={{0,2},{2,0},{4,6},{6,4},{8,10},{10,8},{12,14},{14,12},{16,18},{18,... | collective-permute-start | bytes 1572872 | tf_op jit(solution)/shard_map/ppermute | solution.py:38
  36.5 9.2 %collective-permute-start.9 = (bf16[4,128,256]{2,1,0:T(8,128)(2,1)S(1)}, bf16[4,128,256]{2,1,0:T(8,128)(2,1)S(1)}, u32[]{:S(2)}, u32[]{:S(2)}) collective-permute-start(bf16[4,128,256]{2,1,0:T(8,128)(2,1)S(1)} %get-tuple-element.72), channel_id=1, source_target_pairs={{0,1},{1,0},{2,3},{3,2},{4,5},{5,4},{6,7},{7,6},{8,9},{9,8},{10,11... | collective-permute-start | bytes 786440 | tf_op jit(solution)/shard_map/ppermute | solution.py:38
  41.0 10.3 %collective-permute-start.11 = (bf16[8,128,128]{2,1,0:T(8,128)(2,1)S(1)}, bf16[8,128,128]{2,1,0:T(8,128)(2,1)S(1)}, u32[]{:S(2)}, u32[]{:S(2)}) collective-permute-start(bf16[8,128,128]{2,1,0:T(8,128)(2,1)S(1)} %get-tuple-element.86), channel_id=1, source_target_pairs={{0,1},{1,0},{2,3},{3,2},{4,5},{5,4},{6,7},{7,6},{8,9},{9,8},{10,11... | collective-permute-start | bytes 786440 | tf_op jit(solution)/shard_map/ppermute | solution.py:38
  56.1 2.0 %collective-permute-start.12 = (bf16[64,4096]{1,0:T(8,128)(2,1)S(1)}, bf16[64,4096]{1,0:T(8,128)(2,1)S(1)}, u32[]{:S(2)}, u32[]{:S(2)}) collective-permute-start(bf16[64,4096]{1,0:T(8,128)(2,1)S(1)} %get-tuple-element.88), channel_id=1, source_target_pairs={{0,2},{2,0},{4,6},{6,4},{8,10},{10,8},{12,14},{14,12},{16,18},{18,... | collective-permute-start | bytes 1572872 | tf_op jit(solution)/shard_map/ppermute | solution.py:38
  58.2 8.4 %collective-permute-start.13 = (bf16[32,4096]{1,0:T(8,128)(2,1)S(1)}, bf16[32,4096]{1,0:T(8,128)(2,1)S(1)}, u32[]{:S(2)}, u32[]{:S(2)}) collective-permute-start(bf16[32,4096]{1,0:T(8,128)(2,1)S(1)} %slice.43), channel_id=1, source_target_pairs={{0,4},{2,6},{4,0},{6,2},{8,12},{10,14},{12,8},{14,10},{16,20},{18,... | collective-permute-start | bytes 786440 | tf_op jit(solution)/shard_map/ppermute | solution.py:38
  66.7 8.4 %collective-permute-start.14 = (bf16[8,4096]{1,0:T(8,128)(2,1)S(1)}, bf16[8,4096]{1,0:T(8,128)(2,1)S(1)}, u32[]{:S(2)}, u32[]{:S(2)}) collective-permute-start(bf16[8,4096]{1,0:T(8,128)(2,1)S(1)} %get-tuple-element.95), channel_id=1, source_target_pairs={{0,16},{2,18},{4,20},{6,22},{8,24},{10,26},{12,28},{14,30},{16,0},... | collective-permute-start | bytes 196616 | tf_op jit(solution)/shard_map/ppermute | solution.py:38
  66.8 8.3 %collective-permute-start.15 = (bf16[8,4096]{1,0:T(8,128)(2,1)S(1)}, bf16[8,4096]{1,0:T(8,128)(2,1)S(1)}, u32[]{:S(2)}, u32[]{:S(2)}) collective-permute-start(bf16[8,4096]{1,0:T(8,128)(2,1)S(1)} %get-tuple-element.96), channel_id=1, source_target_pairs={{0,8},{2,10},{4,12},{6,14},{8,0},{10,2},{12,4},{14,6},{16,24},{18,... | collective-permute-start | bytes 196616 | tf_op jit(solution)/shard_map/ppermute | solution.py:38
  67.8 7.3 %collective-permute-start.16 = (bf16[8,4096]{1,0:T(8,128)(2,1)S(1)}, bf16[8,4096]{1,0:T(8,128)(2,1)S(1)}, u32[]{:S(2)}, u32[]{:S(2)}) collective-permute-start(bf16[8,4096]{1,0:T(8,128)(2,1)S(1)} %get-tuple-element.97), channel_id=1, source_target_pairs={{0,24},{2,26},{4,28},{6,30},{8,16},{10,18},{12,20},{14,22},{16,8},... | collective-permute-start | bytes 196616 | tf_op jit(solution)/shard_map/ppermute | solution.py:38

commit v10 on v8

--- a/solution.py
+++ b/solution.py
@@ -109,9 +109,7 @@
     *pieces, gate_w, up_w, own, send = refs
     d_blocks, _, block, _ = gate_w.shape
     x = stack(pieces)
-
-    @pl.loop(0, own.shape[0])
-    def _(c):
+    for c in range(own.shape[0]):
         weights = jnp.concatenate(
             [
                 gate_w[:, first + c].reshape(d_blocks * block, block),
@@ -139,40 +137,39 @@
     )(*pieces, resident(gate_w), resident(up_w))
 
 
-def d_hidden_body(pieces_count, *refs):
+def d_hidden_body(group, pieces_count, *refs):
     y_pieces, x_pieces = refs[:pieces_count], refs[pieces_count : 2 * pieces_count]
-    down_w, own, send, turned = refs[2 * pieces_count :]
+    down_w, own, send, x_turned, y_turned = refs[2 * pieces_count :]
     f_blocks, d_blocks, block, _ = down_w.shape
-    y = stack(y_pieces)
-
-    @pl.loop(0, f_blocks // 2)
-    def _(pair):
+    for d in range(d_blocks):
+        at = slice(d * block, (d + 1) * block)
+        y_turned[at, :] = jnp.concatenate([piece[:, at] for piece in y_pieces], axis=0).T
+    y = y_turned[...]
+    for f in range(0, f_blocks, group):
         weights = jnp.concatenate(
             [
-                down_w[pl.ds(2 * pair, 2), d].reshape(2 * block, block)
+                down_w[f : f + group, d].reshape(group * block, block)
                 for d in range(d_blocks)
             ],
             axis=1,
         )
-        result = lax.dot_general(
-            y, weights, (((1,), (1,)), ((), ())), preferred_element_type=F32
-        )
-        for half in range(2):
-            part = result[:, half * block : (half + 1) * block]
-            own[2 * pair + half] = part
-            send[2 * pair + half] = part.astype(BF16)
-
+        result = jnp.dot(weights, y, preferred_element_type=F32).T
+        for side in range(group):
+            part = result[:, side * block : (side + 1) * block]
+            own[f + side] = part
+            send[f + side] = part.astype(BF16)
     for d in range(d_blocks):
-        columns = slice(d * block, (d + 1) * block)
-        turned[d] = jnp.concatenate([piece[:, columns] for piece in x_pieces], axis=0).T
+        at = slice(d * block, (d + 1) * block)
+        x_turned[d] = jnp.concatenate([piece[:, at] for piece in x_pieces], axis=0).T
 
 
 def d_hidden(y_pieces, x_pieces, down_w):
     f_blocks, d_blocks, block, _ = down_w.shape
     tokens = sum(piece.shape[0] for piece in y_pieces)
     shape = (f_blocks, tokens, block)
-    return pl.pallas_call(
-        functools.partial(d_hidden_body, len(y_pieces)),
+    group = max(n for n in (1, 2, 4) if f_blocks % n == 0)
+    return pl.pallas_call(
+        functools.partial(d_hidden_body, group, len(y_pieces)),
         out_shape=(
             jax.ShapeDtypeStruct(shape, F32),
             jax.ShapeDtypeStruct(shape, BF16),
@@ -180,6 +177,7 @@
         ),
         in_specs=[WHOLE] * (2 * len(y_pieces) + 1),
         out_specs=(WHOLE,) * 3,
+        scratch_shapes=[pltpu.VMEM((d_blocks * block, tokens), BF16)],
         compiler_params=params(),
         cost_estimate=cost(2 * tokens * down_w.size, 2 * down_w.size),
         name="d_hidden",
@@ -397,15 +395,13 @@
             x, weights, index = lax.optimization_barrier((x, weights, index))
         x_recv = swap(x, "wide", wide, 2 * flip)
         if hop < 2:
-            early = (down_count,) if hop == 1 else ()
+            early = (down_count,) if hop == 0 else ()
             weights.append(fill(index, gu_count, vals[hop], d_blocks, f_blocks, early))
-        if hop == 1:
-            y, _ = lax.optimization_barrier((cotangent, weights[1]))
-    index, _ = lax.optimization_barrier((down_index, x))
+    y, index, _ = lax.optimization_barrier((cotangent, down_index, x))
     down_w = fill(index, down_count, down_vals, f_blocks, d_blocks)
     for flip in flips[:-1]:
         y = jnp.concatenate([y, swap(y, "wide", wide, 2 * flip)], axis=0)
-    x, down_w = lax.optimization_barrier((x, down_w))
+        y, down_w = lax.optimization_barrier((y, down_w))
     x_pieces = [x, x_recv, swap(x, "wide", wide, 1), swap(x_recv, "wide", wide, 1)]
     y, _ = lax.optimization_barrier((y, x_recv))
     y_recv = swap(y, "wide", wide, 2 * flips[-1])

time: 73.6 us -> 73.1 us (level)
    pallas_call x3, Pallas kernels: 8.18 us -> 9.59 us  [fill(): pl.pallas_call(fill_body, out_shape=pltpu.VMEM((outer, inner, block, bloc...]
    pallas_call x2, Pallas kernels: 3.73 us -> 2.51 us  [gate_up(): pl.pallas_call(functools.partial(gate_up_body, half * f_blocks // 2), out...]
    pallas_call x1, Pallas kernels: 3.6 us -> 2.63 us  [d_hidden(): pl.pallas_call(functools.partial(d_hidden_body, group, len(y_pieces)), ou...]
  transfers between devices with their start and end apart: 18 -> 18, of which waited for: 10 -> 9; matrix products, arithmetic and copies ran while one was open for 0% -> 0% of each run, Pallas kernels for 43% -> 43%
where the time goes in v10:
time: 73.1 us; the launch traced here: 72.4 us
  Pallas kernels  35.8 us (49%)
  starting transfers between devices  22.6 us (31%)
  waiting for transfers between devices  10.9 us (15%)
  between operations  2.17 us (3%)
  other arithmetic  0.86 us (1%)
    ppermute x18, starting transfers between devices, swap(): return lax.ppermute(array, axis, [(i, i ^ flip) for i in range(size)])  22.6 us
    ppermute x18, waiting for transfers between devices, swap(): return lax.ppermute(array, axis, [(i, i ^ flip) for i in range(size)])  10.9 us
    pallas_call x2, Pallas kernels, gu_grads(): pl.pallas_call(functools.partial(gu_grad_body, first, len(before)), out_s...  10.6 us
    pallas_call x3, Pallas kernels, fill(): pl.pallas_call(fill_body, out_shape=pltpu.VMEM((outer, inner, block, bloc...  9.59 us
    pallas_call x1, Pallas kernels, down_grads(): pl.pallas_call(down_grad_body, out_shape=jax.ShapeDtypeStruct((slots, blo...  5.53 us
    pallas_call x1, Pallas kernels, d_tokens_part(): pl.pallas_call(functools.partial(d_tokens_body, group), out_shape=(jax.Sh...  4.71 us
    pallas_call x1, Pallas kernels, d_hidden(): pl.pallas_call(functools.partial(d_hidden_body, group, len(y_pieces)), ou...  2.63 us
    pallas_call x2, Pallas kernels, gate_up(): pl.pallas_call(functools.partial(gate_up_body, half * f_blocks // 2), out...  2.51 us
  transfers between devices with their start and end apart: 18, of which 9 were waited for; matrix products, arithmetic and copies ran while one was open for 0% of the time, Pallas kernels for 43%

profile of v10, /device:TPU:0, one launch (start us, length us, event | category | flops | bytes accessed | tf_op | source)
XLA Modules:
  0.0 72.4 jit_solution(8486719105813963475)
XLA Ops:
  0.6 4.1 %collective-permute-start = (bf16[8,4096]{1,0:T(8,128)(2,1)}, bf16[8,4096]{1,0:T(8,128)(2,1)S(1)}, u32[]{:S(2)}, u32[]{:S(2)}) collective-permute-start(bf16[8,4096]{1,0:T(8,128)(2,1)} %param.9), channel_id=1, source_target_pairs={{0,16},{2,18},{4,20},{6,22},{8,24},{10,26},{12,28},{14,30},{16,0},... | collective-permute-start | bytes 196616 | tf_op jit(solution)/shard_map/ppermute | solution.py:38
  6.0 3.3 %fill.3.refs_4_ = bf16[32,8,128,128]{3,2,1,0:T(8,128)(2,1)S(1)} custom-call(s32[1,1,192]{2,1,0:T(1,128)} %index.9, s32[1,1]{1,0:T(1,128)S(6)} %copy.17.count, bf16[1,1,192,128,128]{4,3,2,1,0:T(8,128)(2,1)} %source.3, s32[1,1]{1,0:T(1,128)S(6)} %copy.18.refs_0_.count), custom_call_target="tpu_custom_call" | custom-call | bytes 6291456 | tf_op jit(solution)/shard_map/fill/pallas_call | solution.py:92
  9.4 0.5 collective-permute-start.1
  9.8 3.3 %fill.4.refs_5_ = bf16[32,8,128,128]{3,2,1,0:T(8,128)(2,1)S(1)} custom-call(s32[1,1,192]{2,1,0:T(1,128)} %index.9, s32[1,1]{1,0:T(1,128)S(6)} %copy.17.count, bf16[1,1,192,128,128]{4,3,2,1,0:T(8,128)(2,1)} %source.4), custom_call_target="tpu_custom_call" | custom-call | bytes 6291456 | tf_op jit(solution)/shard_map/fill/pallas_call | solution.py:92
  13.1 1.3 %collective-permute-done.1 = bf16[16,4096]{1,0:T(8,128)(2,1)S(1)} collective-permute-done((bf16[16,4096]{1,0:T(8,128)(2,1)S(1)}, bf16[16,4096]{1,0:T(8,128)(2,1)S(1)}, u32[]{:S(2)}, u32[]{:S(2)}) %collective-permute-start.1) | collective-permute-done | bytes 131104 | tf_op jit(solution)/shard_map/ppermute | solution.py:38
  14.4 1.6 %collective-permute-start.6 = (bf16[8,4096]{1,0:T(8,128)(2,1)S(1)}, bf16[8,4096]{1,0:T(8,128)(2,1)S(1)}, u32[]{:S(2)}, u32[]{:S(2)}) collective-permute-start(bf16[8,4096]{1,0:T(8,128)(2,1)S(1)} %copy-done.1), channel_id=1, source_target_pairs={{0,16},{2,18},{4,20},{6,22},{8,24},{10,26},{12,28},{14,30},{16,0},... | collective-permute-start | bytes 196616 | tf_op jit(solution)/shard_map/ppermute | solution.py:38
  16.1 1.5 %collective-permute-start.2 = (bf16[32,4096]{1,0:T(8,128)(2,1)S(1)}, bf16[32,4096]{1,0:T(8,128)(2,1)S(1)}, u32[]{:S(2)}, u32[]{:S(2)}) collective-permute-start(bf16[32,4096]{1,0:T(8,128)(2,1)S(1)} %pad_maximum_fusion.refs_0_.refs_4_), channel_id=1, source_target_pairs={{0,4},{2,6},{4,0},{6,2},{8,12},{10,14},{12,8},{14,10},{16,20},{18,... | collective-permute-start | bytes 786440 | tf_op jit(solution)/shard_map/ppermute | solution.py:38
  17.6 3.1 %fill.5.refs_8_ = bf16[8,32,128,128]{3,2,1,0:T(8,128)(2,1)S(1)} custom-call(s32[1,1,192]{2,1,0:T(1,128)} %index.7, s32[1,1]{1,0:T(1,128)S(6)} %copy.18.refs_0_.count, bf16[1,1,192,128,128]{4,3,2,1,0:T(8,128)(2,1)} %source.5), custom_call_target="tpu_custom_call" | custom-call | bytes 6291456 | tf_op jit(solution)/shard_map/fill/pallas_call | solution.py:92
  20.7 1.8 %collective-permute-start.7 = (bf16[16,4096]{1,0:T(8,128)(2,1)S(1)}, bf16[16,4096]{1,0:T(8,128)(2,1)S(1)}, u32[]{:S(2)}, u32[]{:S(2)}) collective-permute-start(bf16[16,4096]{1,0:T(8,128)(2,1)S(1)} %pad_maximum_fusion.3), channel_id=1, source_target_pairs={{0,8},{2,10},{4,12},{6,14},{8,0},{10,2},{12,4},{14,6},{16,24},{18,... | collective-permute-start | bytes 393224 | tf_op jit(solution)/shard_map/ppermute | solution.py:38
  22.5 0.7 %collective-permute-done.2.refs_1_.refs_5_ = bf16[32,4096]{1,0:T(8,128)(2,1)S(1)} collective-permute-done((bf16[32,4096]{1,0:T(8,128)(2,1)S(1)}, bf16[32,4096]{1,0:T(8,128)(2,1)S(1)}, u32[]{:S(2)}, u32[]{:S(2)}) %collective-permute-start.2) | collective-permute-done | bytes 262176 | tf_op jit(solution)/shard_map/ppermute | solution.py:38
  23.2 2.5 %collective-permute-done.7 = bf16[16,4096]{1,0:T(8,128)(2,1)S(1)} collective-permute-done((bf16[16,4096]{1,0:T(8,128)(2,1)S(1)}, bf16[16,4096]{1,0:T(8,128)(2,1)S(1)}, u32[]{:S(2)}, u32[]{:S(2)}) %collective-permute-start.7) | collective-permute-done | bytes 131104 | tf_op jit(solution)/shard_map/ppermute | solution.py:38
  26.0 1.3 %gate_up.2 = (f32[4,128,256]{2,1,0:T(8,128)S(1)}, bf16[4,128,256]{2,1,0:T(8,128)(2,1)S(1)}) custom-call(bf16[32,4096]{1,0:T(8,128)(2,1)S(1)} %pad_maximum_fusion.refs_0_.refs_4_, bf16[32,4096]{1,0:T(8,128)(2,1)S(1)} %collective-permute-done.2.refs_1_.refs_5_, bf16[32,4096]{1,0:T(8,128)(2,1)S(1)} %collective-permute-done.3.refs_2_.refs_6_, ...), custom_call_target="tpu_custom_call" | custom-call | flops 1073741824 | bytes 8388608 | tf_op jit(solution)/shard_map/gate_up/pallas_call | solution.py:129
  27.3 3.0 %collective-permute-start.5 = (bf16[4,128,256]{2,1,0:T(8,128)(2,1)S(1)}, bf16[4,128,256]{2,1,0:T(8,128)(2,1)S(1)}, u32[]{:S(2)}, u32[]{:S(2)}) collective-permute-start(bf16[4,128,256]{2,1,0:T(8,128)(2,1)S(1)} %get-tuple-element.57), channel_id=1, source_target_pairs={{0,1},{1,0},{2,3},{3,2},{4,5},{5,4},{6,7},{7,6},{8,9},{9,8},{10,11... | collective-permute-start | bytes 786440 | tf_op jit(solution)/shard_map/ppermute | solution.py:38
  30.3 1.3 %gate_up.3 = (f32[4,128,256]{2,1,0:T(8,128)S(1)}, bf16[4,128,256]{2,1,0:T(8,128)(2,1)S(1)}) custom-call(bf16[32,4096]{1,0:T(8,128)(2,1)S(1)} %pad_maximum_fusion.refs_0_.refs_4_, bf16[32,4096]{1,0:T(8,128)(2,1)S(1)} %collective-permute-done.2.refs_1_.refs_5_, bf16[32,4096]{1,0:T(8,128)(2,1)S(1)} %collective-permute-done.3.refs_2_.refs_6_, ...), custom_call_target="tpu_custom_call" | custom-call | flops 1073741824 | bytes 8388608 | tf_op jit(solution)/shard_map/gate_up/pallas_call | solution.py:129
  31.5 0.6 collective-permute-done.9.refs_1_
  32.2 0.5 collective-permute-start.11
  32.7 1.4 %collective-permute-start.8 = (bf16[4,128,256]{2,1,0:T(8,128)(2,1)S(1)}, bf16[4,128,256]{2,1,0:T(8,128)(2,1)S(1)}, u32[]{:S(2)}, u32[]{:S(2)}) collective-permute-start(bf16[4,128,256]{2,1,0:T(8,128)(2,1)S(1)} %get-tuple-element.68), channel_id=1, source_target_pairs={{0,1},{1,0},{2,3},{3,2},{4,5},{5,4},{6,7},{7,6},{8,9},{9,8},{10,11... | collective-permute-start | bytes 786440 | tf_op jit(solution)/shard_map/ppermute | solution.py:38
  34.1 0.5 collective-permute-done.5.refs_1_
  34.8 2.6 %d_hidden.1 = (f32[8,128,128]{2,1,0:T(8,128)S(1)}, bf16[8,128,128]{2,1,0:T(8,128)(2,1)S(1)}, bf16[32,128,128]{2,1,0:T(8,128)(2,1)S(1)}) custom-call(bf16[32,4096]{1,0:T(8,128)(2,1)S(1)} %pad_maximum_fusion.1.refs_0_, bf16[32,4096]{1,0:T(8,128)(2,1)S(1)} %collective-permute-done.9.refs_1_, bf16[32,4096]{1,0:T(8,128)(2,1)S(1)} %collective-permute-done.10.refs_2_, ...), custom_call_target="tpu_custom_call" | custom-call | flops 1073741824 | bytes 8388608 | tf_op jit(solution)/shard_map/d_hidden/pallas_call | solution.py:171
  37.4 2.1 %collective-permute-start.12 = (bf16[8,128,128]{2,1,0:T(8,128)(2,1)S(1)}, bf16[8,128,128]{2,1,0:T(8,128)(2,1)S(1)}, u32[]{:S(2)}, u32[]{:S(2)}) collective-permute-start(bf16[8,128,128]{2,1,0:T(8,128)(2,1)S(1)} %get-tuple-element.78), channel_id=1, source_target_pairs={{0,1},{1,0},{2,3},{3,2},{4,5},{5,4},{6,7},{7,6},{8,9},{9,8},{10,11... | collective-permute-start | bytes 786440 | tf_op jit(solution)/shard_map/ppermute | solution.py:38
  39.5 2.4 %collective-permute-done.8.refs_1_ = bf16[4,128,256]{2,1,0:T(8,128)(2,1)S(1)} collective-permute-done((bf16[4,128,256]{2,1,0:T(8,128)(2,1)S(1)}, bf16[4,128,256]{2,1,0:T(8,128)(2,1)S(1)}, u32[]{:S(2)}, u32[]{:S(2)}) %collective-permute-start.8) | collective-permute-done | bytes 262176 | tf_op jit(solution)/shard_map/ppermute | solution.py:38
  42.0 5.5 %down_grads.1 = bf16[192,128,128]{2,1,0:T(8,128)(2,1)} custom-call(s32[1,1,192]{2,1,0:T(1,128)} %index.7, s32[1,1]{1,0:T(1,128)S(6)} %copy.18.refs_0_.count, bf16[4,128,128]{2,1,0:T(8,128)(2,1)S(1)} %get-tuple-element.65.near, bf16[4,128,128]{2,1,0:T(8,128)(2,1)S(1)} %get-tuple-element.69.far, bf16[32,4096]{1,0:T(8,128)(2,1)S(1)} %pad_maximum_fusion.1.refs_0_, ...), custom_call_target="tpu_custom_call" | custom-call | flops 805306368 | bytes 6291456 | tf_op jit(solution)/shard_map/down_grads/pallas_call | solution.py:356
  47.5 4.7 %d_tokens.1 = (f32[64,4096]{1,0:T(8,128)S(1)}, bf16[64,4096]{1,0:T(8,128)(2,1)S(1)}, bf16[8,128,256]{2,1,0:T(8,128)(2,1)S(1)}) custom-call(f32[4,128,256]{2,1,0:T(8,128)S(1)} %get-tuple-element.58.refs_0_, f32[4,128,256]{2,1,0:T(8,128)S(1)} %get-tuple-element.75.refs_1_, f32[8,128,128]{2,1,0:T(8,128)S(1)} %get-tuple-element.77.refs_2_, ...), custom_call_target="tpu_custom_call" | custom-call | flops 2147483648 | bytes 16777216 | tf_op jit(solution)/shard_map/d_tokens/pallas_call | solution.py:225
  52.3 1.9 %collective-permute-done.13 = bf16[64,4096]{1,0:T(8,128)(2,1)S(1)} collective-permute-done((bf16[64,4096]{1,0:T(8,128)(2,1)S(1)}, bf16[64,4096]{1,0:T(8,128)(2,1)S(1)}, u32[]{:S(2)}, u32[]{:S(2)}) %collective-permute-start.13) | collective-permute-done | bytes 524320 | tf_op jit(solution)/shard_map/ppermute | solution.py:38
  54.4 1.3 %collective-permute-start.14 = (bf16[32,4096]{1,0:T(8,128)(2,1)S(1)}, bf16[32,4096]{1,0:T(8,128)(2,1)S(1)}, u32[]{:S(2)}, u32[]{:S(2)}) collective-permute-start(bf16[32,4096]{1,0:T(8,128)(2,1)S(1)} %slice.43), channel_id=1, source_target_pairs={{0,4},{2,6},{4,0},{6,2},{8,12},{10,14},{12,8},{14,10},{16,20},{18,... | collective-permute-start | bytes 786440 | tf_op jit(solution)/shard_map/ppermute | solution.py:38
  55.7 6.7 %gu_grads.2 = (bf16[192,128,128]{2,1,0:T(8,128)(2,1)}, bf16[192,128,128]{2,1,0:T(8,128)(2,1)}) custom-call(s32[1,1,192]{2,1,0:T(1,128)} %index.9, s32[1,1]{1,0:T(1,128)S(6)} %copy.17.count, bf16[8,128,256]{2,1,0:T(8,128)(2,1)S(1)} %get-tuple-element.90.d_pair, bf16[32,128,128]{2,1,0:T(8,128)(2,1)S(1)} %get-tuple-element.84.turned), custom_call_target="tpu_custom_call" | custom-call | flops 1073741824 | bytes 8388608 | tf_op jit(solution)/shard_map/gu_grads/pallas_call | solution.py:273
  62.9 1.2 %collective-permute-start.15 = (bf16[8,4096]{1,0:T(8,128)(2,1)S(1)}, bf16[8,4096]{1,0:T(8,128)(2,1)S(1)}, u32[]{:S(2)}, u32[]{:S(2)}) collective-permute-start(bf16[8,4096]{1,0:T(8,128)(2,1)S(1)} %get-tuple-element.87), channel_id=1, source_target_pairs={{0,16},{2,18},{4,20},{6,22},{8,24},{10,26},{12,28},{14,30},{16,0},... | collective-permute-start | bytes 196616 | tf_op jit(solution)/shard_map/ppermute | solution.py:38
  64.0 1.6 %collective-permute-start.16 = (bf16[8,4096]{1,0:T(8,128)(2,1)S(1)}, bf16[8,4096]{1,0:T(8,128)(2,1)S(1)}, u32[]{:S(2)}, u32[]{:S(2)}) collective-permute-start(bf16[8,4096]{1,0:T(8,128)(2,1)S(1)} %get-tuple-element.88), channel_id=1, source_target_pairs={{0,8},{2,10},{4,12},{6,14},{8,0},{10,2},{12,4},{14,6},{16,24},{18,... | collective-permute-start | bytes 196616 | tf_op jit(solution)/shard_map/ppermute | solution.py:38
  65.6 1.7 %collective-permute-start.17 = (bf16[8,4096]{1,0:T(8,128)(2,1)S(1)}, bf16[8,4096]{1,0:T(8,128)(2,1)S(1)}, u32[]{:S(2)}, u32[]{:S(2)}) collective-permute-start(bf16[8,4096]{1,0:T(8,128)(2,1)S(1)} %get-tuple-element.89), channel_id=1, source_target_pairs={{0,24},{2,26},{4,28},{6,30},{8,16},{10,18},{12,20},{14,22},{16,8},... | collective-permute-start | bytes 196616 | tf_op jit(solution)/shard_map/ppermute | solution.py:38
  67.3 3.9 %gu_grads.3 = (bf16[192,128,128]{2,1,0:T(8,128)(2,1)}, bf16[192,128,128]{2,1,0:T(8,128)(2,1)}) custom-call(s32[1,1,192]{2,1,0:T(1,128)} %index.9, s32[1,1]{1,0:T(1,128)S(6)} %copy.17.count, bf16[8,128,256]{2,1,0:T(8,128)(2,1)S(1)} %get-tuple-element.90.d_pair, ...), custom_call_target="tpu_custom_call", output_to_operand_aliasing={{0}: (4, {}), {1}: (5, {})} | custom-call | flops 536870912 | bytes 4194304 | tf_op jit(solution)/shard_map/gu_grads/pallas_call | solution.py:273
  71.3 0.5 collective-permute-done.17
  71.8 0.7 fusion.2
  (29 shorter events, 1.2 us)
Async XLA Ops:
  0.6 8.7 %collective-permute-start = (bf16[8,4096]{1,0:T(8,128)(2,1)}, bf16[8,4096]{1,0:T(8,128)(2,1)S(1)}, u32[]{:S(2)}, u32[]{:S(2)}) collective-permute-start(bf16[8,4096]{1,0:T(8,128)(2,1)} %param.9), channel_id=1, source_target_pairs={{0,16},{2,18},{4,20},{6,22},{8,24},{10,26},{12,28},{14,30},{16,0},... | collective-permute-start | bytes 196616 | tf_op jit(solution)/shard_map/ppermute | solution.py:38
  6.0 3.3 %copy-start = (bf16[8,4096]{1,0:T(8,128)(2,1)S(1)}, bf16[8,4096]{1,0:T(8,128)(2,1)}, u32[]{:S(2)}) copy-start(bf16[8,4096]{1,0:T(8,128)(2,1)} %param.9) | copy-start | bytes 196612
  9.4 5.1 %copy-start.1 = (bf16[8,4096]{1,0:T(8,128)(2,1)S(1)}, bf16[8,4096]{1,0:T(8,128)(2,1)}, u32[]{:S(2)}) copy-start(bf16[8,4096]{1,0:T(8,128)(2,1)} %param.10) | copy-start | bytes 196612
  9.4 5.0 %collective-permute-start.1 = (bf16[16,4096]{1,0:T(8,128)(2,1)S(1)}, bf16[16,4096]{1,0:T(8,128)(2,1)S(1)}, u32[]{:S(2)}, u32[]{:S(2)}) collective-permute-start(bf16[16,4096]{1,0:T(8,128)(2,1)S(1)} %pad_maximum_fusion.2), channel_id=1, source_target_pairs={{0,8},{2,10},{4,12},{6,14},{8,0},{10,2},{12,4},{14,6},{16,24},{18,... | collective-permute-start | bytes 393224 | tf_op jit(solution)/shard_map/ppermute | solution.py:38
  14.4 6.2 %collective-permute-start.6 = (bf16[8,4096]{1,0:T(8,128)(2,1)S(1)}, bf16[8,4096]{1,0:T(8,128)(2,1)S(1)}, u32[]{:S(2)}, u32[]{:S(2)}) collective-permute-start(bf16[8,4096]{1,0:T(8,128)(2,1)S(1)} %copy-done.1), channel_id=1, source_target_pairs={{0,16},{2,18},{4,20},{6,22},{8,24},{10,26},{12,28},{14,30},{16,0},... | collective-permute-start | bytes 196616 | tf_op jit(solution)/shard_map/ppermute | solution.py:38
  16.1 7.1 %collective-permute-start.2 = (bf16[32,4096]{1,0:T(8,128)(2,1)S(1)}, bf16[32,4096]{1,0:T(8,128)(2,1)S(1)}, u32[]{:S(2)}, u32[]{:S(2)}) collective-permute-start(bf16[32,4096]{1,0:T(8,128)(2,1)S(1)} %pad_maximum_fusion.refs_0_.refs_4_), channel_id=1, source_target_pairs={{0,4},{2,6},{4,0},{6,2},{8,12},{10,14},{12,8},{14,10},{16,20},{18,... | collective-permute-start | bytes 786440 | tf_op jit(solution)/shard_map/ppermute | solution.py:38
  20.7 5.0 %collective-permute-start.7 = (bf16[16,4096]{1,0:T(8,128)(2,1)S(1)}, bf16[16,4096]{1,0:T(8,128)(2,1)S(1)}, u32[]{:S(2)}, u32[]{:S(2)}) collective-permute-start(bf16[16,4096]{1,0:T(8,128)(2,1)S(1)} %pad_maximum_fusion.3), channel_id=1, source_target_pairs={{0,8},{2,10},{4,12},{6,14},{8,0},{10,2},{12,4},{14,6},{16,24},{18,... | collective-permute-start | bytes 393224 | tf_op jit(solution)/shard_map/ppermute | solution.py:38
  22.4 3.5 %collective-permute-start.3 = (bf16[32,4096]{1,0:T(8,128)(2,1)S(1)}, bf16[32,4096]{1,0:T(8,128)(2,1)S(1)}, u32[]{:S(2)}, u32[]{:S(2)}) collective-permute-start(bf16[32,4096]{1,0:T(8,128)(2,1)S(1)} %pad_maximum_fusion.refs_0_.refs_4_), channel_id=1, source_target_pairs={{0,2},{2,0},{4,6},{6,4},{8,10},{10,8},{12,14},{14,12},{16,18},{18,... | collective-permute-start | bytes 786440 | tf_op jit(solution)/shard_map/ppermute | solution.py:38
  23.2 2.8 %collective-permute-start.4 = (bf16[32,4096]{1,0:T(8,128)(2,1)S(1)}, bf16[32,4096]{1,0:T(8,128)(2,1)S(1)}, u32[]{:S(2)}, u32[]{:S(2)}) collective-permute-start(bf16[32,4096]{1,0:T(8,128)(2,1)S(1)} %collective-permute-done.2.refs_1_.refs_5_), channel_id=1, source_target_pairs={{0,2},{2,0},{4,6},{6,4},{8,10},{10,8},{12,14},{14,12},{16,18},{18,... | collective-permute-start | bytes 786440 | tf_op jit(solution)/shard_map/ppermute | solution.py:38
  25.7 6.4 %collective-permute-start.9 = (bf16[32,4096]{1,0:T(8,128)(2,1)S(1)}, bf16[32,4096]{1,0:T(8,128)(2,1)S(1)}, u32[]{:S(2)}, u32[]{:S(2)}) collective-permute-start(bf16[32,4096]{1,0:T(8,128)(2,1)S(1)} %pad_maximum_fusion.1.refs_0_), channel_id=1, source_target_pairs={{0,4},{2,6},{4,0},{6,2},{8,12},{10,14},{12,8},{14,10},{16,20},{18,... | collective-permute-start | bytes 786440 | tf_op jit(solution)/shard_map/ppermute | solution.py:38
  27.3 7.4 %collective-permute-start.5 = (bf16[4,128,256]{2,1,0:T(8,128)(2,1)S(1)}, bf16[4,128,256]{2,1,0:T(8,128)(2,1)S(1)}, u32[]{:S(2)}, u32[]{:S(2)}) collective-permute-start(bf16[4,128,256]{2,1,0:T(8,128)(2,1)S(1)} %get-tuple-element.57), channel_id=1, source_target_pairs={{0,1},{1,0},{2,3},{3,2},{4,5},{5,4},{6,7},{7,6},{8,9},{9,8},{10,11... | collective-permute-start | bytes 786440 | tf_op jit(solution)/shard_map/ppermute | solution.py:38
  32.2 2.6 %collective-permute-start.10 = (bf16[32,4096]{1,0:T(8,128)(2,1)S(1)}, bf16[32,4096]{1,0:T(8,128)(2,1)S(1)}, u32[]{:S(2)}, u32[]{:S(2)}) collective-permute-start(bf16[32,4096]{1,0:T(8,128)(2,1)S(1)} %pad_maximum_fusion.1.refs_0_), channel_id=1, source_target_pairs={{0,2},{2,0},{4,6},{6,4},{8,10},{10,8},{12,14},{14,12},{16,18},{18,... | collective-permute-start | bytes 786440 | tf_op jit(solution)/shard_map/ppermute | solution.py:38
  32.2 2.6 %collective-permute-start.11 = (bf16[32,4096]{1,0:T(8,128)(2,1)S(1)}, bf16[32,4096]{1,0:T(8,128)(2,1)S(1)}, u32[]{:S(2)}, u32[]{:S(2)}) collective-permute-start(bf16[32,4096]{1,0:T(8,128)(2,1)S(1)} %collective-permute-done.9.refs_1_), channel_id=1, source_target_pairs={{0,2},{2,0},{4,6},{6,4},{8,10},{10,8},{12,14},{14,12},{16,18},{18,... | collective-permute-start | bytes 786440 | tf_op jit(solution)/shard_map/ppermute | solution.py:38
  32.7 9.2 %collective-permute-start.8 = (bf16[4,128,256]{2,1,0:T(8,128)(2,1)S(1)}, bf16[4,128,256]{2,1,0:T(8,128)(2,1)S(1)}, u32[]{:S(2)}, u32[]{:S(2)}) collective-permute-start(bf16[4,128,256]{2,1,0:T(8,128)(2,1)S(1)} %get-tuple-element.68), channel_id=1, source_target_pairs={{0,1},{1,0},{2,3},{3,2},{4,5},{5,4},{6,7},{7,6},{8,9},{9,8},{10,11... | collective-permute-start | bytes 786440 | tf_op jit(solution)/shard_map/ppermute | solution.py:38
  37.4 10.1 %collective-permute-start.12 = (bf16[8,128,128]{2,1,0:T(8,128)(2,1)S(1)}, bf16[8,128,128]{2,1,0:T(8,128)(2,1)S(1)}, u32[]{:S(2)}, u32[]{:S(2)}) collective-permute-start(bf16[8,128,128]{2,1,0:T(8,128)(2,1)S(1)} %get-tuple-element.78), channel_id=1, source_target_pairs={{0,1},{1,0},{2,3},{3,2},{4,5},{5,4},{6,7},{7,6},{8,9},{9,8},{10,11... | collective-permute-start | bytes 786440 | tf_op jit(solution)/shard_map/ppermute | solution.py:38
  52.3 2.0 %collective-permute-start.13 = (bf16[64,4096]{1,0:T(8,128)(2,1)S(1)}, bf16[64,4096]{1,0:T(8,128)(2,1)S(1)}, u32[]{:S(2)}, u32[]{:S(2)}) collective-permute-start(bf16[64,4096]{1,0:T(8,128)(2,1)S(1)} %get-tuple-element.80), channel_id=1, source_target_pairs={{0,2},{2,0},{4,6},{6,4},{8,10},{10,8},{12,14},{14,12},{16,18},{18,... | collective-permute-start | bytes 1572872 | tf_op jit(solution)/shard_map/ppermute | solution.py:38
  54.4 8.4 %collective-permute-start.14 = (bf16[32,4096]{1,0:T(8,128)(2,1)S(1)}, bf16[32,4096]{1,0:T(8,128)(2,1)S(1)}, u32[]{:S(2)}, u32[]{:S(2)}) collective-permute-start(bf16[32,4096]{1,0:T(8,128)(2,1)S(1)} %slice.43), channel_id=1, source_target_pairs={{0,4},{2,6},{4,0},{6,2},{8,12},{10,14},{12,8},{14,10},{16,20},{18,... | collective-permute-start | bytes 786440 | tf_op jit(solution)/shard_map/ppermute | solution.py:38
  62.9 8.4 %collective-permute-start.15 = (bf16[8,4096]{1,0:T(8,128)(2,1)S(1)}, bf16[8,4096]{1,0:T(8,128)(2,1)S(1)}, u32[]{:S(2)}, u32[]{:S(2)}) collective-permute-start(bf16[8,4096]{1,0:T(8,128)(2,1)S(1)} %get-tuple-element.87), channel_id=1, source_target_pairs={{0,16},{2,18},{4,20},{6,22},{8,24},{10,26},{12,28},{14,30},{16,0},... | collective-permute-start | bytes 196616 | tf_op jit(solution)/shard_map/ppermute | solution.py:38
  64.0 7.2 %collective-permute-start.16 = (bf16[8,4096]{1,0:T(8,128)(2,1)S(1)}, bf16[8,4096]{1,0:T(8,128)(2,1)S(1)}, u32[]{:S(2)}, u32[]{:S(2)}) collective-permute-start(bf16[8,4096]{1,0:T(8,128)(2,1)S(1)} %get-tuple-element.88), channel_id=1, source_target_pairs={{0,8},{2,10},{4,12},{6,14},{8,0},{10,2},{12,4},{14,6},{16,24},{18,... | collective-permute-start | bytes 196616 | tf_op jit(solution)/shard_map/ppermute | solution.py:38
  65.6 6.1 %collective-permute-start.17 = (bf16[8,4096]{1,0:T(8,128)(2,1)S(1)}, bf16[8,4096]{1,0:T(8,128)(2,1)S(1)}, u32[]{:S(2)}, u32[]{:S(2)}) collective-permute-start(bf16[8,4096]{1,0:T(8,128)(2,1)S(1)} %get-tuple-element.89), channel_id=1, source_target_pairs={{0,24},{2,26},{4,28},{6,30},{8,16},{10,18},{12,20},{14,22},{16,8},... | collective-permute-start | bytes 196616 | tf_op jit(solution)/shard_map/ppermute | solution.py:38

commit v11 on v10

--- a/solution.py
+++ b/solution.py
@@ -184,11 +184,29 @@
     )(*y_pieces, *x_pieces, resident(down_w))
 
 
-def d_tokens_body(group, *refs):
+def d_tokens_columns(group, begin, grads, gate_w, up_w, own, send):
+    f_blocks, block = gate_w.shape[1:3]
+    half = own.shape[0]
+    for at in range(0, own.shape[1] // block, group):
+        rows = slice(begin + at, begin + at + group)
+        weights = jnp.concatenate(
+            [
+                ref[rows, c].reshape(group * block, block)
+                for c in range(f_blocks)
+                for ref in (gate_w, up_w)
+            ],
+            axis=1,
+        )
+        result = jnp.dot(weights, grads, preferred_element_type=F32).T
+        columns = slice(at * block, (at + group) * block)
+        own[:, columns] = result[:half]
+        send[:, columns] = result[half:].astype(BF16)
+
+
+def d_tokens_first_body(group, *refs):
     *coef, dh_own = refs[:3]
     *dh_recv, gate_w, up_w, own, send, d_pair, turned = refs[3:]
-    d_blocks, f_blocks, block, _ = gate_w.shape
-    half = own.shape[0]
+    f_blocks, block = gate_w.shape[1:3]
     for c in range(f_blocks):
         dh = dh_own[c]
         for part in dh_recv:
@@ -200,42 +218,46 @@
             turned[pl.ds((2 * c + side) * block, block), :] = both[
                 :, side * block : (side + 1) * block
             ].T
-    grads = turned[...]
-
-    for at in range(d_blocks // group):
-        weights = jnp.concatenate(
-            [
-                ref[at * group : (at + 1) * group, c].reshape(group * block, block)
-                for c in range(f_blocks)
-                for ref in (gate_w, up_w)
-            ],
-            axis=1,
-        )
-        result = jnp.dot(weights, grads, preferred_element_type=F32).T
-        columns = slice(at * group * block, (at + 1) * group * block)
-        own[:, columns] = result[:half]
-        send[:, columns] = result[half:].astype(BF16)
-
-
-def d_tokens_part(coef, dh_own, dh_recv, gate_w, up_w):
+    d_tokens_columns(group, 0, turned[...], gate_w, up_w, own, send)
+
+
+def d_tokens_second_body(group, turned, gate_w, up_w, own, send):
+    d_blocks = gate_w.shape[0]
+    d_tokens_columns(group, d_blocks // 2, turned[...], gate_w, up_w, own, send)
+
+
+def d_tokens_parts(coef, dh_own, dh_recv, gate_w, up_w):
     d_blocks, f_blocks, block, _ = gate_w.shape
     tokens = dh_own.shape[1]
-    width = d_blocks * block
-    group = max(n for n in (1, 2, 4) if d_blocks % n == 0)
-    return pl.pallas_call(
-        functools.partial(d_tokens_body, group),
+    half = (tokens // 2, d_blocks // 2 * block)
+    group = max(n for n in (1, 2, 4) if d_blocks // 2 % n == 0)
+    halves = (jax.ShapeDtypeStruct(half, F32), jax.ShapeDtypeStruct(half, BF16))
+    common = dict(
+        compiler_params=params(),
+        cost_estimate=cost(2 * tokens * gate_w.size, 2 * gate_w.size),
+    )
+    weights = resident(gate_w), resident(up_w)
+    own, send, d_pair, turned = pl.pallas_call(
+        functools.partial(d_tokens_first_body, group),
         out_shape=(
-            jax.ShapeDtypeStruct((tokens // 2, width), F32),
-            jax.ShapeDtypeStruct((tokens // 2, width), BF16),
+            *halves,
             jax.ShapeDtypeStruct((f_blocks, tokens, 2 * block), BF16),
+            jax.ShapeDtypeStruct((f_blocks * 2 * block, tokens), BF16),
         ),
         in_specs=[WHOLE] * (5 + len(dh_recv)),
-        out_specs=(WHOLE,) * 3,
-        scratch_shapes=[pltpu.VMEM((f_blocks * 2 * block, tokens), BF16)],
-        compiler_params=params(),
-        cost_estimate=cost(4 * tokens * gate_w.size, 4 * gate_w.size),
-        name="d_tokens",
-    )(*coef, dh_own, *dh_recv, resident(gate_w), resident(up_w))
+        out_specs=(WHOLE,) * 4,
+        name="d_tokens_first",
+        **common,
+    )(*coef, dh_own, *dh_recv, *weights)
+    second = pl.pallas_call(
+        functools.partial(d_tokens_second_body, group),
+        out_shape=halves,
+        in_specs=[WHOLE] * 3,
+        out_specs=(WHOLE,) * 2,
+        name="d_tokens_second",
+        **common,
+    )(turned, *weights)
+    return ((own, send), second), d_pair
 
 
 def step_slots(slots):
@@ -420,16 +442,19 @@
     far_hidden, far_coef = activate(far_own, far_recv)
     down_grad = down_grads(down_index, down_count, y_pieces, near_hidden, far_hidden, slots)
     down_grad, far_coef = lax.optimization_barrier((down_grad, far_coef))
-    own, send, d_pair = d_tokens_part((near_coef, far_coef), dh_own, dh_recv, *weights)
-
-    own = own + swap(send, "wide", wide, 1).astype(F32)
-    kept = own.shape[0] // 2
-    far = own[kept:].astype(BF16)
-    own = own[:kept]
-    cut = slots * 2 // 3 if slots % 3 == 0 else slots
-    far, d_pair = lax.optimization_barrier((far, d_pair))
+    halves, d_pair = d_tokens_parts((near_coef, far_coef), dh_own, dh_recv, *weights)
+
+    halves = [own + swap(send, "wide", wide, 1).astype(F32) for own, send in halves]
+    kept = chips // 2 * rows
+    far = [own[kept:].astype(BF16) for own in halves]
+    cut = slots // 2 if slots % 2 == 0 else slots
+    far[1], d_pair = lax.optimization_barrier((far[1], d_pair))
     grads = gu_grads(gu_index, gu_count, d_pair, turned, slots, 0, cut, ())
-    own = own + swap(far, "wide", wide, 2 * flips[-1]).astype(F32)
+    halves = [
+        own[:kept] + swap(part, "wide", wide, 2 * flips[-1]).astype(F32)
+        for own, part in zip(halves, far)
+    ]
+    own = jnp.concatenate(halves, axis=1)
     sends = [own[p * rows : (p + 1) * rows].astype(BF16) for p in range(1, chips // 2)]
     if cut < slots:
         sends, d_pair, grads = lax.optimization_barrier((sends, d_pair, grads))

time: 73.1 us -> 72.8 us (level)
  waiting for transfers between devices: 10.9 us -> 13.3 us
  starting transfers between devices: 22.6 us -> 21.3 us
  Pallas kernels: 35.8 us -> 34.6 us
    ppermute x18 -> x20, waiting for transfers between devices: 10.9 us -> 13.3 us  [swap(): return lax.ppermute(array, axis, [(i, i ^ flip) for i in range(size)])]
    pallas_call x3, Pallas kernels: 9.59 us -> 8.07 us  [fill(): pl.pallas_call(fill_body, out_shape=pltpu.VMEM((outer, inner, block, bloc...]
    ppermute x18 -> x20, starting transfers between devices: 22.6 us -> 21.3 us  [swap(): return lax.ppermute(array, axis, [(i, i ^ flip) for i in range(size)])]
    pallas_call x1 -> x2, Pallas kernels: 4.71 us -> 4.97 us  [the longest x1 2.54 us: d_tokens_parts(): pl.pallas_call(functools.partial(d_tokens_first_body, group), out_shape=(...]
  transfers between devices with their start and end apart: 18 -> 20, of which waited for: 9 -> 8; matrix products, arithmetic and copies ran while one was open for 0% -> 0% of each run, Pallas kernels for 43% -> 44%
where the time goes in v11:
time: 72.8 us; the launch traced here: 72.3 us
  Pallas kernels  34.6 us (48%)
  starting transfers between devices  21.3 us (29%)
  waiting for transfers between devices  13.3 us (18%)
  between operations  2.2 us (3%)
  other arithmetic  0.89 us (1%)
    ppermute x20, starting transfers between devices, swap(): return lax.ppermute(array, axis, [(i, i ^ flip) for i in range(size)])  21.3 us
    ppermute x20, waiting for transfers between devices, swap(): return lax.ppermute(array, axis, [(i, i ^ flip) for i in range(size)])  13.3 us
    pallas_call x2, Pallas kernels, gu_grads(): pl.pallas_call(functools.partial(gu_grad_body, first, len(before)), out_s...  10.6 us
    pallas_call x3, Pallas kernels, fill(): pl.pallas_call(fill_body, out_shape=pltpu.VMEM((outer, inner, block, bloc...  8.07 us
    pallas_call x1, Pallas kernels, down_grads(): pl.pallas_call(down_grad_body, out_shape=jax.ShapeDtypeStruct((slots, blo...  5.52 us
    pallas_call x1, Pallas kernels, d_hidden(): pl.pallas_call(functools.partial(d_hidden_body, group, len(y_pieces)), ou...  2.63 us
    pallas_call x1, Pallas kernels, d_tokens_parts(): pl.pallas_call(functools.partial(d_tokens_first_body, group), out_shape=(...  2.54 us
    pallas_call x2, Pallas kernels, gate_up(): pl.pallas_call(functools.partial(gate_up_body, half * f_blocks // 2), out...  2.5 us
  transfers between devices with their start and end apart: 20, of which 8 were waited for; matrix products, arithmetic and copies ran while one was open for 0% of the time, Pallas kernels for 44%

profile of v11, /device:TPU:0, one launch (start us, length us, event | category | flops | bytes accessed | tf_op | source)
XLA Modules:
  0.0 72.3 jit_solution(3887185182511657564)
XLA Ops:
  0.6 4.1 %collective-permute-start = (bf16[8,4096]{1,0:T(8,128)(2,1)}, bf16[8,4096]{1,0:T(8,128)(2,1)S(1)}, u32[]{:S(2)}, u32[]{:S(2)}) collective-permute-start(bf16[8,4096]{1,0:T(8,128)(2,1)} %param.9), channel_id=1, source_target_pairs={{0,16},{2,18},{4,20},{6,22},{8,24},{10,26},{12,28},{14,30},{16,0},... | collective-permute-start | bytes 196616 | tf_op jit(solution)/shard_map/ppermute | solution.py:38
  6.0 2.8 %fill.3.refs_4_.gate_w = bf16[32,8,128,128]{3,2,1,0:T(8,128)(2,1)S(1)} custom-call(s32[1,1,192]{2,1,0:T(1,128)} %index.9, s32[1,1]{1,0:T(1,128)S(6)} %copy.17.count, bf16[1,1,192,128,128]{4,3,2,1,0:T(8,128)(2,1)} %source.3, s32[1,1]{1,0:T(1,128)S(6)} %copy.18.refs_0_.count), custom_call_target="tpu_custom_call" | custom-call | bytes 6291456 | tf_op jit(solution)/shard_map/fill/pallas_call | solution.py:92
  8.9 0.9 %collective-permute-start.1 = (bf16[16,4096]{1,0:T(8,128)(2,1)S(1)}, bf16[16,4096]{1,0:T(8,128)(2,1)S(1)}, u32[]{:S(2)}, u32[]{:S(2)}) collective-permute-start(bf16[16,4096]{1,0:T(8,128)(2,1)S(1)} %pad_maximum_fusion.3), channel_id=1, source_target_pairs={{0,8},{2,10},{4,12},{6,14},{8,0},{10,2},{12,4},{14,6},{16,24},{18,... | collective-permute-start | bytes 393224 | tf_op jit(solution)/shard_map/ppermute | solution.py:38
  9.8 2.8 %fill.4.refs_5_.up_w = bf16[32,8,128,128]{3,2,1,0:T(8,128)(2,1)S(1)} custom-call(s32[1,1,192]{2,1,0:T(1,128)} %index.9, s32[1,1]{1,0:T(1,128)S(6)} %copy.17.count, bf16[1,1,192,128,128]{4,3,2,1,0:T(8,128)(2,1)} %source.4), custom_call_target="tpu_custom_call" | custom-call | bytes 6291456 | tf_op jit(solution)/shard_map/fill/pallas_call | solution.py:92
  12.7 2.4 %collective-permute-done.1 = bf16[16,4096]{1,0:T(8,128)(2,1)S(1)} collective-permute-done((bf16[16,4096]{1,0:T(8,128)(2,1)S(1)}, bf16[16,4096]{1,0:T(8,128)(2,1)S(1)}, u32[]{:S(2)}, u32[]{:S(2)}) %collective-permute-start.1) | collective-permute-done | bytes 131104 | tf_op jit(solution)/shard_map/ppermute | solution.py:38
  15.1 0.9 %collective-permute-start.6 = (bf16[8,4096]{1,0:T(8,128)(2,1)S(1)}, bf16[8,4096]{1,0:T(8,128)(2,1)S(1)}, u32[]{:S(2)}, u32[]{:S(2)}) collective-permute-start(bf16[8,4096]{1,0:T(8,128)(2,1)S(1)} %copy-done.1), channel_id=1, source_target_pairs={{0,16},{2,18},{4,20},{6,22},{8,24},{10,26},{12,28},{14,30},{16,0},... | collective-permute-start | bytes 196616 | tf_op jit(solution)/shard_map/ppermute | solution.py:38
  16.1 1.5 %collective-permute-start.2 = (bf16[32,4096]{1,0:T(8,128)(2,1)S(1)}, bf16[32,4096]{1,0:T(8,128)(2,1)S(1)}, u32[]{:S(2)}, u32[]{:S(2)}) collective-permute-start(bf16[32,4096]{1,0:T(8,128)(2,1)S(1)} %pad_maximum_fusion.1.refs_0_.refs_4_), channel_id=1, source_target_pairs={{0,4},{2,6},{4,0},{6,2},{8,12},{10,14},{12,8},{14,10},{16,20},{18,... | collective-permute-start | bytes 786440 | tf_op jit(solution)/shard_map/ppermute | solution.py:38
  17.6 2.4 %fill.5.refs_8_ = bf16[8,32,128,128]{3,2,1,0:T(8,128)(2,1)S(1)} custom-call(s32[1,1,192]{2,1,0:T(1,128)} %index.7, s32[1,1]{1,0:T(1,128)S(6)} %copy.18.refs_0_.count, bf16[1,1,192,128,128]{4,3,2,1,0:T(8,128)(2,1)} %source.5), custom_call_target="tpu_custom_call" | custom-call | bytes 6291456 | tf_op jit(solution)/shard_map/fill/pallas_call | solution.py:92
  20.0 0.9 %collective-permute-done.6 = bf16[8,4096]{1,0:T(8,128)(2,1)S(1)} collective-permute-done((bf16[8,4096]{1,0:T(8,128)(2,1)S(1)}, bf16[8,4096]{1,0:T(8,128)(2,1)S(1)}, u32[]{:S(2)}, u32[]{:S(2)}) %collective-permute-start.6) | collective-permute-done | bytes 65568 | tf_op jit(solution)/shard_map/ppermute | solution.py:38
  20.9 1.5 %collective-permute-start.7 = (bf16[16,4096]{1,0:T(8,128)(2,1)S(1)}, bf16[16,4096]{1,0:T(8,128)(2,1)S(1)}, u32[]{:S(2)}, u32[]{:S(2)}) collective-permute-start(bf16[16,4096]{1,0:T(8,128)(2,1)S(1)} %pad_maximum_fusion.4), channel_id=1, source_target_pairs={{0,8},{2,10},{4,12},{6,14},{8,0},{10,2},{12,4},{14,6},{16,24},{18,... | collective-permute-start | bytes 393224 | tf_op jit(solution)/shard_map/ppermute | solution.py:38
  22.4 1.0 %collective-permute-done.2.refs_1_.refs_5_ = bf16[32,4096]{1,0:T(8,128)(2,1)S(1)} collective-permute-done((bf16[32,4096]{1,0:T(8,128)(2,1)S(1)}, bf16[32,4096]{1,0:T(8,128)(2,1)S(1)}, u32[]{:S(2)}, u32[]{:S(2)}) %collective-permute-start.2) | collective-permute-done | bytes 262176 | tf_op jit(solution)/shard_map/ppermute | solution.py:38
  23.4 2.6 %collective-permute-done.7 = bf16[16,4096]{1,0:T(8,128)(2,1)S(1)} collective-permute-done((bf16[16,4096]{1,0:T(8,128)(2,1)S(1)}, bf16[16,4096]{1,0:T(8,128)(2,1)S(1)}, u32[]{:S(2)}, u32[]{:S(2)}) %collective-permute-start.7) | collective-permute-done | bytes 131104 | tf_op jit(solution)/shard_map/ppermute | solution.py:38
  25.9 1.5 %collective-permute-start.9 = (bf16[32,4096]{1,0:T(8,128)(2,1)S(1)}, bf16[32,4096]{1,0:T(8,128)(2,1)S(1)}, u32[]{:S(2)}, u32[]{:S(2)}) collective-permute-start(bf16[32,4096]{1,0:T(8,128)(2,1)S(1)} %pad_maximum_fusion.2.refs_0_), channel_id=1, source_target_pairs={{0,4},{2,6},{4,0},{6,2},{8,12},{10,14},{12,8},{14,10},{16,20},{18,... | collective-permute-start | bytes 786440 | tf_op jit(solution)/shard_map/ppermute | solution.py:38
  27.4 1.3 %gate_up.2 = (f32[4,128,256]{2,1,0:T(8,128)S(1)}, bf16[4,128,256]{2,1,0:T(8,128)(2,1)S(1)}) custom-call(bf16[32,4096]{1,0:T(8,128)(2,1)S(1)} %pad_maximum_fusion.1.refs_0_.refs_4_, bf16[32,4096]{1,0:T(8,128)(2,1)S(1)} %collective-permute-done.2.refs_1_.refs_5_, bf16[32,4096]{1,0:T(8,128)(2,1)S(1)} %collective-permute-done.3.refs_2_.refs_6_, ...), custom_call_target="tpu_custom_call" | custom-call | flops 1073741824 | bytes 8388608 | tf_op jit(solution)/shard_map/gate_up/pallas_call | solution.py:129
  29.0 1.3 %gate_up.3 = (f32[4,128,256]{2,1,0:T(8,128)S(1)}, bf16[4,128,256]{2,1,0:T(8,128)(2,1)S(1)}) custom-call(bf16[32,4096]{1,0:T(8,128)(2,1)S(1)} %pad_maximum_fusion.1.refs_0_.refs_4_, bf16[32,4096]{1,0:T(8,128)(2,1)S(1)} %collective-permute-done.2.refs_1_.refs_5_, bf16[32,4096]{1,0:T(8,128)(2,1)S(1)} %collective-permute-done.3.refs_2_.refs_6_, ...), custom_call_target="tpu_custom_call" | custom-call | flops 1073741824 | bytes 8388608 | tf_op jit(solution)/shard_map/gate_up/pallas_call | solution.py:129
  30.2 2.2 %collective-permute-done.9.refs_1_ = bf16[32,4096]{1,0:T(8,128)(2,1)S(1)} collective-permute-done((bf16[32,4096]{1,0:T(8,128)(2,1)S(1)}, bf16[32,4096]{1,0:T(8,128)(2,1)S(1)}, u32[]{:S(2)}, u32[]{:S(2)}) %collective-permute-start.9) | collective-permute-done | bytes 262176 | tf_op jit(solution)/shard_map/ppermute | solution.py:38
  32.9 1.4 %collective-permute-start.8 = (bf16[4,128,256]{2,1,0:T(8,128)(2,1)S(1)}, bf16[4,128,256]{2,1,0:T(8,128)(2,1)S(1)}, u32[]{:S(2)}, u32[]{:S(2)}) collective-permute-start(bf16[4,128,256]{2,1,0:T(8,128)(2,1)S(1)} %get-tuple-element.71), channel_id=1, source_target_pairs={{0,1},{1,0},{2,3},{3,2},{4,5},{5,4},{6,7},{7,6},{8,9},{9,8},{10,11... | collective-permute-start | bytes 786440 | tf_op jit(solution)/shard_map/ppermute | solution.py:38
  34.2 0.9 %collective-permute-done.5.refs_1_ = bf16[4,128,256]{2,1,0:T(8,128)(2,1)S(1)} collective-permute-done((bf16[4,128,256]{2,1,0:T(8,128)(2,1)S(1)}, bf16[4,128,256]{2,1,0:T(8,128)(2,1)S(1)}, u32[]{:S(2)}, u32[]{:S(2)}) %collective-permute-start.5) | collective-permute-done | bytes 262176 | tf_op jit(solution)/shard_map/ppermute | solution.py:38
  35.2 2.6 %d_hidden.1 = (f32[8,128,128]{2,1,0:T(8,128)S(1)}, bf16[8,128,128]{2,1,0:T(8,128)(2,1)S(1)}, bf16[32,128,128]{2,1,0:T(8,128)(2,1)S(1)}) custom-call(bf16[32,4096]{1,0:T(8,128)(2,1)S(1)} %pad_maximum_fusion.2.refs_0_, bf16[32,4096]{1,0:T(8,128)(2,1)S(1)} %collective-permute-done.9.refs_1_, bf16[32,4096]{1,0:T(8,128)(2,1)S(1)} %collective-permute-done.10.refs_2_, ...), custom_call_target="tpu_custom_call" | custom-call | flops 1073741824 | bytes 8388608 | tf_op jit(solution)/shard_map/d_hidden/pallas_call | solution.py:171
  37.9 1.1 %collective-permute-start.12 = (bf16[8,128,128]{2,1,0:T(8,128)(2,1)S(1)}, bf16[8,128,128]{2,1,0:T(8,128)(2,1)S(1)}, u32[]{:S(2)}, u32[]{:S(2)}) collective-permute-start(bf16[8,128,128]{2,1,0:T(8,128)(2,1)S(1)} %get-tuple-element.81), channel_id=1, source_target_pairs={{0,1},{1,0},{2,3},{3,2},{4,5},{5,4},{6,7},{7,6},{8,9},{9,8},{10,11... | collective-permute-start | bytes 786440 | tf_op jit(solution)/shard_map/ppermute | solution.py:38
  39.0 3.1 %collective-permute-done.8.refs_1_ = bf16[4,128,256]{2,1,0:T(8,128)(2,1)S(1)} collective-permute-done((bf16[4,128,256]{2,1,0:T(8,128)(2,1)S(1)}, bf16[4,128,256]{2,1,0:T(8,128)(2,1)S(1)}, u32[]{:S(2)}, u32[]{:S(2)}) %collective-permute-start.8) | collective-permute-done | bytes 262176 | tf_op jit(solution)/shard_map/ppermute | solution.py:38
  42.2 5.5 %down_grads.1 = bf16[192,128,128]{2,1,0:T(8,128)(2,1)} custom-call(s32[1,1,192]{2,1,0:T(1,128)} %index.7, s32[1,1]{1,0:T(1,128)S(6)} %copy.18.refs_0_.count, bf16[4,128,128]{2,1,0:T(8,128)(2,1)S(1)} %get-tuple-element.68.near, bf16[4,128,128]{2,1,0:T(8,128)(2,1)S(1)} %get-tuple-element.72.far, bf16[32,4096]{1,0:T(8,128)(2,1)S(1)} %pad_maximum_fusion.2.refs_0_, ...), custom_call_target="tpu_custom_call" | custom-call | flops 805306368 | bytes 6291456 | tf_op jit(solution)/shard_map/down_grads/pallas_call | solution.py:378
  47.7 2.5 %d_tokens_first.1 = (f32[64,2048]{1,0:T(8,128)S(1)}, bf16[64,2048]{1,0:T(8,128)(2,1)S(1)}, bf16[8,128,256]{2,1,0:T(8,128)(2,1)S(1)}, bf16[2048,128]{1,0:T(8,128)(2,1)S(1)}) custom-call(f32[4,128,256]{2,1,0:T(8,128)S(1)} %get-tuple-element.61.refs_0_, f32[4,128,256]{2,1,0:T(8,128)S(1)} %get-tuple-element.78.refs_1_, ...), custom_call_target="tpu_custom_call" | custom-call | flops 1073741824 | bytes 8388608 | tf_op jit(solution)/shard_map/d_tokens_first/pallas_call | solution.py:240
  50.3 2.4 %d_tokens_second.1 = (f32[64,2048]{1,0:T(8,128)S(1)}, bf16[64,2048]{1,0:T(8,128)(2,1)S(1)}) custom-call(bf16[2048,128]{1,0:T(8,128)(2,1)S(1)} %get-tuple-element.84.turned, bf16[32,8,128,128]{3,2,1,0:T(8,128)(2,1)S(1)} %fill.3.refs_4_.gate_w, bf16[32,8,128,128]{3,2,1,0:T(8,128)(2,1)S(1)} %fill.4.refs_5_.up_w), custom_call_target="tpu_custom_call" | custom-call | flops 1073741824 | bytes 8388608 | tf_op jit(solution)/shard_map/d_tokens_second/pallas_call | solution.py:252
  52.8 0.6 collective-permute-start.15
  53.4 1.5 %collective-permute-start.14 = (bf16[32,2048]{1,0:T(8,128)(2,1)S(1)}, bf16[32,2048]{1,0:T(8,128)(2,1)S(1)}, u32[]{:S(2)}, u32[]{:S(2)}) collective-permute-start(bf16[32,2048]{1,0:T(8,128)(2,1)S(1)} %slice.65), channel_id=1, source_target_pairs={{0,4},{2,6},{4,0},{6,2},{8,12},{10,14},{12,8},{14,10},{16,20},{18,... | collective-permute-start | bytes 393224 | tf_op jit(solution)/shard_map/ppermute | solution.py:38
  55.0 1.1 %collective-permute-start.16 = (bf16[32,2048]{1,0:T(8,128)(2,1)S(1)}, bf16[32,2048]{1,0:T(8,128)(2,1)S(1)}, u32[]{:S(2)}, u32[]{:S(2)}) collective-permute-start(bf16[32,2048]{1,0:T(8,128)(2,1)S(1)} %slice.64), channel_id=1, source_target_pairs={{0,4},{2,6},{4,0},{6,2},{8,12},{10,14},{12,8},{14,10},{16,20},{18,... | collective-permute-start | bytes 393224 | tf_op jit(solution)/shard_map/ppermute | solution.py:38
  56.1 5.3 %gu_grads.2 = (bf16[192,128,128]{2,1,0:T(8,128)(2,1)}, bf16[192,128,128]{2,1,0:T(8,128)(2,1)}) custom-call(s32[1,1,192]{2,1,0:T(1,128)} %index.9, s32[1,1]{1,0:T(1,128)S(6)} %copy.17.count, bf16[8,128,256]{2,1,0:T(8,128)(2,1)S(1)} %get-tuple-element.96.d_pair, bf16[32,128,128]{2,1,0:T(8,128)(2,1)S(1)} %get-tuple-element.90.turned), custom_call_target="tpu_custom_call" | custom-call | flops 805306368 | bytes 6291456 | tf_op jit(solution)/shard_map/gu_grads/pallas_call | solution.py:295
  61.8 2.4 %collective-permute-start.17 = (bf16[8,4096]{1,0:T(8,128)(2,1)S(1)}, bf16[8,4096]{1,0:T(8,128)(2,1)S(1)}, u32[]{:S(2)}, u32[]{:S(2)}) collective-permute-start(bf16[8,4096]{1,0:T(8,128)(2,1)S(1)} %get-tuple-element.93), channel_id=1, source_target_pairs={{0,16},{2,18},{4,20},{6,22},{8,24},{10,26},{12,28},{14,30},{16,0},... | collective-permute-start | bytes 196616 | tf_op jit(solution)/shard_map/ppermute | solution.py:38
  64.7 1.6 %collective-permute-start.19 = (bf16[8,4096]{1,0:T(8,128)(2,1)S(1)}, bf16[8,4096]{1,0:T(8,128)(2,1)S(1)}, u32[]{:S(2)}, u32[]{:S(2)}) collective-permute-start(bf16[8,4096]{1,0:T(8,128)(2,1)S(1)} %get-tuple-element.95), channel_id=1, source_target_pairs={{0,24},{2,26},{4,28},{6,30},{8,16},{10,18},{12,20},{14,22},{16,8},... | collective-permute-start | bytes 196616 | tf_op jit(solution)/shard_map/ppermute | solution.py:38
  66.3 5.3 %gu_grads.3 = (bf16[192,128,128]{2,1,0:T(8,128)(2,1)}, bf16[192,128,128]{2,1,0:T(8,128)(2,1)}) custom-call(s32[1,1,192]{2,1,0:T(1,128)} %index.9, s32[1,1]{1,0:T(1,128)S(6)} %copy.17.count, bf16[8,128,256]{2,1,0:T(8,128)(2,1)S(1)} %get-tuple-element.96.d_pair, ...), custom_call_target="tpu_custom_call", output_to_operand_aliasing={{0}: (4, {}), {1}: (5, {})} | custom-call | flops 805306368 | bytes 6291456 | tf_op jit(solution)/shard_map/gu_grads/pallas_call | solution.py:295
  71.6 0.7 fusion.5
  (38 shorter events, 2.2 us)
Async XLA Ops:
  0.6 8.3 %collective-permute-start = (bf16[8,4096]{1,0:T(8,128)(2,1)}, bf16[8,4096]{1,0:T(8,128)(2,1)S(1)}, u32[]{:S(2)}, u32[]{:S(2)}) collective-permute-start(bf16[8,4096]{1,0:T(8,128)(2,1)} %param.9), channel_id=1, source_target_pairs={{0,16},{2,18},{4,20},{6,22},{8,24},{10,26},{12,28},{14,30},{16,0},... | collective-permute-start | bytes 196616 | tf_op jit(solution)/shard_map/ppermute | solution.py:38
  6.0 2.9 %copy-start = (bf16[8,4096]{1,0:T(8,128)(2,1)S(1)}, bf16[8,4096]{1,0:T(8,128)(2,1)}, u32[]{:S(2)}) copy-start(bf16[8,4096]{1,0:T(8,128)(2,1)} %param.9) | copy-start | bytes 196612
  8.9 6.2 %copy-start.1 = (bf16[8,4096]{1,0:T(8,128)(2,1)S(1)}, bf16[8,4096]{1,0:T(8,128)(2,1)}, u32[]{:S(2)}) copy-start(bf16[8,4096]{1,0:T(8,128)(2,1)} %param.10) | copy-start | bytes 196612
  8.9 6.2 %collective-permute-start.1 = (bf16[16,4096]{1,0:T(8,128)(2,1)S(1)}, bf16[16,4096]{1,0:T(8,128)(2,1)S(1)}, u32[]{:S(2)}, u32[]{:S(2)}) collective-permute-start(bf16[16,4096]{1,0:T(8,128)(2,1)S(1)} %pad_maximum_fusion.3), channel_id=1, source_target_pairs={{0,8},{2,10},{4,12},{6,14},{8,0},{10,2},{12,4},{14,6},{16,24},{18,... | collective-permute-start | bytes 393224 | tf_op jit(solution)/shard_map/ppermute | solution.py:38
  15.1 5.7 %collective-permute-start.6 = (bf16[8,4096]{1,0:T(8,128)(2,1)S(1)}, bf16[8,4096]{1,0:T(8,128)(2,1)S(1)}, u32[]{:S(2)}, u32[]{:S(2)}) collective-permute-start(bf16[8,4096]{1,0:T(8,128)(2,1)S(1)} %copy-done.1), channel_id=1, source_target_pairs={{0,16},{2,18},{4,20},{6,22},{8,24},{10,26},{12,28},{14,30},{16,0},... | collective-permute-start | bytes 196616 | tf_op jit(solution)/shard_map/ppermute | solution.py:38
  16.1 7.3 %collective-permute-start.2 = (bf16[32,4096]{1,0:T(8,128)(2,1)S(1)}, bf16[32,4096]{1,0:T(8,128)(2,1)S(1)}, u32[]{:S(2)}, u32[]{:S(2)}) collective-permute-start(bf16[32,4096]{1,0:T(8,128)(2,1)S(1)} %pad_maximum_fusion.1.refs_0_.refs_4_), channel_id=1, source_target_pairs={{0,4},{2,6},{4,0},{6,2},{8,12},{10,14},{12,8},{14,10},{16,20},{18,... | collective-permute-start | bytes 786440 | tf_op jit(solution)/shard_map/ppermute | solution.py:38
  20.9 5.0 %collective-permute-start.7 = (bf16[16,4096]{1,0:T(8,128)(2,1)S(1)}, bf16[16,4096]{1,0:T(8,128)(2,1)S(1)}, u32[]{:S(2)}, u32[]{:S(2)}) collective-permute-start(bf16[16,4096]{1,0:T(8,128)(2,1)S(1)} %pad_maximum_fusion.4), channel_id=1, source_target_pairs={{0,8},{2,10},{4,12},{6,14},{8,0},{10,2},{12,4},{14,6},{16,24},{18,... | collective-permute-start | bytes 393224 | tf_op jit(solution)/shard_map/ppermute | solution.py:38
  22.4 5.0 %collective-permute-start.3 = (bf16[32,4096]{1,0:T(8,128)(2,1)S(1)}, bf16[32,4096]{1,0:T(8,128)(2,1)S(1)}, u32[]{:S(2)}, u32[]{:S(2)}) collective-permute-start(bf16[32,4096]{1,0:T(8,128)(2,1)S(1)} %pad_maximum_fusion.1.refs_0_.refs_4_), channel_id=1, source_target_pairs={{0,2},{2,0},{4,6},{6,4},{8,10},{10,8},{12,14},{14,12},{16,18},{18,... | collective-permute-start | bytes 786440 | tf_op jit(solution)/shard_map/ppermute | solution.py:38
  23.4 4.1 %collective-permute-start.4 = (bf16[32,4096]{1,0:T(8,128)(2,1)S(1)}, bf16[32,4096]{1,0:T(8,128)(2,1)S(1)}, u32[]{:S(2)}, u32[]{:S(2)}) collective-permute-start(bf16[32,4096]{1,0:T(8,128)(2,1)S(1)} %collective-permute-done.2.refs_1_.refs_5_), channel_id=1, source_target_pairs={{0,2},{2,0},{4,6},{6,4},{8,10},{10,8},{12,14},{14,12},{16,18},{18,... | collective-permute-start | bytes 786440 | tf_op jit(solution)/shard_map/ppermute | solution.py:38
  25.9 6.4 %collective-permute-start.9 = (bf16[32,4096]{1,0:T(8,128)(2,1)S(1)}, bf16[32,4096]{1,0:T(8,128)(2,1)S(1)}, u32[]{:S(2)}, u32[]{:S(2)}) collective-permute-start(bf16[32,4096]{1,0:T(8,128)(2,1)S(1)} %pad_maximum_fusion.2.refs_0_), channel_id=1, source_target_pairs={{0,4},{2,6},{4,0},{6,2},{8,12},{10,14},{12,8},{14,10},{16,20},{18,... | collective-permute-start | bytes 786440 | tf_op jit(solution)/shard_map/ppermute | solution.py:38
  28.7 6.4 %collective-permute-start.5 = (bf16[4,128,256]{2,1,0:T(8,128)(2,1)S(1)}, bf16[4,128,256]{2,1,0:T(8,128)(2,1)S(1)}, u32[]{:S(2)}, u32[]{:S(2)}) collective-permute-start(bf16[4,128,256]{2,1,0:T(8,128)(2,1)S(1)} %get-tuple-element.60), channel_id=1, source_target_pairs={{0,1},{1,0},{2,3},{3,2},{4,5},{5,4},{6,7},{7,6},{8,9},{9,8},{10,11... | collective-permute-start | bytes 786440 | tf_op jit(solution)/shard_map/ppermute | solution.py:38
  32.4 2.9 %collective-permute-start.10 = (bf16[32,4096]{1,0:T(8,128)(2,1)S(1)}, bf16[32,4096]{1,0:T(8,128)(2,1)S(1)}, u32[]{:S(2)}, u32[]{:S(2)}) collective-permute-start(bf16[32,4096]{1,0:T(8,128)(2,1)S(1)} %pad_maximum_fusion.2.refs_0_), channel_id=1, source_target_pairs={{0,2},{2,0},{4,6},{6,4},{8,10},{10,8},{12,14},{14,12},{16,18},{18,... | collective-permute-start | bytes 786440 | tf_op jit(solution)/shard_map/ppermute | solution.py:38
  32.4 2.9 %collective-permute-start.11 = (bf16[32,4096]{1,0:T(8,128)(2,1)S(1)}, bf16[32,4096]{1,0:T(8,128)(2,1)S(1)}, u32[]{:S(2)}, u32[]{:S(2)}) collective-permute-start(bf16[32,4096]{1,0:T(8,128)(2,1)S(1)} %collective-permute-done.9.refs_1_), channel_id=1, source_target_pairs={{0,2},{2,0},{4,6},{6,4},{8,10},{10,8},{12,14},{14,12},{16,18},{18,... | collective-permute-start | bytes 786440 | tf_op jit(solution)/shard_map/ppermute | solution.py:38
  32.9 9.2 %collective-permute-start.8 = (bf16[4,128,256]{2,1,0:T(8,128)(2,1)S(1)}, bf16[4,128,256]{2,1,0:T(8,128)(2,1)S(1)}, u32[]{:S(2)}, u32[]{:S(2)}) collective-permute-start(bf16[4,128,256]{2,1,0:T(8,128)(2,1)S(1)} %get-tuple-element.71), channel_id=1, source_target_pairs={{0,1},{1,0},{2,3},{3,2},{4,5},{5,4},{6,7},{7,6},{8,9},{9,8},{10,11... | collective-permute-start | bytes 786440 | tf_op jit(solution)/shard_map/ppermute | solution.py:38
  37.9 9.8 %collective-permute-start.12 = (bf16[8,128,128]{2,1,0:T(8,128)(2,1)S(1)}, bf16[8,128,128]{2,1,0:T(8,128)(2,1)S(1)}, u32[]{:S(2)}, u32[]{:S(2)}) collective-permute-start(bf16[8,128,128]{2,1,0:T(8,128)(2,1)S(1)} %get-tuple-element.81), channel_id=1, source_target_pairs={{0,1},{1,0},{2,3},{3,2},{4,5},{5,4},{6,7},{7,6},{8,9},{9,8},{10,11... | collective-permute-start | bytes 786440 | tf_op jit(solution)/shard_map/ppermute | solution.py:38
  50.3 3.1 %collective-permute-start.13 = (bf16[64,2048]{1,0:T(8,128)(2,1)S(1)}, bf16[64,2048]{1,0:T(8,128)(2,1)S(1)}, u32[]{:S(2)}, u32[]{:S(2)}) collective-permute-start(bf16[64,2048]{1,0:T(8,128)(2,1)S(1)} %get-tuple-element.83), channel_id=1, source_target_pairs={{0,2},{2,0},{4,6},{6,4},{8,10},{10,8},{12,14},{14,12},{16,18},{18,... | collective-permute-start | bytes 786440 | tf_op jit(solution)/shard_map/ppermute | solution.py:38
  52.8 2.1 %collective-permute-start.15 = (bf16[64,2048]{1,0:T(8,128)(2,1)S(1)}, bf16[64,2048]{1,0:T(8,128)(2,1)S(1)}, u32[]{:S(2)}, u32[]{:S(2)}) collective-permute-start(bf16[64,2048]{1,0:T(8,128)(2,1)S(1)} %get-tuple-element.86), channel_id=1, source_target_pairs={{0,2},{2,0},{4,6},{6,4},{8,10},{10,8},{12,14},{14,12},{16,18},{18,... | collective-permute-start | bytes 786440 | tf_op jit(solution)/shard_map/ppermute | solution.py:38
  53.4 8.0 %collective-permute-start.14 = (bf16[32,2048]{1,0:T(8,128)(2,1)S(1)}, bf16[32,2048]{1,0:T(8,128)(2,1)S(1)}, u32[]{:S(2)}, u32[]{:S(2)}) collective-permute-start(bf16[32,2048]{1,0:T(8,128)(2,1)S(1)} %slice.65), channel_id=1, source_target_pairs={{0,4},{2,6},{4,0},{6,2},{8,12},{10,14},{12,8},{14,10},{16,20},{18,... | collective-permute-start | bytes 393224 | tf_op jit(solution)/shard_map/ppermute | solution.py:38
  55.0 6.8 %collective-permute-start.16 = (bf16[32,2048]{1,0:T(8,128)(2,1)S(1)}, bf16[32,2048]{1,0:T(8,128)(2,1)S(1)}, u32[]{:S(2)}, u32[]{:S(2)}) collective-permute-start(bf16[32,2048]{1,0:T(8,128)(2,1)S(1)} %slice.64), channel_id=1, source_target_pairs={{0,4},{2,6},{4,0},{6,2},{8,12},{10,14},{12,8},{14,10},{16,20},{18,... | collective-permute-start | bytes 393224 | tf_op jit(solution)/shard_map/ppermute | solution.py:38
  61.8 9.8 %collective-permute-start.17 = (bf16[8,4096]{1,0:T(8,128)(2,1)S(1)}, bf16[8,4096]{1,0:T(8,128)(2,1)S(1)}, u32[]{:S(2)}, u32[]{:S(2)}) collective-permute-start(bf16[8,4096]{1,0:T(8,128)(2,1)S(1)} %get-tuple-element.93), channel_id=1, source_target_pairs={{0,16},{2,18},{4,20},{6,22},{8,24},{10,26},{12,28},{14,30},{16,0},... | collective-permute-start | bytes 196616 | tf_op jit(solution)/shard_map/ppermute | solution.py:38
  64.2 7.4 %collective-permute-start.18 = (bf16[8,4096]{1,0:T(8,128)(2,1)S(1)}, bf16[8,4096]{1,0:T(8,128)(2,1)S(1)}, u32[]{:S(2)}, u32[]{:S(2)}) collective-permute-start(bf16[8,4096]{1,0:T(8,128)(2,1)S(1)} %get-tuple-element.94), channel_id=1, source_target_pairs={{0,8},{2,10},{4,12},{6,14},{8,0},{10,2},{12,4},{14,6},{16,24},{18,... | collective-permute-start | bytes 196616 | tf_op jit(solution)/shard_map/ppermute | solution.py:38
  64.7 6.9 %collective-permute-start.19 = (bf16[8,4096]{1,0:T(8,128)(2,1)S(1)}, bf16[8,4096]{1,0:T(8,128)(2,1)S(1)}, u32[]{:S(2)}, u32[]{:S(2)}) collective-permute-start(bf16[8,4096]{1,0:T(8,128)(2,1)S(1)} %get-tuple-element.95), channel_id=1, source_target_pairs={{0,24},{2,26},{4,28},{6,30},{8,16},{10,18},{12,20},{14,22},{16,8},... | collective-permute-start | bytes 196616 | tf_op jit(solution)/shard_map/ppermute | solution.py:38

commit v12 on v11

--- a/solution.py
+++ b/solution.py
@@ -261,7 +261,7 @@
 
 
 def step_slots(slots):
-    return max(n for n in range(1, 17) if slots % n == 0)
+    return max(n for n in range(1, 33) if slots % n == 0)
 
 
 def gu_grad_body(first, given, index, count, d_pair, turned, *refs):
@@ -276,13 +276,26 @@
         slots.copy.start()
         slots.copy.wait()
 
-    for j in range(gate_out.shape[0]):
-        slot = (step + first) * gate_out.shape[0] + j
-        d, f = slots.place(slot, f_blocks)
-        result = jnp.dot(turned[d], d_pair[f], preferred_element_type=F32)
-        result = jnp.where(slot < slots.live, result, 0.0).astype(BF16)
-        gate_out[j] = result[:, :block]
-        up_out[j] = result[:, block:]
+    chunk = gate_out.shape[0]
+    begin = (step + first) * chunk
+
+    def work(masked):
+        for j in range(chunk):
+            d, f = slots.place(begin + j, f_blocks)
+            result = jnp.dot(turned[d], d_pair[f], preferred_element_type=F32)
+            if masked:
+                result = jnp.where(begin + j < slots.live, result, 0.0)
+            result = result.astype(BF16)
+            gate_out[j] = result[:, :block]
+            up_out[j] = result[:, block:]
+
+    @pl.when(begin + chunk <= slots.live)
+    def _():
+        work(False)
+
+    @pl.when(begin + chunk > slots.live)
+    def _():
+        work(True)
 
 
 def gu_grads(index, count, d_pair, turned, total, begin, end, before):
@@ -337,29 +350,37 @@
     )(own, *recv)
 
 
-def down_grad_body(index, count, near, far, *refs):
-    *pieces, out, index_here, slots_sem, turned, dense, sem = refs
+def down_blocks(first, hidden, pieces, dense, turned):
+    f_blocks, tokens, block = hidden.shape
+    d_blocks = pieces[0].shape[1] // block
+    group = 2 if f_blocks % 2 == 0 else 1
+    for f in range(f_blocks):
+        turned[f * block : (f + 1) * block, :] = hidden[f].T
+    for d in range(0, d_blocks, 2):
+        y = jnp.concatenate([piece[:, d * block : (d + 2) * block] for piece in pieces], axis=0)
+        for f in range(0, f_blocks, group):
+            rows = turned[f * block : (f + group) * block, :]
+            result = jnp.dot(rows, y, preferred_element_type=F32).astype(BF16)
+            for row in range(group):
+                for side in range(2):
+                    dense[(first + f + row) * d_blocks + d + side] = result[
+                        row * block : (row + 1) * block, side * block : (side + 1) * block
+                    ]
+
+
+def down_first_body(hidden, *refs):
+    *pieces, dense, turned = refs
+    dense[dense.shape[0] - 1] = jnp.zeros(dense.shape[1:], dense.dtype)
+    down_blocks(0, hidden, pieces, dense, turned)
+
+
+def down_second_body(first, index, count, hidden, _, *refs):
+    *pieces, out, dense, index_here, slots_sem, turned, sem = refs
     slots = Slots(index, count, index_here, slots_sem)
     slots.copy.start()
-    block = dense.shape[1]
-    f_blocks = turned.shape[0] // block
-    d_blocks = (dense.shape[0] - 1) // f_blocks
-    zeros = f_blocks * d_blocks
-    dense[zeros] = jnp.zeros(dense.shape[1:], dense.dtype)
-    for f in range(f_blocks):
-        half = (near, far)[f * 2 // f_blocks]
-        turned[f * block : (f + 1) * block, :] = half[f % (f_blocks // 2)].T
-    for d in range(0, d_blocks, 2):
-        y = jnp.concatenate([piece[:, d * block : (d + 2) * block] for piece in pieces], axis=0)
-        for f in range(0, f_blocks, 2):
-            rows = turned[f * block : (f + 2) * block, :]
-            result = jnp.dot(rows, y, preferred_element_type=F32).astype(BF16)
-            for row in range(2):
-                for side in range(2):
-                    dense[(f + row) * d_blocks + d + side] = result[
-                        row * block : (row + 1) * block, side * block : (side + 1) * block
-                    ]
+    down_blocks(first, hidden, pieces, dense, turned)
     slots.copy.wait()
+    zeros = dense.shape[0] - 1
     total = out.shape[0]
 
     @pl.loop(0, total, unroll=max(n for n in (1, 2, 4, 8) if total % n == 0))
@@ -370,26 +391,44 @@
     pltpu.make_async_copy(out, out, sem).wait()
 
 
-def down_grads(index, count, pieces, near, far, slots):
-    f_blocks, tokens, block = near.shape
-    f_blocks = 2 * f_blocks
+def down_first(pieces, hidden, f_blocks):
+    _, tokens, block = hidden.shape
+    blocks = f_blocks * (pieces[0].shape[1] // block) + 1
+    return pl.pallas_call(
+        down_first_body,
+        out_shape=pltpu.VMEM((blocks, block, block), BF16),
+        in_specs=[WHOLE] * (1 + len(pieces)),
+        out_specs=WHOLE,
+        scratch_shapes=[pltpu.VMEM((hidden.shape[0] * block, tokens), BF16)],
+        compiler_params=params(),
+        cost_estimate=cost(blocks * block * block * tokens, 2 * blocks * block * block),
+        name="down_first",
+    )(hidden, *pieces)
+
+
+def down_second(index, count, pieces, hidden, dense, slots):
+    far_blocks, tokens, block = hidden.shape
     d_blocks = pieces[0].shape[1] // block
-    blocks = f_blocks * d_blocks + 1
-    return pl.pallas_call(
-        down_grad_body,
-        out_shape=jax.ShapeDtypeStruct((slots, block, block), BF16),
+    first = (dense.shape[0] - 1) // d_blocks - far_blocks
+    out, _ = pl.pallas_call(
+        functools.partial(down_second_body, first),
+        out_shape=(
+            jax.ShapeDtypeStruct((slots, block, block), BF16),
+            pltpu.VMEM(dense.shape, BF16),
+        ),
         in_specs=[IN_HBM, SCALARS] + [WHOLE] * (2 + len(pieces)),
-        out_specs=IN_HBM,
+        out_specs=(IN_HBM, WHOLE),
         scratch_shapes=[
             *Slots.scratch(index),
-            pltpu.VMEM((f_blocks * block, tokens), BF16),
-            pltpu.VMEM((blocks, block, block), BF16),
+            pltpu.VMEM((far_blocks * block, tokens), BF16),
             pltpu.SemaphoreType.DMA,
         ],
-        compiler_params=params(VMEM_LIMIT + 2 * blocks * block * block),
-        cost_estimate=cost(2 * slots * block * block * tokens, 2 * slots * block * block),
-        name="down_grads",
-    )(in_hbm(index), count, near, far, *pieces)
+        input_output_aliases={3: 1},
+        compiler_params=params(),
+        cost_estimate=cost(slots * block * block * tokens, 2 * slots * block * block),
+        name="down_second",
+    )(in_hbm(index), count, hidden, resident(dense), *pieces)
+    return out
 
 
 def on_device(
@@ -438,9 +477,12 @@
     near_hidden, near_coef = activate(near_own, near_recv)
     down_w, near_hidden = lax.optimization_barrier((down_w, near_hidden))
     dh_own, dh_send, turned = d_hidden(y_pieces, x_pieces, down_w)
+    y_pieces, dh_send = lax.optimization_barrier((y_pieces, dh_send))
     dh_recv = exchange(dh_send)
+    dense = down_first(y_pieces, near_hidden, f_blocks)
+    far_own, dense = lax.optimization_barrier((far_own, dense))
     far_hidden, far_coef = activate(far_own, far_recv)
-    down_grad = down_grads(down_index, down_count, y_pieces, near_hidden, far_hidden, slots)
+    down_grad = down_second(down_index, down_count, y_pieces, far_hidden, dense, slots)
     down_grad, far_coef = lax.optimization_barrier((down_grad, far_coef))
     halves, d_pair = d_tokens_parts((near_coef, far_coef), dh_own, dh_recv, *weights)
 

time: 72.8 us -> 71.3 us (0.979)
  waiting for transfers between devices: 13.3 us -> 10.7 us
  Pallas kernels: 34.6 us -> 36.4 us
    pallas_call x3, Pallas kernels: 8.07 us -> 10.9 us  [fill(): pl.pallas_call(fill_body, out_shape=pltpu.VMEM((outer, inner, block, bloc...]
    ppermute x20, waiting for transfers between devices: 13.3 us -> 10.7 us  [swap(): return lax.ppermute(array, axis, [(i, i ^ flip) for i in range(size)])]
    pallas_call x2, Pallas kernels: 10.6 us -> 9.41 us  [gu_grads(): pl.pallas_call(functools.partial(gu_grad_body, first, len(before)), out_s...]
    pallas_call x1 -> x2, Pallas kernels: 5.52 us -> 5.77 us  [the longest x1 4.48 us: down_second(): pl.pallas_call(functools.partial(down_second_body, first), out_shape=(jax...]
  transfers between devices with their start and end apart: 20 -> 20, of which waited for: 8 -> 9; matrix products, arithmetic and copies ran while one was open for 0% -> 0% of each run, Pallas kernels for 44% -> 48%
where the time goes in v12:
time: 71.3 us; the launch traced here: 70.9 us
  Pallas kernels  36.4 us (51%)
  starting transfers between devices  20.6 us (29%)
  waiting for transfers between devices  10.7 us (15%)
  between operations  2.22 us (3%)
  other arithmetic  0.89 us (1%)
    ppermute x20, starting transfers between devices, swap(): return lax.ppermute(array, axis, [(i, i ^ flip) for i in range(size)])  20.6 us
    pallas_call x3, Pallas kernels, fill(): pl.pallas_call(fill_body, out_shape=pltpu.VMEM((outer, inner, block, bloc...  10.9 us
    ppermute x20, waiting for transfers between devices, swap(): return lax.ppermute(array, axis, [(i, i ^ flip) for i in range(size)])  10.7 us
    pallas_call x2, Pallas kernels, gu_grads(): pl.pallas_call(functools.partial(gu_grad_body, first, len(before)), out_s...  9.41 us
    pallas_call x1, Pallas kernels, down_second(): pl.pallas_call(functools.partial(down_second_body, first), out_shape=(jax...  4.48 us
    pallas_call x1, Pallas kernels, d_hidden(): pl.pallas_call(functools.partial(d_hidden_body, group, len(y_pieces)), ou...  2.63 us
    pallas_call x1, Pallas kernels, d_tokens_parts(): pl.pallas_call(functools.partial(d_tokens_first_body, group), out_shape=(...  2.54 us
    pallas_call x2, Pallas kernels, gate_up(): pl.pallas_call(functools.partial(gate_up_body, half * f_blocks // 2), out...  2.5 us
  transfers between devices with their start and end apart: 20, of which 9 were waited for; matrix products, arithmetic and copies ran while one was open for 0% of the time, Pallas kernels for 48%

profile of v12, /device:TPU:0, one launch (start us, length us, event | category | flops | bytes accessed | tf_op | source)
XLA Modules:
  0.0 70.9 jit_solution(5163323006540603052)
XLA Ops:
  0.6 4.1 %collective-permute-start = (bf16[8,4096]{1,0:T(8,128)(2,1)}, bf16[8,4096]{1,0:T(8,128)(2,1)S(1)}, u32[]{:S(2)}, u32[]{:S(2)}) collective-permute-start(bf16[8,4096]{1,0:T(8,128)(2,1)} %param.9), channel_id=1, source_target_pairs={{0,16},{2,18},{4,20},{6,22},{8,24},{10,26},{12,28},{14,30},{16,0},... | collective-permute-start | bytes 196616 | tf_op jit(solution)/shard_map/ppermute | solution.py:38
  6.0 4.0 %fill.3.refs_4_.gate_w = bf16[32,8,128,128]{3,2,1,0:T(8,128)(2,1)S(1)} custom-call(s32[1,1,192]{2,1,0:T(1,128)} %index.9, s32[1,1]{1,0:T(1,128)S(6)} %copy.19.count, bf16[1,1,192,128,128]{4,3,2,1,0:T(8,128)(2,1)} %source.3, s32[1,1]{1,0:T(1,128)S(6)} %copy.20.refs_0_.count), custom_call_target="tpu_custom_call" | custom-call | bytes 6291456 | tf_op jit(solution)/shard_map/fill/pallas_call | solution.py:92
  10.1 0.9 %collective-permute-start.1 = (bf16[16,4096]{1,0:T(8,128)(2,1)S(1)}, bf16[16,4096]{1,0:T(8,128)(2,1)S(1)}, u32[]{:S(2)}, u32[]{:S(2)}) collective-permute-start(bf16[16,4096]{1,0:T(8,128)(2,1)S(1)} %pad_maximum_fusion.3), channel_id=1, source_target_pairs={{0,8},{2,10},{4,12},{6,14},{8,0},{10,2},{12,4},{14,6},{16,24},{18,... | collective-permute-start | bytes 393224 | tf_op jit(solution)/shard_map/ppermute | solution.py:38
  11.0 4.0 %fill.4.refs_5_.up_w = bf16[32,8,128,128]{3,2,1,0:T(8,128)(2,1)S(1)} custom-call(s32[1,1,192]{2,1,0:T(1,128)} %index.9, s32[1,1]{1,0:T(1,128)S(6)} %copy.19.count, bf16[1,1,192,128,128]{4,3,2,1,0:T(8,128)(2,1)} %source.4), custom_call_target="tpu_custom_call" | custom-call | bytes 6291456 | tf_op jit(solution)/shard_map/fill/pallas_call | solution.py:92
  15.2 0.9 %collective-permute-start.6 = (bf16[8,4096]{1,0:T(8,128)(2,1)S(1)}, bf16[8,4096]{1,0:T(8,128)(2,1)S(1)}, u32[]{:S(2)}, u32[]{:S(2)}) collective-permute-start(bf16[8,4096]{1,0:T(8,128)(2,1)S(1)} %copy-done.1), channel_id=1, source_target_pairs={{0,16},{2,18},{4,20},{6,22},{8,24},{10,26},{12,28},{14,30},{16,0},... | collective-permute-start | bytes 196616 | tf_op jit(solution)/shard_map/ppermute | solution.py:38
  16.1 1.6 %collective-permute-start.2 = (bf16[32,4096]{1,0:T(8,128)(2,1)S(1)}, bf16[32,4096]{1,0:T(8,128)(2,1)S(1)}, u32[]{:S(2)}, u32[]{:S(2)}) collective-permute-start(bf16[32,4096]{1,0:T(8,128)(2,1)S(1)} %pad_maximum_fusion.1.refs_0_.refs_4_), channel_id=1, source_target_pairs={{0,4},{2,6},{4,0},{6,2},{8,12},{10,14},{12,8},{14,10},{16,20},{18,... | collective-permute-start | bytes 786440 | tf_op jit(solution)/shard_map/ppermute | solution.py:38
  17.6 2.9 %fill.5.refs_8_ = bf16[8,32,128,128]{3,2,1,0:T(8,128)(2,1)S(1)} custom-call(s32[1,1,192]{2,1,0:T(1,128)} %index.7, s32[1,1]{1,0:T(1,128)S(6)} %copy.20.refs_0_.count, bf16[1,1,192,128,128]{4,3,2,1,0:T(8,128)(2,1)} %source.5), custom_call_target="tpu_custom_call" | custom-call | bytes 6291456 | tf_op jit(solution)/shard_map/fill/pallas_call | solution.py:92
  21.1 0.8 %collective-permute-start.7 = (bf16[16,4096]{1,0:T(8,128)(2,1)S(1)}, bf16[16,4096]{1,0:T(8,128)(2,1)S(1)}, u32[]{:S(2)}, u32[]{:S(2)}) collective-permute-start(bf16[16,4096]{1,0:T(8,128)(2,1)S(1)} %pad_maximum_fusion.4), channel_id=1, source_target_pairs={{0,8},{2,10},{4,12},{6,14},{8,0},{10,2},{12,4},{14,6},{16,24},{18,... | collective-permute-start | bytes 393224 | tf_op jit(solution)/shard_map/ppermute | solution.py:38
  21.9 1.2 %collective-permute-done.2.refs_1_.refs_5_ = bf16[32,4096]{1,0:T(8,128)(2,1)S(1)} collective-permute-done((bf16[32,4096]{1,0:T(8,128)(2,1)S(1)}, bf16[32,4096]{1,0:T(8,128)(2,1)S(1)}, u32[]{:S(2)}, u32[]{:S(2)}) %collective-permute-start.2) | collective-permute-done | bytes 262176 | tf_op jit(solution)/shard_map/ppermute | solution.py:38
  23.1 3.0 %collective-permute-done.7 = bf16[16,4096]{1,0:T(8,128)(2,1)S(1)} collective-permute-done((bf16[16,4096]{1,0:T(8,128)(2,1)S(1)}, bf16[16,4096]{1,0:T(8,128)(2,1)S(1)}, u32[]{:S(2)}, u32[]{:S(2)}) %collective-permute-start.7) | collective-permute-done | bytes 131104 | tf_op jit(solution)/shard_map/ppermute | solution.py:38
  26.3 1.3 %gate_up.2 = (f32[4,128,256]{2,1,0:T(8,128)S(1)}, bf16[4,128,256]{2,1,0:T(8,128)(2,1)S(1)}) custom-call(bf16[32,4096]{1,0:T(8,128)(2,1)S(1)} %pad_maximum_fusion.1.refs_0_.refs_4_, bf16[32,4096]{1,0:T(8,128)(2,1)S(1)} %collective-permute-done.2.refs_1_.refs_5_, bf16[32,4096]{1,0:T(8,128)(2,1)S(1)} %collective-permute-done.3.refs_2_.refs_6_, ...), custom_call_target="tpu_custom_call" | custom-call | flops 1073741824 | bytes 8388608 | tf_op jit(solution)/shard_map/gate_up/pallas_call | solution.py:129
  27.5 1.8 %collective-permute-start.5 = (bf16[4,128,256]{2,1,0:T(8,128)(2,1)S(1)}, bf16[4,128,256]{2,1,0:T(8,128)(2,1)S(1)}, u32[]{:S(2)}, u32[]{:S(2)}) collective-permute-start(bf16[4,128,256]{2,1,0:T(8,128)(2,1)S(1)} %get-tuple-element.68), channel_id=1, source_target_pairs={{0,1},{1,0},{2,3},{3,2},{4,5},{5,4},{6,7},{7,6},{8,9},{9,8},{10,11... | collective-permute-start | bytes 786440 | tf_op jit(solution)/shard_map/ppermute | solution.py:38
  29.3 1.2 %gate_up.3 = (f32[4,128,256]{2,1,0:T(8,128)S(1)}, bf16[4,128,256]{2,1,0:T(8,128)(2,1)S(1)}) custom-call(bf16[32,4096]{1,0:T(8,128)(2,1)S(1)} %pad_maximum_fusion.1.refs_0_.refs_4_, bf16[32,4096]{1,0:T(8,128)(2,1)S(1)} %collective-permute-done.2.refs_1_.refs_5_, bf16[32,4096]{1,0:T(8,128)(2,1)S(1)} %collective-permute-done.3.refs_2_.refs_6_, ...), custom_call_target="tpu_custom_call" | custom-call | flops 1073741824 | bytes 8388608 | tf_op jit(solution)/shard_map/gate_up/pallas_call | solution.py:129
  30.6 2.0 %collective-permute-done.8.refs_1_ = bf16[32,4096]{1,0:T(8,128)(2,1)S(1)} collective-permute-done((bf16[32,4096]{1,0:T(8,128)(2,1)S(1)}, bf16[32,4096]{1,0:T(8,128)(2,1)S(1)}, u32[]{:S(2)}, u32[]{:S(2)}) %collective-permute-start.8) | collective-permute-done | bytes 262176 | tf_op jit(solution)/shard_map/ppermute | solution.py:38
  33.1 1.1 %collective-permute-start.11 = (bf16[4,128,256]{2,1,0:T(8,128)(2,1)S(1)}, bf16[4,128,256]{2,1,0:T(8,128)(2,1)S(1)}, u32[]{:S(2)}, u32[]{:S(2)}) collective-permute-start(bf16[4,128,256]{2,1,0:T(8,128)(2,1)S(1)} %get-tuple-element.81), channel_id=1, source_target_pairs={{0,1},{1,0},{2,3},{3,2},{4,5},{5,4},{6,7},{7,6},{8,9},{9,8},{10,11... | collective-permute-start | bytes 786440 | tf_op jit(solution)/shard_map/ppermute | solution.py:38
  34.6 2.6 %d_hidden.1 = (f32[8,128,128]{2,1,0:T(8,128)S(1)}, bf16[8,128,128]{2,1,0:T(8,128)(2,1)S(1)}, bf16[32,128,128]{2,1,0:T(8,128)(2,1)S(1)}) custom-call(bf16[32,4096]{1,0:T(8,128)(2,1)S(1)} %pad_maximum_fusion.2.refs_0_, bf16[32,4096]{1,0:T(8,128)(2,1)S(1)} %collective-permute-done.8.refs_1_, bf16[32,4096]{1,0:T(8,128)(2,1)S(1)} %collective-permute-done.9.refs_2_, ...), custom_call_target="tpu_custom_call" | custom-call | flops 1073741824 | bytes 8388608 | tf_op jit(solution)/shard_map/d_hidden/pallas_call | solution.py:171
  37.3 1.7 %collective-permute-start.12 = (bf16[8,128,128]{2,1,0:T(8,128)(2,1)S(1)}, bf16[8,128,128]{2,1,0:T(8,128)(2,1)S(1)}, u32[]{:S(2)}, u32[]{:S(2)}) collective-permute-start(bf16[8,128,128]{2,1,0:T(8,128)(2,1)S(1)} %get-tuple-element.97), channel_id=1, source_target_pairs={{0,1},{1,0},{2,3},{3,2},{4,5},{5,4},{6,7},{7,6},{8,9},{9,8},{10,11... | collective-permute-start | bytes 786440 | tf_op jit(solution)/shard_map/ppermute | solution.py:38
  39.0 1.3 %down_first.1._ = bf16[257,128,128]{2,1,0:T(8,128)(2,1)S(1)} custom-call(bf16[4,128,128]{2,1,0:T(8,128)(2,1)S(1)} %get-tuple-element.78.hidden, bf16[32,4096]{1,0:T(8,128)(2,1)S(1)} %pad_maximum_fusion.2.refs_0_, bf16[32,4096]{1,0:T(8,128)(2,1)S(1)} %collective-permute-done.8.refs_1_, bf16[32,4096]{1,0:T(8,128)(2,1)S(1)} %collective-permute-done.9.refs_2_, ...), custom_call_target="tpu_custom_call" | custom-call | flops 538968064 | bytes 8421376 | tf_op jit(solution)/shard_map/down_first/pallas_call | solution.py:397
  40.3 2.0 %collective-permute-done.11.refs_1_ = bf16[4,128,256]{2,1,0:T(8,128)(2,1)S(1)} collective-permute-done((bf16[4,128,256]{2,1,0:T(8,128)(2,1)S(1)}, bf16[4,128,256]{2,1,0:T(8,128)(2,1)S(1)}, u32[]{:S(2)}, u32[]{:S(2)}) %collective-permute-start.11) | collective-permute-done | bytes 262176 | tf_op jit(solution)/shard_map/ppermute | solution.py:38
  42.4 4.5 %down_second.1 = (bf16[192,128,128]{2,1,0:T(8,128)(2,1)}, bf16[257,128,128]{2,1,0:T(8,128)(2,1)S(1)}) custom-call(s32[1,1,192]{2,1,0:T(1,128)} %index.7, s32[1,1]{1,0:T(1,128)S(6)} %copy.20.refs_0_.count, bf16[4,128,128]{2,1,0:T(8,128)(2,1)S(1)} %get-tuple-element.91.hidden, ...), custom_call_target="tpu_custom_call", output_to_operand_aliasing={{1}: (3, {})} | custom-call | flops 402653184 | bytes 6291456 | tf_op jit(solution)/shard_map/down_second/pallas_call | solution.py:413
  46.9 2.5 %d_tokens_first.1 = (f32[64,2048]{1,0:T(8,128)S(1)}, bf16[64,2048]{1,0:T(8,128)(2,1)S(1)}, bf16[8,128,256]{2,1,0:T(8,128)(2,1)S(1)}, bf16[2048,128]{1,0:T(8,128)(2,1)S(1)}) custom-call(f32[4,128,256]{2,1,0:T(8,128)S(1)} %get-tuple-element.69.refs_0_, f32[4,128,256]{2,1,0:T(8,128)S(1)} %get-tuple-element.95.refs_1_, ...), custom_call_target="tpu_custom_call" | custom-call | flops 1073741824 | bytes 8388608 | tf_op jit(solution)/shard_map/d_tokens_first/pallas_call | solution.py:240
  49.6 2.4 %d_tokens_second.1 = (f32[64,2048]{1,0:T(8,128)S(1)}, bf16[64,2048]{1,0:T(8,128)(2,1)S(1)}) custom-call(bf16[2048,128]{1,0:T(8,128)(2,1)S(1)} %get-tuple-element.100.turned, bf16[32,8,128,128]{3,2,1,0:T(8,128)(2,1)S(1)} %fill.3.refs_4_.gate_w, bf16[32,8,128,128]{3,2,1,0:T(8,128)(2,1)S(1)} %fill.4.refs_5_.up_w), custom_call_target="tpu_custom_call" | custom-call | flops 1073741824 | bytes 8388608 | tf_op jit(solution)/shard_map/d_tokens_second/pallas_call | solution.py:252
  52.0 0.6 collective-permute-start.15
  52.6 0.9 %collective-permute-start.14 = (bf16[32,2048]{1,0:T(8,128)(2,1)S(1)}, bf16[32,2048]{1,0:T(8,128)(2,1)S(1)}, u32[]{:S(2)}, u32[]{:S(2)}) collective-permute-start(bf16[32,2048]{1,0:T(8,128)(2,1)S(1)} %slice.65), channel_id=1, source_target_pairs={{0,4},{2,6},{4,0},{6,2},{8,12},{10,14},{12,8},{14,10},{16,20},{18,... | collective-permute-start | bytes 393224 | tf_op jit(solution)/shard_map/ppermute | solution.py:38
  53.8 1.1 %collective-permute-start.16 = (bf16[32,2048]{1,0:T(8,128)(2,1)S(1)}, bf16[32,2048]{1,0:T(8,128)(2,1)S(1)}, u32[]{:S(2)}, u32[]{:S(2)}) collective-permute-start(bf16[32,2048]{1,0:T(8,128)(2,1)S(1)} %slice.64), channel_id=1, source_target_pairs={{0,4},{2,6},{4,0},{6,2},{8,12},{10,14},{12,8},{14,10},{16,20},{18,... | collective-permute-start | bytes 393224 | tf_op jit(solution)/shard_map/ppermute | solution.py:38
  54.9 4.7 %gu_grads.2 = (bf16[192,128,128]{2,1,0:T(8,128)(2,1)}, bf16[192,128,128]{2,1,0:T(8,128)(2,1)}) custom-call(s32[1,1,192]{2,1,0:T(1,128)} %index.9, s32[1,1]{1,0:T(1,128)S(6)} %copy.19.count, bf16[8,128,256]{2,1,0:T(8,128)(2,1)S(1)} %get-tuple-element.112.d_pair, bf16[32,128,128]{2,1,0:T(8,128)(2,1)S(1)} %get-tuple-element.106.turned), custom_call_target="tpu_custom_call" | custom-call | flops 805306368 | bytes 6291456 | tf_op jit(solution)/shard_map/gu_grads/pallas_call | solution.py:308
  59.6 1.3 %collective-permute-done.16 = bf16[32,2048]{1,0:T(8,128)(2,1)S(1)} collective-permute-done((bf16[32,2048]{1,0:T(8,128)(2,1)S(1)}, bf16[32,2048]{1,0:T(8,128)(2,1)S(1)}, u32[]{:S(2)}, u32[]{:S(2)}) %collective-permute-start.16) | collective-permute-done | bytes 131104 | tf_op jit(solution)/shard_map/ppermute | solution.py:38
  61.0 0.8 %collective-permute-start.17 = (bf16[8,4096]{1,0:T(8,128)(2,1)S(1)}, bf16[8,4096]{1,0:T(8,128)(2,1)S(1)}, u32[]{:S(2)}, u32[]{:S(2)}) collective-permute-start(bf16[8,4096]{1,0:T(8,128)(2,1)S(1)} %get-tuple-element.109), channel_id=1, source_target_pairs={{0,16},{2,18},{4,20},{6,22},{8,24},{10,26},{12,28},{14,30},{16,0},... | collective-permute-start | bytes 196616 | tf_op jit(solution)/shard_map/ppermute | solution.py:38
  61.8 1.6 %collective-permute-start.18 = (bf16[8,4096]{1,0:T(8,128)(2,1)S(1)}, bf16[8,4096]{1,0:T(8,128)(2,1)S(1)}, u32[]{:S(2)}, u32[]{:S(2)}) collective-permute-start(bf16[8,4096]{1,0:T(8,128)(2,1)S(1)} %get-tuple-element.110), channel_id=1, source_target_pairs={{0,8},{2,10},{4,12},{6,14},{8,0},{10,2},{12,4},{14,6},{16,24},{18,... | collective-permute-start | bytes 196616 | tf_op jit(solution)/shard_map/ppermute | solution.py:38
  63.4 2.1 %collective-permute-start.19 = (bf16[8,4096]{1,0:T(8,128)(2,1)S(1)}, bf16[8,4096]{1,0:T(8,128)(2,1)S(1)}, u32[]{:S(2)}, u32[]{:S(2)}) collective-permute-start(bf16[8,4096]{1,0:T(8,128)(2,1)S(1)} %get-tuple-element.111), channel_id=1, source_target_pairs={{0,24},{2,26},{4,28},{6,30},{8,16},{10,18},{12,20},{14,22},{16,8},... | collective-permute-start | bytes 196616 | tf_op jit(solution)/shard_map/ppermute | solution.py:38
  65.5 4.7 %gu_grads.3 = (bf16[192,128,128]{2,1,0:T(8,128)(2,1)}, bf16[192,128,128]{2,1,0:T(8,128)(2,1)}) custom-call(s32[1,1,192]{2,1,0:T(1,128)} %index.9, s32[1,1]{1,0:T(1,128)S(6)} %copy.19.count, bf16[8,128,256]{2,1,0:T(8,128)(2,1)S(1)} %get-tuple-element.112.d_pair, ...), custom_call_target="tpu_custom_call", output_to_operand_aliasing={{0}: (4, {}), {1}: (5, {})} | custom-call | flops 805306368 | bytes 6291456 | tf_op jit(solution)/shard_map/gu_grads/pallas_call | solution.py:308
  70.2 0.7 fusion.5
  (39 shorter events, 2.3 us)
Async XLA Ops:
  0.6 9.4 %collective-permute-start = (bf16[8,4096]{1,0:T(8,128)(2,1)}, bf16[8,4096]{1,0:T(8,128)(2,1)S(1)}, u32[]{:S(2)}, u32[]{:S(2)}) collective-permute-start(bf16[8,4096]{1,0:T(8,128)(2,1)} %param.9), channel_id=1, source_target_pairs={{0,16},{2,18},{4,20},{6,22},{8,24},{10,26},{12,28},{14,30},{16,0},... | collective-permute-start | bytes 196616 | tf_op jit(solution)/shard_map/ppermute | solution.py:38
  6.0 4.0 %copy-start = (bf16[8,4096]{1,0:T(8,128)(2,1)S(1)}, bf16[8,4096]{1,0:T(8,128)(2,1)}, u32[]{:S(2)}) copy-start(bf16[8,4096]{1,0:T(8,128)(2,1)} %param.9) | copy-start | bytes 196612
  10.1 5.1 %copy-start.1 = (bf16[8,4096]{1,0:T(8,128)(2,1)S(1)}, bf16[8,4096]{1,0:T(8,128)(2,1)}, u32[]{:S(2)}) copy-start(bf16[8,4096]{1,0:T(8,128)(2,1)} %param.10) | copy-start | bytes 196612
  10.1 5.0 %collective-permute-start.1 = (bf16[16,4096]{1,0:T(8,128)(2,1)S(1)}, bf16[16,4096]{1,0:T(8,128)(2,1)S(1)}, u32[]{:S(2)}, u32[]{:S(2)}) collective-permute-start(bf16[16,4096]{1,0:T(8,128)(2,1)S(1)} %pad_maximum_fusion.3), channel_id=1, source_target_pairs={{0,8},{2,10},{4,12},{6,14},{8,0},{10,2},{12,4},{14,6},{16,24},{18,... | collective-permute-start | bytes 393224 | tf_op jit(solution)/shard_map/ppermute | solution.py:38
  15.2 5.9 %collective-permute-start.6 = (bf16[8,4096]{1,0:T(8,128)(2,1)S(1)}, bf16[8,4096]{1,0:T(8,128)(2,1)S(1)}, u32[]{:S(2)}, u32[]{:S(2)}) collective-permute-start(bf16[8,4096]{1,0:T(8,128)(2,1)S(1)} %copy-done.1), channel_id=1, source_target_pairs={{0,16},{2,18},{4,20},{6,22},{8,24},{10,26},{12,28},{14,30},{16,0},... | collective-permute-start | bytes 196616 | tf_op jit(solution)/shard_map/ppermute | solution.py:38
  16.1 7.0 %collective-permute-start.2 = (bf16[32,4096]{1,0:T(8,128)(2,1)S(1)}, bf16[32,4096]{1,0:T(8,128)(2,1)S(1)}, u32[]{:S(2)}, u32[]{:S(2)}) collective-permute-start(bf16[32,4096]{1,0:T(8,128)(2,1)S(1)} %pad_maximum_fusion.1.refs_0_.refs_4_), channel_id=1, source_target_pairs={{0,4},{2,6},{4,0},{6,2},{8,12},{10,14},{12,8},{14,10},{16,20},{18,... | collective-permute-start | bytes 786440 | tf_op jit(solution)/shard_map/ppermute | solution.py:38
  21.1 5.0 %collective-permute-start.7 = (bf16[16,4096]{1,0:T(8,128)(2,1)S(1)}, bf16[16,4096]{1,0:T(8,128)(2,1)S(1)}, u32[]{:S(2)}, u32[]{:S(2)}) collective-permute-start(bf16[16,4096]{1,0:T(8,128)(2,1)S(1)} %pad_maximum_fusion.4), channel_id=1, source_target_pairs={{0,8},{2,10},{4,12},{6,14},{8,0},{10,2},{12,4},{14,6},{16,24},{18,... | collective-permute-start | bytes 393224 | tf_op jit(solution)/shard_map/ppermute | solution.py:38
  21.9 4.3 %collective-permute-start.3 = (bf16[32,4096]{1,0:T(8,128)(2,1)S(1)}, bf16[32,4096]{1,0:T(8,128)(2,1)S(1)}, u32[]{:S(2)}, u32[]{:S(2)}) collective-permute-start(bf16[32,4096]{1,0:T(8,128)(2,1)S(1)} %pad_maximum_fusion.1.refs_0_.refs_4_), channel_id=1, source_target_pairs={{0,2},{2,0},{4,6},{6,4},{8,10},{10,8},{12,14},{14,12},{16,18},{18,... | collective-permute-start | bytes 786440 | tf_op jit(solution)/shard_map/ppermute | solution.py:38
  23.1 3.2 %collective-permute-start.4 = (bf16[32,4096]{1,0:T(8,128)(2,1)S(1)}, bf16[32,4096]{1,0:T(8,128)(2,1)S(1)}, u32[]{:S(2)}, u32[]{:S(2)}) collective-permute-start(bf16[32,4096]{1,0:T(8,128)(2,1)S(1)} %collective-permute-done.2.refs_1_.refs_5_), channel_id=1, source_target_pairs={{0,2},{2,0},{4,6},{6,4},{8,10},{10,8},{12,14},{14,12},{16,18},{18,... | collective-permute-start | bytes 786440 | tf_op jit(solution)/shard_map/ppermute | solution.py:38
  26.2 6.4 %collective-permute-start.8 = (bf16[32,4096]{1,0:T(8,128)(2,1)S(1)}, bf16[32,4096]{1,0:T(8,128)(2,1)S(1)}, u32[]{:S(2)}, u32[]{:S(2)}) collective-permute-start(bf16[32,4096]{1,0:T(8,128)(2,1)S(1)} %pad_maximum_fusion.2.refs_0_), channel_id=1, source_target_pairs={{0,4},{2,6},{4,0},{6,2},{8,12},{10,14},{12,8},{14,10},{16,20},{18,... | collective-permute-start | bytes 786440 | tf_op jit(solution)/shard_map/ppermute | solution.py:38
  27.5 7.0 %collective-permute-start.5 = (bf16[4,128,256]{2,1,0:T(8,128)(2,1)S(1)}, bf16[4,128,256]{2,1,0:T(8,128)(2,1)S(1)}, u32[]{:S(2)}, u32[]{:S(2)}) collective-permute-start(bf16[4,128,256]{2,1,0:T(8,128)(2,1)S(1)} %get-tuple-element.68), channel_id=1, source_target_pairs={{0,1},{1,0},{2,3},{3,2},{4,5},{5,4},{6,7},{7,6},{8,9},{9,8},{10,11... | collective-permute-start | bytes 786440 | tf_op jit(solution)/shard_map/ppermute | solution.py:38
  32.6 2.0 %collective-permute-start.9 = (bf16[32,4096]{1,0:T(8,128)(2,1)S(1)}, bf16[32,4096]{1,0:T(8,128)(2,1)S(1)}, u32[]{:S(2)}, u32[]{:S(2)}) collective-permute-start(bf16[32,4096]{1,0:T(8,128)(2,1)S(1)} %pad_maximum_fusion.2.refs_0_), channel_id=1, source_target_pairs={{0,2},{2,0},{4,6},{6,4},{8,10},{10,8},{12,14},{14,12},{16,18},{18,... | collective-permute-start | bytes 786440 | tf_op jit(solution)/shard_map/ppermute | solution.py:38
  32.6 2.0 %collective-permute-start.10 = (bf16[32,4096]{1,0:T(8,128)(2,1)S(1)}, bf16[32,4096]{1,0:T(8,128)(2,1)S(1)}, u32[]{:S(2)}, u32[]{:S(2)}) collective-permute-start(bf16[32,4096]{1,0:T(8,128)(2,1)S(1)} %collective-permute-done.8.refs_1_), channel_id=1, source_target_pairs={{0,2},{2,0},{4,6},{6,4},{8,10},{10,8},{12,14},{14,12},{16,18},{18,... | collective-permute-start | bytes 786440 | tf_op jit(solution)/shard_map/ppermute | solution.py:38
  33.1 9.2 %collective-permute-start.11 = (bf16[4,128,256]{2,1,0:T(8,128)(2,1)S(1)}, bf16[4,128,256]{2,1,0:T(8,128)(2,1)S(1)}, u32[]{:S(2)}, u32[]{:S(2)}) collective-permute-start(bf16[4,128,256]{2,1,0:T(8,128)(2,1)S(1)} %get-tuple-element.81), channel_id=1, source_target_pairs={{0,1},{1,0},{2,3},{3,2},{4,5},{5,4},{6,7},{7,6},{8,9},{9,8},{10,11... | collective-permute-start | bytes 786440 | tf_op jit(solution)/shard_map/ppermute | solution.py:38
  37.3 9.7 %collective-permute-start.12 = (bf16[8,128,128]{2,1,0:T(8,128)(2,1)S(1)}, bf16[8,128,128]{2,1,0:T(8,128)(2,1)S(1)}, u32[]{:S(2)}, u32[]{:S(2)}) collective-permute-start(bf16[8,128,128]{2,1,0:T(8,128)(2,1)S(1)} %get-tuple-element.97), channel_id=1, source_target_pairs={{0,1},{1,0},{2,3},{3,2},{4,5},{5,4},{6,7},{7,6},{8,9},{9,8},{10,11... | collective-permute-start | bytes 786440 | tf_op jit(solution)/shard_map/ppermute | solution.py:38
  49.5 3.1 %collective-permute-start.13 = (bf16[64,2048]{1,0:T(8,128)(2,1)S(1)}, bf16[64,2048]{1,0:T(8,128)(2,1)S(1)}, u32[]{:S(2)}, u32[]{:S(2)}) collective-permute-start(bf16[64,2048]{1,0:T(8,128)(2,1)S(1)} %get-tuple-element.99), channel_id=1, source_target_pairs={{0,2},{2,0},{4,6},{6,4},{8,10},{10,8},{12,14},{14,12},{16,18},{18,... | collective-permute-start | bytes 786440 | tf_op jit(solution)/shard_map/ppermute | solution.py:38
  52.0 1.7 %collective-permute-start.15 = (bf16[64,2048]{1,0:T(8,128)(2,1)S(1)}, bf16[64,2048]{1,0:T(8,128)(2,1)S(1)}, u32[]{:S(2)}, u32[]{:S(2)}) collective-permute-start(bf16[64,2048]{1,0:T(8,128)(2,1)S(1)} %get-tuple-element.102), channel_id=1, source_target_pairs={{0,2},{2,0},{4,6},{6,4},{8,10},{10,8},{12,14},{14,12},{16,18},{18,... | collective-permute-start | bytes 786440 | tf_op jit(solution)/shard_map/ppermute | solution.py:38
  52.6 7.0 %collective-permute-start.14 = (bf16[32,2048]{1,0:T(8,128)(2,1)S(1)}, bf16[32,2048]{1,0:T(8,128)(2,1)S(1)}, u32[]{:S(2)}, u32[]{:S(2)}) collective-permute-start(bf16[32,2048]{1,0:T(8,128)(2,1)S(1)} %slice.65), channel_id=1, source_target_pairs={{0,4},{2,6},{4,0},{6,2},{8,12},{10,14},{12,8},{14,10},{16,20},{18,... | collective-permute-start | bytes 393224 | tf_op jit(solution)/shard_map/ppermute | solution.py:38
  53.8 7.1 %collective-permute-start.16 = (bf16[32,2048]{1,0:T(8,128)(2,1)S(1)}, bf16[32,2048]{1,0:T(8,128)(2,1)S(1)}, u32[]{:S(2)}, u32[]{:S(2)}) collective-permute-start(bf16[32,2048]{1,0:T(8,128)(2,1)S(1)} %slice.64), channel_id=1, source_target_pairs={{0,4},{2,6},{4,0},{6,2},{8,12},{10,14},{12,8},{14,10},{16,20},{18,... | collective-permute-start | bytes 393224 | tf_op jit(solution)/shard_map/ppermute | solution.py:38
  61.0 9.2 %collective-permute-start.17 = (bf16[8,4096]{1,0:T(8,128)(2,1)S(1)}, bf16[8,4096]{1,0:T(8,128)(2,1)S(1)}, u32[]{:S(2)}, u32[]{:S(2)}) collective-permute-start(bf16[8,4096]{1,0:T(8,128)(2,1)S(1)} %get-tuple-element.109), channel_id=1, source_target_pairs={{0,16},{2,18},{4,20},{6,22},{8,24},{10,26},{12,28},{14,30},{16,0},... | collective-permute-start | bytes 196616 | tf_op jit(solution)/shard_map/ppermute | solution.py:38
  61.8 8.4 %collective-permute-start.18 = (bf16[8,4096]{1,0:T(8,128)(2,1)S(1)}, bf16[8,4096]{1,0:T(8,128)(2,1)S(1)}, u32[]{:S(2)}, u32[]{:S(2)}) collective-permute-start(bf16[8,4096]{1,0:T(8,128)(2,1)S(1)} %get-tuple-element.110), channel_id=1, source_target_pairs={{0,8},{2,10},{4,12},{6,14},{8,0},{10,2},{12,4},{14,6},{16,24},{18,... | collective-permute-start | bytes 196616 | tf_op jit(solution)/shard_map/ppermute | solution.py:38
  63.4 6.8 %collective-permute-start.19 = (bf16[8,4096]{1,0:T(8,128)(2,1)S(1)}, bf16[8,4096]{1,0:T(8,128)(2,1)S(1)}, u32[]{:S(2)}, u32[]{:S(2)}) collective-permute-start(bf16[8,4096]{1,0:T(8,128)(2,1)S(1)} %get-tuple-element.111), channel_id=1, source_target_pairs={{0,24},{2,26},{4,28},{6,30},{8,16},{10,18},{12,20},{14,22},{16,8},... | collective-permute-start | bytes 196616 | tf_op jit(solution)/shard_map/ppermute | solution.py:38

commit v13 on v12

--- a/solution.py
+++ b/solution.py
@@ -462,7 +462,7 @@
     down_w = fill(index, down_count, down_vals, f_blocks, d_blocks)
     for flip in flips[:-1]:
         y = jnp.concatenate([y, swap(y, "wide", wide, 2 * flip)], axis=0)
-        y, down_w = lax.optimization_barrier((y, down_w))
+    x, down_w = lax.optimization_barrier((x, down_w))
     x_pieces = [x, x_recv, swap(x, "wide", wide, 1), swap(x_recv, "wide", wide, 1)]
     y, _ = lax.optimization_barrier((y, x_recv))
     y_recv = swap(y, "wide", wide, 2 * flips[-1])
@@ -489,7 +489,7 @@
     halves = [own + swap(send, "wide", wide, 1).astype(F32) for own, send in halves]
     kept = chips // 2 * rows
     far = [own[kept:].astype(BF16) for own in halves]
-    cut = slots // 2 if slots % 2 == 0 else slots
+    cut = slots * 2 // 3 if slots % 3 == 0 else slots
     far[1], d_pair = lax.optimization_barrier((far[1], d_pair))
     grads = gu_grads(gu_index, gu_count, d_pair, turned, slots, 0, cut, ())
     halves = [

time: 71.3 us -> 71.9 us (level)
  starting transfers between devices: 20.6 us -> 27.1 us
  waiting for transfers between devices: 10.7 us -> 6.87 us
  Pallas kernels: 36.4 us -> 34.1 us
    ppermute x20, starting transfers between devices: 20.6 us -> 27.1 us  [swap(): return lax.ppermute(array, axis, [(i, i ^ flip) for i in range(size)])]
    ppermute x20, waiting for transfers between devices: 10.7 us -> 6.87 us  [swap(): return lax.ppermute(array, axis, [(i, i ^ flip) for i in range(size)])]
    pallas_call x3, Pallas kernels: 10.9 us -> 9.03 us  [fill(): pl.pallas_call(fill_body, out_shape=pltpu.VMEM((outer, inner, block, bloc...]
  transfers between devices with their start and end apart: 20 -> 20, of which waited for: 9 -> 8; matrix products, arithmetic and copies ran while one was open for 0% -> 0% of each run, Pallas kernels for 48% -> 44%
where the time goes in v13:
time: 71.9 us; the launch traced here: 71.2 us
  Pallas kernels  34.1 us (47%)
  starting transfers between devices  27.1 us (38%)
  waiting for transfers between devices  6.87 us (10%)
  between operations  2.21 us (3%)
  other arithmetic  0.89 us (1%)
    ppermute x20, starting transfers between devices, swap(): return lax.ppermute(array, axis, [(i, i ^ flip) for i in range(size)])  27.1 us
    pallas_call x3, Pallas kernels, fill(): pl.pallas_call(fill_body, out_shape=pltpu.VMEM((outer, inner, block, bloc...  9.03 us
    pallas_call x2, Pallas kernels, gu_grads(): pl.pallas_call(functools.partial(gu_grad_body, first, len(before)), out_s...  8.91 us
    ppermute x20, waiting for transfers between devices, swap(): return lax.ppermute(array, axis, [(i, i ^ flip) for i in range(size)])  6.87 us
    pallas_call x1, Pallas kernels, down_second(): pl.pallas_call(functools.partial(down_second_body, first), out_shape=(jax...  4.48 us
    pallas_call x1, Pallas kernels, d_hidden(): pl.pallas_call(functools.partial(d_hidden_body, group, len(y_pieces)), ou...  2.63 us
    pallas_call x1, Pallas kernels, d_tokens_parts(): pl.pallas_call(functools.partial(d_tokens_first_body, group), out_shape=(...  2.54 us
    pallas_call x2, Pallas kernels, gate_up(): pl.pallas_call(functools.partial(gate_up_body, half * f_blocks // 2), out...  2.5 us
  transfers between devices with their start and end apart: 20, of which 8 were waited for; matrix products, arithmetic and copies ran while one was open for 0% of the time, Pallas kernels for 44%

profile of v13, /device:TPU:0, one launch (start us, length us, event | category | flops | bytes accessed | tf_op | source)
XLA Modules:
  0.0 71.2 jit_solution(14635201803842978248)
XLA Ops:
  0.6 4.1 %collective-permute-start = (bf16[8,4096]{1,0:T(8,128)(2,1)}, bf16[8,4096]{1,0:T(8,128)(2,1)S(1)}, u32[]{:S(2)}, u32[]{:S(2)}) collective-permute-start(bf16[8,4096]{1,0:T(8,128)(2,1)} %param.9), channel_id=1, source_target_pairs={{0,16},{2,18},{4,20},{6,22},{8,24},{10,26},{12,28},{14,30},{16,0},... | collective-permute-start | bytes 196616 | tf_op jit(solution)/shard_map/ppermute | solution.py:38
  6.0 3.2 %fill.3.refs_4_.gate_w = bf16[32,8,128,128]{3,2,1,0:T(8,128)(2,1)S(1)} custom-call(s32[1,1,192]{2,1,0:T(1,128)} %index.9, s32[1,1]{1,0:T(1,128)S(6)} %copy.19.count, bf16[1,1,192,128,128]{4,3,2,1,0:T(8,128)(2,1)} %source.3, s32[1,1]{1,0:T(1,128)S(6)} %copy.20.refs_0_.count), custom_call_target="tpu_custom_call" | custom-call | bytes 6291456 | tf_op jit(solution)/shard_map/fill/pallas_call | solution.py:92
  9.3 1.7 %collective-permute-start.1 = (bf16[16,4096]{1,0:T(8,128)(2,1)S(1)}, bf16[16,4096]{1,0:T(8,128)(2,1)S(1)}, u32[]{:S(2)}, u32[]{:S(2)}) collective-permute-start(bf16[16,4096]{1,0:T(8,128)(2,1)S(1)} %pad_maximum_fusion.3), channel_id=1, source_target_pairs={{0,8},{2,10},{4,12},{6,14},{8,0},{10,2},{12,4},{14,6},{16,24},{18,... | collective-permute-start | bytes 393224 | tf_op jit(solution)/shard_map/ppermute | solution.py:38
  11.0 3.2 %fill.4.refs_5_.up_w = bf16[32,8,128,128]{3,2,1,0:T(8,128)(2,1)S(1)} custom-call(s32[1,1,192]{2,1,0:T(1,128)} %index.9, s32[1,1]{1,0:T(1,128)S(6)} %copy.19.count, bf16[1,1,192,128,128]{4,3,2,1,0:T(8,128)(2,1)} %source.4), custom_call_target="tpu_custom_call" | custom-call | bytes 6291456 | tf_op jit(solution)/shard_map/fill/pallas_call | solution.py:92
  14.4 1.7 %collective-permute-start.6 = (bf16[8,4096]{1,0:T(8,128)(2,1)S(1)}, bf16[8,4096]{1,0:T(8,128)(2,1)S(1)}, u32[]{:S(2)}, u32[]{:S(2)}) collective-permute-start(bf16[8,4096]{1,0:T(8,128)(2,1)S(1)} %copy-done), channel_id=1, source_target_pairs={{0,16},{2,18},{4,20},{6,22},{8,24},{10,26},{12,28},{14,30},{16,0},... | collective-permute-start | bytes 196616 | tf_op jit(solution)/shard_map/ppermute | solution.py:38
  16.1 1.5 %collective-permute-start.2 = (bf16[32,4096]{1,0:T(8,128)(2,1)S(1)}, bf16[32,4096]{1,0:T(8,128)(2,1)S(1)}, u32[]{:S(2)}, u32[]{:S(2)}) collective-permute-start(bf16[32,4096]{1,0:T(8,128)(2,1)S(1)} %pad_maximum_fusion.1.refs_0_.refs_4_), channel_id=1, source_target_pairs={{0,4},{2,6},{4,0},{6,2},{8,12},{10,14},{12,8},{14,10},{16,20},{18,... | collective-permute-start | bytes 786440 | tf_op jit(solution)/shard_map/ppermute | solution.py:38
  17.6 2.1 %collective-permute-done.6 = bf16[8,4096]{1,0:T(8,128)(2,1)S(1)} collective-permute-done((bf16[8,4096]{1,0:T(8,128)(2,1)S(1)}, bf16[8,4096]{1,0:T(8,128)(2,1)S(1)}, u32[]{:S(2)}, u32[]{:S(2)}) %collective-permute-start.6) | collective-permute-done | bytes 65568 | tf_op jit(solution)/shard_map/ppermute | solution.py:38
  19.7 1.6 %collective-permute-start.7 = (bf16[16,4096]{1,0:T(8,128)(2,1)S(1)}, bf16[16,4096]{1,0:T(8,128)(2,1)S(1)}, u32[]{:S(2)}, u32[]{:S(2)}) collective-permute-start(bf16[16,4096]{1,0:T(8,128)(2,1)S(1)} %pad_maximum_fusion.4), channel_id=1, source_target_pairs={{0,8},{2,10},{4,12},{6,14},{8,0},{10,2},{12,4},{14,6},{16,24},{18,... | collective-permute-start | bytes 393224 | tf_op jit(solution)/shard_map/ppermute | solution.py:38
  21.3 2.6 %fill.5.refs_8_ = bf16[8,32,128,128]{3,2,1,0:T(8,128)(2,1)S(1)} custom-call(s32[1,1,192]{2,1,0:T(1,128)} %index.7, s32[1,1]{1,0:T(1,128)S(6)} %copy.20.refs_0_.count, bf16[1,1,192,128,128]{4,3,2,1,0:T(8,128)(2,1)} %source.5), custom_call_target="tpu_custom_call" | custom-call | bytes 6291456 | tf_op jit(solution)/shard_map/fill/pallas_call | solution.py:92
  24.7 2.2 %collective-permute-start.8 = (bf16[32,4096]{1,0:T(8,128)(2,1)S(1)}, bf16[32,4096]{1,0:T(8,128)(2,1)S(1)}, u32[]{:S(2)}, u32[]{:S(2)}) collective-permute-start(bf16[32,4096]{1,0:T(8,128)(2,1)S(1)} %pad_maximum_fusion.2.refs_0_), channel_id=1, source_target_pairs={{0,4},{2,6},{4,0},{6,2},{8,12},{10,14},{12,8},{14,10},{16,20},{18,... | collective-permute-start | bytes 786440 | tf_op jit(solution)/shard_map/ppermute | solution.py:38
  27.0 1.3 %gate_up.2 = (f32[4,128,256]{2,1,0:T(8,128)S(1)}, bf16[4,128,256]{2,1,0:T(8,128)(2,1)S(1)}) custom-call(bf16[32,4096]{1,0:T(8,128)(2,1)S(1)} %pad_maximum_fusion.1.refs_0_.refs_4_, bf16[32,4096]{1,0:T(8,128)(2,1)S(1)} %collective-permute-done.2.refs_1_.refs_5_, bf16[32,4096]{1,0:T(8,128)(2,1)S(1)} %collective-permute-done.3.refs_2_.refs_6_, ...), custom_call_target="tpu_custom_call" | custom-call | flops 1073741824 | bytes 8388608 | tf_op jit(solution)/shard_map/gate_up/pallas_call | solution.py:129
  28.2 2.4 %collective-permute-start.5 = (bf16[4,128,256]{2,1,0:T(8,128)(2,1)S(1)}, bf16[4,128,256]{2,1,0:T(8,128)(2,1)S(1)}, u32[]{:S(2)}, u32[]{:S(2)}) collective-permute-start(bf16[4,128,256]{2,1,0:T(8,128)(2,1)S(1)} %get-tuple-element.68), channel_id=1, source_target_pairs={{0,1},{1,0},{2,3},{3,2},{4,5},{5,4},{6,7},{7,6},{8,9},{9,8},{10,11... | collective-permute-start | bytes 786440 | tf_op jit(solution)/shard_map/ppermute | solution.py:38
  30.7 1.2 %gate_up.3 = (f32[4,128,256]{2,1,0:T(8,128)S(1)}, bf16[4,128,256]{2,1,0:T(8,128)(2,1)S(1)}) custom-call(bf16[32,4096]{1,0:T(8,128)(2,1)S(1)} %pad_maximum_fusion.1.refs_0_.refs_4_, bf16[32,4096]{1,0:T(8,128)(2,1)S(1)} %collective-permute-done.2.refs_1_.refs_5_, bf16[32,4096]{1,0:T(8,128)(2,1)S(1)} %collective-permute-done.3.refs_2_.refs_6_, ...), custom_call_target="tpu_custom_call" | custom-call | flops 1073741824 | bytes 8388608 | tf_op jit(solution)/shard_map/gate_up/pallas_call | solution.py:129
  31.9 0.9 %collective-permute-done.8.refs_1_ = bf16[32,4096]{1,0:T(8,128)(2,1)S(1)} collective-permute-done((bf16[32,4096]{1,0:T(8,128)(2,1)S(1)}, bf16[32,4096]{1,0:T(8,128)(2,1)S(1)}, u32[]{:S(2)}, u32[]{:S(2)}) %collective-permute-start.8) | collective-permute-done | bytes 262176 | tf_op jit(solution)/shard_map/ppermute | solution.py:38
  33.4 1.5 %collective-permute-start.11 = (bf16[4,128,256]{2,1,0:T(8,128)(2,1)S(1)}, bf16[4,128,256]{2,1,0:T(8,128)(2,1)S(1)}, u32[]{:S(2)}, u32[]{:S(2)}) collective-permute-start(bf16[4,128,256]{2,1,0:T(8,128)(2,1)S(1)} %get-tuple-element.77), channel_id=1, source_target_pairs={{0,1},{1,0},{2,3},{3,2},{4,5},{5,4},{6,7},{7,6},{8,9},{9,8},{10,11... | collective-permute-start | bytes 786440 | tf_op jit(solution)/shard_map/ppermute | solution.py:38
  34.8 0.7 %collective-permute-done.5.refs_1_ = bf16[4,128,256]{2,1,0:T(8,128)(2,1)S(1)} collective-permute-done((bf16[4,128,256]{2,1,0:T(8,128)(2,1)S(1)}, bf16[4,128,256]{2,1,0:T(8,128)(2,1)S(1)}, u32[]{:S(2)}, u32[]{:S(2)}) %collective-permute-start.5) | collective-permute-done | bytes 262176 | tf_op jit(solution)/shard_map/ppermute | solution.py:38
  35.7 2.6 %d_hidden.1 = (f32[8,128,128]{2,1,0:T(8,128)S(1)}, bf16[8,128,128]{2,1,0:T(8,128)(2,1)S(1)}, bf16[32,128,128]{2,1,0:T(8,128)(2,1)S(1)}) custom-call(bf16[32,4096]{1,0:T(8,128)(2,1)S(1)} %pad_maximum_fusion.2.refs_0_, bf16[32,4096]{1,0:T(8,128)(2,1)S(1)} %collective-permute-done.8.refs_1_, bf16[32,4096]{1,0:T(8,128)(2,1)S(1)} %collective-permute-done.9.refs_2_, ...), custom_call_target="tpu_custom_call" | custom-call | flops 1073741824 | bytes 8388608 | tf_op jit(solution)/shard_map/d_hidden/pallas_call | solution.py:171
  38.3 1.6 %collective-permute-start.12 = (bf16[8,128,128]{2,1,0:T(8,128)(2,1)S(1)}, bf16[8,128,128]{2,1,0:T(8,128)(2,1)S(1)}, u32[]{:S(2)}, u32[]{:S(2)}) collective-permute-start(bf16[8,128,128]{2,1,0:T(8,128)(2,1)S(1)} %get-tuple-element.93), channel_id=1, source_target_pairs={{0,1},{1,0},{2,3},{3,2},{4,5},{5,4},{6,7},{7,6},{8,9},{9,8},{10,11... | collective-permute-start | bytes 786440 | tf_op jit(solution)/shard_map/ppermute | solution.py:38
  40.0 1.3 %down_first.1._ = bf16[257,128,128]{2,1,0:T(8,128)(2,1)S(1)} custom-call(bf16[4,128,128]{2,1,0:T(8,128)(2,1)S(1)} %get-tuple-element.74.hidden, bf16[32,4096]{1,0:T(8,128)(2,1)S(1)} %pad_maximum_fusion.2.refs_0_, bf16[32,4096]{1,0:T(8,128)(2,1)S(1)} %collective-permute-done.8.refs_1_, bf16[32,4096]{1,0:T(8,128)(2,1)S(1)} %collective-permute-done.9.refs_2_, ...), custom_call_target="tpu_custom_call" | custom-call | flops 538968064 | bytes 8421376 | tf_op jit(solution)/shard_map/down_first/pallas_call | solution.py:397
  41.3 1.3 %collective-permute-done.11.refs_1_ = bf16[4,128,256]{2,1,0:T(8,128)(2,1)S(1)} collective-permute-done((bf16[4,128,256]{2,1,0:T(8,128)(2,1)S(1)}, bf16[4,128,256]{2,1,0:T(8,128)(2,1)S(1)}, u32[]{:S(2)}, u32[]{:S(2)}) %collective-permute-start.11) | collective-permute-done | bytes 262176 | tf_op jit(solution)/shard_map/ppermute | solution.py:38
  42.7 4.5 %down_second.1 = (bf16[192,128,128]{2,1,0:T(8,128)(2,1)}, bf16[257,128,128]{2,1,0:T(8,128)(2,1)S(1)}) custom-call(s32[1,1,192]{2,1,0:T(1,128)} %index.7, s32[1,1]{1,0:T(1,128)S(6)} %copy.20.refs_0_.count, bf16[4,128,128]{2,1,0:T(8,128)(2,1)S(1)} %get-tuple-element.87.hidden, ...), custom_call_target="tpu_custom_call", output_to_operand_aliasing={{1}: (3, {})} | custom-call | flops 402653184 | bytes 6291456 | tf_op jit(solution)/shard_map/down_second/pallas_call | solution.py:413
  47.2 2.5 %d_tokens_first.1 = (f32[64,2048]{1,0:T(8,128)S(1)}, bf16[64,2048]{1,0:T(8,128)(2,1)S(1)}, bf16[8,128,256]{2,1,0:T(8,128)(2,1)S(1)}, bf16[2048,128]{1,0:T(8,128)(2,1)S(1)}) custom-call(f32[4,128,256]{2,1,0:T(8,128)S(1)} %get-tuple-element.69.refs_0_, f32[4,128,256]{2,1,0:T(8,128)S(1)} %get-tuple-element.91.refs_1_, ...), custom_call_target="tpu_custom_call" | custom-call | flops 1073741824 | bytes 8388608 | tf_op jit(solution)/shard_map/d_tokens_first/pallas_call | solution.py:240
  49.8 2.4 %d_tokens_second.1 = (f32[64,2048]{1,0:T(8,128)S(1)}, bf16[64,2048]{1,0:T(8,128)(2,1)S(1)}) custom-call(bf16[2048,128]{1,0:T(8,128)(2,1)S(1)} %get-tuple-element.96.turned, bf16[32,8,128,128]{3,2,1,0:T(8,128)(2,1)S(1)} %fill.3.refs_4_.gate_w, bf16[32,8,128,128]{3,2,1,0:T(8,128)(2,1)S(1)} %fill.4.refs_5_.up_w), custom_call_target="tpu_custom_call" | custom-call | flops 1073741824 | bytes 8388608 | tf_op jit(solution)/shard_map/d_tokens_second/pallas_call | solution.py:252
  52.3 0.6 collective-permute-start.15
  52.9 1.5 %collective-permute-start.14 = (bf16[32,2048]{1,0:T(8,128)(2,1)S(1)}, bf16[32,2048]{1,0:T(8,128)(2,1)S(1)}, u32[]{:S(2)}, u32[]{:S(2)}) collective-permute-start(bf16[32,2048]{1,0:T(8,128)(2,1)S(1)} %slice.65), channel_id=1, source_target_pairs={{0,4},{2,6},{4,0},{6,2},{8,12},{10,14},{12,8},{14,10},{16,20},{18,... | collective-permute-start | bytes 393224 | tf_op jit(solution)/shard_map/ppermute | solution.py:38
  54.5 1.1 %collective-permute-start.16 = (bf16[32,2048]{1,0:T(8,128)(2,1)S(1)}, bf16[32,2048]{1,0:T(8,128)(2,1)S(1)}, u32[]{:S(2)}, u32[]{:S(2)}) collective-permute-start(bf16[32,2048]{1,0:T(8,128)(2,1)S(1)} %slice.64), channel_id=1, source_target_pairs={{0,4},{2,6},{4,0},{6,2},{8,12},{10,14},{12,8},{14,10},{16,20},{18,... | collective-permute-start | bytes 393224 | tf_op jit(solution)/shard_map/ppermute | solution.py:38
  55.6 5.4 %gu_grads.2 = (bf16[192,128,128]{2,1,0:T(8,128)(2,1)}, bf16[192,128,128]{2,1,0:T(8,128)(2,1)}) custom-call(s32[1,1,192]{2,1,0:T(1,128)} %index.9, s32[1,1]{1,0:T(1,128)S(6)} %copy.19.count, bf16[8,128,256]{2,1,0:T(8,128)(2,1)S(1)} %get-tuple-element.108.d_pair, bf16[32,128,128]{2,1,0:T(8,128)(2,1)S(1)} %get-tuple-element.102.turned), custom_call_target="tpu_custom_call" | custom-call | flops 1073741824 | bytes 8388608 | tf_op jit(solution)/shard_map/gu_grads/pallas_call | solution.py:308
  61.3 2.7 %collective-permute-start.17 = (bf16[8,4096]{1,0:T(8,128)(2,1)S(1)}, bf16[8,4096]{1,0:T(8,128)(2,1)S(1)}, u32[]{:S(2)}, u32[]{:S(2)}) collective-permute-start(bf16[8,4096]{1,0:T(8,128)(2,1)S(1)} %get-tuple-element.105), channel_id=1, source_target_pairs={{0,16},{2,18},{4,20},{6,22},{8,24},{10,26},{12,28},{14,30},{16,0},... | collective-permute-start | bytes 196616 | tf_op jit(solution)/shard_map/ppermute | solution.py:38
  64.1 1.6 %collective-permute-start.19 = (bf16[8,4096]{1,0:T(8,128)(2,1)S(1)}, bf16[8,4096]{1,0:T(8,128)(2,1)S(1)}, u32[]{:S(2)}, u32[]{:S(2)}) collective-permute-start(bf16[8,4096]{1,0:T(8,128)(2,1)S(1)} %get-tuple-element.107), channel_id=1, source_target_pairs={{0,24},{2,26},{4,28},{6,30},{8,16},{10,18},{12,20},{14,22},{16,8},... | collective-permute-start | bytes 196616 | tf_op jit(solution)/shard_map/ppermute | solution.py:38
  65.7 3.5 %gu_grads.3 = (bf16[192,128,128]{2,1,0:T(8,128)(2,1)}, bf16[192,128,128]{2,1,0:T(8,128)(2,1)}) custom-call(s32[1,1,192]{2,1,0:T(1,128)} %index.9, s32[1,1]{1,0:T(1,128)S(6)} %copy.19.count, bf16[8,128,256]{2,1,0:T(8,128)(2,1)S(1)} %get-tuple-element.108.d_pair, ...), custom_call_target="tpu_custom_call", output_to_operand_aliasing={{0}: (4, {}), {1}: (5, {})} | custom-call | flops 536870912 | bytes 4194304 | tf_op jit(solution)/shard_map/gu_grads/pallas_call | solution.py:308
  69.2 1.3 %collective-permute-done.19 = bf16[8,4096]{1,0:T(8,128)(2,1)S(1)} collective-permute-done((bf16[8,4096]{1,0:T(8,128)(2,1)S(1)}, bf16[8,4096]{1,0:T(8,128)(2,1)S(1)}, u32[]{:S(2)}, u32[]{:S(2)}) %collective-permute-start.19) | collective-permute-done | bytes 65568 | tf_op jit(solution)/shard_map/ppermute | solution.py:38
  70.5 0.7 fusion.5
  (39 shorter events, 2.4 us)
Async XLA Ops:
  0.6 8.6 %collective-permute-start = (bf16[8,4096]{1,0:T(8,128)(2,1)}, bf16[8,4096]{1,0:T(8,128)(2,1)S(1)}, u32[]{:S(2)}, u32[]{:S(2)}) collective-permute-start(bf16[8,4096]{1,0:T(8,128)(2,1)} %param.9), channel_id=1, source_target_pairs={{0,16},{2,18},{4,20},{6,22},{8,24},{10,26},{12,28},{14,30},{16,0},... | collective-permute-start | bytes 196616 | tf_op jit(solution)/shard_map/ppermute | solution.py:38
  6.0 3.2 %copy-start.1 = (bf16[8,4096]{1,0:T(8,128)(2,1)S(1)}, bf16[8,4096]{1,0:T(8,128)(2,1)}, u32[]{:S(2)}) copy-start(bf16[8,4096]{1,0:T(8,128)(2,1)} %param.9) | copy-start | bytes 196612
  9.3 5.1 %copy-start = (bf16[8,4096]{1,0:T(8,128)(2,1)S(1)}, bf16[8,4096]{1,0:T(8,128)(2,1)}, u32[]{:S(2)}) copy-start(bf16[8,4096]{1,0:T(8,128)(2,1)} %param.10) | copy-start | bytes 196612
  9.3 5.0 %collective-permute-start.1 = (bf16[16,4096]{1,0:T(8,128)(2,1)S(1)}, bf16[16,4096]{1,0:T(8,128)(2,1)S(1)}, u32[]{:S(2)}, u32[]{:S(2)}) collective-permute-start(bf16[16,4096]{1,0:T(8,128)(2,1)S(1)} %pad_maximum_fusion.3), channel_id=1, source_target_pairs={{0,8},{2,10},{4,12},{6,14},{8,0},{10,2},{12,4},{14,6},{16,24},{18,... | collective-permute-start | bytes 393224 | tf_op jit(solution)/shard_map/ppermute | solution.py:38
  14.4 5.3 %collective-permute-start.6 = (bf16[8,4096]{1,0:T(8,128)(2,1)S(1)}, bf16[8,4096]{1,0:T(8,128)(2,1)S(1)}, u32[]{:S(2)}, u32[]{:S(2)}) collective-permute-start(bf16[8,4096]{1,0:T(8,128)(2,1)S(1)} %copy-done), channel_id=1, source_target_pairs={{0,16},{2,18},{4,20},{6,22},{8,24},{10,26},{12,28},{14,30},{16,0},... | collective-permute-start | bytes 196616 | tf_op jit(solution)/shard_map/ppermute | solution.py:38
  16.1 7.9 %collective-permute-start.2 = (bf16[32,4096]{1,0:T(8,128)(2,1)S(1)}, bf16[32,4096]{1,0:T(8,128)(2,1)S(1)}, u32[]{:S(2)}, u32[]{:S(2)}) collective-permute-start(bf16[32,4096]{1,0:T(8,128)(2,1)S(1)} %pad_maximum_fusion.1.refs_0_.refs_4_), channel_id=1, source_target_pairs={{0,4},{2,6},{4,0},{6,2},{8,12},{10,14},{12,8},{14,10},{16,20},{18,... | collective-permute-start | bytes 786440 | tf_op jit(solution)/shard_map/ppermute | solution.py:38
  19.7 5.0 %collective-permute-start.7 = (bf16[16,4096]{1,0:T(8,128)(2,1)S(1)}, bf16[16,4096]{1,0:T(8,128)(2,1)S(1)}, u32[]{:S(2)}, u32[]{:S(2)}) collective-permute-start(bf16[16,4096]{1,0:T(8,128)(2,1)S(1)} %pad_maximum_fusion.4), channel_id=1, source_target_pairs={{0,8},{2,10},{4,12},{6,14},{8,0},{10,2},{12,4},{14,6},{16,24},{18,... | collective-permute-start | bytes 393224 | tf_op jit(solution)/shard_map/ppermute | solution.py:38
  23.9 3.1 %collective-permute-start.3 = (bf16[32,4096]{1,0:T(8,128)(2,1)S(1)}, bf16[32,4096]{1,0:T(8,128)(2,1)S(1)}, u32[]{:S(2)}, u32[]{:S(2)}) collective-permute-start(bf16[32,4096]{1,0:T(8,128)(2,1)S(1)} %pad_maximum_fusion.1.refs_0_.refs_4_), channel_id=1, source_target_pairs={{0,2},{2,0},{4,6},{6,4},{8,10},{10,8},{12,14},{14,12},{16,18},{18,... | collective-permute-start | bytes 786440 | tf_op jit(solution)/shard_map/ppermute | solution.py:38
  24.0 3.0 %collective-permute-start.4 = (bf16[32,4096]{1,0:T(8,128)(2,1)S(1)}, bf16[32,4096]{1,0:T(8,128)(2,1)S(1)}, u32[]{:S(2)}, u32[]{:S(2)}) collective-permute-start(bf16[32,4096]{1,0:T(8,128)(2,1)S(1)} %collective-permute-done.2.refs_1_.refs_5_), channel_id=1, source_target_pairs={{0,2},{2,0},{4,6},{6,4},{8,10},{10,8},{12,14},{14,12},{16,18},{18,... | collective-permute-start | bytes 786440 | tf_op jit(solution)/shard_map/ppermute | solution.py:38
  24.7 8.1 %collective-permute-start.8 = (bf16[32,4096]{1,0:T(8,128)(2,1)S(1)}, bf16[32,4096]{1,0:T(8,128)(2,1)S(1)}, u32[]{:S(2)}, u32[]{:S(2)}) collective-permute-start(bf16[32,4096]{1,0:T(8,128)(2,1)S(1)} %pad_maximum_fusion.2.refs_0_), channel_id=1, source_target_pairs={{0,4},{2,6},{4,0},{6,2},{8,12},{10,14},{12,8},{14,10},{16,20},{18,... | collective-permute-start | bytes 786440 | tf_op jit(solution)/shard_map/ppermute | solution.py:38
  28.2 7.3 %collective-permute-start.5 = (bf16[4,128,256]{2,1,0:T(8,128)(2,1)S(1)}, bf16[4,128,256]{2,1,0:T(8,128)(2,1)S(1)}, u32[]{:S(2)}, u32[]{:S(2)}) collective-permute-start(bf16[4,128,256]{2,1,0:T(8,128)(2,1)S(1)} %get-tuple-element.68), channel_id=1, source_target_pairs={{0,1},{1,0},{2,3},{3,2},{4,5},{5,4},{6,7},{7,6},{8,9},{9,8},{10,11... | collective-permute-start | bytes 786440 | tf_op jit(solution)/shard_map/ppermute | solution.py:38
  32.9 2.8 %collective-permute-start.9 = (bf16[32,4096]{1,0:T(8,128)(2,1)S(1)}, bf16[32,4096]{1,0:T(8,128)(2,1)S(1)}, u32[]{:S(2)}, u32[]{:S(2)}) collective-permute-start(bf16[32,4096]{1,0:T(8,128)(2,1)S(1)} %pad_maximum_fusion.2.refs_0_), channel_id=1, source_target_pairs={{0,2},{2,0},{4,6},{6,4},{8,10},{10,8},{12,14},{14,12},{16,18},{18,... | collective-permute-start | bytes 786440 | tf_op jit(solution)/shard_map/ppermute | solution.py:38
  32.9 2.8 %collective-permute-start.10 = (bf16[32,4096]{1,0:T(8,128)(2,1)S(1)}, bf16[32,4096]{1,0:T(8,128)(2,1)S(1)}, u32[]{:S(2)}, u32[]{:S(2)}) collective-permute-start(bf16[32,4096]{1,0:T(8,128)(2,1)S(1)} %collective-permute-done.8.refs_1_), channel_id=1, source_target_pairs={{0,2},{2,0},{4,6},{6,4},{8,10},{10,8},{12,14},{14,12},{16,18},{18,... | collective-permute-start | bytes 786440 | tf_op jit(solution)/shard_map/ppermute | solution.py:38
  33.4 9.2 %collective-permute-start.11 = (bf16[4,128,256]{2,1,0:T(8,128)(2,1)S(1)}, bf16[4,128,256]{2,1,0:T(8,128)(2,1)S(1)}, u32[]{:S(2)}, u32[]{:S(2)}) collective-permute-start(bf16[4,128,256]{2,1,0:T(8,128)(2,1)S(1)} %get-tuple-element.77), channel_id=1, source_target_pairs={{0,1},{1,0},{2,3},{3,2},{4,5},{5,4},{6,7},{7,6},{8,9},{9,8},{10,11... | collective-permute-start | bytes 786440 | tf_op jit(solution)/shard_map/ppermute | solution.py:38
  38.3 8.9 %collective-permute-start.12 = (bf16[8,128,128]{2,1,0:T(8,128)(2,1)S(1)}, bf16[8,128,128]{2,1,0:T(8,128)(2,1)S(1)}, u32[]{:S(2)}, u32[]{:S(2)}) collective-permute-start(bf16[8,128,128]{2,1,0:T(8,128)(2,1)S(1)} %get-tuple-element.93), channel_id=1, source_target_pairs={{0,1},{1,0},{2,3},{3,2},{4,5},{5,4},{6,7},{7,6},{8,9},{9,8},{10,11... | collective-permute-start | bytes 786440 | tf_op jit(solution)/shard_map/ppermute | solution.py:38
  49.7 3.1 %collective-permute-start.13 = (bf16[64,2048]{1,0:T(8,128)(2,1)S(1)}, bf16[64,2048]{1,0:T(8,128)(2,1)S(1)}, u32[]{:S(2)}, u32[]{:S(2)}) collective-permute-start(bf16[64,2048]{1,0:T(8,128)(2,1)S(1)} %get-tuple-element.95), channel_id=1, source_target_pairs={{0,2},{2,0},{4,6},{6,4},{8,10},{10,8},{12,14},{14,12},{16,18},{18,... | collective-permute-start | bytes 786440 | tf_op jit(solution)/shard_map/ppermute | solution.py:38
  52.3 2.2 %collective-permute-start.15 = (bf16[64,2048]{1,0:T(8,128)(2,1)S(1)}, bf16[64,2048]{1,0:T(8,128)(2,1)S(1)}, u32[]{:S(2)}, u32[]{:S(2)}) collective-permute-start(bf16[64,2048]{1,0:T(8,128)(2,1)S(1)} %get-tuple-element.98), channel_id=1, source_target_pairs={{0,2},{2,0},{4,6},{6,4},{8,10},{10,8},{12,14},{14,12},{16,18},{18,... | collective-permute-start | bytes 786440 | tf_op jit(solution)/shard_map/ppermute | solution.py:38
  52.9 8.1 %collective-permute-start.14 = (bf16[32,2048]{1,0:T(8,128)(2,1)S(1)}, bf16[32,2048]{1,0:T(8,128)(2,1)S(1)}, u32[]{:S(2)}, u32[]{:S(2)}) collective-permute-start(bf16[32,2048]{1,0:T(8,128)(2,1)S(1)} %slice.65), channel_id=1, source_target_pairs={{0,4},{2,6},{4,0},{6,2},{8,12},{10,14},{12,8},{14,10},{16,20},{18,... | collective-permute-start | bytes 393224 | tf_op jit(solution)/shard_map/ppermute | solution.py:38
  54.5 6.7 %collective-permute-start.16 = (bf16[32,2048]{1,0:T(8,128)(2,1)S(1)}, bf16[32,2048]{1,0:T(8,128)(2,1)S(1)}, u32[]{:S(2)}, u32[]{:S(2)}) collective-permute-start(bf16[32,2048]{1,0:T(8,128)(2,1)S(1)} %slice.64), channel_id=1, source_target_pairs={{0,4},{2,6},{4,0},{6,2},{8,12},{10,14},{12,8},{14,10},{16,20},{18,... | collective-permute-start | bytes 393224 | tf_op jit(solution)/shard_map/ppermute | solution.py:38
  61.3 7.9 %collective-permute-start.17 = (bf16[8,4096]{1,0:T(8,128)(2,1)S(1)}, bf16[8,4096]{1,0:T(8,128)(2,1)S(1)}, u32[]{:S(2)}, u32[]{:S(2)}) collective-permute-start(bf16[8,4096]{1,0:T(8,128)(2,1)S(1)} %get-tuple-element.105), channel_id=1, source_target_pairs={{0,16},{2,18},{4,20},{6,22},{8,24},{10,26},{12,28},{14,30},{16,0},... | collective-permute-start | bytes 196616 | tf_op jit(solution)/shard_map/ppermute | solution.py:38
  64.0 5.3 %collective-permute-start.18 = (bf16[8,4096]{1,0:T(8,128)(2,1)S(1)}, bf16[8,4096]{1,0:T(8,128)(2,1)S(1)}, u32[]{:S(2)}, u32[]{:S(2)}) collective-permute-start(bf16[8,4096]{1,0:T(8,128)(2,1)S(1)} %get-tuple-element.106), channel_id=1, source_target_pairs={{0,8},{2,10},{4,12},{6,14},{8,0},{10,2},{12,4},{14,6},{16,24},{18,... | collective-permute-start | bytes 196616 | tf_op jit(solution)/shard_map/ppermute | solution.py:38
  64.1 6.4 %collective-permute-start.19 = (bf16[8,4096]{1,0:T(8,128)(2,1)S(1)}, bf16[8,4096]{1,0:T(8,128)(2,1)S(1)}, u32[]{:S(2)}, u32[]{:S(2)}) collective-permute-start(bf16[8,4096]{1,0:T(8,128)(2,1)S(1)} %get-tuple-element.107), channel_id=1, source_target_pairs={{0,24},{2,26},{4,28},{6,30},{8,16},{10,18},{12,20},{14,22},{16,8},... | collective-permute-start | bytes 196616 | tf_op jit(solution)/shard_map/ppermute | solution.py:38

commit v14 on v13

--- a/solution.py
+++ b/solution.py
@@ -448,20 +448,21 @@
 
     flips = [chips >> hop for hop in range(1, chips.bit_length())]
     vals = (gate_vals, up_vals)
-    x, index = tokens, gu_index
+    x, y, index = tokens, cotangent, gu_index
     weights = []
     for hop, flip in enumerate(flips):
         if hop > 0:
             x = jnp.concatenate([x, x_recv], axis=0)
-            x, weights, index = lax.optimization_barrier((x, weights, index))
+            y = jnp.concatenate([y, y_recv], axis=0)
+            x, y, weights, index = lax.optimization_barrier((x, y, weights, index))
         x_recv = swap(x, "wide", wide, 2 * flip)
+        if hop < len(flips) - 1:
+            y_recv = swap(y, "wide", wide, 2 * flip)
         if hop < 2:
             early = (down_count,) if hop == 0 else ()
             weights.append(fill(index, gu_count, vals[hop], d_blocks, f_blocks, early))
-    y, index, _ = lax.optimization_barrier((cotangent, down_index, x))
+    index, _ = lax.optimization_barrier((down_index, x))
     down_w = fill(index, down_count, down_vals, f_blocks, d_blocks)
-    for flip in flips[:-1]:
-        y = jnp.concatenate([y, swap(y, "wide", wide, 2 * flip)], axis=0)
     x, down_w = lax.optimization_barrier((x, down_w))
     x_pieces = [x, x_recv, swap(x, "wide", wide, 1), swap(x_recv, "wide", wide, 1)]
     y, _ = lax.optimization_barrier((y, x_recv))

time: 71.9 us -> 75.7 us (1.053)
  waiting for transfers between devices: 6.87 us -> 15.5 us
  starting transfers between devices: 27.1 us -> 24 us
  Pallas kernels: 34.1 us -> 32.4 us
    ppermute x20, waiting for transfers between devices: 6.87 us -> 15.5 us  [swap(): return lax.ppermute(array, axis, [(i, i ^ flip) for i in range(size)])]
    ppermute x20, starting transfers between devices: 27.1 us -> 24 us  [swap(): return lax.ppermute(array, axis, [(i, i ^ flip) for i in range(size)])]
    pallas_call x3, Pallas kernels: 9.03 us -> 7.37 us  [fill(): pl.pallas_call(fill_body, out_shape=pltpu.VMEM((outer, inner, block, bloc...]
  transfers between devices with their start and end apart: 20 -> 20, of which waited for: 8 -> 8; matrix products, arithmetic and copies ran while one was open for 0% -> 0% of each run, Pallas kernels for 44% -> 40%
where the time goes in v14:
time: 75.7 us; the launch traced here: 75.1 us
  Pallas kernels  32.4 us (43%)
  starting transfers between devices  24 us (32%)
  waiting for transfers between devices  15.5 us (20%)
  between operations  2.21 us (3%)
  other arithmetic  0.89 us (1%)
    ppermute x20, starting transfers between devices, swap(): return lax.ppermute(array, axis, [(i, i ^ flip) for i in range(size)])  24 us
    ppermute x20, waiting for transfers between devices, swap(): return lax.ppermute(array, axis, [(i, i ^ flip) for i in range(size)])  15.5 us
    pallas_call x2, Pallas kernels, gu_grads(): pl.pallas_call(functools.partial(gu_grad_body, first, len(before)), out_s...  8.91 us
    pallas_call x3, Pallas kernels, fill(): pl.pallas_call(fill_body, out_shape=pltpu.VMEM((outer, inner, block, bloc...  7.37 us
    pallas_call x1, Pallas kernels, down_second(): pl.pallas_call(functools.partial(down_second_body, first), out_shape=(jax...  4.48 us
    pallas_call x1, Pallas kernels, d_hidden(): pl.pallas_call(functools.partial(d_hidden_body, group, len(y_pieces)), ou...  2.63 us
    pallas_call x1, Pallas kernels, d_tokens_parts(): pl.pallas_call(functools.partial(d_tokens_first_body, group), out_shape=(...  2.54 us
    pallas_call x2, Pallas kernels, gate_up(): pl.pallas_call(functools.partial(gate_up_body, half * f_blocks // 2), out...  2.5 us
  transfers between devices with their start and end apart: 20, of which 8 were waited for; matrix products, arithmetic and copies ran while one was open for 0% of the time, Pallas kernels for 40%

profile of v14, /device:TPU:0, one launch (start us, length us, event | category | flops | bytes accessed | tf_op | source)
XLA Modules:
  0.0 75.1 jit_solution(13529699254937626814)
XLA Ops:
  0.6 4.1 %collective-permute-start = (bf16[8,4096]{1,0:T(8,128)(2,1)}, bf16[8,4096]{1,0:T(8,128)(2,1)S(1)}, u32[]{:S(2)}, u32[]{:S(2)}) collective-permute-start(bf16[8,4096]{1,0:T(8,128)(2,1)} %param.9), channel_id=1, source_target_pairs={{0,16},{2,18},{4,20},{6,22},{8,24},{10,26},{12,28},{14,30},{16,0},... | collective-permute-start | bytes 196616 | tf_op jit(solution)/shard_map/ppermute | solution.py:38
  6.1 2.5 %fill.3.refs_4_.gate_w = bf16[32,8,128,128]{3,2,1,0:T(8,128)(2,1)S(1)} custom-call(s32[1,1,192]{2,1,0:T(1,128)} %index.9, s32[1,1]{1,0:T(1,128)S(6)} %copy.19.count, bf16[1,1,192,128,128]{4,3,2,1,0:T(8,128)(2,1)} %source.3, s32[1,1]{1,0:T(1,128)S(6)} %copy.20.refs_0_.count), custom_call_target="tpu_custom_call" | custom-call | bytes 6291456 | tf_op jit(solution)/shard_map/fill/pallas_call | solution.py:92
  8.7 2.7 %collective-permute-done.1 = bf16[8,4096]{1,0:T(8,128)(2,1)S(1)} collective-permute-done((bf16[8,4096]{1,0:T(8,128)(2,1)}, bf16[8,4096]{1,0:T(8,128)(2,1)S(1)}, u32[]{:S(2)}, u32[]{:S(2)}) %collective-permute-start.1) | collective-permute-done | bytes 65568 | tf_op jit(solution)/shard_map/ppermute | solution.py:38
  11.4 0.7 collective-permute-start.2
  12.2 1.4 %collective-permute-start.3 = (bf16[16,4096]{1,0:T(8,128)(2,1)S(1)}, bf16[16,4096]{1,0:T(8,128)(2,1)S(1)}, u32[]{:S(2)}, u32[]{:S(2)}) collective-permute-start(bf16[16,4096]{1,0:T(8,128)(2,1)S(1)} %pad_maximum_fusion.4), channel_id=1, source_target_pairs={{0,8},{2,10},{4,12},{6,14},{8,0},{10,2},{12,4},{14,6},{16,24},{18,... | collective-permute-start | bytes 393224 | tf_op jit(solution)/shard_map/ppermute | solution.py:38
  13.5 2.5 %fill.4.refs_5_.up_w = bf16[32,8,128,128]{3,2,1,0:T(8,128)(2,1)S(1)} custom-call(s32[1,1,192]{2,1,0:T(1,128)} %index.9, s32[1,1]{1,0:T(1,128)S(6)} %copy.19.count, bf16[1,1,192,128,128]{4,3,2,1,0:T(8,128)(2,1)} %source.4), custom_call_target="tpu_custom_call" | custom-call | bytes 6291456 | tf_op jit(solution)/shard_map/fill/pallas_call | solution.py:92
  16.0 1.3 %collective-permute-done.2 = bf16[16,4096]{1,0:T(8,128)(2,1)S(1)} collective-permute-done((bf16[16,4096]{1,0:T(8,128)(2,1)S(1)}, bf16[16,4096]{1,0:T(8,128)(2,1)S(1)}, u32[]{:S(2)}, u32[]{:S(2)}) %collective-permute-start.2) | collective-permute-done | bytes 131104 | tf_op jit(solution)/shard_map/ppermute | solution.py:38
  17.3 1.4 %collective-permute-done.3 = bf16[16,4096]{1,0:T(8,128)(2,1)S(1)} collective-permute-done((bf16[16,4096]{1,0:T(8,128)(2,1)S(1)}, bf16[16,4096]{1,0:T(8,128)(2,1)S(1)}, u32[]{:S(2)}, u32[]{:S(2)}) %collective-permute-start.3) | collective-permute-done | bytes 131104 | tf_op jit(solution)/shard_map/ppermute | solution.py:38
  18.7 2.6 %collective-permute-start.4 = (bf16[32,4096]{1,0:T(8,128)(2,1)S(1)}, bf16[32,4096]{1,0:T(8,128)(2,1)S(1)}, u32[]{:S(2)}, u32[]{:S(2)}) collective-permute-start(bf16[32,4096]{1,0:T(8,128)(2,1)S(1)} %pad_maximum_fusion.1.refs_0_.refs_4_), channel_id=1, source_target_pairs={{0,4},{2,6},{4,0},{6,2},{8,12},{10,14},{12,8},{14,10},{16,20},{18,... | collective-permute-start | bytes 786440 | tf_op jit(solution)/shard_map/ppermute | solution.py:38
  21.3 2.3 %fill.5.refs_8_ = bf16[8,32,128,128]{3,2,1,0:T(8,128)(2,1)S(1)} custom-call(s32[1,1,192]{2,1,0:T(1,128)} %index.7, s32[1,1]{1,0:T(1,128)S(6)} %copy.20.refs_0_.count, bf16[1,1,192,128,128]{4,3,2,1,0:T(8,128)(2,1)} %source.5), custom_call_target="tpu_custom_call" | custom-call | bytes 6291456 | tf_op jit(solution)/shard_map/fill/pallas_call | solution.py:92
  23.7 3.0 %collective-permute-done.4.refs_1_.refs_5_ = bf16[32,4096]{1,0:T(8,128)(2,1)S(1)} collective-permute-done((bf16[32,4096]{1,0:T(8,128)(2,1)S(1)}, bf16[32,4096]{1,0:T(8,128)(2,1)S(1)}, u32[]{:S(2)}, u32[]{:S(2)}) %collective-permute-start.4) | collective-permute-done | bytes 262176 | tf_op jit(solution)/shard_map/ppermute | solution.py:38
  26.7 1.7 %collective-permute-start.8 = (bf16[32,4096]{1,0:T(8,128)(2,1)S(1)}, bf16[32,4096]{1,0:T(8,128)(2,1)S(1)}, u32[]{:S(2)}, u32[]{:S(2)}) collective-permute-start(bf16[32,4096]{1,0:T(8,128)(2,1)S(1)} %pad_maximum_fusion.2.refs_0_), channel_id=1, source_target_pairs={{0,4},{2,6},{4,0},{6,2},{8,12},{10,14},{12,8},{14,10},{16,20},{18,... | collective-permute-start | bytes 786440 | tf_op jit(solution)/shard_map/ppermute | solution.py:38
  28.5 1.3 %gate_up.2 = (f32[4,128,256]{2,1,0:T(8,128)S(1)}, bf16[4,128,256]{2,1,0:T(8,128)(2,1)S(1)}) custom-call(bf16[32,4096]{1,0:T(8,128)(2,1)S(1)} %pad_maximum_fusion.1.refs_0_.refs_4_, bf16[32,4096]{1,0:T(8,128)(2,1)S(1)} %collective-permute-done.4.refs_1_.refs_5_, bf16[32,4096]{1,0:T(8,128)(2,1)S(1)} %collective-permute-done.5.refs_2_.refs_6_, ...), custom_call_target="tpu_custom_call" | custom-call | flops 1073741824 | bytes 8388608 | tf_op jit(solution)/shard_map/gate_up/pallas_call | solution.py:129
  29.7 1.6 %collective-permute-start.7 = (bf16[4,128,256]{2,1,0:T(8,128)(2,1)S(1)}, bf16[4,128,256]{2,1,0:T(8,128)(2,1)S(1)}, u32[]{:S(2)}, u32[]{:S(2)}) collective-permute-start(bf16[4,128,256]{2,1,0:T(8,128)(2,1)S(1)} %get-tuple-element.70), channel_id=1, source_target_pairs={{0,1},{1,0},{2,3},{3,2},{4,5},{5,4},{6,7},{7,6},{8,9},{9,8},{10,11... | collective-permute-start | bytes 786440 | tf_op jit(solution)/shard_map/ppermute | solution.py:38
  31.3 1.2 %gate_up.3 = (f32[4,128,256]{2,1,0:T(8,128)S(1)}, bf16[4,128,256]{2,1,0:T(8,128)(2,1)S(1)}) custom-call(bf16[32,4096]{1,0:T(8,128)(2,1)S(1)} %pad_maximum_fusion.1.refs_0_.refs_4_, bf16[32,4096]{1,0:T(8,128)(2,1)S(1)} %collective-permute-done.4.refs_1_.refs_5_, bf16[32,4096]{1,0:T(8,128)(2,1)S(1)} %collective-permute-done.5.refs_2_.refs_6_, ...), custom_call_target="tpu_custom_call" | custom-call | flops 1073741824 | bytes 8388608 | tf_op jit(solution)/shard_map/gate_up/pallas_call | solution.py:129
  32.6 2.9 %collective-permute-done.8.refs_1_ = bf16[32,4096]{1,0:T(8,128)(2,1)S(1)} collective-permute-done((bf16[32,4096]{1,0:T(8,128)(2,1)S(1)}, bf16[32,4096]{1,0:T(8,128)(2,1)S(1)}, u32[]{:S(2)}, u32[]{:S(2)}) %collective-permute-start.8) | collective-permute-done | bytes 262176 | tf_op jit(solution)/shard_map/ppermute | solution.py:38
  36.0 1.7 %collective-permute-start.11 = (bf16[4,128,256]{2,1,0:T(8,128)(2,1)S(1)}, bf16[4,128,256]{2,1,0:T(8,128)(2,1)S(1)}, u32[]{:S(2)}, u32[]{:S(2)}) collective-permute-start(bf16[4,128,256]{2,1,0:T(8,128)(2,1)S(1)} %get-tuple-element.79), channel_id=1, source_target_pairs={{0,1},{1,0},{2,3},{3,2},{4,5},{5,4},{6,7},{7,6},{8,9},{9,8},{10,11... | collective-permute-start | bytes 786440 | tf_op jit(solution)/shard_map/ppermute | solution.py:38
  38.4 2.6 %d_hidden.1 = (f32[8,128,128]{2,1,0:T(8,128)S(1)}, bf16[8,128,128]{2,1,0:T(8,128)(2,1)S(1)}, bf16[32,128,128]{2,1,0:T(8,128)(2,1)S(1)}) custom-call(bf16[32,4096]{1,0:T(8,128)(2,1)S(1)} %pad_maximum_fusion.2.refs_0_, bf16[32,4096]{1,0:T(8,128)(2,1)S(1)} %collective-permute-done.8.refs_1_, bf16[32,4096]{1,0:T(8,128)(2,1)S(1)} %collective-permute-done.9.refs_2_, ...), custom_call_target="tpu_custom_call" | custom-call | flops 1073741824 | bytes 8388608 | tf_op jit(solution)/shard_map/d_hidden/pallas_call | solution.py:171
  41.0 1.6 %collective-permute-start.12 = (bf16[8,128,128]{2,1,0:T(8,128)(2,1)S(1)}, bf16[8,128,128]{2,1,0:T(8,128)(2,1)S(1)}, u32[]{:S(2)}, u32[]{:S(2)}) collective-permute-start(bf16[8,128,128]{2,1,0:T(8,128)(2,1)S(1)} %get-tuple-element.95), channel_id=1, source_target_pairs={{0,1},{1,0},{2,3},{3,2},{4,5},{5,4},{6,7},{7,6},{8,9},{9,8},{10,11... | collective-permute-start | bytes 786440 | tf_op jit(solution)/shard_map/ppermute | solution.py:38
  42.6 1.3 %down_first.1._ = bf16[257,128,128]{2,1,0:T(8,128)(2,1)S(1)} custom-call(bf16[4,128,128]{2,1,0:T(8,128)(2,1)S(1)} %get-tuple-element.76.hidden, bf16[32,4096]{1,0:T(8,128)(2,1)S(1)} %pad_maximum_fusion.2.refs_0_, bf16[32,4096]{1,0:T(8,128)(2,1)S(1)} %collective-permute-done.8.refs_1_, bf16[32,4096]{1,0:T(8,128)(2,1)S(1)} %collective-permute-done.9.refs_2_, ...), custom_call_target="tpu_custom_call" | custom-call | flops 538968064 | bytes 8421376 | tf_op jit(solution)/shard_map/down_first/pallas_call | solution.py:397
  43.9 1.3 %collective-permute-done.11.refs_1_ = bf16[4,128,256]{2,1,0:T(8,128)(2,1)S(1)} collective-permute-done((bf16[4,128,256]{2,1,0:T(8,128)(2,1)S(1)}, bf16[4,128,256]{2,1,0:T(8,128)(2,1)S(1)}, u32[]{:S(2)}, u32[]{:S(2)}) %collective-permute-start.11) | collective-permute-done | bytes 262176 | tf_op jit(solution)/shard_map/ppermute | solution.py:38
  45.3 4.5 %down_second.1 = (bf16[192,128,128]{2,1,0:T(8,128)(2,1)}, bf16[257,128,128]{2,1,0:T(8,128)(2,1)S(1)}) custom-call(s32[1,1,192]{2,1,0:T(1,128)} %index.7, s32[1,1]{1,0:T(1,128)S(6)} %copy.20.refs_0_.count, bf16[4,128,128]{2,1,0:T(8,128)(2,1)S(1)} %get-tuple-element.89.hidden, ...), custom_call_target="tpu_custom_call", output_to_operand_aliasing={{1}: (3, {})} | custom-call | flops 402653184 | bytes 6291456 | tf_op jit(solution)/shard_map/down_second/pallas_call | solution.py:413
  49.8 2.5 %d_tokens_first.1 = (f32[64,2048]{1,0:T(8,128)S(1)}, bf16[64,2048]{1,0:T(8,128)(2,1)S(1)}, bf16[8,128,256]{2,1,0:T(8,128)(2,1)S(1)}, bf16[2048,128]{1,0:T(8,128)(2,1)S(1)}) custom-call(f32[4,128,256]{2,1,0:T(8,128)S(1)} %get-tuple-element.71.refs_0_, f32[4,128,256]{2,1,0:T(8,128)S(1)} %get-tuple-element.93.refs_1_, ...), custom_call_target="tpu_custom_call" | custom-call | flops 1073741824 | bytes 8388608 | tf_op jit(solution)/shard_map/d_tokens_first/pallas_call | solution.py:240
  52.4 2.4 %d_tokens_second.1 = (f32[64,2048]{1,0:T(8,128)S(1)}, bf16[64,2048]{1,0:T(8,128)(2,1)S(1)}) custom-call(bf16[2048,128]{1,0:T(8,128)(2,1)S(1)} %get-tuple-element.98.turned, bf16[32,8,128,128]{3,2,1,0:T(8,128)(2,1)S(1)} %fill.3.refs_4_.gate_w, bf16[32,8,128,128]{3,2,1,0:T(8,128)(2,1)S(1)} %fill.4.refs_5_.up_w), custom_call_target="tpu_custom_call" | custom-call | flops 1073741824 | bytes 8388608 | tf_op jit(solution)/shard_map/d_tokens_second/pallas_call | solution.py:252
  55.5 1.8 %collective-permute-start.14 = (bf16[32,2048]{1,0:T(8,128)(2,1)S(1)}, bf16[32,2048]{1,0:T(8,128)(2,1)S(1)}, u32[]{:S(2)}, u32[]{:S(2)}) collective-permute-start(bf16[32,2048]{1,0:T(8,128)(2,1)S(1)} %slice.65), channel_id=1, source_target_pairs={{0,4},{2,6},{4,0},{6,2},{8,12},{10,14},{12,8},{14,10},{16,20},{18,... | collective-permute-start | bytes 393224 | tf_op jit(solution)/shard_map/ppermute | solution.py:38
  57.4 1.1 %collective-permute-start.16 = (bf16[32,2048]{1,0:T(8,128)(2,1)S(1)}, bf16[32,2048]{1,0:T(8,128)(2,1)S(1)}, u32[]{:S(2)}, u32[]{:S(2)}) collective-permute-start(bf16[32,2048]{1,0:T(8,128)(2,1)S(1)} %slice.64), channel_id=1, source_target_pairs={{0,4},{2,6},{4,0},{6,2},{8,12},{10,14},{12,8},{14,10},{16,20},{18,... | collective-permute-start | bytes 393224 | tf_op jit(solution)/shard_map/ppermute | solution.py:38
  58.5 5.4 %gu_grads.2 = (bf16[192,128,128]{2,1,0:T(8,128)(2,1)}, bf16[192,128,128]{2,1,0:T(8,128)(2,1)}) custom-call(s32[1,1,192]{2,1,0:T(1,128)} %index.9, s32[1,1]{1,0:T(1,128)S(6)} %copy.19.count, bf16[8,128,256]{2,1,0:T(8,128)(2,1)S(1)} %get-tuple-element.110.d_pair, bf16[32,128,128]{2,1,0:T(8,128)(2,1)S(1)} %get-tuple-element.104.turned), custom_call_target="tpu_custom_call" | custom-call | flops 1073741824 | bytes 8388608 | tf_op jit(solution)/shard_map/gu_grads/pallas_call | solution.py:308
  64.1 2.9 %collective-permute-start.17 = (bf16[8,4096]{1,0:T(8,128)(2,1)S(1)}, bf16[8,4096]{1,0:T(8,128)(2,1)S(1)}, u32[]{:S(2)}, u32[]{:S(2)}) collective-permute-start(bf16[8,4096]{1,0:T(8,128)(2,1)S(1)} %get-tuple-element.107), channel_id=1, source_target_pairs={{0,16},{2,18},{4,20},{6,22},{8,24},{10,26},{12,28},{14,30},{16,0},... | collective-permute-start | bytes 196616 | tf_op jit(solution)/shard_map/ppermute | solution.py:38
  66.9 1.4 %collective-permute-start.18 = (bf16[8,4096]{1,0:T(8,128)(2,1)S(1)}, bf16[8,4096]{1,0:T(8,128)(2,1)S(1)}, u32[]{:S(2)}, u32[]{:S(2)}) collective-permute-start(bf16[8,4096]{1,0:T(8,128)(2,1)S(1)} %get-tuple-element.108), channel_id=1, source_target_pairs={{0,8},{2,10},{4,12},{6,14},{8,0},{10,2},{12,4},{14,6},{16,24},{18,... | collective-permute-start | bytes 196616 | tf_op jit(solution)/shard_map/ppermute | solution.py:38
  68.5 3.5 %gu_grads.3 = (bf16[192,128,128]{2,1,0:T(8,128)(2,1)}, bf16[192,128,128]{2,1,0:T(8,128)(2,1)}) custom-call(s32[1,1,192]{2,1,0:T(1,128)} %index.9, s32[1,1]{1,0:T(1,128)S(6)} %copy.19.count, bf16[8,128,256]{2,1,0:T(8,128)(2,1)S(1)} %get-tuple-element.110.d_pair, ...), custom_call_target="tpu_custom_call", output_to_operand_aliasing={{0}: (4, {}), {1}: (5, {})} | custom-call | flops 536870912 | bytes 4194304 | tf_op jit(solution)/shard_map/gu_grads/pallas_call | solution.py:308
  72.0 2.4 %collective-permute-done.19 = bf16[8,4096]{1,0:T(8,128)(2,1)S(1)} collective-permute-done((bf16[8,4096]{1,0:T(8,128)(2,1)S(1)}, bf16[8,4096]{1,0:T(8,128)(2,1)S(1)}, u32[]{:S(2)}, u32[]{:S(2)}) %collective-permute-start.19) | collective-permute-done | bytes 65568 | tf_op jit(solution)/shard_map/ppermute | solution.py:38
  74.4 0.7 fusion.5
  (39 shorter events, 2.6 us)
Async XLA Ops:
  0.6 8.0 %collective-permute-start = (bf16[8,4096]{1,0:T(8,128)(2,1)}, bf16[8,4096]{1,0:T(8,128)(2,1)S(1)}, u32[]{:S(2)}, u32[]{:S(2)}) collective-permute-start(bf16[8,4096]{1,0:T(8,128)(2,1)} %param.9), channel_id=1, source_target_pairs={{0,16},{2,18},{4,20},{6,22},{8,24},{10,26},{12,28},{14,30},{16,0},... | collective-permute-start | bytes 196616 | tf_op jit(solution)/shard_map/ppermute | solution.py:38
  4.7 6.7 %collective-permute-start.1 = (bf16[8,4096]{1,0:T(8,128)(2,1)}, bf16[8,4096]{1,0:T(8,128)(2,1)S(1)}, u32[]{:S(2)}, u32[]{:S(2)}) collective-permute-start(bf16[8,4096]{1,0:T(8,128)(2,1)} %param.10), channel_id=1, source_target_pairs={{0,16},{2,18},{4,20},{6,22},{8,24},{10,26},{12,28},{14,30},{16,0},... | collective-permute-start | bytes 196616 | tf_op jit(solution)/shard_map/ppermute | solution.py:38
  6.1 2.6 %copy-start = (bf16[8,4096]{1,0:T(8,128)(2,1)S(1)}, bf16[8,4096]{1,0:T(8,128)(2,1)}, u32[]{:S(2)}) copy-start(bf16[8,4096]{1,0:T(8,128)(2,1)} %param.9) | copy-start | bytes 196612
  6.1 5.3 %copy-start.1 = (bf16[8,4096]{1,0:T(8,128)(2,1)S(1)}, bf16[8,4096]{1,0:T(8,128)(2,1)}, u32[]{:S(2)}) copy-start(bf16[8,4096]{1,0:T(8,128)(2,1)} %param.10) | copy-start | bytes 196612
  11.4 5.9 %collective-permute-start.2 = (bf16[16,4096]{1,0:T(8,128)(2,1)S(1)}, bf16[16,4096]{1,0:T(8,128)(2,1)S(1)}, u32[]{:S(2)}, u32[]{:S(2)}) collective-permute-start(bf16[16,4096]{1,0:T(8,128)(2,1)S(1)} %pad_maximum_fusion.3), channel_id=1, source_target_pairs={{0,8},{2,10},{4,12},{6,14},{8,0},{10,2},{12,4},{14,6},{16,24},{18,... | collective-permute-start | bytes 393224 | tf_op jit(solution)/shard_map/ppermute | solution.py:38
  12.2 6.6 %collective-permute-start.3 = (bf16[16,4096]{1,0:T(8,128)(2,1)S(1)}, bf16[16,4096]{1,0:T(8,128)(2,1)S(1)}, u32[]{:S(2)}, u32[]{:S(2)}) collective-permute-start(bf16[16,4096]{1,0:T(8,128)(2,1)S(1)} %pad_maximum_fusion.4), channel_id=1, source_target_pairs={{0,8},{2,10},{4,12},{6,14},{8,0},{10,2},{12,4},{14,6},{16,24},{18,... | collective-permute-start | bytes 393224 | tf_op jit(solution)/shard_map/ppermute | solution.py:38
  18.7 8.0 %collective-permute-start.4 = (bf16[32,4096]{1,0:T(8,128)(2,1)S(1)}, bf16[32,4096]{1,0:T(8,128)(2,1)S(1)}, u32[]{:S(2)}, u32[]{:S(2)}) collective-permute-start(bf16[32,4096]{1,0:T(8,128)(2,1)S(1)} %pad_maximum_fusion.1.refs_0_.refs_4_), channel_id=1, source_target_pairs={{0,4},{2,6},{4,0},{6,2},{8,12},{10,14},{12,8},{14,10},{16,20},{18,... | collective-permute-start | bytes 786440 | tf_op jit(solution)/shard_map/ppermute | solution.py:38
  23.7 4.8 %collective-permute-start.5 = (bf16[32,4096]{1,0:T(8,128)(2,1)S(1)}, bf16[32,4096]{1,0:T(8,128)(2,1)S(1)}, u32[]{:S(2)}, u32[]{:S(2)}) collective-permute-start(bf16[32,4096]{1,0:T(8,128)(2,1)S(1)} %pad_maximum_fusion.1.refs_0_.refs_4_), channel_id=1, source_target_pairs={{0,2},{2,0},{4,6},{6,4},{8,10},{10,8},{12,14},{14,12},{16,18},{18,... | collective-permute-start | bytes 786440 | tf_op jit(solution)/shard_map/ppermute | solution.py:38
  26.7 1.8 %collective-permute-start.6 = (bf16[32,4096]{1,0:T(8,128)(2,1)S(1)}, bf16[32,4096]{1,0:T(8,128)(2,1)S(1)}, u32[]{:S(2)}, u32[]{:S(2)}) collective-permute-start(bf16[32,4096]{1,0:T(8,128)(2,1)S(1)} %collective-permute-done.4.refs_1_.refs_5_), channel_id=1, source_target_pairs={{0,2},{2,0},{4,6},{6,4},{8,10},{10,8},{12,14},{14,12},{16,18},{18,... | collective-permute-start | bytes 786440 | tf_op jit(solution)/shard_map/ppermute | solution.py:38
  26.7 8.7 %collective-permute-start.8 = (bf16[32,4096]{1,0:T(8,128)(2,1)S(1)}, bf16[32,4096]{1,0:T(8,128)(2,1)S(1)}, u32[]{:S(2)}, u32[]{:S(2)}) collective-permute-start(bf16[32,4096]{1,0:T(8,128)(2,1)S(1)} %pad_maximum_fusion.2.refs_0_), channel_id=1, source_target_pairs={{0,4},{2,6},{4,0},{6,2},{8,12},{10,14},{12,8},{14,10},{16,20},{18,... | collective-permute-start | bytes 786440 | tf_op jit(solution)/shard_map/ppermute | solution.py:38
  29.7 8.5 %collective-permute-start.7 = (bf16[4,128,256]{2,1,0:T(8,128)(2,1)S(1)}, bf16[4,128,256]{2,1,0:T(8,128)(2,1)S(1)}, u32[]{:S(2)}, u32[]{:S(2)}) collective-permute-start(bf16[4,128,256]{2,1,0:T(8,128)(2,1)S(1)} %get-tuple-element.70), channel_id=1, source_target_pairs={{0,1},{1,0},{2,3},{3,2},{4,5},{5,4},{6,7},{7,6},{8,9},{9,8},{10,11... | collective-permute-start | bytes 786440 | tf_op jit(solution)/shard_map/ppermute | solution.py:38
  35.5 2.9 %collective-permute-start.9 = (bf16[32,4096]{1,0:T(8,128)(2,1)S(1)}, bf16[32,4096]{1,0:T(8,128)(2,1)S(1)}, u32[]{:S(2)}, u32[]{:S(2)}) collective-permute-start(bf16[32,4096]{1,0:T(8,128)(2,1)S(1)} %pad_maximum_fusion.2.refs_0_), channel_id=1, source_target_pairs={{0,2},{2,0},{4,6},{6,4},{8,10},{10,8},{12,14},{14,12},{16,18},{18,... | collective-permute-start | bytes 786440 | tf_op jit(solution)/shard_map/ppermute | solution.py:38
  35.5 2.9 %collective-permute-start.10 = (bf16[32,4096]{1,0:T(8,128)(2,1)S(1)}, bf16[32,4096]{1,0:T(8,128)(2,1)S(1)}, u32[]{:S(2)}, u32[]{:S(2)}) collective-permute-start(bf16[32,4096]{1,0:T(8,128)(2,1)S(1)} %collective-permute-done.8.refs_1_), channel_id=1, source_target_pairs={{0,2},{2,0},{4,6},{6,4},{8,10},{10,8},{12,14},{14,12},{16,18},{18,... | collective-permute-start | bytes 786440 | tf_op jit(solution)/shard_map/ppermute | solution.py:38
  36.0 9.2 %collective-permute-start.11 = (bf16[4,128,256]{2,1,0:T(8,128)(2,1)S(1)}, bf16[4,128,256]{2,1,0:T(8,128)(2,1)S(1)}, u32[]{:S(2)}, u32[]{:S(2)}) collective-permute-start(bf16[4,128,256]{2,1,0:T(8,128)(2,1)S(1)} %get-tuple-element.79), channel_id=1, source_target_pairs={{0,1},{1,0},{2,3},{3,2},{4,5},{5,4},{6,7},{7,6},{8,9},{9,8},{10,11... | collective-permute-start | bytes 786440 | tf_op jit(solution)/shard_map/ppermute | solution.py:38
  41.0 8.8 %collective-permute-start.12 = (bf16[8,128,128]{2,1,0:T(8,128)(2,1)S(1)}, bf16[8,128,128]{2,1,0:T(8,128)(2,1)S(1)}, u32[]{:S(2)}, u32[]{:S(2)}) collective-permute-start(bf16[8,128,128]{2,1,0:T(8,128)(2,1)S(1)} %get-tuple-element.95), channel_id=1, source_target_pairs={{0,1},{1,0},{2,3},{3,2},{4,5},{5,4},{6,7},{7,6},{8,9},{9,8},{10,11... | collective-permute-start | bytes 786440 | tf_op jit(solution)/shard_map/ppermute | solution.py:38
  52.3 3.1 %collective-permute-start.13 = (bf16[64,2048]{1,0:T(8,128)(2,1)S(1)}, bf16[64,2048]{1,0:T(8,128)(2,1)S(1)}, u32[]{:S(2)}, u32[]{:S(2)}) collective-permute-start(bf16[64,2048]{1,0:T(8,128)(2,1)S(1)} %get-tuple-element.97), channel_id=1, source_target_pairs={{0,2},{2,0},{4,6},{6,4},{8,10},{10,8},{12,14},{14,12},{16,18},{18,... | collective-permute-start | bytes 786440 | tf_op jit(solution)/shard_map/ppermute | solution.py:38
  54.9 2.4 %collective-permute-start.15 = (bf16[64,2048]{1,0:T(8,128)(2,1)S(1)}, bf16[64,2048]{1,0:T(8,128)(2,1)S(1)}, u32[]{:S(2)}, u32[]{:S(2)}) collective-permute-start(bf16[64,2048]{1,0:T(8,128)(2,1)S(1)} %get-tuple-element.100), channel_id=1, source_target_pairs={{0,2},{2,0},{4,6},{6,4},{8,10},{10,8},{12,14},{14,12},{16,18},{18,... | collective-permute-start | bytes 786440 | tf_op jit(solution)/shard_map/ppermute | solution.py:38
  55.5 8.4 %collective-permute-start.14 = (bf16[32,2048]{1,0:T(8,128)(2,1)S(1)}, bf16[32,2048]{1,0:T(8,128)(2,1)S(1)}, u32[]{:S(2)}, u32[]{:S(2)}) collective-permute-start(bf16[32,2048]{1,0:T(8,128)(2,1)S(1)} %slice.65), channel_id=1, source_target_pairs={{0,4},{2,6},{4,0},{6,2},{8,12},{10,14},{12,8},{14,10},{16,20},{18,... | collective-permute-start | bytes 393224 | tf_op jit(solution)/shard_map/ppermute | solution.py:38
  57.4 6.6 %collective-permute-start.16 = (bf16[32,2048]{1,0:T(8,128)(2,1)S(1)}, bf16[32,2048]{1,0:T(8,128)(2,1)S(1)}, u32[]{:S(2)}, u32[]{:S(2)}) collective-permute-start(bf16[32,2048]{1,0:T(8,128)(2,1)S(1)} %slice.64), channel_id=1, source_target_pairs={{0,4},{2,6},{4,0},{6,2},{8,12},{10,14},{12,8},{14,10},{16,20},{18,... | collective-permute-start | bytes 393224 | tf_op jit(solution)/shard_map/ppermute | solution.py:38
  64.1 7.9 %collective-permute-start.17 = (bf16[8,4096]{1,0:T(8,128)(2,1)S(1)}, bf16[8,4096]{1,0:T(8,128)(2,1)S(1)}, u32[]{:S(2)}, u32[]{:S(2)}) collective-permute-start(bf16[8,4096]{1,0:T(8,128)(2,1)S(1)} %get-tuple-element.107), channel_id=1, source_target_pairs={{0,16},{2,18},{4,20},{6,22},{8,24},{10,26},{12,28},{14,30},{16,0},... | collective-permute-start | bytes 196616 | tf_op jit(solution)/shard_map/ppermute | solution.py:38
  66.9 5.1 %collective-permute-start.18 = (bf16[8,4096]{1,0:T(8,128)(2,1)S(1)}, bf16[8,4096]{1,0:T(8,128)(2,1)S(1)}, u32[]{:S(2)}, u32[]{:S(2)}) collective-permute-start(bf16[8,4096]{1,0:T(8,128)(2,1)S(1)} %get-tuple-element.108), channel_id=1, source_target_pairs={{0,8},{2,10},{4,12},{6,14},{8,0},{10,2},{12,4},{14,6},{16,24},{18,... | collective-permute-start | bytes 196616 | tf_op jit(solution)/shard_map/ppermute | solution.py:38
  68.4 6.1 %collective-permute-start.19 = (bf16[8,4096]{1,0:T(8,128)(2,1)S(1)}, bf16[8,4096]{1,0:T(8,128)(2,1)S(1)}, u32[]{:S(2)}, u32[]{:S(2)}) collective-permute-start(bf16[8,4096]{1,0:T(8,128)(2,1)S(1)} %get-tuple-element.109), channel_id=1, source_target_pairs={{0,24},{2,26},{4,28},{6,30},{8,16},{10,18},{12,20},{14,22},{16,8},... | collective-permute-start | bytes 196616 | tf_op jit(solution)/shard_map/ppermute | solution.py:38

commit v15 on v13

--- a/solution.py
+++ b/solution.py
@@ -138,8 +138,8 @@
 
 
 def d_hidden_body(group, pieces_count, *refs):
-    y_pieces, x_pieces = refs[:pieces_count], refs[pieces_count : 2 * pieces_count]
-    down_w, own, send, x_turned, y_turned = refs[2 * pieces_count :]
+    y_pieces, x_pieces = refs[:pieces_count], refs[pieces_count:-5]
+    down_w, own, send, x_turned, y_turned = refs[-5:]
     f_blocks, d_blocks, block, _ = down_w.shape
     for d in range(d_blocks):
         at = slice(d * block, (d + 1) * block)
@@ -167,7 +167,7 @@
     f_blocks, d_blocks, block, _ = down_w.shape
     tokens = sum(piece.shape[0] for piece in y_pieces)
     shape = (f_blocks, tokens, block)
-    group = max(n for n in (1, 2, 4) if f_blocks % n == 0)
+    group = max(n for n in (1, 2, 4, 8) if f_blocks % n == 0)
     return pl.pallas_call(
         functools.partial(d_hidden_body, group, len(y_pieces)),
         out_shape=(
@@ -175,7 +175,7 @@
             jax.ShapeDtypeStruct(shape, BF16),
             jax.ShapeDtypeStruct((d_blocks, block, tokens), BF16),
         ),
-        in_specs=[WHOLE] * (2 * len(y_pieces) + 1),
+        in_specs=[WHOLE] * (len(y_pieces) + len(x_pieces) + 1),
         out_specs=(WHOLE,) * 3,
         scratch_shapes=[pltpu.VMEM((d_blocks * block, tokens), BF16)],
         compiler_params=params(),
@@ -230,7 +230,7 @@
     d_blocks, f_blocks, block, _ = gate_w.shape
     tokens = dh_own.shape[1]
     half = (tokens // 2, d_blocks // 2 * block)
-    group = max(n for n in (1, 2, 4) if d_blocks // 2 % n == 0)
+    group = max(n for n in (1, 2, 4, 8) if d_blocks // 2 % n == 0)
     halves = (jax.ShapeDtypeStruct(half, F32), jax.ShapeDtypeStruct(half, BF16))
     common = dict(
         compiler_params=params(),
@@ -293,9 +293,14 @@
     def _():
         work(False)
 
-    @pl.when(begin + chunk > slots.live)
+    @pl.when((begin + chunk > slots.live) & (begin < slots.live))
     def _():
         work(True)
+
+    @pl.when(begin >= slots.live)
+    def _():
+        gate_out[...] = jnp.zeros(gate_out.shape, gate_out.dtype)
+        up_out[...] = jnp.zeros(up_out.shape, up_out.dtype)
 
 
 def gu_grads(index, count, d_pair, turned, total, begin, end, before):

time: 71.9 us -> 72 us (level)
  Pallas kernels: 34.1 us -> 31.3 us
  waiting for transfers between devices: 6.87 us -> 9.21 us
    ppermute x20, waiting for transfers between devices: 6.87 us -> 9.21 us  [swap(): return lax.ppermute(array, axis, [(i, i ^ flip) for i in range(size)])]
    pallas_call x3, Pallas kernels: 9.03 us -> 7.27 us  [fill(): pl.pallas_call(fill_body, out_shape=pltpu.VMEM((outer, inner, block, bloc...]
    pallas_call x2, Pallas kernels: 8.91 us -> 7.95 us  [gu_grads(): pl.pallas_call(functools.partial(gu_grad_body, first, len(before)), out_s...]
  transfers between devices with their start and end apart: 20 -> 20, of which waited for: 8 -> 9; matrix products, arithmetic and copies ran while one was open for 0% -> 0% of each run, Pallas kernels for 44% -> 40%
where the time goes in v15:
time: 72 us; the launch traced here: 71 us
  Pallas kernels  31.3 us (43%)
  starting transfers between devices  27.4 us (38%)
  waiting for transfers between devices  9.21 us (13%)
  between operations  2.19 us (3%)
  other arithmetic  0.89 us (1%)
    ppermute x20, starting transfers between devices, swap(): return lax.ppermute(array, axis, [(i, i ^ flip) for i in range(size)])  27.4 us
    ppermute x20, waiting for transfers between devices, swap(): return lax.ppermute(array, axis, [(i, i ^ flip) for i in range(size)])  9.21 us
    pallas_call x2, Pallas kernels, gu_grads(): pl.pallas_call(functools.partial(gu_grad_body, first, len(before)), out_s...  7.95 us
    pallas_call x3, Pallas kernels, fill(): pl.pallas_call(fill_body, out_shape=pltpu.VMEM((outer, inner, block, bloc...  7.27 us
    pallas_call x1, Pallas kernels, down_second(): pl.pallas_call(functools.partial(down_second_body, first), out_shape=(jax...  4.48 us
    pallas_call x1, Pallas kernels, d_hidden(): pl.pallas_call(functools.partial(d_hidden_body, group, len(y_pieces)), ou...  2.56 us
    pallas_call x1, Pallas kernels, d_tokens_parts(): pl.pallas_call(functools.partial(d_tokens_first_body, group), out_shape=(...  2.54 us
    pallas_call x2, Pallas kernels, gate_up(): pl.pallas_call(functools.partial(gate_up_body, half * f_blocks // 2), out...  2.51 us
  transfers between devices with their start and end apart: 20, of which 9 were waited for; matrix products, arithmetic and copies ran while one was open for 0% of the time, Pallas kernels for 40%

profile of v15, /device:TPU:0, one launch (start us, length us, event | category | flops | bytes accessed | tf_op | source)
XLA Modules:
  0.0 71.0 jit_solution(11924224087695460386)
XLA Ops:
  0.6 4.1 %collective-permute-start = (bf16[8,4096]{1,0:T(8,128)(2,1)}, bf16[8,4096]{1,0:T(8,128)(2,1)S(1)}, u32[]{:S(2)}, u32[]{:S(2)}) collective-permute-start(bf16[8,4096]{1,0:T(8,128)(2,1)} %param.9), channel_id=1, source_target_pairs={{0,16},{2,18},{4,20},{6,22},{8,24},{10,26},{12,28},{14,30},{16,0},... | collective-permute-start | bytes 196616 | tf_op jit(solution)/shard_map/ppermute | solution.py:38
  6.0 2.3 %fill.3.refs_4_.gate_w = bf16[32,8,128,128]{3,2,1,0:T(8,128)(2,1)S(1)} custom-call(s32[1,1,192]{2,1,0:T(1,128)} %index.9, s32[1,1]{1,0:T(1,128)S(6)} %copy.19.count, bf16[1,1,192,128,128]{4,3,2,1,0:T(8,128)(2,1)} %source.3, s32[1,1]{1,0:T(1,128)S(6)} %copy.20.refs_0_.count), custom_call_target="tpu_custom_call" | custom-call | bytes 6291456 | tf_op jit(solution)/shard_map/fill/pallas_call | solution.py:92
  8.6 2.0 %collective-permute-start.1 = (bf16[16,4096]{1,0:T(8,128)(2,1)S(1)}, bf16[16,4096]{1,0:T(8,128)(2,1)S(1)}, u32[]{:S(2)}, u32[]{:S(2)}) collective-permute-start(bf16[16,4096]{1,0:T(8,128)(2,1)S(1)} %pad_maximum_fusion.3), channel_id=1, source_target_pairs={{0,8},{2,10},{4,12},{6,14},{8,0},{10,2},{12,4},{14,6},{16,24},{18,... | collective-permute-start | bytes 393224 | tf_op jit(solution)/shard_map/ppermute | solution.py:38
  10.6 2.2 %fill.4.refs_5_.up_w = bf16[32,8,128,128]{3,2,1,0:T(8,128)(2,1)S(1)} custom-call(s32[1,1,192]{2,1,0:T(1,128)} %index.9, s32[1,1]{1,0:T(1,128)S(6)} %copy.19.count, bf16[1,1,192,128,128]{4,3,2,1,0:T(8,128)(2,1)} %source.4), custom_call_target="tpu_custom_call" | custom-call | bytes 6291456 | tf_op jit(solution)/shard_map/fill/pallas_call | solution.py:92
  12.9 0.8 %collective-permute-done.1 = bf16[16,4096]{1,0:T(8,128)(2,1)S(1)} collective-permute-done((bf16[16,4096]{1,0:T(8,128)(2,1)S(1)}, bf16[16,4096]{1,0:T(8,128)(2,1)S(1)}, u32[]{:S(2)}, u32[]{:S(2)}) %collective-permute-start.1) | collective-permute-done | bytes 131104 | tf_op jit(solution)/shard_map/ppermute | solution.py:38
  13.7 2.4 %collective-permute-start.6 = (bf16[8,4096]{1,0:T(8,128)(2,1)S(1)}, bf16[8,4096]{1,0:T(8,128)(2,1)S(1)}, u32[]{:S(2)}, u32[]{:S(2)}) collective-permute-start(bf16[8,4096]{1,0:T(8,128)(2,1)S(1)} %copy-done), channel_id=1, source_target_pairs={{0,16},{2,18},{4,20},{6,22},{8,24},{10,26},{12,28},{14,30},{16,0},... | collective-permute-start | bytes 196616 | tf_op jit(solution)/shard_map/ppermute | solution.py:38
  16.1 1.5 %collective-permute-start.2 = (bf16[32,4096]{1,0:T(8,128)(2,1)S(1)}, bf16[32,4096]{1,0:T(8,128)(2,1)S(1)}, u32[]{:S(2)}, u32[]{:S(2)}) collective-permute-start(bf16[32,4096]{1,0:T(8,128)(2,1)S(1)} %pad_maximum_fusion.1.refs_0_.refs_4_), channel_id=1, source_target_pairs={{0,4},{2,6},{4,0},{6,2},{8,12},{10,14},{12,8},{14,10},{16,20},{18,... | collective-permute-start | bytes 786440 | tf_op jit(solution)/shard_map/ppermute | solution.py:38
  17.6 1.3 %collective-permute-done.6 = bf16[8,4096]{1,0:T(8,128)(2,1)S(1)} collective-permute-done((bf16[8,4096]{1,0:T(8,128)(2,1)S(1)}, bf16[8,4096]{1,0:T(8,128)(2,1)S(1)}, u32[]{:S(2)}, u32[]{:S(2)}) %collective-permute-start.6) | collective-permute-done | bytes 65568 | tf_op jit(solution)/shard_map/ppermute | solution.py:38
  18.9 2.0 %collective-permute-start.7 = (bf16[16,4096]{1,0:T(8,128)(2,1)S(1)}, bf16[16,4096]{1,0:T(8,128)(2,1)S(1)}, u32[]{:S(2)}, u32[]{:S(2)}) collective-permute-start(bf16[16,4096]{1,0:T(8,128)(2,1)S(1)} %pad_maximum_fusion.4), channel_id=1, source_target_pairs={{0,8},{2,10},{4,12},{6,14},{8,0},{10,2},{12,4},{14,6},{16,24},{18,... | collective-permute-start | bytes 393224 | tf_op jit(solution)/shard_map/ppermute | solution.py:38
  20.9 2.8 %fill.5.refs_8_ = bf16[8,32,128,128]{3,2,1,0:T(8,128)(2,1)S(1)} custom-call(s32[1,1,192]{2,1,0:T(1,128)} %index.7, s32[1,1]{1,0:T(1,128)S(6)} %copy.20.refs_0_.count, bf16[1,1,192,128,128]{4,3,2,1,0:T(8,128)(2,1)} %source.5), custom_call_target="tpu_custom_call" | custom-call | bytes 6291456 | tf_op jit(solution)/shard_map/fill/pallas_call | solution.py:92
  24.3 2.1 %collective-permute-start.8 = (bf16[32,4096]{1,0:T(8,128)(2,1)S(1)}, bf16[32,4096]{1,0:T(8,128)(2,1)S(1)}, u32[]{:S(2)}, u32[]{:S(2)}) collective-permute-start(bf16[32,4096]{1,0:T(8,128)(2,1)S(1)} %pad_maximum_fusion.2.refs_0_), channel_id=1, source_target_pairs={{0,4},{2,6},{4,0},{6,2},{8,12},{10,14},{12,8},{14,10},{16,20},{18,... | collective-permute-start | bytes 786440 | tf_op jit(solution)/shard_map/ppermute | solution.py:38
  26.4 1.3 %gate_up.2 = (f32[4,128,256]{2,1,0:T(8,128)S(1)}, bf16[4,128,256]{2,1,0:T(8,128)(2,1)S(1)}) custom-call(bf16[32,4096]{1,0:T(8,128)(2,1)S(1)} %pad_maximum_fusion.1.refs_0_.refs_4_, bf16[32,4096]{1,0:T(8,128)(2,1)S(1)} %collective-permute-done.2.refs_1_.refs_5_, bf16[32,4096]{1,0:T(8,128)(2,1)S(1)} %collective-permute-done.3.refs_2_.refs_6_, ...), custom_call_target="tpu_custom_call" | custom-call | flops 1073741824 | bytes 8388608 | tf_op jit(solution)/shard_map/gate_up/pallas_call | solution.py:129
  27.6 1.3 %collective-permute-start.5 = (bf16[4,128,256]{2,1,0:T(8,128)(2,1)S(1)}, bf16[4,128,256]{2,1,0:T(8,128)(2,1)S(1)}, u32[]{:S(2)}, u32[]{:S(2)}) collective-permute-start(bf16[4,128,256]{2,1,0:T(8,128)(2,1)S(1)} %get-tuple-element.68), channel_id=1, source_target_pairs={{0,1},{1,0},{2,3},{3,2},{4,5},{5,4},{6,7},{7,6},{8,9},{9,8},{10,11... | collective-permute-start | bytes 786440 | tf_op jit(solution)/shard_map/ppermute | solution.py:38
  28.9 1.3 %gate_up.3 = (f32[4,128,256]{2,1,0:T(8,128)S(1)}, bf16[4,128,256]{2,1,0:T(8,128)(2,1)S(1)}) custom-call(bf16[32,4096]{1,0:T(8,128)(2,1)S(1)} %pad_maximum_fusion.1.refs_0_.refs_4_, bf16[32,4096]{1,0:T(8,128)(2,1)S(1)} %collective-permute-done.2.refs_1_.refs_5_, bf16[32,4096]{1,0:T(8,128)(2,1)S(1)} %collective-permute-done.3.refs_2_.refs_6_, ...), custom_call_target="tpu_custom_call" | custom-call | flops 1073741824 | bytes 8388608 | tf_op jit(solution)/shard_map/gate_up/pallas_call | solution.py:129
  30.2 2.4 %collective-permute-done.8.refs_1_ = bf16[32,4096]{1,0:T(8,128)(2,1)S(1)} collective-permute-done((bf16[32,4096]{1,0:T(8,128)(2,1)S(1)}, bf16[32,4096]{1,0:T(8,128)(2,1)S(1)}, u32[]{:S(2)}, u32[]{:S(2)}) %collective-permute-start.8) | collective-permute-done | bytes 262176 | tf_op jit(solution)/shard_map/ppermute | solution.py:38
  33.2 1.5 %collective-permute-start.11 = (bf16[4,128,256]{2,1,0:T(8,128)(2,1)S(1)}, bf16[4,128,256]{2,1,0:T(8,128)(2,1)S(1)}, u32[]{:S(2)}, u32[]{:S(2)}) collective-permute-start(bf16[4,128,256]{2,1,0:T(8,128)(2,1)S(1)} %get-tuple-element.77), channel_id=1, source_target_pairs={{0,1},{1,0},{2,3},{3,2},{4,5},{5,4},{6,7},{7,6},{8,9},{9,8},{10,11... | collective-permute-start | bytes 786440 | tf_op jit(solution)/shard_map/ppermute | solution.py:38
  34.7 0.7 collective-permute-done.5.refs_1_
  35.5 2.6 %d_hidden.1 = (f32[8,128,128]{2,1,0:T(8,128)S(1)}, bf16[8,128,128]{2,1,0:T(8,128)(2,1)S(1)}, bf16[32,128,128]{2,1,0:T(8,128)(2,1)S(1)}) custom-call(bf16[32,4096]{1,0:T(8,128)(2,1)S(1)} %pad_maximum_fusion.2.refs_0_, bf16[32,4096]{1,0:T(8,128)(2,1)S(1)} %collective-permute-done.8.refs_1_, bf16[32,4096]{1,0:T(8,128)(2,1)S(1)} %collective-permute-done.9.refs_2_, ...), custom_call_target="tpu_custom_call" | custom-call | flops 1073741824 | bytes 8388608 | tf_op jit(solution)/shard_map/d_hidden/pallas_call | solution.py:171
  38.0 1.6 %collective-permute-start.12 = (bf16[8,128,128]{2,1,0:T(8,128)(2,1)S(1)}, bf16[8,128,128]{2,1,0:T(8,128)(2,1)S(1)}, u32[]{:S(2)}, u32[]{:S(2)}) collective-permute-start(bf16[8,128,128]{2,1,0:T(8,128)(2,1)S(1)} %get-tuple-element.93), channel_id=1, source_target_pairs={{0,1},{1,0},{2,3},{3,2},{4,5},{5,4},{6,7},{7,6},{8,9},{9,8},{10,11... | collective-permute-start | bytes 786440 | tf_op jit(solution)/shard_map/ppermute | solution.py:38
  39.6 1.3 %down_first.1._ = bf16[257,128,128]{2,1,0:T(8,128)(2,1)S(1)} custom-call(bf16[4,128,128]{2,1,0:T(8,128)(2,1)S(1)} %get-tuple-element.74.hidden, bf16[32,4096]{1,0:T(8,128)(2,1)S(1)} %pad_maximum_fusion.2.refs_0_, bf16[32,4096]{1,0:T(8,128)(2,1)S(1)} %collective-permute-done.8.refs_1_, bf16[32,4096]{1,0:T(8,128)(2,1)S(1)} %collective-permute-done.9.refs_2_, ...), custom_call_target="tpu_custom_call" | custom-call | flops 538968064 | bytes 8421376 | tf_op jit(solution)/shard_map/down_first/pallas_call | solution.py:402
  40.9 1.4 %collective-permute-done.11.refs_1_ = bf16[4,128,256]{2,1,0:T(8,128)(2,1)S(1)} collective-permute-done((bf16[4,128,256]{2,1,0:T(8,128)(2,1)S(1)}, bf16[4,128,256]{2,1,0:T(8,128)(2,1)S(1)}, u32[]{:S(2)}, u32[]{:S(2)}) %collective-permute-start.11) | collective-permute-done | bytes 262176 | tf_op jit(solution)/shard_map/ppermute | solution.py:38
  42.5 4.5 %down_second.1 = (bf16[192,128,128]{2,1,0:T(8,128)(2,1)}, bf16[257,128,128]{2,1,0:T(8,128)(2,1)S(1)}) custom-call(s32[1,1,192]{2,1,0:T(1,128)} %index.7, s32[1,1]{1,0:T(1,128)S(6)} %copy.20.refs_0_.count, bf16[4,128,128]{2,1,0:T(8,128)(2,1)S(1)} %get-tuple-element.87.hidden, ...), custom_call_target="tpu_custom_call", output_to_operand_aliasing={{1}: (3, {})} | custom-call | flops 402653184 | bytes 6291456 | tf_op jit(solution)/shard_map/down_second/pallas_call | solution.py:418
  47.0 2.5 %d_tokens_first.1 = (f32[64,2048]{1,0:T(8,128)S(1)}, bf16[64,2048]{1,0:T(8,128)(2,1)S(1)}, bf16[8,128,256]{2,1,0:T(8,128)(2,1)S(1)}, bf16[2048,128]{1,0:T(8,128)(2,1)S(1)}) custom-call(f32[4,128,256]{2,1,0:T(8,128)S(1)} %get-tuple-element.69.refs_0_, f32[4,128,256]{2,1,0:T(8,128)S(1)} %get-tuple-element.91.refs_1_, ...), custom_call_target="tpu_custom_call" | custom-call | flops 1073741824 | bytes 8388608 | tf_op jit(solution)/shard_map/d_tokens_first/pallas_call | solution.py:240
  49.6 2.4 %d_tokens_second.1 = (f32[64,2048]{1,0:T(8,128)S(1)}, bf16[64,2048]{1,0:T(8,128)(2,1)S(1)}) custom-call(bf16[2048,128]{1,0:T(8,128)(2,1)S(1)} %get-tuple-element.96.turned, bf16[32,8,128,128]{3,2,1,0:T(8,128)(2,1)S(1)} %fill.3.refs_4_.gate_w, bf16[32,8,128,128]{3,2,1,0:T(8,128)(2,1)S(1)} %fill.4.refs_5_.up_w), custom_call_target="tpu_custom_call" | custom-call | flops 1073741824 | bytes 8388608 | tf_op jit(solution)/shard_map/d_tokens_second/pallas_call | solution.py:252
  52.7 1.5 %collective-permute-start.14 = (bf16[32,2048]{1,0:T(8,128)(2,1)S(1)}, bf16[32,2048]{1,0:T(8,128)(2,1)S(1)}, u32[]{:S(2)}, u32[]{:S(2)}) collective-permute-start(bf16[32,2048]{1,0:T(8,128)(2,1)S(1)} %slice.65), channel_id=1, source_target_pairs={{0,4},{2,6},{4,0},{6,2},{8,12},{10,14},{12,8},{14,10},{16,20},{18,... | collective-permute-start | bytes 393224 | tf_op jit(solution)/shard_map/ppermute | solution.py:38
  54.3 1.1 %collective-permute-start.16 = (bf16[32,2048]{1,0:T(8,128)(2,1)S(1)}, bf16[32,2048]{1,0:T(8,128)(2,1)S(1)}, u32[]{:S(2)}, u32[]{:S(2)}) collective-permute-start(bf16[32,2048]{1,0:T(8,128)(2,1)S(1)} %slice.64), channel_id=1, source_target_pairs={{0,4},{2,6},{4,0},{6,2},{8,12},{10,14},{12,8},{14,10},{16,20},{18,... | collective-permute-start | bytes 393224 | tf_op jit(solution)/shard_map/ppermute | solution.py:38
  55.4 5.0 %gu_grads.2 = (bf16[192,128,128]{2,1,0:T(8,128)(2,1)}, bf16[192,128,128]{2,1,0:T(8,128)(2,1)}) custom-call(s32[1,1,192]{2,1,0:T(1,128)} %index.9, s32[1,1]{1,0:T(1,128)S(6)} %copy.19.count, bf16[8,128,256]{2,1,0:T(8,128)(2,1)S(1)} %get-tuple-element.108.d_pair, bf16[32,128,128]{2,1,0:T(8,128)(2,1)S(1)} %get-tuple-element.102.turned), custom_call_target="tpu_custom_call" | custom-call | flops 1073741824 | bytes 8388608 | tf_op jit(solution)/shard_map/gu_grads/pallas_call | solution.py:313
  61.1 3.1 %collective-permute-start.17 = (bf16[8,4096]{1,0:T(8,128)(2,1)S(1)}, bf16[8,4096]{1,0:T(8,128)(2,1)S(1)}, u32[]{:S(2)}, u32[]{:S(2)}) collective-permute-start(bf16[8,4096]{1,0:T(8,128)(2,1)S(1)} %get-tuple-element.105), channel_id=1, source_target_pairs={{0,16},{2,18},{4,20},{6,22},{8,24},{10,26},{12,28},{14,30},{16,0},... | collective-permute-start | bytes 196616 | tf_op jit(solution)/shard_map/ppermute | solution.py:38
  64.2 1.5 %collective-permute-start.19 = (bf16[8,4096]{1,0:T(8,128)(2,1)S(1)}, bf16[8,4096]{1,0:T(8,128)(2,1)S(1)}, u32[]{:S(2)}, u32[]{:S(2)}) collective-permute-start(bf16[8,4096]{1,0:T(8,128)(2,1)S(1)} %get-tuple-element.107), channel_id=1, source_target_pairs={{0,24},{2,26},{4,28},{6,30},{8,16},{10,18},{12,20},{14,22},{16,8},... | collective-permute-start | bytes 196616 | tf_op jit(solution)/shard_map/ppermute | solution.py:38
  65.7 3.0 %gu_grads.3 = (bf16[192,128,128]{2,1,0:T(8,128)(2,1)}, bf16[192,128,128]{2,1,0:T(8,128)(2,1)}) custom-call(s32[1,1,192]{2,1,0:T(1,128)} %index.9, s32[1,1]{1,0:T(1,128)S(6)} %copy.19.count, bf16[8,128,256]{2,1,0:T(8,128)(2,1)S(1)} %get-tuple-element.108.d_pair, ...), custom_call_target="tpu_custom_call", output_to_operand_aliasing={{0}: (4, {}), {1}: (5, {})} | custom-call | flops 536870912 | bytes 4194304 | tf_op jit(solution)/shard_map/gu_grads/pallas_call | solution.py:313
  69.0 1.3 %collective-permute-done.19 = bf16[8,4096]{1,0:T(8,128)(2,1)S(1)} collective-permute-done((bf16[8,4096]{1,0:T(8,128)(2,1)S(1)}, bf16[8,4096]{1,0:T(8,128)(2,1)S(1)}, u32[]{:S(2)}, u32[]{:S(2)}) %collective-permute-start.19) | collective-permute-done | bytes 65568 | tf_op jit(solution)/shard_map/ppermute | solution.py:38
  70.4 0.7 fusion.5
  (39 shorter events, 3.5 us)
Async XLA Ops:
  0.6 8.0 %collective-permute-start = (bf16[8,4096]{1,0:T(8,128)(2,1)}, bf16[8,4096]{1,0:T(8,128)(2,1)S(1)}, u32[]{:S(2)}, u32[]{:S(2)}) collective-permute-start(bf16[8,4096]{1,0:T(8,128)(2,1)} %param.9), channel_id=1, source_target_pairs={{0,16},{2,18},{4,20},{6,22},{8,24},{10,26},{12,28},{14,30},{16,0},... | collective-permute-start | bytes 196616 | tf_op jit(solution)/shard_map/ppermute | solution.py:38
  6.0 2.6 %copy-start.1 = (bf16[8,4096]{1,0:T(8,128)(2,1)S(1)}, bf16[8,4096]{1,0:T(8,128)(2,1)}, u32[]{:S(2)}) copy-start(bf16[8,4096]{1,0:T(8,128)(2,1)} %param.9) | copy-start | bytes 196612
  8.6 5.1 %copy-start = (bf16[8,4096]{1,0:T(8,128)(2,1)S(1)}, bf16[8,4096]{1,0:T(8,128)(2,1)}, u32[]{:S(2)}) copy-start(bf16[8,4096]{1,0:T(8,128)(2,1)} %param.10) | copy-start | bytes 196612
  8.6 5.0 %collective-permute-start.1 = (bf16[16,4096]{1,0:T(8,128)(2,1)S(1)}, bf16[16,4096]{1,0:T(8,128)(2,1)S(1)}, u32[]{:S(2)}, u32[]{:S(2)}) collective-permute-start(bf16[16,4096]{1,0:T(8,128)(2,1)S(1)} %pad_maximum_fusion.3), channel_id=1, source_target_pairs={{0,8},{2,10},{4,12},{6,14},{8,0},{10,2},{12,4},{14,6},{16,24},{18,... | collective-permute-start | bytes 393224 | tf_op jit(solution)/shard_map/ppermute | solution.py:38
  13.7 5.2 %collective-permute-start.6 = (bf16[8,4096]{1,0:T(8,128)(2,1)S(1)}, bf16[8,4096]{1,0:T(8,128)(2,1)S(1)}, u32[]{:S(2)}, u32[]{:S(2)}) collective-permute-start(bf16[8,4096]{1,0:T(8,128)(2,1)S(1)} %copy-done), channel_id=1, source_target_pairs={{0,16},{2,18},{4,20},{6,22},{8,24},{10,26},{12,28},{14,30},{16,0},... | collective-permute-start | bytes 196616 | tf_op jit(solution)/shard_map/ppermute | solution.py:38
  16.1 7.7 %collective-permute-start.2 = (bf16[32,4096]{1,0:T(8,128)(2,1)S(1)}, bf16[32,4096]{1,0:T(8,128)(2,1)S(1)}, u32[]{:S(2)}, u32[]{:S(2)}) collective-permute-start(bf16[32,4096]{1,0:T(8,128)(2,1)S(1)} %pad_maximum_fusion.1.refs_0_.refs_4_), channel_id=1, source_target_pairs={{0,4},{2,6},{4,0},{6,2},{8,12},{10,14},{12,8},{14,10},{16,20},{18,... | collective-permute-start | bytes 786440 | tf_op jit(solution)/shard_map/ppermute | solution.py:38
  18.9 5.3 %collective-permute-start.7 = (bf16[16,4096]{1,0:T(8,128)(2,1)S(1)}, bf16[16,4096]{1,0:T(8,128)(2,1)S(1)}, u32[]{:S(2)}, u32[]{:S(2)}) collective-permute-start(bf16[16,4096]{1,0:T(8,128)(2,1)S(1)} %pad_maximum_fusion.4), channel_id=1, source_target_pairs={{0,8},{2,10},{4,12},{6,14},{8,0},{10,2},{12,4},{14,6},{16,24},{18,... | collective-permute-start | bytes 393224 | tf_op jit(solution)/shard_map/ppermute | solution.py:38
  23.7 2.7 %collective-permute-start.3 = (bf16[32,4096]{1,0:T(8,128)(2,1)S(1)}, bf16[32,4096]{1,0:T(8,128)(2,1)S(1)}, u32[]{:S(2)}, u32[]{:S(2)}) collective-permute-start(bf16[32,4096]{1,0:T(8,128)(2,1)S(1)} %pad_maximum_fusion.1.refs_0_.refs_4_), channel_id=1, source_target_pairs={{0,2},{2,0},{4,6},{6,4},{8,10},{10,8},{12,14},{14,12},{16,18},{18,... | collective-permute-start | bytes 786440 | tf_op jit(solution)/shard_map/ppermute | solution.py:38
  23.8 2.6 %collective-permute-start.4 = (bf16[32,4096]{1,0:T(8,128)(2,1)S(1)}, bf16[32,4096]{1,0:T(8,128)(2,1)S(1)}, u32[]{:S(2)}, u32[]{:S(2)}) collective-permute-start(bf16[32,4096]{1,0:T(8,128)(2,1)S(1)} %collective-permute-done.2.refs_1_.refs_5_), channel_id=1, source_target_pairs={{0,2},{2,0},{4,6},{6,4},{8,10},{10,8},{12,14},{14,12},{16,18},{18,... | collective-permute-start | bytes 786440 | tf_op jit(solution)/shard_map/ppermute | solution.py:38
  24.3 8.4 %collective-permute-start.8 = (bf16[32,4096]{1,0:T(8,128)(2,1)S(1)}, bf16[32,4096]{1,0:T(8,128)(2,1)S(1)}, u32[]{:S(2)}, u32[]{:S(2)}) collective-permute-start(bf16[32,4096]{1,0:T(8,128)(2,1)S(1)} %pad_maximum_fusion.2.refs_0_), channel_id=1, source_target_pairs={{0,4},{2,6},{4,0},{6,2},{8,12},{10,14},{12,8},{14,10},{16,20},{18,... | collective-permute-start | bytes 786440 | tf_op jit(solution)/shard_map/ppermute | solution.py:38
  27.6 7.7 %collective-permute-start.5 = (bf16[4,128,256]{2,1,0:T(8,128)(2,1)S(1)}, bf16[4,128,256]{2,1,0:T(8,128)(2,1)S(1)}, u32[]{:S(2)}, u32[]{:S(2)}) collective-permute-start(bf16[4,128,256]{2,1,0:T(8,128)(2,1)S(1)} %get-tuple-element.68), channel_id=1, source_target_pairs={{0,1},{1,0},{2,3},{3,2},{4,5},{5,4},{6,7},{7,6},{8,9},{9,8},{10,11... | collective-permute-start | bytes 786440 | tf_op jit(solution)/shard_map/ppermute | solution.py:38
  32.7 2.8 %collective-permute-start.9 = (bf16[32,4096]{1,0:T(8,128)(2,1)S(1)}, bf16[32,4096]{1,0:T(8,128)(2,1)S(1)}, u32[]{:S(2)}, u32[]{:S(2)}) collective-permute-start(bf16[32,4096]{1,0:T(8,128)(2,1)S(1)} %pad_maximum_fusion.2.refs_0_), channel_id=1, source_target_pairs={{0,2},{2,0},{4,6},{6,4},{8,10},{10,8},{12,14},{14,12},{16,18},{18,... | collective-permute-start | bytes 786440 | tf_op jit(solution)/shard_map/ppermute | solution.py:38
  32.7 2.8 %collective-permute-start.10 = (bf16[32,4096]{1,0:T(8,128)(2,1)S(1)}, bf16[32,4096]{1,0:T(8,128)(2,1)S(1)}, u32[]{:S(2)}, u32[]{:S(2)}) collective-permute-start(bf16[32,4096]{1,0:T(8,128)(2,1)S(1)} %collective-permute-done.8.refs_1_), channel_id=1, source_target_pairs={{0,2},{2,0},{4,6},{6,4},{8,10},{10,8},{12,14},{14,12},{16,18},{18,... | collective-permute-start | bytes 786440 | tf_op jit(solution)/shard_map/ppermute | solution.py:38
  33.2 9.2 %collective-permute-start.11 = (bf16[4,128,256]{2,1,0:T(8,128)(2,1)S(1)}, bf16[4,128,256]{2,1,0:T(8,128)(2,1)S(1)}, u32[]{:S(2)}, u32[]{:S(2)}) collective-permute-start(bf16[4,128,256]{2,1,0:T(8,128)(2,1)S(1)} %get-tuple-element.77), channel_id=1, source_target_pairs={{0,1},{1,0},{2,3},{3,2},{4,5},{5,4},{6,7},{7,6},{8,9},{9,8},{10,11... | collective-permute-start | bytes 786440 | tf_op jit(solution)/shard_map/ppermute | solution.py:38
  38.0 8.9 %collective-permute-start.12 = (bf16[8,128,128]{2,1,0:T(8,128)(2,1)S(1)}, bf16[8,128,128]{2,1,0:T(8,128)(2,1)S(1)}, u32[]{:S(2)}, u32[]{:S(2)}) collective-permute-start(bf16[8,128,128]{2,1,0:T(8,128)(2,1)S(1)} %get-tuple-element.93), channel_id=1, source_target_pairs={{0,1},{1,0},{2,3},{3,2},{4,5},{5,4},{6,7},{7,6},{8,9},{9,8},{10,11... | collective-permute-start | bytes 786440 | tf_op jit(solution)/shard_map/ppermute | solution.py:38
  49.5 3.1 %collective-permute-start.13 = (bf16[64,2048]{1,0:T(8,128)(2,1)S(1)}, bf16[64,2048]{1,0:T(8,128)(2,1)S(1)}, u32[]{:S(2)}, u32[]{:S(2)}) collective-permute-start(bf16[64,2048]{1,0:T(8,128)(2,1)S(1)} %get-tuple-element.95), channel_id=1, source_target_pairs={{0,2},{2,0},{4,6},{6,4},{8,10},{10,8},{12,14},{14,12},{16,18},{18,... | collective-permute-start | bytes 786440 | tf_op jit(solution)/shard_map/ppermute | solution.py:38
  52.0 2.2 %collective-permute-start.15 = (bf16[64,2048]{1,0:T(8,128)(2,1)S(1)}, bf16[64,2048]{1,0:T(8,128)(2,1)S(1)}, u32[]{:S(2)}, u32[]{:S(2)}) collective-permute-start(bf16[64,2048]{1,0:T(8,128)(2,1)S(1)} %get-tuple-element.98), channel_id=1, source_target_pairs={{0,2},{2,0},{4,6},{6,4},{8,10},{10,8},{12,14},{14,12},{16,18},{18,... | collective-permute-start | bytes 786440 | tf_op jit(solution)/shard_map/ppermute | solution.py:38
  52.7 7.7 %collective-permute-start.14 = (bf16[32,2048]{1,0:T(8,128)(2,1)S(1)}, bf16[32,2048]{1,0:T(8,128)(2,1)S(1)}, u32[]{:S(2)}, u32[]{:S(2)}) collective-permute-start(bf16[32,2048]{1,0:T(8,128)(2,1)S(1)} %slice.65), channel_id=1, source_target_pairs={{0,4},{2,6},{4,0},{6,2},{8,12},{10,14},{12,8},{14,10},{16,20},{18,... | collective-permute-start | bytes 393224 | tf_op jit(solution)/shard_map/ppermute | solution.py:38
  54.3 6.7 %collective-permute-start.16 = (bf16[32,2048]{1,0:T(8,128)(2,1)S(1)}, bf16[32,2048]{1,0:T(8,128)(2,1)S(1)}, u32[]{:S(2)}, u32[]{:S(2)}) collective-permute-start(bf16[32,2048]{1,0:T(8,128)(2,1)S(1)} %slice.64), channel_id=1, source_target_pairs={{0,4},{2,6},{4,0},{6,2},{8,12},{10,14},{12,8},{14,10},{16,20},{18,... | collective-permute-start | bytes 393224 | tf_op jit(solution)/shard_map/ppermute | solution.py:38
  61.1 7.7 %collective-permute-start.17 = (bf16[8,4096]{1,0:T(8,128)(2,1)S(1)}, bf16[8,4096]{1,0:T(8,128)(2,1)S(1)}, u32[]{:S(2)}, u32[]{:S(2)}) collective-permute-start(bf16[8,4096]{1,0:T(8,128)(2,1)S(1)} %get-tuple-element.105), channel_id=1, source_target_pairs={{0,16},{2,18},{4,20},{6,22},{8,24},{10,26},{12,28},{14,30},{16,0},... | collective-permute-start | bytes 196616 | tf_op jit(solution)/shard_map/ppermute | solution.py:38
  64.2 4.9 %collective-permute-start.18 = (bf16[8,4096]{1,0:T(8,128)(2,1)S(1)}, bf16[8,4096]{1,0:T(8,128)(2,1)S(1)}, u32[]{:S(2)}, u32[]{:S(2)}) collective-permute-start(bf16[8,4096]{1,0:T(8,128)(2,1)S(1)} %get-tuple-element.106), channel_id=1, source_target_pairs={{0,8},{2,10},{4,12},{6,14},{8,0},{10,2},{12,4},{14,6},{16,24},{18,... | collective-permute-start | bytes 196616 | tf_op jit(solution)/shard_map/ppermute | solution.py:38
  64.2 6.2 %collective-permute-start.19 = (bf16[8,4096]{1,0:T(8,128)(2,1)S(1)}, bf16[8,4096]{1,0:T(8,128)(2,1)S(1)}, u32[]{:S(2)}, u32[]{:S(2)}) collective-permute-start(bf16[8,4096]{1,0:T(8,128)(2,1)S(1)} %get-tuple-element.107), channel_id=1, source_target_pairs={{0,24},{2,26},{4,28},{6,30},{8,16},{10,18},{12,20},{14,22},{16,8},... | collective-permute-start | bytes 196616 | tf_op jit(solution)/shard_map/ppermute | solution.py:38

commit v16 on v15

--- a/solution.py
+++ b/solution.py
@@ -70,10 +70,20 @@
 
     slots.copy.wait()
 
-    @pl.loop(0, slots.live)
-    def _(s):
+    def start(s):
         high, low = slots.place(s, inner)
         pltpu.make_async_copy(source.at[0, 0, s], target.at[high, low], sem).start()
+
+    eights, rest = split_index(slots.live, 8)
+
+    @pl.loop(0, eights)
+    def _(eight):
+        for s in range(8):
+            start(eight * 8 + s)
+
+    @pl.loop(0, rest)
+    def _(s):
+        start(eights * 8 + s)
 
     many, few = split_index(slots.live, chunk)
 
@@ -461,7 +471,7 @@
             x, weights, index = lax.optimization_barrier((x, weights, index))
         x_recv = swap(x, "wide", wide, 2 * flip)
         if hop < 2:
-            early = (down_count,) if hop == 0 else ()
+            early = (down_count,) if hop == 1 else ()
             weights.append(fill(index, gu_count, vals[hop], d_blocks, f_blocks, early))
     y, index, _ = lax.optimization_barrier((cotangent, down_index, x))
     down_w = fill(index, down_count, down_vals, f_blocks, d_blocks)

time: 72 us -> 72.6 us (level); the launches traced: 71 us -> 73 us
  waiting for transfers between devices: 9.21 us -> 10.9 us
    ppermute x20, waiting for transfers between devices: 9.21 us -> 10.9 us  [swap(): return lax.ppermute(array, axis, [(i, i ^ flip) for i in range(size)])]
  transfers between devices with their start and end apart: 20 -> 20, of which waited for: 9 -> 11; matrix products, arithmetic and copies ran while one was open for 0% -> 0% of each run, Pallas kernels for 40% -> 39%
where the time goes in v16:
time: 72.6 us; the launch traced here: 73 us
  Pallas kernels  31 us (43%)
  starting transfers between devices  28.1 us (39%)
  waiting for transfers between devices  10.9 us (15%)
  between operations  2.19 us (3%)
  other arithmetic  0.89 us (1%)
    ppermute x20, starting transfers between devices, swap(): return lax.ppermute(array, axis, [(i, i ^ flip) for i in range(size)])  28.1 us
    ppermute x20, waiting for transfers between devices, swap(): return lax.ppermute(array, axis, [(i, i ^ flip) for i in range(size)])  10.9 us
    pallas_call x2, Pallas kernels, gu_grads(): pl.pallas_call(functools.partial(gu_grad_body, first, len(before)), out_s...  7.95 us
    pallas_call x3, Pallas kernels, fill(): pl.pallas_call(fill_body, out_shape=pltpu.VMEM((outer, inner, block, bloc...  6.99 us
    pallas_call x1, Pallas kernels, down_second(): pl.pallas_call(functools.partial(down_second_body, first), out_shape=(jax...  4.48 us
    pallas_call x1, Pallas kernels, d_hidden(): pl.pallas_call(functools.partial(d_hidden_body, group, len(y_pieces)), ou...  2.56 us
    pallas_call x1, Pallas kernels, d_tokens_parts(): pl.pallas_call(functools.partial(d_tokens_first_body, group), out_shape=(...  2.54 us
    pallas_call x2, Pallas kernels, gate_up(): pl.pallas_call(functools.partial(gate_up_body, half * f_blocks // 2), out...  2.51 us
  transfers between devices with their start and end apart: 20, of which 11 were waited for; matrix products, arithmetic and copies ran while one was open for 0% of the time, Pallas kernels for 39%

profile of v16, /device:TPU:0, one launch (start us, length us, event | category | flops | bytes accessed | tf_op | source)
XLA Modules:
  0.0 73.0 jit_solution(15721220485493049746)
XLA Ops:
  0.6 4.1 %collective-permute-start = (bf16[8,4096]{1,0:T(8,128)(2,1)}, bf16[8,4096]{1,0:T(8,128)(2,1)S(1)}, u32[]{:S(2)}, u32[]{:S(2)}) collective-permute-start(bf16[8,4096]{1,0:T(8,128)(2,1)} %param.9), channel_id=1, source_target_pairs={{0,16},{2,18},{4,20},{6,22},{8,24},{10,26},{12,28},{14,30},{16,0},... | collective-permute-start | bytes 196616 | tf_op jit(solution)/shard_map/ppermute | solution.py:38
  5.4 2.1 %fill.3.refs_4_.gate_w = bf16[32,8,128,128]{3,2,1,0:T(8,128)(2,1)S(1)} custom-call(s32[1,1,192]{2,1,0:T(1,128)} %index.9, s32[1,1]{1,0:T(1,128)S(6)} %copy.19.count, bf16[1,1,192,128,128]{4,3,2,1,0:T(8,128)(2,1)} %source.3), custom_call_target="tpu_custom_call" | custom-call | bytes 6291456 | tf_op jit(solution)/shard_map/fill/pallas_call | solution.py:102
  7.5 1.1 %collective-permute-done = bf16[8,4096]{1,0:T(8,128)(2,1)S(1)} collective-permute-done((bf16[8,4096]{1,0:T(8,128)(2,1)}, bf16[8,4096]{1,0:T(8,128)(2,1)S(1)}, u32[]{:S(2)}, u32[]{:S(2)}) %collective-permute-start) | collective-permute-done | bytes 65568 | tf_op jit(solution)/shard_map/ppermute | solution.py:38
  8.6 1.1 %collective-permute-start.1 = (bf16[16,4096]{1,0:T(8,128)(2,1)S(1)}, bf16[16,4096]{1,0:T(8,128)(2,1)S(1)}, u32[]{:S(2)}, u32[]{:S(2)}) collective-permute-start(bf16[16,4096]{1,0:T(8,128)(2,1)S(1)} %pad_maximum_fusion.3), channel_id=1, source_target_pairs={{0,8},{2,10},{4,12},{6,14},{8,0},{10,2},{12,4},{14,6},{16,24},{18,... | collective-permute-start | bytes 393224 | tf_op jit(solution)/shard_map/ppermute | solution.py:38
  10.3 2.1 %fill.4.refs_5_.up_w = bf16[32,8,128,128]{3,2,1,0:T(8,128)(2,1)S(1)} custom-call(s32[1,1,192]{2,1,0:T(1,128)} %index.9, s32[1,1]{1,0:T(1,128)S(6)} %copy.19.count, bf16[1,1,192,128,128]{4,3,2,1,0:T(8,128)(2,1)} %source.4, s32[1,1]{1,0:T(1,128)S(6)} %copy.20.refs_0_.count), custom_call_target="tpu_custom_call" | custom-call | bytes 6291456 | tf_op jit(solution)/shard_map/fill/pallas_call | solution.py:102
  12.4 1.2 %collective-permute-done.1 = bf16[16,4096]{1,0:T(8,128)(2,1)S(1)} collective-permute-done((bf16[16,4096]{1,0:T(8,128)(2,1)S(1)}, bf16[16,4096]{1,0:T(8,128)(2,1)S(1)}, u32[]{:S(2)}, u32[]{:S(2)}) %collective-permute-start.1) | collective-permute-done | bytes 131104 | tf_op jit(solution)/shard_map/ppermute | solution.py:38
  13.7 2.6 %collective-permute-start.6 = (bf16[8,4096]{1,0:T(8,128)(2,1)S(1)}, bf16[8,4096]{1,0:T(8,128)(2,1)S(1)}, u32[]{:S(2)}, u32[]{:S(2)}) collective-permute-start(bf16[8,4096]{1,0:T(8,128)(2,1)S(1)} %copy-done), channel_id=1, source_target_pairs={{0,16},{2,18},{4,20},{6,22},{8,24},{10,26},{12,28},{14,30},{16,0},... | collective-permute-start | bytes 196616 | tf_op jit(solution)/shard_map/ppermute | solution.py:38
  16.2 1.3 %collective-permute-start.2 = (bf16[32,4096]{1,0:T(8,128)(2,1)S(1)}, bf16[32,4096]{1,0:T(8,128)(2,1)S(1)}, u32[]{:S(2)}, u32[]{:S(2)}) collective-permute-start(bf16[32,4096]{1,0:T(8,128)(2,1)S(1)} %pad_maximum_fusion.1.refs_0_.refs_4_), channel_id=1, source_target_pairs={{0,4},{2,6},{4,0},{6,2},{8,12},{10,14},{12,8},{14,10},{16,20},{18,... | collective-permute-start | bytes 786440 | tf_op jit(solution)/shard_map/ppermute | solution.py:38
  17.6 1.3 %collective-permute-done.6 = bf16[8,4096]{1,0:T(8,128)(2,1)S(1)} collective-permute-done((bf16[8,4096]{1,0:T(8,128)(2,1)S(1)}, bf16[8,4096]{1,0:T(8,128)(2,1)S(1)}, u32[]{:S(2)}, u32[]{:S(2)}) %collective-permute-start.6) | collective-permute-done | bytes 65568 | tf_op jit(solution)/shard_map/ppermute | solution.py:38
  18.9 1.5 %collective-permute-start.7 = (bf16[16,4096]{1,0:T(8,128)(2,1)S(1)}, bf16[16,4096]{1,0:T(8,128)(2,1)S(1)}, u32[]{:S(2)}, u32[]{:S(2)}) collective-permute-start(bf16[16,4096]{1,0:T(8,128)(2,1)S(1)} %pad_maximum_fusion.4), channel_id=1, source_target_pairs={{0,8},{2,10},{4,12},{6,14},{8,0},{10,2},{12,4},{14,6},{16,24},{18,... | collective-permute-start | bytes 393224 | tf_op jit(solution)/shard_map/ppermute | solution.py:38
  20.4 2.8 %fill.5.refs_8_ = bf16[8,32,128,128]{3,2,1,0:T(8,128)(2,1)S(1)} custom-call(s32[1,1,192]{2,1,0:T(1,128)} %index.7, s32[1,1]{1,0:T(1,128)S(6)} %copy.20.refs_0_.count, bf16[1,1,192,128,128]{4,3,2,1,0:T(8,128)(2,1)} %source.5), custom_call_target="tpu_custom_call" | custom-call | bytes 6291456 | tf_op jit(solution)/shard_map/fill/pallas_call | solution.py:102
  24.0 2.6 %collective-permute-start.8 = (bf16[32,4096]{1,0:T(8,128)(2,1)S(1)}, bf16[32,4096]{1,0:T(8,128)(2,1)S(1)}, u32[]{:S(2)}, u32[]{:S(2)}) collective-permute-start(bf16[32,4096]{1,0:T(8,128)(2,1)S(1)} %pad_maximum_fusion.2.refs_0_), channel_id=1, source_target_pairs={{0,4},{2,6},{4,0},{6,2},{8,12},{10,14},{12,8},{14,10},{16,20},{18,... | collective-permute-start | bytes 786440 | tf_op jit(solution)/shard_map/ppermute | solution.py:38
  26.6 1.3 %gate_up.2 = (f32[4,128,256]{2,1,0:T(8,128)S(1)}, bf16[4,128,256]{2,1,0:T(8,128)(2,1)S(1)}) custom-call(bf16[32,4096]{1,0:T(8,128)(2,1)S(1)} %pad_maximum_fusion.1.refs_0_.refs_4_, bf16[32,4096]{1,0:T(8,128)(2,1)S(1)} %collective-permute-done.2.refs_1_.refs_5_, bf16[32,4096]{1,0:T(8,128)(2,1)S(1)} %collective-permute-done.3.refs_2_.refs_6_, ...), custom_call_target="tpu_custom_call" | custom-call | flops 1073741824 | bytes 8388608 | tf_op jit(solution)/shard_map/gate_up/pallas_call | solution.py:139
  27.8 2.1 %collective-permute-start.5 = (bf16[4,128,256]{2,1,0:T(8,128)(2,1)S(1)}, bf16[4,128,256]{2,1,0:T(8,128)(2,1)S(1)}, u32[]{:S(2)}, u32[]{:S(2)}) collective-permute-start(bf16[4,128,256]{2,1,0:T(8,128)(2,1)S(1)} %get-tuple-element.68), channel_id=1, source_target_pairs={{0,1},{1,0},{2,3},{3,2},{4,5},{5,4},{6,7},{7,6},{8,9},{9,8},{10,11... | collective-permute-start | bytes 786440 | tf_op jit(solution)/shard_map/ppermute | solution.py:38
  29.9 1.2 %gate_up.3 = (f32[4,128,256]{2,1,0:T(8,128)S(1)}, bf16[4,128,256]{2,1,0:T(8,128)(2,1)S(1)}) custom-call(bf16[32,4096]{1,0:T(8,128)(2,1)S(1)} %pad_maximum_fusion.1.refs_0_.refs_4_, bf16[32,4096]{1,0:T(8,128)(2,1)S(1)} %collective-permute-done.2.refs_1_.refs_5_, bf16[32,4096]{1,0:T(8,128)(2,1)S(1)} %collective-permute-done.3.refs_2_.refs_6_, ...), custom_call_target="tpu_custom_call" | custom-call | flops 1073741824 | bytes 8388608 | tf_op jit(solution)/shard_map/gate_up/pallas_call | solution.py:139
  31.2 1.3 %collective-permute-done.8.refs_1_ = bf16[32,4096]{1,0:T(8,128)(2,1)S(1)} collective-permute-done((bf16[32,4096]{1,0:T(8,128)(2,1)S(1)}, bf16[32,4096]{1,0:T(8,128)(2,1)S(1)}, u32[]{:S(2)}, u32[]{:S(2)}) %collective-permute-start.8) | collective-permute-done | bytes 262176 | tf_op jit(solution)/shard_map/ppermute | solution.py:38
  33.0 1.8 %collective-permute-start.11 = (bf16[4,128,256]{2,1,0:T(8,128)(2,1)S(1)}, bf16[4,128,256]{2,1,0:T(8,128)(2,1)S(1)}, u32[]{:S(2)}, u32[]{:S(2)}) collective-permute-start(bf16[4,128,256]{2,1,0:T(8,128)(2,1)S(1)} %get-tuple-element.77), channel_id=1, source_target_pairs={{0,1},{1,0},{2,3},{3,2},{4,5},{5,4},{6,7},{7,6},{8,9},{9,8},{10,11... | collective-permute-start | bytes 786440 | tf_op jit(solution)/shard_map/ppermute | solution.py:38
  35.1 2.6 %d_hidden.1 = (f32[8,128,128]{2,1,0:T(8,128)S(1)}, bf16[8,128,128]{2,1,0:T(8,128)(2,1)S(1)}, bf16[32,128,128]{2,1,0:T(8,128)(2,1)S(1)}) custom-call(bf16[32,4096]{1,0:T(8,128)(2,1)S(1)} %pad_maximum_fusion.2.refs_0_, bf16[32,4096]{1,0:T(8,128)(2,1)S(1)} %collective-permute-done.8.refs_1_, bf16[32,4096]{1,0:T(8,128)(2,1)S(1)} %collective-permute-done.9.refs_2_, ...), custom_call_target="tpu_custom_call" | custom-call | flops 1073741824 | bytes 8388608 | tf_op jit(solution)/shard_map/d_hidden/pallas_call | solution.py:181
  37.6 1.8 %collective-permute-start.12 = (bf16[8,128,128]{2,1,0:T(8,128)(2,1)S(1)}, bf16[8,128,128]{2,1,0:T(8,128)(2,1)S(1)}, u32[]{:S(2)}, u32[]{:S(2)}) collective-permute-start(bf16[8,128,128]{2,1,0:T(8,128)(2,1)S(1)} %get-tuple-element.93), channel_id=1, source_target_pairs={{0,1},{1,0},{2,3},{3,2},{4,5},{5,4},{6,7},{7,6},{8,9},{9,8},{10,11... | collective-permute-start | bytes 786440 | tf_op jit(solution)/shard_map/ppermute | solution.py:38
  39.4 1.3 %down_first.1._ = bf16[257,128,128]{2,1,0:T(8,128)(2,1)S(1)} custom-call(bf16[4,128,128]{2,1,0:T(8,128)(2,1)S(1)} %get-tuple-element.74.hidden, bf16[32,4096]{1,0:T(8,128)(2,1)S(1)} %pad_maximum_fusion.2.refs_0_, bf16[32,4096]{1,0:T(8,128)(2,1)S(1)} %collective-permute-done.8.refs_1_, bf16[32,4096]{1,0:T(8,128)(2,1)S(1)} %collective-permute-done.9.refs_2_, ...), custom_call_target="tpu_custom_call" | custom-call | flops 538968064 | bytes 8421376 | tf_op jit(solution)/shard_map/down_first/pallas_call | solution.py:412
  40.7 1.4 %collective-permute-done.11.refs_1_ = bf16[4,128,256]{2,1,0:T(8,128)(2,1)S(1)} collective-permute-done((bf16[4,128,256]{2,1,0:T(8,128)(2,1)S(1)}, bf16[4,128,256]{2,1,0:T(8,128)(2,1)S(1)}, u32[]{:S(2)}, u32[]{:S(2)}) %collective-permute-start.11) | collective-permute-done | bytes 262176 | tf_op jit(solution)/shard_map/ppermute | solution.py:38
  42.2 4.5 %down_second.1 = (bf16[192,128,128]{2,1,0:T(8,128)(2,1)}, bf16[257,128,128]{2,1,0:T(8,128)(2,1)S(1)}) custom-call(s32[1,1,192]{2,1,0:T(1,128)} %index.7, s32[1,1]{1,0:T(1,128)S(6)} %copy.20.refs_0_.count, bf16[4,128,128]{2,1,0:T(8,128)(2,1)S(1)} %get-tuple-element.87.hidden, ...), custom_call_target="tpu_custom_call", output_to_operand_aliasing={{1}: (3, {})} | custom-call | flops 402653184 | bytes 6291456 | tf_op jit(solution)/shard_map/down_second/pallas_call | solution.py:428
  46.8 2.5 %d_tokens_first.1 = (f32[64,2048]{1,0:T(8,128)S(1)}, bf16[64,2048]{1,0:T(8,128)(2,1)S(1)}, bf16[8,128,256]{2,1,0:T(8,128)(2,1)S(1)}, bf16[2048,128]{1,0:T(8,128)(2,1)S(1)}) custom-call(f32[4,128,256]{2,1,0:T(8,128)S(1)} %get-tuple-element.69.refs_0_, f32[4,128,256]{2,1,0:T(8,128)S(1)} %get-tuple-element.91.refs_1_, ...), custom_call_target="tpu_custom_call" | custom-call | flops 1073741824 | bytes 8388608 | tf_op jit(solution)/shard_map/d_tokens_first/pallas_call | solution.py:250
  49.5 2.4 %d_tokens_second.1 = (f32[64,2048]{1,0:T(8,128)S(1)}, bf16[64,2048]{1,0:T(8,128)(2,1)S(1)}) custom-call(bf16[2048,128]{1,0:T(8,128)(2,1)S(1)} %get-tuple-element.96.turned, bf16[32,8,128,128]{3,2,1,0:T(8,128)(2,1)S(1)} %fill.3.refs_4_.gate_w, bf16[32,8,128,128]{3,2,1,0:T(8,128)(2,1)S(1)} %fill.4.refs_5_.up_w), custom_call_target="tpu_custom_call" | custom-call | flops 1073741824 | bytes 8388608 | tf_op jit(solution)/shard_map/d_tokens_second/pallas_call | solution.py:262
  52.5 1.4 %collective-permute-start.14 = (bf16[32,2048]{1,0:T(8,128)(2,1)S(1)}, bf16[32,2048]{1,0:T(8,128)(2,1)S(1)}, u32[]{:S(2)}, u32[]{:S(2)}) collective-permute-start(bf16[32,2048]{1,0:T(8,128)(2,1)S(1)} %slice.65), channel_id=1, source_target_pairs={{0,4},{2,6},{4,0},{6,2},{8,12},{10,14},{12,8},{14,10},{16,20},{18,... | collective-permute-start | bytes 393224 | tf_op jit(solution)/shard_map/ppermute | solution.py:38
  54.0 1.1 %collective-permute-start.16 = (bf16[32,2048]{1,0:T(8,128)(2,1)S(1)}, bf16[32,2048]{1,0:T(8,128)(2,1)S(1)}, u32[]{:S(2)}, u32[]{:S(2)}) collective-permute-start(bf16[32,2048]{1,0:T(8,128)(2,1)S(1)} %slice.64), channel_id=1, source_target_pairs={{0,4},{2,6},{4,0},{6,2},{8,12},{10,14},{12,8},{14,10},{16,20},{18,... | collective-permute-start | bytes 393224 | tf_op jit(solution)/shard_map/ppermute | solution.py:38
  55.1 5.0 %gu_grads.2 = (bf16[192,128,128]{2,1,0:T(8,128)(2,1)}, bf16[192,128,128]{2,1,0:T(8,128)(2,1)}) custom-call(s32[1,1,192]{2,1,0:T(1,128)} %index.9, s32[1,1]{1,0:T(1,128)S(6)} %copy.19.count, bf16[8,128,256]{2,1,0:T(8,128)(2,1)S(1)} %get-tuple-element.108.d_pair, bf16[32,128,128]{2,1,0:T(8,128)(2,1)S(1)} %get-tuple-element.102.turned), custom_call_target="tpu_custom_call" | custom-call | flops 1073741824 | bytes 8388608 | tf_op jit(solution)/shard_map/gu_grads/pallas_call | solution.py:323
  60.1 0.7 collective-permute-done.16
  60.9 2.7 %collective-permute-start.17 = (bf16[8,4096]{1,0:T(8,128)(2,1)S(1)}, bf16[8,4096]{1,0:T(8,128)(2,1)S(1)}, u32[]{:S(2)}, u32[]{:S(2)}) collective-permute-start(bf16[8,4096]{1,0:T(8,128)(2,1)S(1)} %get-tuple-element.105), channel_id=1, source_target_pairs={{0,16},{2,18},{4,20},{6,22},{8,24},{10,26},{12,28},{14,30},{16,0},... | collective-permute-start | bytes 196616 | tf_op jit(solution)/shard_map/ppermute | solution.py:38
  63.7 2.7 %collective-permute-start.18 = (bf16[8,4096]{1,0:T(8,128)(2,1)S(1)}, bf16[8,4096]{1,0:T(8,128)(2,1)S(1)}, u32[]{:S(2)}, u32[]{:S(2)}) collective-permute-start(bf16[8,4096]{1,0:T(8,128)(2,1)S(1)} %get-tuple-element.106), channel_id=1, source_target_pairs={{0,8},{2,10},{4,12},{6,14},{8,0},{10,2},{12,4},{14,6},{16,24},{18,... | collective-permute-start | bytes 196616 | tf_op jit(solution)/shard_map/ppermute | solution.py:38
  66.3 3.0 %gu_grads.3 = (bf16[192,128,128]{2,1,0:T(8,128)(2,1)}, bf16[192,128,128]{2,1,0:T(8,128)(2,1)}) custom-call(s32[1,1,192]{2,1,0:T(1,128)} %index.9, s32[1,1]{1,0:T(1,128)S(6)} %copy.19.count, bf16[8,128,256]{2,1,0:T(8,128)(2,1)S(1)} %get-tuple-element.108.d_pair, ...), custom_call_target="tpu_custom_call", output_to_operand_aliasing={{0}: (4, {}), {1}: (5, {})} | custom-call | flops 536870912 | bytes 4194304 | tf_op jit(solution)/shard_map/gu_grads/pallas_call | solution.py:323
  69.3 3.0 %collective-permute-done.19 = bf16[8,4096]{1,0:T(8,128)(2,1)S(1)} collective-permute-done((bf16[8,4096]{1,0:T(8,128)(2,1)S(1)}, bf16[8,4096]{1,0:T(8,128)(2,1)S(1)}, u32[]{:S(2)}, u32[]{:S(2)}) %collective-permute-start.19) | collective-permute-done | bytes 65568 | tf_op jit(solution)/shard_map/ppermute | solution.py:38
  (39 shorter events, 3.4 us)
Async XLA Ops:
  0.6 8.0 %collective-permute-start = (bf16[8,4096]{1,0:T(8,128)(2,1)}, bf16[8,4096]{1,0:T(8,128)(2,1)S(1)}, u32[]{:S(2)}, u32[]{:S(2)}) collective-permute-start(bf16[8,4096]{1,0:T(8,128)(2,1)} %param.9), channel_id=1, source_target_pairs={{0,16},{2,18},{4,20},{6,22},{8,24},{10,26},{12,28},{14,30},{16,0},... | collective-permute-start | bytes 196616 | tf_op jit(solution)/shard_map/ppermute | solution.py:38
  5.4 3.2 %copy-start.1 = (bf16[8,4096]{1,0:T(8,128)(2,1)S(1)}, bf16[8,4096]{1,0:T(8,128)(2,1)}, u32[]{:S(2)}) copy-start(bf16[8,4096]{1,0:T(8,128)(2,1)} %param.9) | copy-start | bytes 196612
  8.6 5.0 %collective-permute-start.1 = (bf16[16,4096]{1,0:T(8,128)(2,1)S(1)}, bf16[16,4096]{1,0:T(8,128)(2,1)S(1)}, u32[]{:S(2)}, u32[]{:S(2)}) collective-permute-start(bf16[16,4096]{1,0:T(8,128)(2,1)S(1)} %pad_maximum_fusion.3), channel_id=1, source_target_pairs={{0,8},{2,10},{4,12},{6,14},{8,0},{10,2},{12,4},{14,6},{16,24},{18,... | collective-permute-start | bytes 393224 | tf_op jit(solution)/shard_map/ppermute | solution.py:38
  10.3 3.3 %copy-start = (bf16[8,4096]{1,0:T(8,128)(2,1)S(1)}, bf16[8,4096]{1,0:T(8,128)(2,1)}, u32[]{:S(2)}) copy-start(bf16[8,4096]{1,0:T(8,128)(2,1)} %param.10) | copy-start | bytes 196612
  13.7 5.2 %collective-permute-start.6 = (bf16[8,4096]{1,0:T(8,128)(2,1)S(1)}, bf16[8,4096]{1,0:T(8,128)(2,1)S(1)}, u32[]{:S(2)}, u32[]{:S(2)}) collective-permute-start(bf16[8,4096]{1,0:T(8,128)(2,1)S(1)} %copy-done), channel_id=1, source_target_pairs={{0,16},{2,18},{4,20},{6,22},{8,24},{10,26},{12,28},{14,30},{16,0},... | collective-permute-start | bytes 196616 | tf_op jit(solution)/shard_map/ppermute | solution.py:38
  16.2 7.4 %collective-permute-start.2 = (bf16[32,4096]{1,0:T(8,128)(2,1)S(1)}, bf16[32,4096]{1,0:T(8,128)(2,1)S(1)}, u32[]{:S(2)}, u32[]{:S(2)}) collective-permute-start(bf16[32,4096]{1,0:T(8,128)(2,1)S(1)} %pad_maximum_fusion.1.refs_0_.refs_4_), channel_id=1, source_target_pairs={{0,4},{2,6},{4,0},{6,2},{8,12},{10,14},{12,8},{14,10},{16,20},{18,... | collective-permute-start | bytes 786440 | tf_op jit(solution)/shard_map/ppermute | solution.py:38
  18.9 5.0 %collective-permute-start.7 = (bf16[16,4096]{1,0:T(8,128)(2,1)S(1)}, bf16[16,4096]{1,0:T(8,128)(2,1)S(1)}, u32[]{:S(2)}, u32[]{:S(2)}) collective-permute-start(bf16[16,4096]{1,0:T(8,128)(2,1)S(1)} %pad_maximum_fusion.4), channel_id=1, source_target_pairs={{0,8},{2,10},{4,12},{6,14},{8,0},{10,2},{12,4},{14,6},{16,24},{18,... | collective-permute-start | bytes 393224 | tf_op jit(solution)/shard_map/ppermute | solution.py:38
  23.2 3.4 %collective-permute-start.3 = (bf16[32,4096]{1,0:T(8,128)(2,1)S(1)}, bf16[32,4096]{1,0:T(8,128)(2,1)S(1)}, u32[]{:S(2)}, u32[]{:S(2)}) collective-permute-start(bf16[32,4096]{1,0:T(8,128)(2,1)S(1)} %pad_maximum_fusion.1.refs_0_.refs_4_), channel_id=1, source_target_pairs={{0,2},{2,0},{4,6},{6,4},{8,10},{10,8},{12,14},{14,12},{16,18},{18,... | collective-permute-start | bytes 786440 | tf_op jit(solution)/shard_map/ppermute | solution.py:38
  23.6 2.9 %collective-permute-start.4 = (bf16[32,4096]{1,0:T(8,128)(2,1)S(1)}, bf16[32,4096]{1,0:T(8,128)(2,1)S(1)}, u32[]{:S(2)}, u32[]{:S(2)}) collective-permute-start(bf16[32,4096]{1,0:T(8,128)(2,1)S(1)} %collective-permute-done.2.refs_1_.refs_5_), channel_id=1, source_target_pairs={{0,2},{2,0},{4,6},{6,4},{8,10},{10,8},{12,14},{14,12},{16,18},{18,... | collective-permute-start | bytes 786440 | tf_op jit(solution)/shard_map/ppermute | solution.py:38
  24.0 8.5 %collective-permute-start.8 = (bf16[32,4096]{1,0:T(8,128)(2,1)S(1)}, bf16[32,4096]{1,0:T(8,128)(2,1)S(1)}, u32[]{:S(2)}, u32[]{:S(2)}) collective-permute-start(bf16[32,4096]{1,0:T(8,128)(2,1)S(1)} %pad_maximum_fusion.2.refs_0_), channel_id=1, source_target_pairs={{0,4},{2,6},{4,0},{6,2},{8,12},{10,14},{12,8},{14,10},{16,20},{18,... | collective-permute-start | bytes 786440 | tf_op jit(solution)/shard_map/ppermute | solution.py:38
  27.8 7.1 %collective-permute-start.5 = (bf16[4,128,256]{2,1,0:T(8,128)(2,1)S(1)}, bf16[4,128,256]{2,1,0:T(8,128)(2,1)S(1)}, u32[]{:S(2)}, u32[]{:S(2)}) collective-permute-start(bf16[4,128,256]{2,1,0:T(8,128)(2,1)S(1)} %get-tuple-element.68), channel_id=1, source_target_pairs={{0,1},{1,0},{2,3},{3,2},{4,5},{5,4},{6,7},{7,6},{8,9},{9,8},{10,11... | collective-permute-start | bytes 786440 | tf_op jit(solution)/shard_map/ppermute | solution.py:38
  32.4 2.6 %collective-permute-start.9 = (bf16[32,4096]{1,0:T(8,128)(2,1)S(1)}, bf16[32,4096]{1,0:T(8,128)(2,1)S(1)}, u32[]{:S(2)}, u32[]{:S(2)}) collective-permute-start(bf16[32,4096]{1,0:T(8,128)(2,1)S(1)} %pad_maximum_fusion.2.refs_0_), channel_id=1, source_target_pairs={{0,2},{2,0},{4,6},{6,4},{8,10},{10,8},{12,14},{14,12},{16,18},{18,... | collective-permute-start | bytes 786440 | tf_op jit(solution)/shard_map/ppermute | solution.py:38
  32.4 2.6 %collective-permute-start.10 = (bf16[32,4096]{1,0:T(8,128)(2,1)S(1)}, bf16[32,4096]{1,0:T(8,128)(2,1)S(1)}, u32[]{:S(2)}, u32[]{:S(2)}) collective-permute-start(bf16[32,4096]{1,0:T(8,128)(2,1)S(1)} %collective-permute-done.8.refs_1_), channel_id=1, source_target_pairs={{0,2},{2,0},{4,6},{6,4},{8,10},{10,8},{12,14},{14,12},{16,18},{18,... | collective-permute-start | bytes 786440 | tf_op jit(solution)/shard_map/ppermute | solution.py:38
  33.0 9.2 %collective-permute-start.11 = (bf16[4,128,256]{2,1,0:T(8,128)(2,1)S(1)}, bf16[4,128,256]{2,1,0:T(8,128)(2,1)S(1)}, u32[]{:S(2)}, u32[]{:S(2)}) collective-permute-start(bf16[4,128,256]{2,1,0:T(8,128)(2,1)S(1)} %get-tuple-element.77), channel_id=1, source_target_pairs={{0,1},{1,0},{2,3},{3,2},{4,5},{5,4},{6,7},{7,6},{8,9},{9,8},{10,11... | collective-permute-start | bytes 786440 | tf_op jit(solution)/shard_map/ppermute | solution.py:38
  37.6 9.2 %collective-permute-start.12 = (bf16[8,128,128]{2,1,0:T(8,128)(2,1)S(1)}, bf16[8,128,128]{2,1,0:T(8,128)(2,1)S(1)}, u32[]{:S(2)}, u32[]{:S(2)}) collective-permute-start(bf16[8,128,128]{2,1,0:T(8,128)(2,1)S(1)} %get-tuple-element.93), channel_id=1, source_target_pairs={{0,1},{1,0},{2,3},{3,2},{4,5},{5,4},{6,7},{7,6},{8,9},{9,8},{10,11... | collective-permute-start | bytes 786440 | tf_op jit(solution)/shard_map/ppermute | solution.py:38
  49.4 3.1 %collective-permute-start.13 = (bf16[64,2048]{1,0:T(8,128)(2,1)S(1)}, bf16[64,2048]{1,0:T(8,128)(2,1)S(1)}, u32[]{:S(2)}, u32[]{:S(2)}) collective-permute-start(bf16[64,2048]{1,0:T(8,128)(2,1)S(1)} %get-tuple-element.95), channel_id=1, source_target_pairs={{0,2},{2,0},{4,6},{6,4},{8,10},{10,8},{12,14},{14,12},{16,18},{18,... | collective-permute-start | bytes 786440 | tf_op jit(solution)/shard_map/ppermute | solution.py:38
  51.9 2.1 %collective-permute-start.15 = (bf16[64,2048]{1,0:T(8,128)(2,1)S(1)}, bf16[64,2048]{1,0:T(8,128)(2,1)S(1)}, u32[]{:S(2)}, u32[]{:S(2)}) collective-permute-start(bf16[64,2048]{1,0:T(8,128)(2,1)S(1)} %get-tuple-element.98), channel_id=1, source_target_pairs={{0,2},{2,0},{4,6},{6,4},{8,10},{10,8},{12,14},{14,12},{16,18},{18,... | collective-permute-start | bytes 786440 | tf_op jit(solution)/shard_map/ppermute | solution.py:38
  52.5 7.6 %collective-permute-start.14 = (bf16[32,2048]{1,0:T(8,128)(2,1)S(1)}, bf16[32,2048]{1,0:T(8,128)(2,1)S(1)}, u32[]{:S(2)}, u32[]{:S(2)}) collective-permute-start(bf16[32,2048]{1,0:T(8,128)(2,1)S(1)} %slice.65), channel_id=1, source_target_pairs={{0,4},{2,6},{4,0},{6,2},{8,12},{10,14},{12,8},{14,10},{16,20},{18,... | collective-permute-start | bytes 393224 | tf_op jit(solution)/shard_map/ppermute | solution.py:38
  54.0 6.8 %collective-permute-start.16 = (bf16[32,2048]{1,0:T(8,128)(2,1)S(1)}, bf16[32,2048]{1,0:T(8,128)(2,1)S(1)}, u32[]{:S(2)}, u32[]{:S(2)}) collective-permute-start(bf16[32,2048]{1,0:T(8,128)(2,1)S(1)} %slice.64), channel_id=1, source_target_pairs={{0,4},{2,6},{4,0},{6,2},{8,12},{10,14},{12,8},{14,10},{16,20},{18,... | collective-permute-start | bytes 393224 | tf_op jit(solution)/shard_map/ppermute | solution.py:38
  60.9 8.4 %collective-permute-start.17 = (bf16[8,4096]{1,0:T(8,128)(2,1)S(1)}, bf16[8,4096]{1,0:T(8,128)(2,1)S(1)}, u32[]{:S(2)}, u32[]{:S(2)}) collective-permute-start(bf16[8,4096]{1,0:T(8,128)(2,1)S(1)} %get-tuple-element.105), channel_id=1, source_target_pairs={{0,16},{2,18},{4,20},{6,22},{8,24},{10,26},{12,28},{14,30},{16,0},... | collective-permute-start | bytes 196616 | tf_op jit(solution)/shard_map/ppermute | solution.py:38
  63.7 5.7 %collective-permute-start.18 = (bf16[8,4096]{1,0:T(8,128)(2,1)S(1)}, bf16[8,4096]{1,0:T(8,128)(2,1)S(1)}, u32[]{:S(2)}, u32[]{:S(2)}) collective-permute-start(bf16[8,4096]{1,0:T(8,128)(2,1)S(1)} %get-tuple-element.106), channel_id=1, source_target_pairs={{0,8},{2,10},{4,12},{6,14},{8,0},{10,2},{12,4},{14,6},{16,24},{18,... | collective-permute-start | bytes 196616 | tf_op jit(solution)/shard_map/ppermute | solution.py:38
  66.3 6.1 %collective-permute-start.19 = (bf16[8,4096]{1,0:T(8,128)(2,1)S(1)}, bf16[8,4096]{1,0:T(8,128)(2,1)S(1)}, u32[]{:S(2)}, u32[]{:S(2)}) collective-permute-start(bf16[8,4096]{1,0:T(8,128)(2,1)S(1)} %get-tuple-element.107), channel_id=1, source_target_pairs={{0,24},{2,26},{4,28},{6,30},{8,16},{10,18},{12,20},{14,22},{16,8},... | collective-permute-start | bytes 196616 | tf_op jit(solution)/shard_map/ppermute | solution.py:38

commit v17 on v15

--- a/solution.py
+++ b/solution.py
@@ -469,12 +469,11 @@
         y = jnp.concatenate([y, swap(y, "wide", wide, 2 * flip)], axis=0)
     x, down_w = lax.optimization_barrier((x, down_w))
     x_pieces = [x, x_recv, swap(x, "wide", wide, 1), swap(x_recv, "wide", wide, 1)]
-    y, _ = lax.optimization_barrier((y, x_recv))
-    y_recv = swap(y, "wide", wide, 2 * flips[-1])
 
     near_own, near_send = gate_up(x_pieces, *weights, 0)
     near_recv = exchange(near_send)
-    late, _ = lax.optimization_barrier((x, near_send))
+    late, y, _ = lax.optimization_barrier((x, y, near_send))
+    y_recv = swap(y, "wide", wide, 2 * flips[-1])
     far_own, far_send = gate_up([late, *x_pieces[1:]], *weights, 1)
     far_recv = exchange(far_send)
     y, y_recv, _ = lax.optimization_barrier((y, y_recv, far_send))

time: 72 us -> 74.4 us (1.033)
  starting transfers between devices: 27.4 us -> 22.7 us
  waiting for transfers between devices: 9.21 us -> 13.5 us
  Pallas kernels: 31.3 us -> 34.4 us
    ppermute x20, starting transfers between devices: 27.4 us -> 22.7 us  [swap(): return lax.ppermute(array, axis, [(i, i ^ flip) for i in range(size)])]
    ppermute x20, waiting for transfers between devices: 9.21 us -> 13.5 us  [swap(): return lax.ppermute(array, axis, [(i, i ^ flip) for i in range(size)])]
    pallas_call x3, Pallas kernels: 7.27 us -> 9.91 us  [fill(): pl.pallas_call(fill_body, out_shape=pltpu.VMEM((outer, inner, block, bloc...]
  transfers between devices with their start and end apart: 20 -> 20, of which waited for: 9 -> 9; matrix products, arithmetic and copies ran while one was open for 0% -> 0% of each run, Pallas kernels for 40% -> 41%
where the time goes in v17:
time: 74.4 us; the launch traced here: 73.8 us
  Pallas kernels  34.4 us (46%)
  starting transfers between devices  22.7 us (31%)
  waiting for transfers between devices  13.5 us (18%)
  between operations  2.21 us (3%)
  other arithmetic  0.89 us (1%)
    ppermute x20, starting transfers between devices, swap(): return lax.ppermute(array, axis, [(i, i ^ flip) for i in range(size)])  22.7 us
    ppermute x20, waiting for transfers between devices, swap(): return lax.ppermute(array, axis, [(i, i ^ flip) for i in range(size)])  13.5 us
    pallas_call x3, Pallas kernels, fill(): pl.pallas_call(fill_body, out_shape=pltpu.VMEM((outer, inner, block, bloc...  9.91 us
    pallas_call x2, Pallas kernels, gu_grads(): pl.pallas_call(functools.partial(gu_grad_body, first, len(before)), out_s...  8.45 us
    pallas_call x1, Pallas kernels, down_second(): pl.pallas_call(functools.partial(down_second_body, first), out_shape=(jax...  4.48 us
    pallas_call x1, Pallas kernels, d_hidden(): pl.pallas_call(functools.partial(d_hidden_body, group, len(y_pieces)), ou...  2.56 us
    pallas_call x1, Pallas kernels, d_tokens_parts(): pl.pallas_call(functools.partial(d_tokens_first_body, group), out_shape=(...  2.54 us
    pallas_call x2, Pallas kernels, gate_up(): pl.pallas_call(functools.partial(gate_up_body, half * f_blocks // 2), out...  2.5 us
  transfers between devices with their start and end apart: 20, of which 9 were waited for; matrix products, arithmetic and copies ran while one was open for 0% of the time, Pallas kernels for 41%

profile of v17, /device:TPU:0, one launch (start us, length us, event | category | flops | bytes accessed | tf_op | source)
XLA Modules:
  0.0 73.8 jit_solution(17557885919557922244)
XLA Ops:
  0.6 4.1 %collective-permute-start = (bf16[8,4096]{1,0:T(8,128)(2,1)}, bf16[8,4096]{1,0:T(8,128)(2,1)S(1)}, u32[]{:S(2)}, u32[]{:S(2)}) collective-permute-start(bf16[8,4096]{1,0:T(8,128)(2,1)} %param.9), channel_id=1, source_target_pairs={{0,16},{2,18},{4,20},{6,22},{8,24},{10,26},{12,28},{14,30},{16,0},... | collective-permute-start | bytes 196616 | tf_op jit(solution)/shard_map/ppermute | solution.py:38
  6.0 3.3 %fill.3.refs_4_.gate_w = bf16[32,8,128,128]{3,2,1,0:T(8,128)(2,1)S(1)} custom-call(s32[1,1,192]{2,1,0:T(1,128)} %index.9, s32[1,1]{1,0:T(1,128)S(6)} %copy.19.count, bf16[1,1,192,128,128]{4,3,2,1,0:T(8,128)(2,1)} %source.3, s32[1,1]{1,0:T(1,128)S(6)} %copy.20.refs_0_.count), custom_call_target="tpu_custom_call" | custom-call | bytes 6291456 | tf_op jit(solution)/shard_map/fill/pallas_call | solution.py:92
  9.4 1.7 %collective-permute-start.1 = (bf16[16,4096]{1,0:T(8,128)(2,1)S(1)}, bf16[16,4096]{1,0:T(8,128)(2,1)S(1)}, u32[]{:S(2)}, u32[]{:S(2)}) collective-permute-start(bf16[16,4096]{1,0:T(8,128)(2,1)S(1)} %pad_maximum_fusion.3), channel_id=1, source_target_pairs={{0,8},{2,10},{4,12},{6,14},{8,0},{10,2},{12,4},{14,6},{16,24},{18,... | collective-permute-start | bytes 393224 | tf_op jit(solution)/shard_map/ppermute | solution.py:38
  11.1 3.3 %fill.4.refs_5_.up_w = bf16[32,8,128,128]{3,2,1,0:T(8,128)(2,1)S(1)} custom-call(s32[1,1,192]{2,1,0:T(1,128)} %index.9, s32[1,1]{1,0:T(1,128)S(6)} %copy.19.count, bf16[1,1,192,128,128]{4,3,2,1,0:T(8,128)(2,1)} %source.4), custom_call_target="tpu_custom_call" | custom-call | bytes 6291456 | tf_op jit(solution)/shard_map/fill/pallas_call | solution.py:92
  14.5 1.5 %collective-permute-start.6 = (bf16[8,4096]{1,0:T(8,128)(2,1)S(1)}, bf16[8,4096]{1,0:T(8,128)(2,1)S(1)}, u32[]{:S(2)}, u32[]{:S(2)}) collective-permute-start(bf16[8,4096]{1,0:T(8,128)(2,1)S(1)} %copy-done), channel_id=1, source_target_pairs={{0,16},{2,18},{4,20},{6,22},{8,24},{10,26},{12,28},{14,30},{16,0},... | collective-permute-start | bytes 196616 | tf_op jit(solution)/shard_map/ppermute | solution.py:38
  16.1 1.5 %collective-permute-start.2 = (bf16[32,4096]{1,0:T(8,128)(2,1)S(1)}, bf16[32,4096]{1,0:T(8,128)(2,1)S(1)}, u32[]{:S(2)}, u32[]{:S(2)}) collective-permute-start(bf16[32,4096]{1,0:T(8,128)(2,1)S(1)} %pad_maximum_fusion.1.refs_0_.refs_4_), channel_id=1, source_target_pairs={{0,4},{2,6},{4,0},{6,2},{8,12},{10,14},{12,8},{14,10},{16,20},{18,... | collective-permute-start | bytes 786440 | tf_op jit(solution)/shard_map/ppermute | solution.py:38
  17.6 2.2 %collective-permute-done.6 = bf16[8,4096]{1,0:T(8,128)(2,1)S(1)} collective-permute-done((bf16[8,4096]{1,0:T(8,128)(2,1)S(1)}, bf16[8,4096]{1,0:T(8,128)(2,1)S(1)}, u32[]{:S(2)}, u32[]{:S(2)}) %collective-permute-start.6) | collective-permute-done | bytes 65568 | tf_op jit(solution)/shard_map/ppermute | solution.py:38
  19.8 1.6 %collective-permute-start.7 = (bf16[16,4096]{1,0:T(8,128)(2,1)S(1)}, bf16[16,4096]{1,0:T(8,128)(2,1)S(1)}, u32[]{:S(2)}, u32[]{:S(2)}) collective-permute-start(bf16[16,4096]{1,0:T(8,128)(2,1)S(1)} %pad_maximum_fusion.4), channel_id=1, source_target_pairs={{0,8},{2,10},{4,12},{6,14},{8,0},{10,2},{12,4},{14,6},{16,24},{18,... | collective-permute-start | bytes 393224 | tf_op jit(solution)/shard_map/ppermute | solution.py:38
  21.4 3.3 %fill.5.refs_8_ = bf16[8,32,128,128]{3,2,1,0:T(8,128)(2,1)S(1)} custom-call(s32[1,1,192]{2,1,0:T(1,128)} %index.7, s32[1,1]{1,0:T(1,128)S(6)} %copy.20.refs_0_.count, bf16[1,1,192,128,128]{4,3,2,1,0:T(8,128)(2,1)} %source.5), custom_call_target="tpu_custom_call" | custom-call | bytes 6291456 | tf_op jit(solution)/shard_map/fill/pallas_call | solution.py:92
  25.3 1.0 %collective-permute-done.3.refs_2_.refs_6_ = bf16[32,4096]{1,0:T(8,128)(2,1)S(1)} collective-permute-done((bf16[32,4096]{1,0:T(8,128)(2,1)S(1)}, bf16[32,4096]{1,0:T(8,128)(2,1)S(1)}, u32[]{:S(2)}, u32[]{:S(2)}) %collective-permute-start.3) | collective-permute-done | bytes 262176 | tf_op jit(solution)/shard_map/ppermute | solution.py:38
  26.7 1.3 %gate_up.2 = (f32[4,128,256]{2,1,0:T(8,128)S(1)}, bf16[4,128,256]{2,1,0:T(8,128)(2,1)S(1)}) custom-call(bf16[32,4096]{1,0:T(8,128)(2,1)S(1)} %pad_maximum_fusion.1.refs_0_.refs_4_, bf16[32,4096]{1,0:T(8,128)(2,1)S(1)} %collective-permute-done.2.refs_1_.refs_5_, bf16[32,4096]{1,0:T(8,128)(2,1)S(1)} %collective-permute-done.3.refs_2_.refs_6_, ...), custom_call_target="tpu_custom_call" | custom-call | flops 1073741824 | bytes 8388608 | tf_op jit(solution)/shard_map/gate_up/pallas_call | solution.py:129
  28.1 1.9 %collective-permute-start.5 = (bf16[4,128,256]{2,1,0:T(8,128)(2,1)S(1)}, bf16[4,128,256]{2,1,0:T(8,128)(2,1)S(1)}, u32[]{:S(2)}, u32[]{:S(2)}) collective-permute-start(bf16[4,128,256]{2,1,0:T(8,128)(2,1)S(1)} %get-tuple-element.68), channel_id=1, source_target_pairs={{0,1},{1,0},{2,3},{3,2},{4,5},{5,4},{6,7},{7,6},{8,9},{9,8},{10,11... | collective-permute-start | bytes 786440 | tf_op jit(solution)/shard_map/ppermute | solution.py:38
  30.0 1.3 %gate_up.3 = (f32[4,128,256]{2,1,0:T(8,128)S(1)}, bf16[4,128,256]{2,1,0:T(8,128)(2,1)S(1)}) custom-call(bf16[32,4096]{1,0:T(8,128)(2,1)S(1)} %pad_maximum_fusion.1.refs_0_.refs_4_, bf16[32,4096]{1,0:T(8,128)(2,1)S(1)} %collective-permute-done.2.refs_1_.refs_5_, bf16[32,4096]{1,0:T(8,128)(2,1)S(1)} %collective-permute-done.3.refs_2_.refs_6_, ...), custom_call_target="tpu_custom_call" | custom-call | flops 1073741824 | bytes 8388608 | tf_op jit(solution)/shard_map/gate_up/pallas_call | solution.py:129
  31.3 5.1 %collective-permute-done.8.refs_1_ = bf16[32,4096]{1,0:T(8,128)(2,1)S(1)} collective-permute-done((bf16[32,4096]{1,0:T(8,128)(2,1)S(1)}, bf16[32,4096]{1,0:T(8,128)(2,1)S(1)}, u32[]{:S(2)}, u32[]{:S(2)}) %collective-permute-start.8) | collective-permute-done | bytes 262176 | tf_op jit(solution)/shard_map/ppermute | solution.py:38
  36.8 1.3 %collective-permute-start.11 = (bf16[4,128,256]{2,1,0:T(8,128)(2,1)S(1)}, bf16[4,128,256]{2,1,0:T(8,128)(2,1)S(1)}, u32[]{:S(2)}, u32[]{:S(2)}) collective-permute-start(bf16[4,128,256]{2,1,0:T(8,128)(2,1)S(1)} %get-tuple-element.77), channel_id=1, source_target_pairs={{0,1},{1,0},{2,3},{3,2},{4,5},{5,4},{6,7},{7,6},{8,9},{9,8},{10,11... | collective-permute-start | bytes 786440 | tf_op jit(solution)/shard_map/ppermute | solution.py:38
  38.3 2.6 %d_hidden.1 = (f32[8,128,128]{2,1,0:T(8,128)S(1)}, bf16[8,128,128]{2,1,0:T(8,128)(2,1)S(1)}, bf16[32,128,128]{2,1,0:T(8,128)(2,1)S(1)}) custom-call(bf16[32,4096]{1,0:T(8,128)(2,1)S(1)} %pad_maximum_fusion.2.refs_0_, bf16[32,4096]{1,0:T(8,128)(2,1)S(1)} %collective-permute-done.8.refs_1_, bf16[32,4096]{1,0:T(8,128)(2,1)S(1)} %collective-permute-done.9.refs_2_, ...), custom_call_target="tpu_custom_call" | custom-call | flops 1073741824 | bytes 8388608 | tf_op jit(solution)/shard_map/d_hidden/pallas_call | solution.py:171
  40.9 1.3 %collective-permute-start.12 = (bf16[8,128,128]{2,1,0:T(8,128)(2,1)S(1)}, bf16[8,128,128]{2,1,0:T(8,128)(2,1)S(1)}, u32[]{:S(2)}, u32[]{:S(2)}) collective-permute-start(bf16[8,128,128]{2,1,0:T(8,128)(2,1)S(1)} %get-tuple-element.93), channel_id=1, source_target_pairs={{0,1},{1,0},{2,3},{3,2},{4,5},{5,4},{6,7},{7,6},{8,9},{9,8},{10,11... | collective-permute-start | bytes 786440 | tf_op jit(solution)/shard_map/ppermute | solution.py:38
  42.2 1.3 %down_first.1._ = bf16[257,128,128]{2,1,0:T(8,128)(2,1)S(1)} custom-call(bf16[4,128,128]{2,1,0:T(8,128)(2,1)S(1)} %get-tuple-element.75.hidden, bf16[32,4096]{1,0:T(8,128)(2,1)S(1)} %pad_maximum_fusion.2.refs_0_, bf16[32,4096]{1,0:T(8,128)(2,1)S(1)} %collective-permute-done.8.refs_1_, bf16[32,4096]{1,0:T(8,128)(2,1)S(1)} %collective-permute-done.9.refs_2_, ...), custom_call_target="tpu_custom_call" | custom-call | flops 538968064 | bytes 8421376 | tf_op jit(solution)/shard_map/down_first/pallas_call | solution.py:402
  43.5 2.5 %collective-permute-done.11.refs_1_ = bf16[4,128,256]{2,1,0:T(8,128)(2,1)S(1)} collective-permute-done((bf16[4,128,256]{2,1,0:T(8,128)(2,1)S(1)}, bf16[4,128,256]{2,1,0:T(8,128)(2,1)S(1)}, u32[]{:S(2)}, u32[]{:S(2)}) %collective-permute-start.11) | collective-permute-done | bytes 262176 | tf_op jit(solution)/shard_map/ppermute | solution.py:38
  46.2 4.5 %down_second.1 = (bf16[192,128,128]{2,1,0:T(8,128)(2,1)}, bf16[257,128,128]{2,1,0:T(8,128)(2,1)S(1)}) custom-call(s32[1,1,192]{2,1,0:T(1,128)} %index.7, s32[1,1]{1,0:T(1,128)S(6)} %copy.20.refs_0_.count, bf16[4,128,128]{2,1,0:T(8,128)(2,1)S(1)} %get-tuple-element.87.hidden, ...), custom_call_target="tpu_custom_call", output_to_operand_aliasing={{1}: (3, {})} | custom-call | flops 402653184 | bytes 6291456 | tf_op jit(solution)/shard_map/down_second/pallas_call | solution.py:418
  50.7 2.5 %d_tokens_first.1 = (f32[64,2048]{1,0:T(8,128)S(1)}, bf16[64,2048]{1,0:T(8,128)(2,1)S(1)}, bf16[8,128,256]{2,1,0:T(8,128)(2,1)S(1)}, bf16[2048,128]{1,0:T(8,128)(2,1)S(1)}) custom-call(f32[4,128,256]{2,1,0:T(8,128)S(1)} %get-tuple-element.69.refs_0_, f32[4,128,256]{2,1,0:T(8,128)S(1)} %get-tuple-element.91.refs_1_, ...), custom_call_target="tpu_custom_call" | custom-call | flops 1073741824 | bytes 8388608 | tf_op jit(solution)/shard_map/d_tokens_first/pallas_call | solution.py:240
  53.3 2.4 %d_tokens_second.1 = (f32[64,2048]{1,0:T(8,128)S(1)}, bf16[64,2048]{1,0:T(8,128)(2,1)S(1)}) custom-call(bf16[2048,128]{1,0:T(8,128)(2,1)S(1)} %get-tuple-element.96.turned, bf16[32,8,128,128]{3,2,1,0:T(8,128)(2,1)S(1)} %fill.3.refs_4_.gate_w, bf16[32,8,128,128]{3,2,1,0:T(8,128)(2,1)S(1)} %fill.4.refs_5_.up_w), custom_call_target="tpu_custom_call" | custom-call | flops 1073741824 | bytes 8388608 | tf_op jit(solution)/shard_map/d_tokens_second/pallas_call | solution.py:252
  55.7 0.6 collective-permute-start.15
  56.7 0.7 collective-permute-done.15
  57.5 1.1 %collective-permute-start.16 = (bf16[32,2048]{1,0:T(8,128)(2,1)S(1)}, bf16[32,2048]{1,0:T(8,128)(2,1)S(1)}, u32[]{:S(2)}, u32[]{:S(2)}) collective-permute-start(bf16[32,2048]{1,0:T(8,128)(2,1)S(1)} %slice.64), channel_id=1, source_target_pairs={{0,4},{2,6},{4,0},{6,2},{8,12},{10,14},{12,8},{14,10},{16,20},{18,... | collective-permute-start | bytes 393224 | tf_op jit(solution)/shard_map/ppermute | solution.py:38
  58.6 5.5 %gu_grads.2 = (bf16[192,128,128]{2,1,0:T(8,128)(2,1)}, bf16[192,128,128]{2,1,0:T(8,128)(2,1)}) custom-call(s32[1,1,192]{2,1,0:T(1,128)} %index.9, s32[1,1]{1,0:T(1,128)S(6)} %copy.19.count, bf16[8,128,256]{2,1,0:T(8,128)(2,1)S(1)} %get-tuple-element.108.d_pair, bf16[32,128,128]{2,1,0:T(8,128)(2,1)S(1)} %get-tuple-element.102.turned), custom_call_target="tpu_custom_call" | custom-call | flops 1073741824 | bytes 8388608 | tf_op jit(solution)/shard_map/gu_grads/pallas_call | solution.py:313
  64.1 0.6 collective-permute-done.16
  64.8 1.8 %collective-permute-start.17 = (bf16[8,4096]{1,0:T(8,128)(2,1)S(1)}, bf16[8,4096]{1,0:T(8,128)(2,1)S(1)}, u32[]{:S(2)}, u32[]{:S(2)}) collective-permute-start(bf16[8,4096]{1,0:T(8,128)(2,1)S(1)} %get-tuple-element.105), channel_id=1, source_target_pairs={{0,16},{2,18},{4,20},{6,22},{8,24},{10,26},{12,28},{14,30},{16,0},... | collective-permute-start | bytes 196616 | tf_op jit(solution)/shard_map/ppermute | solution.py:38
  66.9 2.3 %collective-permute-start.19 = (bf16[8,4096]{1,0:T(8,128)(2,1)S(1)}, bf16[8,4096]{1,0:T(8,128)(2,1)S(1)}, u32[]{:S(2)}, u32[]{:S(2)}) collective-permute-start(bf16[8,4096]{1,0:T(8,128)(2,1)S(1)} %get-tuple-element.107), channel_id=1, source_target_pairs={{0,24},{2,26},{4,28},{6,30},{8,16},{10,18},{12,20},{14,22},{16,8},... | collective-permute-start | bytes 196616 | tf_op jit(solution)/shard_map/ppermute | solution.py:38
  69.2 3.0 %gu_grads.3 = (bf16[192,128,128]{2,1,0:T(8,128)(2,1)}, bf16[192,128,128]{2,1,0:T(8,128)(2,1)}) custom-call(s32[1,1,192]{2,1,0:T(1,128)} %index.9, s32[1,1]{1,0:T(1,128)S(6)} %copy.19.count, bf16[8,128,256]{2,1,0:T(8,128)(2,1)S(1)} %get-tuple-element.108.d_pair, ...), custom_call_target="tpu_custom_call", output_to_operand_aliasing={{0}: (4, {}), {1}: (5, {})} | custom-call | flops 536870912 | bytes 4194304 | tf_op jit(solution)/shard_map/gu_grads/pallas_call | solution.py:313
  72.2 0.9 %collective-permute-done.19 = bf16[8,4096]{1,0:T(8,128)(2,1)S(1)} collective-permute-done((bf16[8,4096]{1,0:T(8,128)(2,1)S(1)}, bf16[8,4096]{1,0:T(8,128)(2,1)S(1)}, u32[]{:S(2)}, u32[]{:S(2)}) %collective-permute-start.19) | collective-permute-done | bytes 65568 | tf_op jit(solution)/shard_map/ppermute | solution.py:38
  73.1 0.7 fusion.5
  (39 shorter events, 3.1 us)
Async XLA Ops:
  0.6 8.7 %collective-permute-start = (bf16[8,4096]{1,0:T(8,128)(2,1)}, bf16[8,4096]{1,0:T(8,128)(2,1)S(1)}, u32[]{:S(2)}, u32[]{:S(2)}) collective-permute-start(bf16[8,4096]{1,0:T(8,128)(2,1)} %param.9), channel_id=1, source_target_pairs={{0,16},{2,18},{4,20},{6,22},{8,24},{10,26},{12,28},{14,30},{16,0},... | collective-permute-start | bytes 196616 | tf_op jit(solution)/shard_map/ppermute | solution.py:38
  6.0 3.3 %copy-start.1 = (bf16[8,4096]{1,0:T(8,128)(2,1)S(1)}, bf16[8,4096]{1,0:T(8,128)(2,1)}, u32[]{:S(2)}) copy-start(bf16[8,4096]{1,0:T(8,128)(2,1)} %param.9) | copy-start | bytes 196612
  9.4 5.1 %copy-start = (bf16[8,4096]{1,0:T(8,128)(2,1)S(1)}, bf16[8,4096]{1,0:T(8,128)(2,1)}, u32[]{:S(2)}) copy-start(bf16[8,4096]{1,0:T(8,128)(2,1)} %param.10) | copy-start | bytes 196612
  9.4 5.1 %collective-permute-start.1 = (bf16[16,4096]{1,0:T(8,128)(2,1)S(1)}, bf16[16,4096]{1,0:T(8,128)(2,1)S(1)}, u32[]{:S(2)}, u32[]{:S(2)}) collective-permute-start(bf16[16,4096]{1,0:T(8,128)(2,1)S(1)} %pad_maximum_fusion.3), channel_id=1, source_target_pairs={{0,8},{2,10},{4,12},{6,14},{8,0},{10,2},{12,4},{14,6},{16,24},{18,... | collective-permute-start | bytes 393224 | tf_op jit(solution)/shard_map/ppermute | solution.py:38
  14.5 5.2 %collective-permute-start.6 = (bf16[8,4096]{1,0:T(8,128)(2,1)S(1)}, bf16[8,4096]{1,0:T(8,128)(2,1)S(1)}, u32[]{:S(2)}, u32[]{:S(2)}) collective-permute-start(bf16[8,4096]{1,0:T(8,128)(2,1)S(1)} %copy-done), channel_id=1, source_target_pairs={{0,16},{2,18},{4,20},{6,22},{8,24},{10,26},{12,28},{14,30},{16,0},... | collective-permute-start | bytes 196616 | tf_op jit(solution)/shard_map/ppermute | solution.py:38
  16.1 8.7 %collective-permute-start.2 = (bf16[32,4096]{1,0:T(8,128)(2,1)S(1)}, bf16[32,4096]{1,0:T(8,128)(2,1)S(1)}, u32[]{:S(2)}, u32[]{:S(2)}) collective-permute-start(bf16[32,4096]{1,0:T(8,128)(2,1)S(1)} %pad_maximum_fusion.1.refs_0_.refs_4_), channel_id=1, source_target_pairs={{0,4},{2,6},{4,0},{6,2},{8,12},{10,14},{12,8},{14,10},{16,20},{18,... | collective-permute-start | bytes 786440 | tf_op jit(solution)/shard_map/ppermute | solution.py:38
  19.8 5.5 %collective-permute-start.7 = (bf16[16,4096]{1,0:T(8,128)(2,1)S(1)}, bf16[16,4096]{1,0:T(8,128)(2,1)S(1)}, u32[]{:S(2)}, u32[]{:S(2)}) collective-permute-start(bf16[16,4096]{1,0:T(8,128)(2,1)S(1)} %pad_maximum_fusion.4), channel_id=1, source_target_pairs={{0,8},{2,10},{4,12},{6,14},{8,0},{10,2},{12,4},{14,6},{16,24},{18,... | collective-permute-start | bytes 393224 | tf_op jit(solution)/shard_map/ppermute | solution.py:38
  24.7 1.6 %collective-permute-start.3 = (bf16[32,4096]{1,0:T(8,128)(2,1)S(1)}, bf16[32,4096]{1,0:T(8,128)(2,1)S(1)}, u32[]{:S(2)}, u32[]{:S(2)}) collective-permute-start(bf16[32,4096]{1,0:T(8,128)(2,1)S(1)} %pad_maximum_fusion.1.refs_0_.refs_4_), channel_id=1, source_target_pairs={{0,2},{2,0},{4,6},{6,4},{8,10},{10,8},{12,14},{14,12},{16,18},{18,... | collective-permute-start | bytes 786440 | tf_op jit(solution)/shard_map/ppermute | solution.py:38
  24.8 1.9 %collective-permute-start.4 = (bf16[32,4096]{1,0:T(8,128)(2,1)S(1)}, bf16[32,4096]{1,0:T(8,128)(2,1)S(1)}, u32[]{:S(2)}, u32[]{:S(2)}) collective-permute-start(bf16[32,4096]{1,0:T(8,128)(2,1)S(1)} %collective-permute-done.2.refs_1_.refs_5_), channel_id=1, source_target_pairs={{0,2},{2,0},{4,6},{6,4},{8,10},{10,8},{12,14},{14,12},{16,18},{18,... | collective-permute-start | bytes 786440 | tf_op jit(solution)/shard_map/ppermute | solution.py:38
  27.9 8.4 %collective-permute-start.8 = (bf16[32,4096]{1,0:T(8,128)(2,1)S(1)}, bf16[32,4096]{1,0:T(8,128)(2,1)S(1)}, u32[]{:S(2)}, u32[]{:S(2)}) collective-permute-start(bf16[32,4096]{1,0:T(8,128)(2,1)S(1)} %pad_maximum_fusion.2.refs_0_), channel_id=1, source_target_pairs={{0,4},{2,6},{4,0},{6,2},{8,12},{10,14},{12,8},{14,10},{16,20},{18,... | collective-permute-start | bytes 786440 | tf_op jit(solution)/shard_map/ppermute | solution.py:38
  28.1 10.1 %collective-permute-start.5 = (bf16[4,128,256]{2,1,0:T(8,128)(2,1)S(1)}, bf16[4,128,256]{2,1,0:T(8,128)(2,1)S(1)}, u32[]{:S(2)}, u32[]{:S(2)}) collective-permute-start(bf16[4,128,256]{2,1,0:T(8,128)(2,1)S(1)} %get-tuple-element.68), channel_id=1, source_target_pairs={{0,1},{1,0},{2,3},{3,2},{4,5},{5,4},{6,7},{7,6},{8,9},{9,8},{10,11... | collective-permute-start | bytes 786440 | tf_op jit(solution)/shard_map/ppermute | solution.py:38
  36.3 2.0 %collective-permute-start.9 = (bf16[32,4096]{1,0:T(8,128)(2,1)S(1)}, bf16[32,4096]{1,0:T(8,128)(2,1)S(1)}, u32[]{:S(2)}, u32[]{:S(2)}) collective-permute-start(bf16[32,4096]{1,0:T(8,128)(2,1)S(1)} %pad_maximum_fusion.2.refs_0_), channel_id=1, source_target_pairs={{0,2},{2,0},{4,6},{6,4},{8,10},{10,8},{12,14},{14,12},{16,18},{18,... | collective-permute-start | bytes 786440 | tf_op jit(solution)/shard_map/ppermute | solution.py:38
  36.3 2.0 %collective-permute-start.10 = (bf16[32,4096]{1,0:T(8,128)(2,1)S(1)}, bf16[32,4096]{1,0:T(8,128)(2,1)S(1)}, u32[]{:S(2)}, u32[]{:S(2)}) collective-permute-start(bf16[32,4096]{1,0:T(8,128)(2,1)S(1)} %collective-permute-done.8.refs_1_), channel_id=1, source_target_pairs={{0,2},{2,0},{4,6},{6,4},{8,10},{10,8},{12,14},{14,12},{16,18},{18,... | collective-permute-start | bytes 786440 | tf_op jit(solution)/shard_map/ppermute | solution.py:38
  36.8 9.2 %collective-permute-start.11 = (bf16[4,128,256]{2,1,0:T(8,128)(2,1)S(1)}, bf16[4,128,256]{2,1,0:T(8,128)(2,1)S(1)}, u32[]{:S(2)}, u32[]{:S(2)}) collective-permute-start(bf16[4,128,256]{2,1,0:T(8,128)(2,1)S(1)} %get-tuple-element.77), channel_id=1, source_target_pairs={{0,1},{1,0},{2,3},{3,2},{4,5},{5,4},{6,7},{7,6},{8,9},{9,8},{10,11... | collective-permute-start | bytes 786440 | tf_op jit(solution)/shard_map/ppermute | solution.py:38
  40.9 9.8 %collective-permute-start.12 = (bf16[8,128,128]{2,1,0:T(8,128)(2,1)S(1)}, bf16[8,128,128]{2,1,0:T(8,128)(2,1)S(1)}, u32[]{:S(2)}, u32[]{:S(2)}) collective-permute-start(bf16[8,128,128]{2,1,0:T(8,128)(2,1)S(1)} %get-tuple-element.93), channel_id=1, source_target_pairs={{0,1},{1,0},{2,3},{3,2},{4,5},{5,4},{6,7},{7,6},{8,9},{9,8},{10,11... | collective-permute-start | bytes 786440 | tf_op jit(solution)/shard_map/ppermute | solution.py:38
  53.2 3.1 %collective-permute-start.13 = (bf16[64,2048]{1,0:T(8,128)(2,1)S(1)}, bf16[64,2048]{1,0:T(8,128)(2,1)S(1)}, u32[]{:S(2)}, u32[]{:S(2)}) collective-permute-start(bf16[64,2048]{1,0:T(8,128)(2,1)S(1)} %get-tuple-element.95), channel_id=1, source_target_pairs={{0,2},{2,0},{4,6},{6,4},{8,10},{10,8},{12,14},{14,12},{16,18},{18,... | collective-permute-start | bytes 786440 | tf_op jit(solution)/shard_map/ppermute | solution.py:38
  55.7 1.7 %collective-permute-start.15 = (bf16[64,2048]{1,0:T(8,128)(2,1)S(1)}, bf16[64,2048]{1,0:T(8,128)(2,1)S(1)}, u32[]{:S(2)}, u32[]{:S(2)}) collective-permute-start(bf16[64,2048]{1,0:T(8,128)(2,1)S(1)} %get-tuple-element.98), channel_id=1, source_target_pairs={{0,2},{2,0},{4,6},{6,4},{8,10},{10,8},{12,14},{14,12},{16,18},{18,... | collective-permute-start | bytes 786440 | tf_op jit(solution)/shard_map/ppermute | solution.py:38
  56.4 7.7 %collective-permute-start.14 = (bf16[32,2048]{1,0:T(8,128)(2,1)S(1)}, bf16[32,2048]{1,0:T(8,128)(2,1)S(1)}, u32[]{:S(2)}, u32[]{:S(2)}) collective-permute-start(bf16[32,2048]{1,0:T(8,128)(2,1)S(1)} %slice.65), channel_id=1, source_target_pairs={{0,4},{2,6},{4,0},{6,2},{8,12},{10,14},{12,8},{14,10},{16,20},{18,... | collective-permute-start | bytes 393224 | tf_op jit(solution)/shard_map/ppermute | solution.py:38
  57.5 7.1 %collective-permute-start.16 = (bf16[32,2048]{1,0:T(8,128)(2,1)S(1)}, bf16[32,2048]{1,0:T(8,128)(2,1)S(1)}, u32[]{:S(2)}, u32[]{:S(2)}) collective-permute-start(bf16[32,2048]{1,0:T(8,128)(2,1)S(1)} %slice.64), channel_id=1, source_target_pairs={{0,4},{2,6},{4,0},{6,2},{8,12},{10,14},{12,8},{14,10},{16,20},{18,... | collective-permute-start | bytes 393224 | tf_op jit(solution)/shard_map/ppermute | solution.py:38
  64.8 7.5 %collective-permute-start.17 = (bf16[8,4096]{1,0:T(8,128)(2,1)S(1)}, bf16[8,4096]{1,0:T(8,128)(2,1)S(1)}, u32[]{:S(2)}, u32[]{:S(2)}) collective-permute-start(bf16[8,4096]{1,0:T(8,128)(2,1)S(1)} %get-tuple-element.105), channel_id=1, source_target_pairs={{0,16},{2,18},{4,20},{6,22},{8,24},{10,26},{12,28},{14,30},{16,0},... | collective-permute-start | bytes 196616 | tf_op jit(solution)/shard_map/ppermute | solution.py:38
  66.6 5.6 %collective-permute-start.18 = (bf16[8,4096]{1,0:T(8,128)(2,1)S(1)}, bf16[8,4096]{1,0:T(8,128)(2,1)S(1)}, u32[]{:S(2)}, u32[]{:S(2)}) collective-permute-start(bf16[8,4096]{1,0:T(8,128)(2,1)S(1)} %get-tuple-element.106), channel_id=1, source_target_pairs={{0,8},{2,10},{4,12},{6,14},{8,0},{10,2},{12,4},{14,6},{16,24},{18,... | collective-permute-start | bytes 196616 | tf_op jit(solution)/shard_map/ppermute | solution.py:38
  66.9 6.2 %collective-permute-start.19 = (bf16[8,4096]{1,0:T(8,128)(2,1)S(1)}, bf16[8,4096]{1,0:T(8,128)(2,1)S(1)}, u32[]{:S(2)}, u32[]{:S(2)}) collective-permute-start(bf16[8,4096]{1,0:T(8,128)(2,1)S(1)} %get-tuple-element.107), channel_id=1, source_target_pairs={{0,24},{2,26},{4,28},{6,30},{8,16},{10,18},{12,20},{14,22},{16,8},... | collective-permute-start | bytes 196616 | tf_op jit(solution)/shard_map/ppermute | solution.py:38

commit v18 on v15

--- a/solution.py
+++ b/solution.py
@@ -468,7 +468,8 @@
     for flip in flips[:-1]:
         y = jnp.concatenate([y, swap(y, "wide", wide, 2 * flip)], axis=0)
     x, down_w = lax.optimization_barrier((x, down_w))
-    x_pieces = [x, x_recv, swap(x, "wide", wide, 1), swap(x_recv, "wide", wide, 1)]
+    x = jnp.concatenate([x, x_recv], axis=0)
+    x_pieces = [x, swap(x, "wide", wide, 1)]
     y, _ = lax.optimization_barrier((y, x_recv))
     y_recv = swap(y, "wide", wide, 2 * flips[-1])
 

time: 72 us -> 72.3 us (level)
  Pallas kernels: 31.3 us -> 32.2 us
    pallas_call x3, Pallas kernels: 7.27 us -> 8.11 us  [fill(): pl.pallas_call(fill_body, out_shape=pltpu.VMEM((outer, inner, block, bloc...]
    ppermute x20 -> x19, starting transfers between devices: 27.4 us -> 27.1 us  [swap(): return lax.ppermute(array, axis, [(i, i ^ flip) for i in range(size)])]
    ppermute x20 -> x19, waiting for transfers between devices: 9.21 us -> 9.14 us  [swap(): return lax.ppermute(array, axis, [(i, i ^ flip) for i in range(size)])]
  transfers between devices with their start and end apart: 20 -> 19, of which waited for: 9 -> 9; matrix products, arithmetic and copies ran while one was open for 0% -> 0% of each run, Pallas kernels for 40% -> 41%
where the time goes in v18:
time: 72.3 us; the launch traced here: 71.6 us
  Pallas kernels  32.2 us (45%)
  starting transfers between devices  27.1 us (37%)
  waiting for transfers between devices  9.14 us (13%)
  between operations  2.2 us (3%)
  other arithmetic  0.89 us (1%)
    ppermute x19, starting transfers between devices, swap(): return lax.ppermute(array, axis, [(i, i ^ flip) for i in range(size)])  27.1 us
    ppermute x19, waiting for transfers between devices, swap(): return lax.ppermute(array, axis, [(i, i ^ flip) for i in range(size)])  9.14 us
    pallas_call x3, Pallas kernels, fill(): pl.pallas_call(fill_body, out_shape=pltpu.VMEM((outer, inner, block, bloc...  8.11 us
    pallas_call x2, Pallas kernels, gu_grads(): pl.pallas_call(functools.partial(gu_grad_body, first, len(before)), out_s...  8.01 us
    pallas_call x1, Pallas kernels, down_second(): pl.pallas_call(functools.partial(down_second_body, first), out_shape=(jax...  4.48 us
    pallas_call x1, Pallas kernels, d_hidden(): pl.pallas_call(functools.partial(d_hidden_body, group, len(y_pieces)), ou...  2.56 us
    pallas_call x1, Pallas kernels, d_tokens_parts(): pl.pallas_call(functools.partial(d_tokens_first_body, group), out_shape=(...  2.54 us
    pallas_call x2, Pallas kernels, gate_up(): pl.pallas_call(functools.partial(gate_up_body, half * f_blocks // 2), out...  2.5 us
  transfers between devices with their start and end apart: 19, of which 9 were waited for; matrix products, arithmetic and copies ran while one was open for 0% of the time, Pallas kernels for 41%

profile of v18, /device:TPU:0, one launch (start us, length us, event | category | flops | bytes accessed | tf_op | source)
XLA Modules:
  0.0 71.6 jit_solution(655406448182047535)
XLA Ops:
  0.6 4.1 %collective-permute-start = (bf16[8,4096]{1,0:T(8,128)(2,1)}, bf16[8,4096]{1,0:T(8,128)(2,1)S(1)}, u32[]{:S(2)}, u32[]{:S(2)}) collective-permute-start(bf16[8,4096]{1,0:T(8,128)(2,1)} %param.9), channel_id=1, source_target_pairs={{0,16},{2,18},{4,20},{6,22},{8,24},{10,26},{12,28},{14,30},{16,0},... | collective-permute-start | bytes 196616 | tf_op jit(solution)/shard_map/ppermute | solution.py:38
  6.0 2.4 %fill.3.refs_2_.refs_4_.gate_w = bf16[32,8,128,128]{3,2,1,0:T(8,128)(2,1)S(1)} custom-call(s32[1,1,192]{2,1,0:T(1,128)} %index.9, s32[1,1]{1,0:T(1,128)S(6)} %copy.20.count, bf16[1,1,192,128,128]{4,3,2,1,0:T(8,128)(2,1)} %source.3, s32[1,1]{1,0:T(1,128)S(6)} %copy.21.refs_0_.count), custom_call_target="tpu_custom_call" | custom-call | bytes 6291456 | tf_op jit(solution)/shard_map/fill/pallas_call | solution.py:92
  8.6 1.4 %collective-permute-start.1 = (bf16[16,4096]{1,0:T(8,128)(2,1)S(1)}, bf16[16,4096]{1,0:T(8,128)(2,1)S(1)}, u32[]{:S(2)}, u32[]{:S(2)}) collective-permute-start(bf16[16,4096]{1,0:T(8,128)(2,1)S(1)} %pad_maximum_fusion.3), channel_id=1, source_target_pairs={{0,8},{2,10},{4,12},{6,14},{8,0},{10,2},{12,4},{14,6},{16,24},{18,... | collective-permute-start | bytes 393224 | tf_op jit(solution)/shard_map/ppermute | solution.py:38
  10.0 2.4 %fill.4.refs_3_.refs_5_.up_w = bf16[32,8,128,128]{3,2,1,0:T(8,128)(2,1)S(1)} custom-call(s32[1,1,192]{2,1,0:T(1,128)} %index.9, s32[1,1]{1,0:T(1,128)S(6)} %copy.20.count, bf16[1,1,192,128,128]{4,3,2,1,0:T(8,128)(2,1)} %source.4), custom_call_target="tpu_custom_call" | custom-call | bytes 6291456 | tf_op jit(solution)/shard_map/fill/pallas_call | solution.py:92
  12.5 1.2 %collective-permute-done.1 = bf16[16,4096]{1,0:T(8,128)(2,1)S(1)} collective-permute-done((bf16[16,4096]{1,0:T(8,128)(2,1)S(1)}, bf16[16,4096]{1,0:T(8,128)(2,1)S(1)}, u32[]{:S(2)}, u32[]{:S(2)}) %collective-permute-start.1) | collective-permute-done | bytes 131104 | tf_op jit(solution)/shard_map/ppermute | solution.py:38
  13.7 1.9 %collective-permute-start.2 = (bf16[32,4096]{1,0:T(8,128)(2,1)S(1)}, bf16[32,4096]{1,0:T(8,128)(2,1)S(1)}, u32[]{:S(2)}, u32[]{:S(2)}) collective-permute-start(bf16[32,4096]{1,0:T(8,128)(2,1)S(1)} %pad_maximum_fusion.1), channel_id=1, source_target_pairs={{0,4},{2,6},{4,0},{6,2},{8,12},{10,14},{12,8},{14,10},{16,20},{18,... | collective-permute-start | bytes 786440 | tf_op jit(solution)/shard_map/ppermute | solution.py:38
  15.6 2.0 %collective-permute-start.5 = (bf16[8,4096]{1,0:T(8,128)(2,1)S(1)}, bf16[8,4096]{1,0:T(8,128)(2,1)S(1)}, u32[]{:S(2)}, u32[]{:S(2)}) collective-permute-start(bf16[8,4096]{1,0:T(8,128)(2,1)S(1)} %copy-done), channel_id=1, source_target_pairs={{0,16},{2,18},{4,20},{6,22},{8,24},{10,26},{12,28},{14,30},{16,0},... | collective-permute-start | bytes 196616 | tf_op jit(solution)/shard_map/ppermute | solution.py:38
  17.6 3.2 %fill.5.refs_6_ = bf16[8,32,128,128]{3,2,1,0:T(8,128)(2,1)S(1)} custom-call(s32[1,1,192]{2,1,0:T(1,128)} %index.7, s32[1,1]{1,0:T(1,128)S(6)} %copy.21.refs_0_.count, bf16[1,1,192,128,128]{4,3,2,1,0:T(8,128)(2,1)} %source.5), custom_call_target="tpu_custom_call" | custom-call | bytes 6291456 | tf_op jit(solution)/shard_map/fill/pallas_call | solution.py:92
  20.9 1.8 %collective-permute-start.6 = (bf16[16,4096]{1,0:T(8,128)(2,1)S(1)}, bf16[16,4096]{1,0:T(8,128)(2,1)S(1)}, u32[]{:S(2)}, u32[]{:S(2)}) collective-permute-start(bf16[16,4096]{1,0:T(8,128)(2,1)S(1)} %pad_maximum_fusion.4), channel_id=1, source_target_pairs={{0,8},{2,10},{4,12},{6,14},{8,0},{10,2},{12,4},{14,6},{16,24},{18,... | collective-permute-start | bytes 393224 | tf_op jit(solution)/shard_map/ppermute | solution.py:38
  22.8 3.1 %collective-permute-done.6 = bf16[16,4096]{1,0:T(8,128)(2,1)S(1)} collective-permute-done((bf16[16,4096]{1,0:T(8,128)(2,1)S(1)}, bf16[16,4096]{1,0:T(8,128)(2,1)S(1)}, u32[]{:S(2)}, u32[]{:S(2)}) %collective-permute-start.6) | collective-permute-done | bytes 131104 | tf_op jit(solution)/shard_map/ppermute | solution.py:38
  26.4 1.3 %gate_up.2 = (f32[4,128,256]{2,1,0:T(8,128)S(1)}, bf16[4,128,256]{2,1,0:T(8,128)(2,1)S(1)}) custom-call(bf16[64,4096]{1,0:T(8,128)(2,1)S(1)} %constant_dynamic-update-slice_fusion.refs_0_.refs_4_, bf16[64,4096]{1,0:T(8,128)(2,1)S(1)} %collective-permute-done.3.refs_1_.refs_5_, bf16[32,8,128,128]{3,2,1,0:T(8,128)(2,1)S(1)} %fill.3.refs_2_.refs_4_.gate_w, ...), custom_call_target="tpu_custom_call" | custom-call | flops 1073741824 | bytes 8388608 | tf_op jit(solution)/shard_map/gate_up/pallas_call | solution.py:129
  27.6 3.1 %collective-permute-start.4 = (bf16[4,128,256]{2,1,0:T(8,128)(2,1)S(1)}, bf16[4,128,256]{2,1,0:T(8,128)(2,1)S(1)}, u32[]{:S(2)}, u32[]{:S(2)}) collective-permute-start(bf16[4,128,256]{2,1,0:T(8,128)(2,1)S(1)} %get-tuple-element.68), channel_id=1, source_target_pairs={{0,1},{1,0},{2,3},{3,2},{4,5},{5,4},{6,7},{7,6},{8,9},{9,8},{10,11... | collective-permute-start | bytes 786440 | tf_op jit(solution)/shard_map/ppermute | solution.py:38
  30.8 1.2 %gate_up.3 = (f32[4,128,256]{2,1,0:T(8,128)S(1)}, bf16[4,128,256]{2,1,0:T(8,128)(2,1)S(1)}) custom-call(bf16[64,4096]{1,0:T(8,128)(2,1)S(1)} %constant_dynamic-update-slice_fusion.refs_0_.refs_4_, bf16[64,4096]{1,0:T(8,128)(2,1)S(1)} %collective-permute-done.3.refs_1_.refs_5_, bf16[32,8,128,128]{3,2,1,0:T(8,128)(2,1)S(1)} %fill.3.refs_2_.refs_4_.gate_w, ...), custom_call_target="tpu_custom_call" | custom-call | flops 1073741824 | bytes 8388608 | tf_op jit(solution)/shard_map/gate_up/pallas_call | solution.py:129
  32.4 0.5 collective-permute-start.9
  32.9 1.9 %collective-permute-start.10 = (bf16[4,128,256]{2,1,0:T(8,128)(2,1)S(1)}, bf16[4,128,256]{2,1,0:T(8,128)(2,1)S(1)}, u32[]{:S(2)}, u32[]{:S(2)}) collective-permute-start(bf16[4,128,256]{2,1,0:T(8,128)(2,1)S(1)} %get-tuple-element.77), channel_id=1, source_target_pairs={{0,1},{1,0},{2,3},{3,2},{4,5},{5,4},{6,7},{7,6},{8,9},{9,8},{10,11... | collective-permute-start | bytes 786440 | tf_op jit(solution)/shard_map/ppermute | solution.py:38
  35.3 2.6 %d_hidden.1 = (f32[8,128,128]{2,1,0:T(8,128)S(1)}, bf16[8,128,128]{2,1,0:T(8,128)(2,1)S(1)}, bf16[32,128,128]{2,1,0:T(8,128)(2,1)S(1)}) custom-call(bf16[32,4096]{1,0:T(8,128)(2,1)S(1)} %pad_maximum_fusion.2.refs_0_, bf16[32,4096]{1,0:T(8,128)(2,1)S(1)} %collective-permute-done.7.refs_1_, bf16[32,4096]{1,0:T(8,128)(2,1)S(1)} %collective-permute-done.8.refs_2_, ...), custom_call_target="tpu_custom_call" | custom-call | flops 1073741824 | bytes 8388608 | tf_op jit(solution)/shard_map/d_hidden/pallas_call | solution.py:171
  37.8 2.1 %collective-permute-start.11 = (bf16[8,128,128]{2,1,0:T(8,128)(2,1)S(1)}, bf16[8,128,128]{2,1,0:T(8,128)(2,1)S(1)}, u32[]{:S(2)}, u32[]{:S(2)}) collective-permute-start(bf16[8,128,128]{2,1,0:T(8,128)(2,1)S(1)} %get-tuple-element.93), channel_id=1, source_target_pairs={{0,1},{1,0},{2,3},{3,2},{4,5},{5,4},{6,7},{7,6},{8,9},{9,8},{10,11... | collective-permute-start | bytes 786440 | tf_op jit(solution)/shard_map/ppermute | solution.py:38
  39.9 1.3 %down_first.1._ = bf16[257,128,128]{2,1,0:T(8,128)(2,1)S(1)} custom-call(bf16[4,128,128]{2,1,0:T(8,128)(2,1)S(1)} %get-tuple-element.74.hidden, bf16[32,4096]{1,0:T(8,128)(2,1)S(1)} %pad_maximum_fusion.2.refs_0_, bf16[32,4096]{1,0:T(8,128)(2,1)S(1)} %collective-permute-done.7.refs_1_, bf16[32,4096]{1,0:T(8,128)(2,1)S(1)} %collective-permute-done.8.refs_2_, ...), custom_call_target="tpu_custom_call" | custom-call | flops 538968064 | bytes 8421376 | tf_op jit(solution)/shard_map/down_first/pallas_call | solution.py:402
  41.2 0.8 %collective-permute-done.10.refs_1_ = bf16[4,128,256]{2,1,0:T(8,128)(2,1)S(1)} collective-permute-done((bf16[4,128,256]{2,1,0:T(8,128)(2,1)S(1)}, bf16[4,128,256]{2,1,0:T(8,128)(2,1)S(1)}, u32[]{:S(2)}, u32[]{:S(2)}) %collective-permute-start.10) | collective-permute-done | bytes 262176 | tf_op jit(solution)/shard_map/ppermute | solution.py:38
  42.2 4.5 %down_second.1 = (bf16[192,128,128]{2,1,0:T(8,128)(2,1)}, bf16[257,128,128]{2,1,0:T(8,128)(2,1)S(1)}) custom-call(s32[1,1,192]{2,1,0:T(1,128)} %index.7, s32[1,1]{1,0:T(1,128)S(6)} %copy.21.refs_0_.count, bf16[4,128,128]{2,1,0:T(8,128)(2,1)S(1)} %get-tuple-element.87.hidden, ...), custom_call_target="tpu_custom_call", output_to_operand_aliasing={{1}: (3, {})} | custom-call | flops 402653184 | bytes 6291456 | tf_op jit(solution)/shard_map/down_second/pallas_call | solution.py:418
  46.8 2.5 %d_tokens_first.1 = (f32[64,2048]{1,0:T(8,128)S(1)}, bf16[64,2048]{1,0:T(8,128)(2,1)S(1)}, bf16[8,128,256]{2,1,0:T(8,128)(2,1)S(1)}, bf16[2048,128]{1,0:T(8,128)(2,1)S(1)}) custom-call(f32[4,128,256]{2,1,0:T(8,128)S(1)} %get-tuple-element.69.refs_0_, f32[4,128,256]{2,1,0:T(8,128)S(1)} %get-tuple-element.91.refs_1_, ...), custom_call_target="tpu_custom_call" | custom-call | flops 1073741824 | bytes 8388608 | tf_op jit(solution)/shard_map/d_tokens_first/pallas_call | solution.py:240
  49.4 2.4 %d_tokens_second.1 = (f32[64,2048]{1,0:T(8,128)S(1)}, bf16[64,2048]{1,0:T(8,128)(2,1)S(1)}) custom-call(bf16[2048,128]{1,0:T(8,128)(2,1)S(1)} %get-tuple-element.96.turned, bf16[32,8,128,128]{3,2,1,0:T(8,128)(2,1)S(1)} %fill.3.refs_2_.refs_4_.gate_w, bf16[32,8,128,128]{3,2,1,0:T(8,128)(2,1)S(1)} %fill.4.refs_3_.refs_5_.up_w), custom_call_target="tpu_custom_call" | custom-call | flops 1073741824 | bytes 8388608 | tf_op jit(solution)/shard_map/d_tokens_second/pallas_call | solution.py:252
  51.9 0.6 collective-permute-start.14
  52.5 1.7 %collective-permute-start.13 = (bf16[32,2048]{1,0:T(8,128)(2,1)S(1)}, bf16[32,2048]{1,0:T(8,128)(2,1)S(1)}, u32[]{:S(2)}, u32[]{:S(2)}) collective-permute-start(bf16[32,2048]{1,0:T(8,128)(2,1)S(1)} %slice.65), channel_id=1, source_target_pairs={{0,4},{2,6},{4,0},{6,2},{8,12},{10,14},{12,8},{14,10},{16,20},{18,... | collective-permute-start | bytes 393224 | tf_op jit(solution)/shard_map/ppermute | solution.py:38
  54.2 1.1 %collective-permute-start.15 = (bf16[32,2048]{1,0:T(8,128)(2,1)S(1)}, bf16[32,2048]{1,0:T(8,128)(2,1)S(1)}, u32[]{:S(2)}, u32[]{:S(2)}) collective-permute-start(bf16[32,2048]{1,0:T(8,128)(2,1)S(1)} %slice.64), channel_id=1, source_target_pairs={{0,4},{2,6},{4,0},{6,2},{8,12},{10,14},{12,8},{14,10},{16,20},{18,... | collective-permute-start | bytes 393224 | tf_op jit(solution)/shard_map/ppermute | solution.py:38
  55.3 5.0 %gu_grads.2 = (bf16[192,128,128]{2,1,0:T(8,128)(2,1)}, bf16[192,128,128]{2,1,0:T(8,128)(2,1)}) custom-call(s32[1,1,192]{2,1,0:T(1,128)} %index.9, s32[1,1]{1,0:T(1,128)S(6)} %copy.20.count, bf16[8,128,256]{2,1,0:T(8,128)(2,1)S(1)} %get-tuple-element.108.d_pair, bf16[32,128,128]{2,1,0:T(8,128)(2,1)S(1)} %get-tuple-element.102.turned), custom_call_target="tpu_custom_call" | custom-call | flops 1073741824 | bytes 8388608 | tf_op jit(solution)/shard_map/gu_grads/pallas_call | solution.py:313
  60.9 2.0 %collective-permute-start.16 = (bf16[8,4096]{1,0:T(8,128)(2,1)S(1)}, bf16[8,4096]{1,0:T(8,128)(2,1)S(1)}, u32[]{:S(2)}, u32[]{:S(2)}) collective-permute-start(bf16[8,4096]{1,0:T(8,128)(2,1)S(1)} %get-tuple-element.105), channel_id=1, source_target_pairs={{0,16},{2,18},{4,20},{6,22},{8,24},{10,26},{12,28},{14,30},{16,0},... | collective-permute-start | bytes 196616 | tf_op jit(solution)/shard_map/ppermute | solution.py:38
  62.9 2.0 %collective-permute-start.17 = (bf16[8,4096]{1,0:T(8,128)(2,1)S(1)}, bf16[8,4096]{1,0:T(8,128)(2,1)S(1)}, u32[]{:S(2)}, u32[]{:S(2)}) collective-permute-start(bf16[8,4096]{1,0:T(8,128)(2,1)S(1)} %get-tuple-element.106), channel_id=1, source_target_pairs={{0,8},{2,10},{4,12},{6,14},{8,0},{10,2},{12,4},{14,6},{16,24},{18,... | collective-permute-start | bytes 196616 | tf_op jit(solution)/shard_map/ppermute | solution.py:38
  64.9 0.5 collective-permute-start.18
  65.4 3.0 %gu_grads.3 = (bf16[192,128,128]{2,1,0:T(8,128)(2,1)}, bf16[192,128,128]{2,1,0:T(8,128)(2,1)}) custom-call(s32[1,1,192]{2,1,0:T(1,128)} %index.9, s32[1,1]{1,0:T(1,128)S(6)} %copy.20.count, bf16[8,128,256]{2,1,0:T(8,128)(2,1)S(1)} %get-tuple-element.108.d_pair, ...), custom_call_target="tpu_custom_call", output_to_operand_aliasing={{0}: (4, {}), {1}: (5, {})} | custom-call | flops 536870912 | bytes 4194304 | tf_op jit(solution)/shard_map/gu_grads/pallas_call | solution.py:313
  68.4 2.6 %collective-permute-done.18 = bf16[8,4096]{1,0:T(8,128)(2,1)S(1)} collective-permute-done((bf16[8,4096]{1,0:T(8,128)(2,1)S(1)}, bf16[8,4096]{1,0:T(8,128)(2,1)S(1)}, u32[]{:S(2)}, u32[]{:S(2)}) %collective-permute-start.18) | collective-permute-done | bytes 65568 | tf_op jit(solution)/shard_map/ppermute | solution.py:38
  71.0 0.7 fusion.5
  (39 shorter events, 2.6 us)
Async XLA Ops:
  0.6 8.0 %collective-permute-start = (bf16[8,4096]{1,0:T(8,128)(2,1)}, bf16[8,4096]{1,0:T(8,128)(2,1)S(1)}, u32[]{:S(2)}, u32[]{:S(2)}) collective-permute-start(bf16[8,4096]{1,0:T(8,128)(2,1)} %param.9), channel_id=1, source_target_pairs={{0,16},{2,18},{4,20},{6,22},{8,24},{10,26},{12,28},{14,30},{16,0},... | collective-permute-start | bytes 196616 | tf_op jit(solution)/shard_map/ppermute | solution.py:38
  6.0 2.6 %copy-start.1 = (bf16[8,4096]{1,0:T(8,128)(2,1)S(1)}, bf16[8,4096]{1,0:T(8,128)(2,1)}, u32[]{:S(2)}) copy-start(bf16[8,4096]{1,0:T(8,128)(2,1)} %param.9) | copy-start | bytes 196612
  8.6 7.0 %copy-start = (bf16[8,4096]{1,0:T(8,128)(2,1)S(1)}, bf16[8,4096]{1,0:T(8,128)(2,1)}, u32[]{:S(2)}) copy-start(bf16[8,4096]{1,0:T(8,128)(2,1)} %param.10) | copy-start | bytes 196612
  8.6 5.0 %collective-permute-start.1 = (bf16[16,4096]{1,0:T(8,128)(2,1)S(1)}, bf16[16,4096]{1,0:T(8,128)(2,1)S(1)}, u32[]{:S(2)}, u32[]{:S(2)}) collective-permute-start(bf16[16,4096]{1,0:T(8,128)(2,1)S(1)} %pad_maximum_fusion.3), channel_id=1, source_target_pairs={{0,8},{2,10},{4,12},{6,14},{8,0},{10,2},{12,4},{14,6},{16,24},{18,... | collective-permute-start | bytes 393224 | tf_op jit(solution)/shard_map/ppermute | solution.py:38
  13.7 9.0 %collective-permute-start.2 = (bf16[32,4096]{1,0:T(8,128)(2,1)S(1)}, bf16[32,4096]{1,0:T(8,128)(2,1)S(1)}, u32[]{:S(2)}, u32[]{:S(2)}) collective-permute-start(bf16[32,4096]{1,0:T(8,128)(2,1)S(1)} %pad_maximum_fusion.1), channel_id=1, source_target_pairs={{0,4},{2,6},{4,0},{6,2},{8,12},{10,14},{12,8},{14,10},{16,20},{18,... | collective-permute-start | bytes 786440 | tf_op jit(solution)/shard_map/ppermute | solution.py:38
  15.6 5.3 %collective-permute-start.5 = (bf16[8,4096]{1,0:T(8,128)(2,1)S(1)}, bf16[8,4096]{1,0:T(8,128)(2,1)S(1)}, u32[]{:S(2)}, u32[]{:S(2)}) collective-permute-start(bf16[8,4096]{1,0:T(8,128)(2,1)S(1)} %copy-done), channel_id=1, source_target_pairs={{0,16},{2,18},{4,20},{6,22},{8,24},{10,26},{12,28},{14,30},{16,0},... | collective-permute-start | bytes 196616 | tf_op jit(solution)/shard_map/ppermute | solution.py:38
  20.9 5.0 %collective-permute-start.6 = (bf16[16,4096]{1,0:T(8,128)(2,1)S(1)}, bf16[16,4096]{1,0:T(8,128)(2,1)S(1)}, u32[]{:S(2)}, u32[]{:S(2)}) collective-permute-start(bf16[16,4096]{1,0:T(8,128)(2,1)S(1)} %pad_maximum_fusion.4), channel_id=1, source_target_pairs={{0,8},{2,10},{4,12},{6,14},{8,0},{10,2},{12,4},{14,6},{16,24},{18,... | collective-permute-start | bytes 393224 | tf_op jit(solution)/shard_map/ppermute | solution.py:38
  22.7 3.7 %collective-permute-start.3 = (bf16[64,4096]{1,0:T(8,128)(2,1)S(1)}, bf16[64,4096]{1,0:T(8,128)(2,1)S(1)}, u32[]{:S(2)}, u32[]{:S(2)}) collective-permute-start(bf16[64,4096]{1,0:T(8,128)(2,1)S(1)} %constant_dynamic-update-slice_fusion.refs_0_.refs_4_), channel_id=1, source_target_pairs={{0,2},{2,0},{4,6},{6,4},{8,10},{10,8},{12,14},{14,12},{16,18},{18,... | collective-permute-start | bytes 1572872 | tf_op jit(solution)/shard_map/ppermute | solution.py:38
  25.9 6.4 %collective-permute-start.7 = (bf16[32,4096]{1,0:T(8,128)(2,1)S(1)}, bf16[32,4096]{1,0:T(8,128)(2,1)S(1)}, u32[]{:S(2)}, u32[]{:S(2)}) collective-permute-start(bf16[32,4096]{1,0:T(8,128)(2,1)S(1)} %pad_maximum_fusion.2.refs_0_), channel_id=1, source_target_pairs={{0,4},{2,6},{4,0},{6,2},{8,12},{10,14},{12,8},{14,10},{16,20},{18,... | collective-permute-start | bytes 786440 | tf_op jit(solution)/shard_map/ppermute | solution.py:38
  27.6 7.5 %collective-permute-start.4 = (bf16[4,128,256]{2,1,0:T(8,128)(2,1)S(1)}, bf16[4,128,256]{2,1,0:T(8,128)(2,1)S(1)}, u32[]{:S(2)}, u32[]{:S(2)}) collective-permute-start(bf16[4,128,256]{2,1,0:T(8,128)(2,1)S(1)} %get-tuple-element.68), channel_id=1, source_target_pairs={{0,1},{1,0},{2,3},{3,2},{4,5},{5,4},{6,7},{7,6},{8,9},{9,8},{10,11... | collective-permute-start | bytes 786440 | tf_op jit(solution)/shard_map/ppermute | solution.py:38
  32.4 2.9 %collective-permute-start.8 = (bf16[32,4096]{1,0:T(8,128)(2,1)S(1)}, bf16[32,4096]{1,0:T(8,128)(2,1)S(1)}, u32[]{:S(2)}, u32[]{:S(2)}) collective-permute-start(bf16[32,4096]{1,0:T(8,128)(2,1)S(1)} %pad_maximum_fusion.2.refs_0_), channel_id=1, source_target_pairs={{0,2},{2,0},{4,6},{6,4},{8,10},{10,8},{12,14},{14,12},{16,18},{18,... | collective-permute-start | bytes 786440 | tf_op jit(solution)/shard_map/ppermute | solution.py:38
  32.4 2.9 %collective-permute-start.9 = (bf16[32,4096]{1,0:T(8,128)(2,1)S(1)}, bf16[32,4096]{1,0:T(8,128)(2,1)S(1)}, u32[]{:S(2)}, u32[]{:S(2)}) collective-permute-start(bf16[32,4096]{1,0:T(8,128)(2,1)S(1)} %collective-permute-done.7.refs_1_), channel_id=1, source_target_pairs={{0,2},{2,0},{4,6},{6,4},{8,10},{10,8},{12,14},{14,12},{16,18},{18,... | collective-permute-start | bytes 786440 | tf_op jit(solution)/shard_map/ppermute | solution.py:38
  32.9 9.2 %collective-permute-start.10 = (bf16[4,128,256]{2,1,0:T(8,128)(2,1)S(1)}, bf16[4,128,256]{2,1,0:T(8,128)(2,1)S(1)}, u32[]{:S(2)}, u32[]{:S(2)}) collective-permute-start(bf16[4,128,256]{2,1,0:T(8,128)(2,1)S(1)} %get-tuple-element.77), channel_id=1, source_target_pairs={{0,1},{1,0},{2,3},{3,2},{4,5},{5,4},{6,7},{7,6},{8,9},{9,8},{10,11... | collective-permute-start | bytes 786440 | tf_op jit(solution)/shard_map/ppermute | solution.py:38
  37.8 9.0 %collective-permute-start.11 = (bf16[8,128,128]{2,1,0:T(8,128)(2,1)S(1)}, bf16[8,128,128]{2,1,0:T(8,128)(2,1)S(1)}, u32[]{:S(2)}, u32[]{:S(2)}) collective-permute-start(bf16[8,128,128]{2,1,0:T(8,128)(2,1)S(1)} %get-tuple-element.93), channel_id=1, source_target_pairs={{0,1},{1,0},{2,3},{3,2},{4,5},{5,4},{6,7},{7,6},{8,9},{9,8},{10,11... | collective-permute-start | bytes 786440 | tf_op jit(solution)/shard_map/ppermute | solution.py:38
  49.4 3.1 %collective-permute-start.12 = (bf16[64,2048]{1,0:T(8,128)(2,1)S(1)}, bf16[64,2048]{1,0:T(8,128)(2,1)S(1)}, u32[]{:S(2)}, u32[]{:S(2)}) collective-permute-start(bf16[64,2048]{1,0:T(8,128)(2,1)S(1)} %get-tuple-element.95), channel_id=1, source_target_pairs={{0,2},{2,0},{4,6},{6,4},{8,10},{10,8},{12,14},{14,12},{16,18},{18,... | collective-permute-start | bytes 786440 | tf_op jit(solution)/shard_map/ppermute | solution.py:38
  51.9 2.3 %collective-permute-start.14 = (bf16[64,2048]{1,0:T(8,128)(2,1)S(1)}, bf16[64,2048]{1,0:T(8,128)(2,1)S(1)}, u32[]{:S(2)}, u32[]{:S(2)}) collective-permute-start(bf16[64,2048]{1,0:T(8,128)(2,1)S(1)} %get-tuple-element.98), channel_id=1, source_target_pairs={{0,2},{2,0},{4,6},{6,4},{8,10},{10,8},{12,14},{14,12},{16,18},{18,... | collective-permute-start | bytes 786440 | tf_op jit(solution)/shard_map/ppermute | solution.py:38
  52.5 7.9 %collective-permute-start.13 = (bf16[32,2048]{1,0:T(8,128)(2,1)S(1)}, bf16[32,2048]{1,0:T(8,128)(2,1)S(1)}, u32[]{:S(2)}, u32[]{:S(2)}) collective-permute-start(bf16[32,2048]{1,0:T(8,128)(2,1)S(1)} %slice.65), channel_id=1, source_target_pairs={{0,4},{2,6},{4,0},{6,2},{8,12},{10,14},{12,8},{14,10},{16,20},{18,... | collective-permute-start | bytes 393224 | tf_op jit(solution)/shard_map/ppermute | solution.py:38
  54.2 6.6 %collective-permute-start.15 = (bf16[32,2048]{1,0:T(8,128)(2,1)S(1)}, bf16[32,2048]{1,0:T(8,128)(2,1)S(1)}, u32[]{:S(2)}, u32[]{:S(2)}) collective-permute-start(bf16[32,2048]{1,0:T(8,128)(2,1)S(1)} %slice.64), channel_id=1, source_target_pairs={{0,4},{2,6},{4,0},{6,2},{8,12},{10,14},{12,8},{14,10},{16,20},{18,... | collective-permute-start | bytes 393224 | tf_op jit(solution)/shard_map/ppermute | solution.py:38
  60.9 7.5 %collective-permute-start.16 = (bf16[8,4096]{1,0:T(8,128)(2,1)S(1)}, bf16[8,4096]{1,0:T(8,128)(2,1)S(1)}, u32[]{:S(2)}, u32[]{:S(2)}) collective-permute-start(bf16[8,4096]{1,0:T(8,128)(2,1)S(1)} %get-tuple-element.105), channel_id=1, source_target_pairs={{0,16},{2,18},{4,20},{6,22},{8,24},{10,26},{12,28},{14,30},{16,0},... | collective-permute-start | bytes 196616 | tf_op jit(solution)/shard_map/ppermute | solution.py:38
  62.9 5.5 %collective-permute-start.17 = (bf16[8,4096]{1,0:T(8,128)(2,1)S(1)}, bf16[8,4096]{1,0:T(8,128)(2,1)S(1)}, u32[]{:S(2)}, u32[]{:S(2)}) collective-permute-start(bf16[8,4096]{1,0:T(8,128)(2,1)S(1)} %get-tuple-element.106), channel_id=1, source_target_pairs={{0,8},{2,10},{4,12},{6,14},{8,0},{10,2},{12,4},{14,6},{16,24},{18,... | collective-permute-start | bytes 196616 | tf_op jit(solution)/shard_map/ppermute | solution.py:38
  64.9 6.1 %collective-permute-start.18 = (bf16[8,4096]{1,0:T(8,128)(2,1)S(1)}, bf16[8,4096]{1,0:T(8,128)(2,1)S(1)}, u32[]{:S(2)}, u32[]{:S(2)}) collective-permute-start(bf16[8,4096]{1,0:T(8,128)(2,1)S(1)} %get-tuple-element.107), channel_id=1, source_target_pairs={{0,24},{2,26},{4,28},{6,30},{8,16},{10,18},{12,20},{14,22},{16,8},... | collective-permute-start | bytes 196616 | tf_op jit(solution)/shard_map/ppermute | solution.py:38
